TPU v7x, 32 devices: a whole 2x2x4 slice. The times are simulated.
32 devices in a mesh: seq: 8 (over z, core), head: 4 (over y, x).
Axes of the slice: x: 2, y: 2, z: 4, core: 2. Of those that a mesh axis runs over, the one named last changes fastest.
Arguments:
- queries: bfloat16 [24576, 8, 128], P('seq', 'head'), may hold values from -6 to 6
- keys: bfloat16 [24576, 8, 128], P('seq', 'head'), may hold values from -6 to 6
- values: bfloat16 [24576, 8, 128], P('seq', 'head'), may hold values from -60 to 60
- cotangent: bfloat16 [24576, 8, 128], P('seq', 'head'), may hold values from -6 to 6
- doc_lengths: int32 [6], replicated, may hold values from 1 to 18432, 24576 in all
Outputs:
- output: bfloat16 [24576, 8, 128], P('seq', 'head')
- grad_queries: bfloat16 [24576, 8, 128], P('seq', 'head')
- grad_keys: bfloat16 [24576, 8, 128], P('seq', 'head')
- grad_values: bfloat16 [24576, 8, 128], P('seq', 'head')
All inputs are finite; a program needn't handle non-finite values.
Results may differ from a plain program's by a relative error of at most 0.0058.
Values sent between devices are 32-bit elements; how exact they have to be, the bound alone decides.
No kernel may reach another device: no remote copies, remote signals or barrier semaphores. Data moves between devices by JAX's collectives and lax.ppermute only.
A program may use at most 128 MiB of HBM per device.

v0:
```python
import jax
import jax.numpy as jnp
from jax import lax
from jax.sharding import PartitionSpec as P

GROUP = 256


EPSILON = 1e-06


def segment_of(places, doc_ends):
    return jnp.sum((doc_ends[None, :] <= places[:, None]).astype(jnp.int32), axis=1)


def group_prefix(running, inputs):
    added, keeping = inputs
    return (jnp.where(keeping, running, 0.0) + added, running)


def per_device(queries, keys, values, cotangent, doc_lengths):
    tokens_here, heads_here, head_width = queries.shape
    n_groups = tokens_here // GROUP
    device_index = lax.axis_index("seq")
    width_all = float(heads_here * lax.axis_size("head") * head_width)
    doc_ends = jnp.cumsum(doc_lengths)
    anchor = device_index * tokens_here
    positions = anchor + jnp.arange(tokens_here, dtype=jnp.int32)
    segment = segment_of(positions, doc_ends).reshape(n_groups, GROUP)
    group_first = anchor + jnp.arange(n_groups, dtype=jnp.int32) * GROUP
    before_group = segment_of(group_first - 1, doc_ends)
    after_group = segment_of(group_first + GROUP, doc_ends)
    edges = segment_of(jnp.stack([anchor - 1, anchor + tokens_here]), doc_ends)
    before_shard = edges[0]
    after_shard = edges[1]

    def blocks(array):
        return array.reshape(n_groups, GROUP, heads_here, head_width)

    query_blocks = blocks(queries)
    key_blocks = blocks(keys)
    value_blocks = blocks(values)
    grad_blocks = blocks(cotangent)
    causal = jnp.arange(GROUP)[:, None] >= jnp.arange(GROUP)[None, :]
    within = causal[None] & (segment[:, :, None] == segment[:, None, :])
    scores = jnp.einsum(
        "nthd,nshd->nhts", query_blocks, key_blocks, preferred_element_type=jnp.float32
    )
    probs = jnp.where(within[:, None], scores, 0.0).astype(jnp.bfloat16)
    mixed = jnp.einsum("nhts,nshd->nthd", probs, value_blocks, preferred_element_type=jnp.float32)
    tail = (segment == segment[:, -1:]).astype(jnp.bfloat16)[:, :, None, None]
    group_sums = jnp.einsum(
        "nthi,nthj->nhij", key_blocks * tail, value_blocks, preferred_element_type=jnp.float32
    )
    keep_forward = segment[:, -1] == before_group
    zero_state = jnp.zeros((heads_here, head_width, head_width), jnp.float32)
    shard_state, local_states = lax.scan(group_prefix, zero_state, (group_sums, keep_forward))
    portion = lax.all_gather(shard_state[None], "seq", axis=0, tiled=True)
    owners = jnp.arange(portion.shape[0], dtype=jnp.int32)
    closing_seg = segment_of((owners + 1) * tokens_here - 1, doc_ends)
    weight = ((owners < device_index) & (closing_seg == before_shard)).astype(jnp.float32)
    remote_state = jnp.sum(weight[:, None, None, None] * portion, axis=0)
    local_bf = local_states.astype(jnp.bfloat16)
    remote_bf = remote_state.astype(jnp.bfloat16)
    gate_local = (segment == before_group[:, None]).astype(jnp.float32)[:, :, None, None]
    gate_remote = (segment == before_shard).astype(jnp.float32)[:, :, None, None]
    mixed = mixed + gate_local * jnp.einsum(
        "nthi,nhij->nthj", query_blocks, local_bf, preferred_element_type=jnp.float32
    )
    mixed = mixed + gate_remote * jnp.einsum(
        "nthi,hij->nthj", query_blocks, remote_bf, preferred_element_type=jnp.float32
    )
    squares = jnp.sum(mixed * mixed, axis=(2, 3))
    grad_in = grad_blocks.astype(jnp.float32)
    total_squares = lax.psum(squares, "head")
    root = jnp.sqrt(total_squares / width_all + EPSILON)
    normed = mixed / root[:, :, None, None]
    centre = lax.psum(jnp.sum(grad_in * normed, axis=(2, 3)), "head") / width_all
    output = normed.astype(jnp.bfloat16).reshape(tokens_here, heads_here, head_width)
    grad_mixed = ((grad_in - normed * centre[:, :, None, None]) / root[:, :, None, None]).astype(
        jnp.bfloat16
    )
    grad_probs = jnp.where(
        within[:, None],
        jnp.einsum("nthd,nshd->nhts", grad_mixed, value_blocks, preferred_element_type=jnp.float32),
        0.0,
    ).astype(jnp.bfloat16)
    grad_query = jnp.einsum(
        "nhts,nshd->nthd", grad_probs, key_blocks, preferred_element_type=jnp.float32
    )
    grad_query = grad_query + gate_local * jnp.einsum(
        "nthj,nhij->nthi", grad_mixed, local_bf, preferred_element_type=jnp.float32
    )
    grad_query = grad_query + gate_remote * jnp.einsum(
        "nthj,hij->nthi", grad_mixed, remote_bf, preferred_element_type=jnp.float32
    )
    head_part = (segment == segment[:, :1]).astype(jnp.bfloat16)[:, :, None, None]
    group_back = jnp.einsum(
        "nthi,nthj->nhij", query_blocks * head_part, grad_mixed, preferred_element_type=jnp.float32
    )
    keep_backward = segment[:, 0] == after_group
    shard_back, local_back = lax.scan(
        group_prefix, zero_state, (group_back, keep_backward), reverse=True
    )
    portion = lax.all_gather(shard_back[None], "seq", axis=0, tiled=True)
    owners = jnp.arange(portion.shape[0], dtype=jnp.int32)
    opening_seg = segment_of(owners * tokens_here, doc_ends)
    weight = ((owners > device_index) & (opening_seg == after_shard)).astype(jnp.float32)
    remote_back = jnp.sum(weight[:, None, None, None] * portion, axis=0)
    back_local_bf = local_back.astype(jnp.bfloat16)
    back_remote_bf = remote_back.astype(jnp.bfloat16)
    later_local = (segment == after_group[:, None]).astype(jnp.float32)[:, :, None, None]
    later_remote = (segment == after_shard).astype(jnp.float32)[:, :, None, None]
    grad_key = jnp.einsum(
        "nhts,nthd->nshd", grad_probs, query_blocks, preferred_element_type=jnp.float32
    )
    grad_key = grad_key + later_local * jnp.einsum(
        "nshj,nhij->nshi", value_blocks, back_local_bf, preferred_element_type=jnp.float32
    )
    grad_key = grad_key + later_remote * jnp.einsum(
        "nshj,hij->nshi", value_blocks, back_remote_bf, preferred_element_type=jnp.float32
    )
    grad_value = jnp.einsum(
        "nhts,nthd->nshd", probs, grad_mixed, preferred_element_type=jnp.float32
    )
    grad_value = grad_value + later_local * jnp.einsum(
        "nshi,nhij->nshj", key_blocks, back_local_bf, preferred_element_type=jnp.float32
    )
    grad_value = grad_value + later_remote * jnp.einsum(
        "nshi,hij->nshj", key_blocks, back_remote_bf, preferred_element_type=jnp.float32
    )
    shape = (tokens_here, heads_here, head_width)
    return (
        output,
        grad_query.astype(jnp.bfloat16).reshape(shape),
        grad_key.astype(jnp.bfloat16).reshape(shape),
        grad_value.astype(jnp.bfloat16).reshape(shape),
    )


def solution(mesh):
    return jax.shard_map(
        per_device,
        mesh=mesh,
        in_specs=(
            P("seq", "head", None),
            P("seq", "head", None),
            P("seq", "head", None),
            P("seq", "head", None),
            P(),
        ),
        out_specs=(
            P("seq", "head", None),
            P("seq", "head", None),
            P("seq", "head", None),
            P("seq", "head", None),
        ),
        check_vma=False,
    )
```

profile of v0, /device:TPU:0, one launch (start us, length us, event | category | flops | bytes accessed | tf_op | source)
XLA Modules:
  0.0 243.7 jit_solution(1651689886152906568)
XLA Ops:
  9.3 3.5 %copy.177 = bf16[12,256,2,128]{1,3,2,0:T(8,128)(2,1)S(1)} copy(bf16[12,256,2,128]{3,2,1,0:T(2,128)(2,1)} %bitcast.117) | data formatting | bytes 3145728 | tf_op jit(solution)/shard_map/reshape | solution.py:38
  14.3 1.7 fusion.5
  17.1 34.0 %while.30 = (s32[]{:T(128)}, f32[2,128,128]{2,1,0:T(8,128)S(1)}, bf16[12,2,128,128]{3,2,1,0:T(8,128)(2,1)}, pred[12]{0:T(512)(128)(4,1)S(1)}, f32[12,2,128,128]{3,2,1,0:T(8,128)}, /*index=5*/s32[]{:T(128)}, s32[]{:T(128)}) while((s32[]{:T(128)}, f32[2,128,128]{2,1,0:T(8,128)S(1)}, bf16[12,2,128,128]{3,2,1,0:T(8,128)(2,1)}, ...), condition=%wide.region_4.5_spmd.clone, body=%wide.region_3.4_spmd.clone.sunk | while | flops 131075 | bytes 590435 | solution.py:57
  51.8 4.8 %copy.197 = bf16[12,256,2,128]{1,3,2,0:T(8,128)(2,1)} copy(bf16[12,256,2,128]{3,2,1,0:T(2,128)(2,1)} %bitcast.118) | data formatting | bytes 3145728 | tf_op jit(solution)/shard_map/reshape | solution.py:38
  56.7 2.9 %copy.186 = bf16[3072,2,128]{2,0,1:T(8,128)(2,1)} copy(bf16[3072,2,128]{2,1,0:T(2,128)(2,1)} %param.12) | data formatting | bytes 3145728 | tf_op args[3]
  64.5 2.7 %fusion.12 = f32[12,2,256,128]{3,2,1,0:T(8,128)} fusion(bf16[12,2,256,256]{3,2,1,0:T(8,128)(2,1)S(1)} %select_convert_fusion.1, bf16[12,256,2,128]{3,2,1,0:T(2,128)(2,1)S(1)} %bitcast.106), kind=kOutput, calls=%fused_computation.32 | convolution fusion | flops 402653184 | bytes 7864320 | tf_op jit(solution)/shard_map/nhts,nshd->nthd/dot_general | solution.py:50
  67.2 9.5 %all-gather.5.cloned.1.call-done = f32[16,128,128]{2,1,0:T(8,128)} async-done(((f32[2,128,128]{2,1,0:T(8,128)}), f32[16,128,128]{2,1,0:T(8,128)}) %all-gather.5.cloned.1.call-update) | async-done | bytes 1048592 | tf_op jit(solution)/shard_map/all_gather | solution.py:58
  78.2 2.3 fusion.25
  81.0 3.1 %multiply_reduce_fusion.1 = (f32[12,256]{1,0:T(8,128)S(1)}, f32[12,256,2,128]{3,1,2,0:T(8,128)}) fusion(f32[2,128,12,256]{1,3,0,2:T(8,128)S(1)} %fusion.25, f32[12,256]{1,0:T(8,128)S(1)} %get-tuple-element.221, bf16[12,256,2,128]{1,3,2,0:T(8,128)(2,1)S(1)} %copy-done.2, bf16[12,2,128,128]{3,2,1,0:T(8,128)(2,1)S(1)} %copy-done.18, ...), kind=kOutput, calls=%fused_computation.18 | convolution fusion | flops 206042112 | bytes 11833344 | tf_op jit(solution)/shard_map/nthi,nhij->nthj/dot_general | solution.py:67
  84.1 15.9 %psum.14 = f32[12,256]{1,0:T(8,128)S(1)} all-reduce(f32[12,256]{1,0:T(8,128)S(1)} %get-tuple-element.228), channel_id=1, replica_groups=mesh['seq'=8,'head'=4] {'head'}, use_global_device_ids=true, to_apply=%region_9.10 | all-reduce | flops 3072 | bytes 24576 | tf_op jit(solution)/shard_map/psum | solution.py:75
  100.0 2.9 %multiply_reduce_fusion = f32[12,256]{1,0:T(8,128)S(1)} fusion(f32[12,256,2,128]{3,1,2,0:T(8,128)} %get-tuple-element.229, f32[12,256]{1,0:T(8,128)S(1)} %add_sqrt_fusion, bf16[12,256,2,128]{3,1,0,2:T(8,128)(2,1)} %bitcast.111), kind=kLoop, calls=%fused_computation.17 | loop fusion | flops 3142656 | bytes 4743168 | tf_op jit(solution)/shard_map/reduce_sum | solution.py:78
  102.9 13.9 %psum.15 = f32[12,256]{1,0:T(8,128)S(1)} all-reduce(f32[12,256]{1,0:T(8,128)S(1)} %multiply_reduce_fusion), channel_id=1, replica_groups=mesh['seq'=8,'head'=4] {'head'}, use_global_device_ids=true, to_apply=%region_11.12 | all-reduce | flops 3072 | bytes 24576 | tf_op jit(solution)/shard_map/psum | solution.py:78
  116.8 3.8 %divide_convert_fusion = (bf16[12,256,2,128]{3,1,2,0:T(8,128)(2,1)S(1)}, bf16[12,256,2,128]{3,1,2,0:T(8,128)(2,1)}) fusion(f32[12,256]{1,0:T(8,128)S(1)} %broadcast_multiply_fusion, f32[12,256]{1,0:T(8,128)S(1)} %add_sqrt_fusion, f32[12,256,2,128]{3,1,2,0:T(8,128)} %get-tuple-element.229, bf16[12,256,2,128]{3,1,0,2:T(8,128)(2,1)} %bitcast.112), kind=kLoop, calls=%fused_computation.16 | loop fusion | flops 5505024 | bytes 7888896 | tf_op jit(solution)/shard_map/convert_element_type | solution.py:80
  120.6 2.6 %select_convert_fusion = bf16[12,2,256,256]{3,2,1,0:T(8,128)(2,1)} fusion(pred[12,256,256]{2,1,0:T(8,128)(4,1)S(1)} %copy-done.22, bf16[12,256,2,128]{3,1,2,0:T(8,128)(2,1)S(1)} %get-tuple-element.218, bf16[12,256,2,128]{3,2,1,0:T(2,128)(2,1)S(1)} %bitcast.109), kind=kOutput, calls=%fused_computation.4 | convolution fusion | flops 405798912 | bytes 7077888 | tf_op jit(solution)/shard_map/nthd,nshd->nhts/dot_general | solution.py:85
  123.3 1.7 fusion.3
  126.0 34.2 %while.31 = (s32[]{:T(128)}, f32[2,128,128]{2,1,0:T(8,128)S(1)}, bf16[12,2,128,128]{3,2,1,0:T(8,128)(2,1)}, pred[12]{0:T(512)(128)(4,1)S(1)}, f32[12,2,128,128]{...) while((s32[]{:T(128)}, f32[2,128,128]{2,1,0:T(8,128)S(1)}, ...), condition=%wide.region_14.15_spmd.clone, body=%wide.region_13.14_spmd.clone.sunk | while | flops 131076 | bytes 589947 | solution.py:102
  160.9 3.0 %fusion.36 = f32[12,2,256,128]{3,2,1,0:T(8,128)S(1)} fusion(bf16[12,2,256,256]{3,2,1,0:T(8,128)(2,1)} %select_convert_fusion, bf16[12,256,2,128]{1,3,2,0:T(8,128)(2,1)S(1)} %copy.177), kind=kOutput, calls=%fused_computation.80 | convolution fusion | flops 402653184 | bytes 7864320 | tf_op jit(solution)/shard_map/nhts,nshd->nthd/dot_general | solution.py:88
  165.8 13.8 %copy.213 = bf16[3072,2,128]{2,1,0:T(2,128)(2,1)} copy(bf16[3072,2,128]{2,0,1:T(8,128)(2,1)S(1)} %bitcast.113) | data formatting | bytes 3145728
  179.7 14.0 %copy.212 = bf16[3072,2,128]{2,1,0:T(2,128)(2,1)} copy(bf16[3072,2,128]{2,0,1:T(8,128)(2,1)S(1)} %bitcast.114) | data formatting | bytes 3145728
  193.8 2.3 fusion.8
  196.5 2.7 %fusion.38 = f32[12,2,128,256]{2,3,1,0:T(8,128)} fusion(bf16[12,256,2,128]{3,1,2,0:T(8,128)(2,1)S(1)} %copy-done.6, bf16[12,2,256,256]{3,2,1,0:T(8,128)(2,1)S(1)} %copy-done.10), kind=kOutput, calls=%fused_computation.82 | convolution fusion | flops 402653184 | bytes 7864320 | tf_op jit(solution)/shard_map/nhts,nthd->nshd/dot_general | solution.py:123
  199.8 2.7 %fusion.37 = f32[12,2,256,128]{3,2,1,0:T(8,128)} fusion(bf16[12,2,256,256]{3,2,1,0:T(8,128)(2,1)S(1)} %copy-done.11, bf16[12,256,2,128]{1,3,2,0:T(8,128)(2,1)S(1)} %copy-done.4), kind=kOutput, calls=%fused_computation.81 | convolution fusion | flops 402653184 | bytes 7864320 | tf_op jit(solution)/shard_map/nhts,nthd->nshd/dot_general | solution.py:114
  207.6 14.0 %copy.215 = bf16[3072,2,128]{2,1,0:T(2,128)(2,1)} copy(bf16[3072,2,128]{2,0,1:T(8,128)(2,1)S(1)} %bitcast.115) | data formatting | bytes 3145728
  223.1 13.8 %copy.214 = bf16[3072,2,128]{2,1,0:T(2,128)(2,1)} copy(bf16[3072,2,128]{2,0,1:T(8,128)(2,1)S(1)} %bitcast.116) | data formatting | bytes 3145728
  (160 shorter events, 91.1 us)
Async XLA Ops:
  7.2 7.1 %copy-start = (bf16[3072,2,128]{2,1,0:T(2,128)(2,1)S(1)}, bf16[3072,2,128]{2,1,0:T(2,128)(2,1)}, u32[]{:S(2)}) copy-start(bf16[3072,2,128]{2,1,0:T(2,128)(2,1)} %param.11) | copy-start | bytes 4718596
  7.2 69.5 %all-gather.5.cloned.1.call-start = ((), (), s32[]{:S(2)}) async-start(), calls=%async_computation | async-start | bytes 1179648 | tf_op jit(solution)/shard_map/all_gather | solution.py:58
  51.1 0.7 copy-start.8
  51.8 150.7 %all-gather.7.cloned.1.call-start = ((), (), s32[]{:S(2)}) async-start(), calls=%async_computation.1 | async-start | bytes 1179648 | tf_op jit(solution)/shard_map/all_gather | solution.py:105
  56.7 5.2 %copy-start.1 = (bf16[12,256,2,128]{1,3,2,0:T(8,128)(2,1)S(1)}, bf16[12,256,2,128]{1,3,2,0:T(8,128)(2,1)}, u32[]{:S(2)}) copy-start(bf16[12,256,2,128]{1,3,2,0:T(8,128)(2,1)} %copy.197) | copy-start | bytes 4718596
  61.8 1.1 copy-start.21
  62.9 1.6 copy-start.9
  76.7 3.8 %copy-start.18 = (bf16[12,2,128,128]{3,2,1,0:T(8,128)(2,1)S(1)}, bf16[12,2,128,128]{3,2,1,0:T(8,128)(2,1)}, u32[]{:S(2)}) copy-start(bf16[12,2,128,128]{3,2,1,0:T(8,128)(2,1)} %get-tuple-element.136) | copy-start | bytes 2359300
  78.2 2.3 copy-start.2
  78.2 2.8 %copy-start.15 = (f32[12,2,256,128]{3,2,1,0:T(8,128)S(1)}, f32[12,2,256,128]{3,2,1,0:T(8,128)}, u32[]{:S(2)}) copy-start(f32[12,2,256,128]{3,2,1,0:T(8,128)} %fusion.12) | copy-start | bytes 9437188
  116.8 3.8 %copy-start.22 = (pred[12,256,256]{2,1,0:T(8,128)(4,1)S(1)}, pred[12,256,256]{2,1,0:T(8,128)(4,1)}, u32[]{:S(2)}) copy-start(pred[12,256,256]{2,1,0:T(8,128)(4,1)} %copy-done.21) | copy-start | bytes 2359300
  120.6 2.7 %copy-start.5 = (bf16[12,256,2,128]{3,1,2,0:T(8,128)(2,1)}, bf16[12,256,2,128]{3,1,2,0:T(8,128)(2,1)S(1)}, u32[]{:S(2)}) copy-start(bf16[12,256,2,128]{3,1,2,0:T(8,128)(2,1)S(1)} %get-tuple-element.218) | copy-start | bytes 4718596
  120.6 2.7 %copy-start.3 = (bf16[12,256,2,128]{1,3,2,0:T(8,128)(2,1)S(1)}, bf16[12,256,2,128]{1,3,2,0:T(8,128)(2,1)}, u32[]{:S(2)}) copy-start(bf16[12,256,2,128]{1,3,2,0:T(8,128)(2,1)} %copy.197) | copy-start | bytes 4718596
  160.9 3.0 %copy-start.6 = (bf16[12,256,2,128]{3,1,2,0:T(8,128)(2,1)S(1)}, bf16[12,256,2,128]{3,1,2,0:T(8,128)(2,1)}, u32[]{:S(2)}) copy-start(bf16[12,256,2,128]{3,1,2,0:T(8,128)(2,1)} %copy-done.5) | copy-start | bytes 4718596
  160.9 3.0 %copy-start.19 = (bf16[12,2,128,128]{3,2,1,0:T(8,128)(2,1)S(1)}, bf16[12,2,128,128]{3,2,1,0:T(8,128)(2,1)}, u32[]{:S(2)}) copy-start(bf16[12,2,128,128]{3,2,1,0:T(8,128)(2,1)} %get-tuple-element.136) | copy-start | bytes 2359300
  165.8 13.8 %copy-start.20 = (bf16[12,256,2,128]{3,1,2,0:T(8,128)(2,1)S(1)}, bf16[12,256,2,128]{3,1,2,0:T(8,128)(2,1)}, u32[]{:S(2)}) copy-start(bf16[12,256,2,128]{3,1,2,0:T(8,128)(2,1)} %get-tuple-element.219) | copy-start | bytes 4718596
  179.7 14.0 %copy-start.16 = (bf16[12,2,128,128]{3,2,1,0:T(8,128)(2,1)S(1)}, bf16[12,2,128,128]{3,2,1,0:T(8,128)(2,1)}, u32[]{:S(2)}) copy-start(bf16[12,2,128,128]{3,2,1,0:T(8,128)(2,1)} %get-tuple-element.138) | copy-start | bytes 2359300
  193.8 2.7 %copy-start.10 = (bf16[12,2,256,256]{3,2,1,0:T(8,128)(2,1)S(1)}, bf16[12,2,256,256]{3,2,1,0:T(8,128)(2,1)}, u32[]{:S(2)}) copy-start(bf16[12,2,256,256]{3,2,1,0:T(8,128)(2,1)} %copy-done.9) | copy-start | bytes 9437188
  196.5 2.7 %copy-start.4 = (bf16[12,256,2,128]{1,3,2,0:T(8,128)(2,1)S(1)}, bf16[12,256,2,128]{1,3,2,0:T(8,128)(2,1)}, u32[]{:S(2)}) copy-start(bf16[12,256,2,128]{1,3,2,0:T(8,128)(2,1)} %copy.197) | copy-start | bytes 4718596
  196.5 3.3 %copy-start.11 = (bf16[12,2,256,256]{3,2,1,0:T(8,128)(2,1)S(1)}, bf16[12,2,256,256]{3,2,1,0:T(8,128)(2,1)}, u32[]{:S(2)}) copy-start(bf16[12,2,256,256]{3,2,1,0:T(8,128)(2,1)} %select_convert_fusion) | copy-start | bytes 9437188
  203.8 1.9 copy-start.14
  203.8 2.1 copy-start.17
  207.5 14.2 %copy-start.13 = (f32[12,2,256,128]{3,2,1,0:T(8,128)S(1)}, f32[12,2,256,128]{3,2,1,0:T(8,128)}, u32[]{:S(2)}) copy-start(f32[12,2,256,128]{3,2,1,0:T(8,128)} %fusion.37) | copy-start | bytes 9437188
  207.6 14.1 %copy-start.12 = (f32[12,2,128,256]{2,3,1,0:T(8,128)S(1)}, f32[12,2,128,256]{2,3,1,0:T(8,128)}, u32[]{:S(2)}) copy-start(f32[12,2,128,256]{2,3,1,0:T(8,128)} %fusion.8) | copy-start | bytes 9437188
  (1 other events, 0.7 us)
Sparse Core Ops, SparseCore 0:
  51.9 24.7 all-gather.4
  161.0 20.9 all-gather.6
where the time goes:
time: 245 us; the launch traced here: 244 us
  local copies, waits for them, and re-layouts  90.3 us (37%)
  other arithmetic  67.9 us (28%)
  matrix products  31.1 us (13%)
  blocking collectives  29.9 us (12%)
  between operations  14.4 us (6%)
  waiting for transfers between devices  9.52 us (4%)
    unnamed x51, local copies, waits for them, and re-layouts  64.3 us
    add x24, other arithmetic, group_prefix(): return (jnp.where(keeping, running, 0.0) + added, running)  38.1 us
    psum x1, blocking collectives, per_device(): total_squares = lax.psum(squares, 'head')  15.9 us
    dynamic_update_slice x24, other arithmetic, per_device(): lax.scan(group_prefix, zero_state, (group_sums, keep_forward))  15.2 us
    dynamic_slice x24, local copies, waits for them, and re-layouts, per_device(): lax.scan(group_prefix, zero_state, (group_sums, keep_forward))  14.3 us
    psum x1, blocking collectives, per_device(): lax.psum(jnp.sum(grad_in * normed, axis=(2, 3)), 'head') / width_all  13.9 us
    all_gather x1, waiting for transfers between devices, per_device(): portion = lax.all_gather(shard_state[None], 'seq', axis=0, tiled=True)  9.49 us
    reshape x2, local copies, waits for them, and re-layouts, blocks(): return array.reshape(n_groups, GROUP, heads_here, head_width)  8.35 us
  transfers between devices with their start and end apart: 2, of which 1 were waited for; matrix products, arithmetic and copies ran while one was open for 22% of the time, Pallas kernels for 0%

commit v1 on v0

v1 whole, which is shorter than its diff:
```python
import functools

import jax
import jax.numpy as jnp
from jax import lax
from jax.experimental import pallas as pl
from jax.experimental.pallas import tpu as pltpu
from jax.sharding import PartitionSpec as P

GROUP = 256
EPSILON = 1e-06
F32 = jnp.float32
BF16 = jnp.bfloat16

NN = (((1,), (0,)), ((), ()))
NT = (((1,), (1,)), ((), ()))
TN = (((0,), (0,)), ((), ()))


def dot(a, b, dims=NN):
    return lax.dot_general(a, b, dims, preferred_element_type=F32)


def doc_ends_of(doc_ref):
    ends, total = [], jnp.int32(0)
    for j in range(doc_ref.shape[0]):
        total = total + doc_ref[j]
        ends.append(total)
    return ends


def start_of(ends, place):
    found = jnp.int32(0)
    for end in ends:
        found = jnp.where(end <= place, end, found)
    return found


def end_of(ends, place):
    found = jnp.int32(2**30)
    for end in reversed(ends):
        found = jnp.where(end > place, end, found)
    return found


def rows_iota(width):
    return lax.broadcasted_iota(jnp.int32, (GROUP, width), 0)


def group_mask(ends, first):
    place = rows_iota(128) + first
    begin = jnp.zeros((GROUP, 128), jnp.int32)
    for end in ends:
        begin = jnp.where(place >= end, end, begin)
    begin = begin - first
    begin = jnp.concatenate([begin] * (GROUP // 128), axis=1)
    column = lax.broadcasted_iota(jnp.int32, (GROUP, GROUP), 1)
    return (column >= begin) & (column <= rows_iota(GROUP))


def keep_rows(keep, x):
    return jnp.where(keep, x.astype(F32), 0.0).astype(BF16)


def split_heads(src_ref, tmp_ref, g, heads):
    rows = pl.ds(pl.multiple_of(g * (GROUP * heads), GROUP * heads), GROUP * heads)
    tmp_ref[rows, :] = src_ref[rows, :].astype(F32)
    return [
        tmp_ref[pl.ds(g * (GROUP * heads) + h, GROUP, stride=heads), :] for h in range(heads)
    ]


def group_rows(g):
    return pl.ds(pl.multiple_of(g * GROUP, GROUP), GROUP)


def state_kernel(doc_ref, k2_ref, v2_ref, kd_ref, vd_ref, mine_ref, send_ref, tmpk, tmpv, acc):
    tokens, width = kd_ref.shape
    heads = width // 128
    half = heads // 2
    shard = lax.axis_index("seq")
    core = shard % 2
    anchor = shard * tokens
    ends = doc_ends_of(doc_ref)
    tail = start_of(ends, anchor + tokens - 1) - anchor
    acc[...] = jnp.zeros_like(acc)
    for g in range(tokens // GROUP):
        keep = rows_iota(128) + g * GROUP >= tail
        ks = split_heads(k2_ref, tmpk, g, heads)
        vs = split_heads(v2_ref, tmpv, g, heads)
        for h in range(heads):
            lanes = slice(h * 128, (h + 1) * 128)
            v = vs[h].astype(BF16)
            kd_ref[group_rows(g), lanes] = ks[h].astype(BF16)
            vd_ref[group_rows(g), lanes] = v
            acc[h] += dot(jnp.where(keep, ks[h], 0.0).astype(BF16), v, TN)
    mine_ref[...] = acc[pl.ds(core * half, half)]
    send_ref[...] = acc[pl.ds((1 - core) * half, half)]


def local_kernel(
    doc_ref, kd_ref, vd_ref, q2_ref, c2_ref, qd_ref, qt_ref, cd_ref, p_ref, o_ref, sb_ref, tmpq, tmpc, state
):
    tokens, width = kd_ref.shape
    heads = width // 128
    anchor = lax.axis_index("seq") * tokens
    ends = doc_ends_of(doc_ref)
    state[...] = jnp.zeros_like(state)

    def body(g, carry):
        first = anchor + g * GROUP
        rows = group_rows(g)
        mask = group_mask(ends, first)
        place = rows_iota(128)
        opened = place < end_of(ends, first - 1) - first
        begin = start_of(ends, first + GROUP - 1)
        tail = place >= begin - first
        kept = (begin < first).astype(F32)
        qs = split_heads(q2_ref, tmpq, g, heads)
        cs = split_heads(c2_ref, tmpc, g, heads)
        for h in range(heads):
            lanes = slice(h * 128, (h + 1) * 128)
            q = qs[h].astype(BF16)
            k = kd_ref[rows, lanes]
            v = vd_ref[rows, lanes]
            qd_ref[rows, lanes] = q
            qt_ref[lanes, rows] = qs[h].T.astype(BF16)
            cd_ref[rows, lanes] = cs[h].astype(BF16)
            p = jnp.where(mask, dot(q, k, NT), 0.0).astype(BF16)
            p_ref[h, rows, :] = p
            sb = state[h].astype(BF16)
            sb_ref[g, h] = sb
            o_ref[rows, lanes] = dot(p, v) + dot(jnp.where(opened, qs[h], 0.0).astype(BF16), sb)
            state[h] = state[h] * kept + dot(keep_rows(tail, k), v, TN)
        return carry

    lax.fori_loop(0, tokens // GROUP, body, 0)


def place_halves(core, out_ref, own_ref, other_ref):
    half = own_ref.shape[0]
    out_ref[pl.ds(core * half, half)] = own_ref[...].astype(BF16)
    out_ref[pl.ds((1 - core) * half, half)] = other_ref[...].astype(BF16)


def stats_kernel(doc_ref, qd_ref, ol_ref, cd_ref, own_ref, other_ref, o_ref, sin_ref, st_ref):
    tokens, width = qd_ref.shape
    heads = width // 128
    shard = lax.axis_index("seq")
    anchor = shard * tokens
    ends = doc_ends_of(doc_ref)
    opened_to = end_of(ends, anchor - 1) - anchor
    place_halves(shard % 2, sin_ref, own_ref, other_ref)
    row = lax.broadcasted_iota(jnp.int32, (8, 128), 0)
    pick0 = (row == 0).astype(F32).astype(BF16)
    pick1 = (row == 1).astype(F32).astype(BF16)
    for g in range(tokens // GROUP):
        rows = group_rows(g)
        opened = rows_iota(128) + g * GROUP < opened_to
        squares = jnp.zeros((GROUP, 128), F32)
        inner = jnp.zeros((GROUP, 128), F32)
        for h in range(heads):
            lanes = slice(h * 128, (h + 1) * 128)
            o = ol_ref[rows, lanes] + dot(keep_rows(opened, qd_ref[rows, lanes]), sin_ref[h])
            o_ref[rows, lanes] = o
            squares += o * o
            inner += o * cd_ref[rows, lanes].astype(F32)
        both = dot(pick0, squares.astype(BF16), NT) + dot(pick1, inner.astype(BF16), NT)
        for r in range(st_ref.shape[0]):
            st_ref[r, :, rows] = both[:2]


def norm_kernel(
    width_all, doc_ref, st_ref, o_ref, cd_ref, qt_ref, dob_ref, inv_ref, mine_ref, send_ref, acc
):
    tokens, width = cd_ref.shape
    heads = width // 128
    half = heads // 2
    shard = lax.axis_index("seq")
    core = shard % 2
    anchor = shard * tokens
    ends = doc_ends_of(doc_ref)
    head_to = end_of(ends, anchor) - anchor
    acc[...] = jnp.zeros_like(acc)
    for g in range(tokens // GROUP):
        rows = group_rows(g)
        keep = rows_iota(128) + g * GROUP < head_to
        total = st_ref[0, :, rows]
        for r in range(1, st_ref.shape[0]):
            total = total + st_ref[r, :, rows]
        total = total * (1.0 / width_all)
        inv = lax.rsqrt(total[0:1] + EPSILON)
        slope = total[1:2] * inv * inv * inv
        columns = jnp.concatenate([inv, slope, jnp.zeros((6, GROUP), F32)], axis=0).T
        inv_col = jnp.broadcast_to(columns[:, 0:1], (GROUP, 128))
        slope_col = jnp.broadcast_to(columns[:, 1:2], (GROUP, 128))
        inv_ref[rows, :] = inv_col
        for h in range(heads):
            lanes = slice(h * 128, (h + 1) * 128)
            dob = inv_col * cd_ref[rows, lanes].astype(F32) - slope_col * o_ref[rows, lanes]
            dob_ref[rows, lanes] = dob.astype(BF16)
            acc[h] += dot(qt_ref[lanes, rows], jnp.where(keep, dob, 0.0).astype(BF16))
    mine_ref[...] = acc[pl.ds(core * half, half)]
    send_ref[...] = acc[pl.ds((1 - core) * half, half)]


def grad_kernel(
    doc_ref, o_ref, inv_ref, dob_ref, p_ref, qd_ref, qt_ref, kd_ref, vd_ref, sb_ref, sin_ref,
    dk_ref, dv_ref, out_ref, gq_ref, tmpo, tmpq, bufo, bufq, state, sems,
):
    tokens, width = kd_ref.shape
    heads = width // 128
    n_groups = tokens // GROUP
    anchor = lax.axis_index("seq") * tokens
    ends = doc_ends_of(doc_ref)
    opened_to = end_of(ends, anchor - 1)
    state[...] = jnp.zeros_like(state)

    def copies(g):
        pairs = pl.ds(pl.multiple_of(g * GROUP * heads, GROUP * heads), GROUP * heads)
        return (
            pltpu.make_async_copy(bufo.at[pairs], out_ref.at[pairs], sems.at[0, g]),
            pltpu.make_async_copy(bufq.at[pairs], gq_ref.at[pairs], sems.at[1, g]),
        )

    def body(i, carry):
        g = n_groups - 1 - i
        first = anchor + g * GROUP
        rows = group_rows(g)
        pairs = pl.ds(pl.multiple_of(g * GROUP * heads, GROUP * heads), GROUP * heads)
        mask = group_mask(ends, first)
        place = rows_iota(128)
        opened = place < end_of(ends, first - 1) - first
        opened_far = place < opened_to - first
        closing = place >= start_of(ends, first + GROUP) - first
        end = end_of(ends, first)
        head_part = place < end - first
        kept = (end > first + GROUP).astype(F32)
        for h in range(heads):
            lanes = slice(h * 128, (h + 1) * 128)
            q = qd_ref[rows, lanes]
            k = kd_ref[rows, lanes]
            v = vd_ref[rows, lanes]
            dob = dob_ref[rows, lanes]
            dp = jnp.where(mask, dot(dob, v, NT), 0.0).astype(BF16)
            gq = (
                dot(dp, k)
                + dot(keep_rows(opened, dob), sb_ref[g, h], NT)
                + dot(keep_rows(opened_far, dob), sin_ref[h], NT)
            )
            mine = pl.ds(g * (GROUP * heads) + h, GROUP, stride=heads)
            tmpq[mine, :] = gq
            tmpo[mine, :] = o_ref[rows, lanes] * inv_ref[rows, :]
            rb = state[h].astype(BF16)
            dk_ref[rows, lanes] = dot(dp, q, TN) + dot(keep_rows(closing, v), rb, NT)
            dv_ref[rows, lanes] = dot(p_ref[h, rows, :], dob, TN) + dot(keep_rows(closing, k), rb)
            state[h] = state[h] * kept + dot(qt_ref[lanes, rows], keep_rows(head_part, dob))
        bufq[pairs, :] = tmpq[pairs, :].astype(BF16)
        bufo[pairs, :] = tmpo[pairs, :].astype(BF16)
        for copy in copies(g):
            copy.start()
        return carry

    lax.fori_loop(0, n_groups, body, 0)

    def drain(g, carry):
        for copy in copies(g):
            copy.wait()
        return carry

    lax.fori_loop(0, n_groups, drain, 0)


def final_kernel(
    doc_ref, dk_ref, dv_ref, kd_ref, vd_ref, own_ref, other_ref, gk_ref, gv_ref, rin, tmpk, tmpv, bufk, bufv, sems
):
    tokens, width = kd_ref.shape
    heads = width // 128
    n_groups = tokens // GROUP
    shard = lax.axis_index("seq")
    anchor = shard * tokens
    ends = doc_ends_of(doc_ref)
    begin = start_of(ends, anchor + tokens) - anchor
    place_halves(shard % 2, rin, own_ref, other_ref)
    started = []
    for g in range(n_groups):
        rows = group_rows(g)
        pairs = pl.ds(g * GROUP * heads, GROUP * heads)
        closing = rows_iota(128) + g * GROUP >= begin
        for h in range(heads):
            lanes = slice(h * 128, (h + 1) * 128)
            mine = pl.ds(g * (GROUP * heads) + h, GROUP, stride=heads)
            tmpk[mine, :] = dk_ref[rows, lanes] + dot(keep_rows(closing, vd_ref[rows, lanes]), rin[h], NT)
            tmpv[mine, :] = dv_ref[rows, lanes] + dot(keep_rows(closing, kd_ref[rows, lanes]), rin[h])
        bufk[pairs, :] = tmpk[pairs, :].astype(BF16)
        bufv[pairs, :] = tmpv[pairs, :].astype(BF16)
        for n, (buf, out) in enumerate(((bufk, gk_ref), (bufv, gv_ref))):
            copy = pltpu.make_async_copy(buf.at[pairs], out.at[pairs], sems.at[n, g])
            copy.start()
            started.append(copy)
    for copy in started:
        copy.wait()


def call(kernel, name, outs, scratch, out_any=(), flops=0, n_in=0):
    vmem = pl.BlockSpec(memory_space=pltpu.VMEM)
    specs = [pl.BlockSpec(memory_space=pl.ANY) if i in out_any else vmem for i in range(len(outs))]
    return pl.pallas_call(
        kernel,
        name=name,
        out_shape=[jax.ShapeDtypeStruct(s, d) for s, d in outs],
        in_specs=[pl.BlockSpec(memory_space=pltpu.SMEM)] + [vmem] * n_in,
        out_specs=specs,
        scratch_shapes=scratch,
        cost_estimate=pl.CostEstimate(flops=flops, bytes_accessed=8 << 20, transcendentals=0),
        compiler_params=pltpu.CompilerParams(vmem_limit_bytes=30 << 20),
    )


def segment(ends, place):
    return jnp.sum((ends <= place).astype(jnp.int32))


def per_device(queries, keys, values, cotangent, doc_lengths):
    tokens, heads, head_width = queries.shape
    width = heads * head_width
    half = heads // 2
    n_groups = tokens // GROUP
    n_seq = lax.axis_size("seq")
    n_head = lax.axis_size("head")
    shard = lax.axis_index("seq")
    core = shard % 2
    chip = shard // 2
    n_chips = n_seq // 2
    ends = jnp.cumsum(doc_lengths)
    seg = functools.partial(segment, ends)
    chip_first = chip * (2 * tokens)
    middle = chip_first + tokens
    chip_end = middle + tokens

    def pairs(x):
        return x.reshape(tokens * heads, head_width)

    q2, k2, v2, c2 = pairs(queries), pairs(keys), pairs(values), pairs(cotangent)
    full = (tokens, width)
    piece = (half, head_width, head_width)
    state_shape = (heads, head_width, head_width)
    flat = (tokens * heads, head_width)
    swap_pairs = [(i, i ^ 1) for i in range(n_seq)]

    def swap(x):
        return lax.ppermute(x, "seq", swap_pairs)

    def exchange(mine, got, sign, after):
        near = jnp.where(core == (0 if sign > 0 else 1), mine, got)
        far = jnp.where(core == (0 if sign > 0 else 1), got, mine)
        if sign > 0:
            joined = seg(middle - 1) == seg(chip_end - 1)
            onward = seg(chip_first - 1) == seg(middle - 1)
        else:
            joined = seg(middle) == seg(chip_first)
            onward = seg(chip_end) == seg(middle)
        chip_state = far + joined.astype(F32) * near
        chip_state, after = lax.optimization_barrier((chip_state, after))
        total = jnp.zeros(piece, F32)
        for k in range(1, n_chips):
            links = [(i, i + 2 * k * sign) for i in range(n_seq) if 0 <= i + 2 * k * sign < n_seq]
            arrived = lax.ppermute(chip_state, "seq", links)
            if sign > 0:
                same = seg(chip_first - 2 * tokens * (k - 1) - 1) == seg(chip_first - 1)
            else:
                same = seg(chip_end + 2 * tokens * (k - 1)) == seg(chip_end)
            total = total + same.astype(F32) * arrived
        return near, onward.astype(F32), total, after

    def finish(near, onward, total, sign):
        farther = near + onward * total
        is_near = core == (0 if sign > 0 else 1)
        own = jnp.where(is_near, total, farther)
        send = jnp.where(is_near, farther, total)
        return own, swap(send)

    mm = 2 * tokens * heads * head_width * head_width
    kd, vd, mine, send = call(
        state_kernel,
        "shard_state",
        [(full, BF16), (full, BF16), (piece, F32), (piece, F32)],
        [pltpu.VMEM(flat, F32), pltpu.VMEM(flat, F32), pltpu.VMEM(state_shape, F32)],
        n_in=2,
        flops=mm,
    )(doc_lengths, k2, v2)
    near, onward, total, (kd_b, vd_b) = exchange(mine, swap(send), 1, (kd, vd))
    qd, qt, cd, probs, o_local, sb = call(
        local_kernel,
        "local_mix",
        [
            (full, BF16),
            ((width, tokens), BF16),
            (full, BF16),
            ((heads, tokens, GROUP), BF16),
            (full, F32),
            ((n_groups, heads, head_width, head_width), BF16),
        ],
        [pltpu.VMEM(flat, F32), pltpu.VMEM(flat, F32), pltpu.VMEM(state_shape, F32)],
        n_in=4,
        flops=6 * mm,
    )(doc_lengths, kd_b, vd_b, q2, c2)
    own, other = finish(near, onward, total, 1)
    o, sin, stats = call(
        stats_kernel,
        "mix_and_stats",
        [(full, F32), (state_shape, BF16), ((n_head, 2, tokens), F32)],
        [],
        n_in=5,
        flops=mm,
    )(doc_lengths, qd, o_local, cd, own, other)
    stats = lax.all_to_all(stats, "head", 0, 0)
    dob, inv, mine, send = call(
        functools.partial(norm_kernel, float(width * n_head)),
        "norm_back",
        [(full, BF16), ((tokens, head_width), F32), (piece, F32), (piece, F32)],
        [pltpu.VMEM(state_shape, F32)],
        n_in=4,
        flops=mm,
    )(doc_lengths, stats, o, cd, qt)
    near, onward, total, (dob_b, inv_b) = exchange(mine, swap(send), -1, (dob, inv))
    dk, dv, output, grad_q = call(
        grad_kernel,
        "local_grads",
        [(full, F32), (full, F32), (flat, BF16), (flat, BF16)],
        [
            pltpu.VMEM(flat, F32),
            pltpu.VMEM(flat, F32),
            pltpu.VMEM(flat, BF16),
            pltpu.VMEM(flat, BF16),
            pltpu.VMEM(state_shape, F32),
            pltpu.SemaphoreType.DMA((2, n_groups)),
        ],
        n_in=10,
        out_any=(2, 3),
        flops=12 * mm,
    )(doc_lengths, o, inv_b, dob_b, probs, qd, qt, kd, vd, sb, sin)
    own, other = finish(near, onward, total, -1)
    grad_k, grad_v = call(
        final_kernel,
        "final_grads",
        [(flat, BF16), (flat, BF16)],
        [
            pltpu.VMEM(state_shape, BF16),
            pltpu.VMEM(flat, F32),
            pltpu.VMEM(flat, F32),
            pltpu.VMEM(flat, BF16),
            pltpu.VMEM(flat, BF16),
            pltpu.SemaphoreType.DMA((2, n_groups)),
        ],
        n_in=6,
        out_any=(0, 1),
        flops=2 * mm,
    )(doc_lengths, dk, dv, kd, vd, own, other)
    return tuple(x.reshape(queries.shape) for x in (output, grad_q, grad_k, grad_v))


def solution(mesh):
    spec = P("seq", "head", None)
    return jax.shard_map(
        per_device,
        mesh=mesh,
        in_specs=(spec, spec, spec, spec, P()),
        out_specs=(spec, spec, spec, spec),
        check_vma=False,
    )
```

time: 245 us -> 90 us (0.37)
  local copies, waits for them, and re-layouts: 90.3 us -> 20.8 us
  other arithmetic: 67.9 us -> 1.17 us
  matrix products: 31.1 us -> 0 us
  Pallas kernels: 0 us -> 29.4 us
  blocking collectives: 29.9 us -> 8.46 us
  starting transfers between devices: 0.08 us -> 15.3 us
  waiting for transfers between devices: 9.52 us -> 2.12 us
  between operations: 14.4 us -> 11.3 us
    unnamed x51 -> x40, local copies, waits for them, and re-layouts: 64.3 us -> 20.8 us
    add x26 -> x2, other arithmetic: 38.2 us -> 0.03 us  [exchange(): chip_state = far + joined.astype(F32) * near]
    dot_general x16 -> x0, matrix products: 31.1 us -> none  [the longest x1 3.06 us: per_device(): jnp.einsum('nthi,nhij->nthj', query_blocks, local_bf, preferred_element_t...]
    psum x2 -> x0, blocking collectives: 29.9 us -> none  [the longest x1 15.9 us: per_device(): total_squares = lax.psum(squares, 'head')]
    pallas_call x0 -> x6, Pallas kernels: none -> 29.4 us  [the longest x1 11.9 us: per_device(): call(grad_kernel, 'local_grads', [(full, F32), (full, F32), (flat, BF16),...]
    ppermute x0 -> x10, starting transfers between devices: none -> 15.3 us  [the longest x6 14.2 us: exchange(): arrived = lax.ppermute(chip_state, 'seq', links)]
    dynamic_update_slice x24 -> x0, other arithmetic: 15.2 us -> none  [per_device(): lax.scan(group_prefix, zero_state, (group_sums, keep_forward))]
    dynamic_slice x24 -> x0, local copies, waits for them, and re-layouts: 14.3 us -> none  [per_device(): lax.scan(group_prefix, zero_state, (group_sums, keep_forward))]
  transfers between devices with their start and end apart: 2 -> 10, of which waited for: 1 -> 2; matrix products, arithmetic and copies ran while one was open for 22% -> 1% of each run, Pallas kernels for 0% -> 22%
where the time goes in v1:
time: 90 us; the launch traced here: 88.5 us
  Pallas kernels  29.4 us (33%)
  local copies, waits for them, and re-layouts  20.8 us (23%)
  starting transfers between devices  15.3 us (17%)
  between operations  11.3 us (13%)
  blocking collectives  8.46 us (9%)
  waiting for transfers between devices  2.12 us (2%)
  other arithmetic  1.17 us (1%)
    unnamed x40, local copies, waits for them, and re-layouts  20.8 us
    ppermute x6, starting transfers between devices, exchange(): arrived = lax.ppermute(chip_state, 'seq', links)  14.2 us
    pallas_call x1, Pallas kernels, per_device(): call(grad_kernel, 'local_grads', [(full, F32), (full, F32), (flat, BF16),...  11.9 us
    all_to_all x1, blocking collectives, per_device(): stats = lax.all_to_all(stats, 'head', 0, 0)  8.46 us
    pallas_call x1, Pallas kernels, per_device(): call(local_kernel, 'local_mix', [(full, BF16), ((width, tokens), BF16), (...  7.58 us
    pallas_call x1, Pallas kernels, per_device(): call(final_kernel, 'final_grads', [(flat, BF16), (flat, BF16)], [pltpu.VM...  3.06 us
    pallas_call x1, Pallas kernels, per_device(): call(functools.partial(norm_kernel, float(width * n_head)), 'norm_back',...  2.73 us
    pallas_call x1, Pallas kernels, per_device(): call(state_kernel, 'shard_state', [(full, BF16), (full, BF16), (piece, F3...  2.23 us
  transfers between devices with their start and end apart: 10, of which 2 were waited for; matrix products, arithmetic and copies ran while one was open for 1% of the time, Pallas kernels for 22%

profile of v1, /device:TPU:0, one launch (start us, length us, event | category | flops | bytes accessed | tf_op | source)
XLA Modules:
  0.0 88.5 jit_solution(10887295959657900314)
XLA Ops:
  0.6 1.4 %copy-done.12 = bf16[3072,2,128]{2,1,0:T(2,128)(2,1)S(1)} copy-done((bf16[3072,2,128]{2,1,0:T(2,128)(2,1)S(1)}, bf16[3072,2,128]{2,1,0:T(2,128)(2,1)}, u32[]{:S(2)}) %copy-start.12) | copy-done | bytes 1572888
  2.0 1.4 %copy-done.13 = bf16[3072,2,128]{2,1,0:T(2,128)(2,1)S(1)} copy-done((bf16[3072,2,128]{2,1,0:T(2,128)(2,1)S(1)}, bf16[3072,2,128]{2,1,0:T(2,128)(2,1)}, u32[]{:S(2)}) %copy-start.13) | copy-done | bytes 1572888
  4.1 2.2 %shard_state.1 = (bf16[3072,256]{1,0:T(8,128)(2,1)S(1)}, bf16[3072,256]{1,0:T(8,128)(2,1)S(1)}, f32[1,128,128]{2,1,0:T(8,128)S(1)}, f32[1,128,128]{2,1,0:T(8,128)S(1)}) custom-call(s32[6]{0:T(128)S(1)} %copy-done.18, bf16[6144,128]{1,0:T(8,128)(2,1)S(1)} %bitcast.9, bf16[6144,128]{1,0:T(8,128)(2,1)S(1)} %bitcast.10), custom_call_target="tpu_custom_call" | custom-call | flops 201326592 | bytes 8388608 | tf_op jit(solution)/shard_map/shard_state/pallas_call | solution.py:384
  13.2 4.5 %collective-permute-start.1 = (f32[1,128,128]{2,1,0:T(8,128)S(1)}, f32[1,128,128]{2,1,0:T(8,128)S(1)}, u32[]{:S(2)}, u32[]{:S(2)}) collective-permute-start(f32[1,128,128]{2,1,0:T(8,128)S(1)} %multiply_add_fusion.5), channel_id=1, source_target_pairs={{0,8},{4,12},{8,16},{12,20},{16,24},{20,28},{1,9},{5,13},{9,17},{1... | collective-permute-start | bytes 196616 | tf_op jit(solution)/shard_map/ppermute | solution.py:368
  17.7 4.5 %collective-permute-start.2 = (f32[1,128,128]{2,1,0:T(8,128)S(1)}, f32[1,128,128]{2,1,0:T(8,128)S(1)}, u32[]{:S(2)}, u32[]{:S(2)}) collective-permute-start(f32[1,128,128]{2,1,0:T(8,128)S(1)} %multiply_add_fusion.5), channel_id=1, source_target_pairs={{0,16},{4,20},{8,24},{12,28},{1,17},{5,21},{9,25},{13,29},{2,18},{... | collective-permute-start | bytes 196616 | tf_op jit(solution)/shard_map/ppermute | solution.py:368
  22.2 1.3 %collective-permute-start.3 = (f32[1,128,128]{2,1,0:T(8,128)S(1)}, f32[1,128,128]{2,1,0:T(8,128)S(1)}, u32[]{:S(2)}, u32[]{:S(2)}) collective-permute-start(f32[1,128,128]{2,1,0:T(8,128)S(1)} %multiply_add_fusion.5), channel_id=1, source_target_pairs={{0,24},{4,28},{1,25},{5,29},{2,26},{6,30},{3,27},{7,31}} | collective-permute-start | bytes 196616 | tf_op jit(solution)/shard_map/ppermute | solution.py:368
  23.6 1.4 %copy-done.14 = bf16[3072,2,128]{2,1,0:T(2,128)(2,1)S(1)} copy-done((bf16[3072,2,128]{2,1,0:T(2,128)(2,1)S(1)}, bf16[3072,2,128]{2,1,0:T(2,128)(2,1)}, u32[]{:S(2)}) %copy-start.14) | copy-done | bytes 1572888
  25.0 1.4 %copy-done.15 = bf16[3072,2,128]{2,1,0:T(2,128)(2,1)S(1)} copy-done((bf16[3072,2,128]{2,1,0:T(2,128)(2,1)S(1)}, bf16[3072,2,128]{2,1,0:T(2,128)(2,1)}, u32[]{:S(2)}) %copy-start.15) | copy-done | bytes 1572888
  26.4 7.6 %local_mix.1 = (bf16[3072,256]{1,0:T(8,128)(2,1)S(1)}, bf16[256,3072]{1,0:T(8,128)(2,1)S(1)}, bf16[3072,256]{1,0:T(8,128)(2,1)S(1)}, bf16[2,3072,256]{2,1,0:T(8,...) custom-call(s32[6]{0:T(128)S(1)} %copy-done.19, ...), custom_call_target="tpu_custom_call" | custom-call | flops 1207959552 | bytes 8388608 | tf_op jit(solution)/shard_map/local_mix/pallas_call | solution.py:393
  34.0 1.6 %copy-done.6 = bf16[2,3072,256]{2,1,0:T(8,128)(2,1)} copy-done((bf16[2,3072,256]{2,1,0:T(8,128)(2,1)}, bf16[2,3072,256]{2,1,0:T(8,128)(2,1)S(1)}, u32[]{:S(2)}) %copy-start.6) | copy-done | bytes 3145752
  37.0 1.8 %mix_and_stats.1 = (f32[3072,256]{1,0:T(8,128)S(1)}, bf16[2,128,128]{2,1,0:T(8,128)(2,1)S(1)}, f32[4,2,3072]{2,1,0:T(2,128)S(1)}) custom-call(s32[6]{0:T(128)S(1)} %copy-done.19, bf16[3072,256]{1,0:T(8,128)(2,1)S(1)} %get-tuple-element.39.qd_ref, f32[3072,256]{1,0:T(8,128)S(1)} %get-tuple-element.40.ol_ref, bf16[3072,256]{1,0:T(8,128)(2,1)S(1)} %get-tuple-element.41.cd_ref, ...), custom_call_target="tpu_custom_call" | custom-call | flops 201326592 | bytes 8388608 | tf_op jit(solution)/shard_map/mix_and_stats/pallas_call | solution.py:409
  38.9 8.5 %all_to_all.5.st_ref = f32[4,2,3072]{2,1,0:T(2,128)S(1)} all-to-all(f32[4,2,3072]{2,1,0:T(2,128)S(1)} %get-tuple-element.44), channel_id=1, replica_groups=mesh['seq'=8,'head'=4] {'head'}, dimensions={0} | all-to-all | bytes 196608 | tf_op jit(solution)/shard_map/all_to_all | solution.py:417
  47.3 2.7 %norm_back.1 = (bf16[3072,256]{1,0:T(8,128)(2,1)S(1)}, f32[3072,128]{1,0:T(8,128)S(1)}, f32[1,128,128]{2,1,0:T(8,128)S(1)}, f32[1,128,128]{2,1,0:T(8,128)S(1)}) custom-call(s32[6]{0:T(128)S(1)} %copy-done.19, f32[4,2,3072]{2,1,0:T(2,128)S(1)} %all_to_all.5.st_ref, f32[3072,256]{1,0:T(8,128)S(1)} %get-tuple-element.43.o_ref, ...), custom_call_target="tpu_custom_call" | custom-call | flops 201326592 | bytes 8388608 | tf_op jit(solution)/shard_map/norm_back/pallas_call | solution.py:418
  57.5 1.3 %collective-permute-start.6 = (f32[1,128,128]{2,1,0:T(8,128)S(1)}, f32[1,128,128]{2,1,0:T(8,128)S(1)}, u32[]{:S(2)}, u32[]{:S(2)}) collective-permute-start(f32[1,128,128]{2,1,0:T(8,128)S(1)} %multiply_add_fusion.2), channel_id=1, source_target_pairs={{8,0},{12,4},{16,8},{20,12},{24,16},{28,20},{9,1},{13,5},{17,9},{2... | collective-permute-start | bytes 196616 | tf_op jit(solution)/shard_map/ppermute | solution.py:368
  58.8 1.3 %collective-permute-start.7 = (f32[1,128,128]{2,1,0:T(8,128)S(1)}, f32[1,128,128]{2,1,0:T(8,128)S(1)}, u32[]{:S(2)}, u32[]{:S(2)}) collective-permute-start(f32[1,128,128]{2,1,0:T(8,128)S(1)} %multiply_add_fusion.2), channel_id=1, source_target_pairs={{16,0},{20,4},{24,8},{28,12},{17,1},{21,5},{25,9},{29,13},{18,2},{... | collective-permute-start | bytes 196616 | tf_op jit(solution)/shard_map/ppermute | solution.py:368
  60.1 1.3 %collective-permute-start.8 = (f32[1,128,128]{2,1,0:T(8,128)S(1)}, f32[1,128,128]{2,1,0:T(8,128)S(1)}, u32[]{:S(2)}, u32[]{:S(2)}) collective-permute-start(f32[1,128,128]{2,1,0:T(8,128)S(1)} %multiply_add_fusion.2), channel_id=1, source_target_pairs={{24,0},{28,4},{25,1},{29,5},{26,2},{30,6},{27,3},{31,7}} | collective-permute-start | bytes 196616 | tf_op jit(solution)/shard_map/ppermute | solution.py:368
  61.4 1.9 %copy-done.1 = f32[3072,256]{1,0:T(8,128)S(1)} copy-done((f32[3072,256]{1,0:T(8,128)S(1)}, f32[3072,256]{1,0:T(8,128)}, u32[]{:S(2)}) %copy-start.1) | copy-done | bytes 3145752
  63.3 1.4 %copy-done.3 = bf16[3072,256]{1,0:T(8,128)(2,1)S(1)} copy-done((bf16[3072,256]{1,0:T(8,128)(2,1)S(1)}, bf16[3072,256]{1,0:T(8,128)(2,1)}, u32[]{:S(2)}) %copy-start.3) | copy-done | bytes 1572888
  64.7 1.4 %copy-done.5 = bf16[256,3072]{1,0:T(8,128)(2,1)S(1)} copy-done((bf16[256,3072]{1,0:T(8,128)(2,1)S(1)}, bf16[256,3072]{1,0:T(8,128)(2,1)}, u32[]{:S(2)}) %copy-start.5) | copy-done | bytes 1572888
  66.1 1.9 %copy-done.7 = bf16[2,3072,256]{2,1,0:T(8,128)(2,1)S(1)} copy-done((bf16[2,3072,256]{2,1,0:T(8,128)(2,1)S(1)}, bf16[2,3072,256]{2,1,0:T(8,128)(2,1)}, u32[]{:S(2)}) %copy-start.7) | copy-done | bytes 3145752
  68.0 1.4 %copy-done.9 = bf16[3072,256]{1,0:T(8,128)(2,1)S(1)} copy-done((bf16[3072,256]{1,0:T(8,128)(2,1)S(1)}, bf16[3072,256]{1,0:T(8,128)(2,1)}, u32[]{:S(2)}) %copy-start.9) | copy-done | bytes 1572888
  69.4 1.4 %copy-done.11 = f32[3072,128]{1,0:T(8,128)S(1)} copy-done((f32[3072,128]{1,0:T(8,128)S(1)}, f32[3072,128]{1,0:T(8,128)}, u32[]{:S(2)}) %copy-start.11) | copy-done | bytes 1572888
  72.0 11.9 %local_grads.1 = (f32[3072,256]{1,0:T(8,128)S(1)}, f32[3072,256]{1,0:T(8,128)S(1)}, bf16[6144,128]{1,0:T(8,128)(2,1)}, bf16[6144,128]{1,0:T(8,128)(2,1)}) custom-call(s32[6]{0:T(128)S(1)} %copy-done.19, f32[3072,256]{1,0:T(8,128)S(1)} %copy-done.1, f32[3072,128]{1,0:T(8,128)S(1)} %copy-done.11, bf16[3072,256]{1,0:T(8,128)(2,1)S(1)} %copy-done.9, ...), custom_call_target="tpu_custom_call" | custom-call | flops 2415919104 | bytes 8388608 | tf_op jit(solution)/shard_map/local_grads/pallas_call | solution.py:427
  85.5 3.1 %final_grads.1 = (bf16[6144,128]{1,0:T(8,128)(2,1)}, bf16[6144,128]{1,0:T(8,128)(2,1)}) custom-call(s32[6]{0:T(128)S(1)} %copy-done.19, f32[3072,256]{1,0:T(8,128)S(1)} %get-tuple-element.57.dk_ref, f32[3072,256]{1,0:T(8,128)S(1)} %get-tuple-element.58.dv_ref, bf16[3072,256]{1,0:T(8,128)(2,1)S(1)} %get-tuple-element.37.kd_ref, ...), custom_call_target="tpu_custom_call" | custom-call | flops 402653184 | bytes 8388608 | tf_op jit(solution)/shard_map/final_grads/pallas_call | solution.py:444
  (51 shorter events, 8.6 us)
Async XLA Ops:
  0.6 1.4 %copy-start.12 = (bf16[3072,2,128]{2,1,0:T(2,128)(2,1)S(1)}, bf16[3072,2,128]{2,1,0:T(2,128)(2,1)}, u32[]{:S(2)}) copy-start(bf16[3072,2,128]{2,1,0:T(2,128)(2,1)} %param.6) | copy-start | bytes 4718596
  2.0 1.4 %copy-start.13 = (bf16[3072,2,128]{2,1,0:T(2,128)(2,1)S(1)}, bf16[3072,2,128]{2,1,0:T(2,128)(2,1)}, u32[]{:S(2)}) copy-start(bf16[3072,2,128]{2,1,0:T(2,128)(2,1)} %param.7) | copy-start | bytes 4718596
  4.1 2.7 %copy-start.19 = (s32[6]{0:T(128)S(1)}, s32[6]{0:T(128)}, u32[]{:S(2)}) copy-start(s32[6]{0:T(128)} %doc_ref.11) | copy-start | bytes 76
  6.3 6.8 %collective-permute-start = (f32[1,128,128]{2,1,0:T(8,128)S(1)}, f32[1,128,128]{2,1,0:T(8,128)S(1)}, u32[]{:S(2)}, u32[]{:S(2)}) collective-permute-start(f32[1,128,128]{2,1,0:T(8,128)S(1)} %get-tuple-element.33), channel_id=1, source_target_pairs={{0,4},{4,0},{8,12},{12,8},{16,20},{20,16},{24,28},{28,24},{1,5},{5... | collective-permute-start | bytes 196616 | tf_op jit(solution)/shard_map/ppermute | solution.py:352
  13.2 22.4 %collective-permute-start.1 = (f32[1,128,128]{2,1,0:T(8,128)S(1)}, f32[1,128,128]{2,1,0:T(8,128)S(1)}, u32[]{:S(2)}, u32[]{:S(2)}) collective-permute-start(f32[1,128,128]{2,1,0:T(8,128)S(1)} %multiply_add_fusion.5), channel_id=1, source_target_pairs={{0,8},{4,12},{8,16},{12,20},{16,24},{20,28},{1,9},{5,13},{9,17},{1... | collective-permute-start | bytes 196616 | tf_op jit(solution)/shard_map/ppermute | solution.py:368
  17.7 17.9 %collective-permute-start.2 = (f32[1,128,128]{2,1,0:T(8,128)S(1)}, f32[1,128,128]{2,1,0:T(8,128)S(1)}, u32[]{:S(2)}, u32[]{:S(2)}) collective-permute-start(f32[1,128,128]{2,1,0:T(8,128)S(1)} %multiply_add_fusion.5), channel_id=1, source_target_pairs={{0,16},{4,20},{8,24},{12,28},{1,17},{5,21},{9,25},{13,29},{2,18},{... | collective-permute-start | bytes 196616 | tf_op jit(solution)/shard_map/ppermute | solution.py:368
  22.2 13.4 %collective-permute-start.3 = (f32[1,128,128]{2,1,0:T(8,128)S(1)}, f32[1,128,128]{2,1,0:T(8,128)S(1)}, u32[]{:S(2)}, u32[]{:S(2)}) collective-permute-start(f32[1,128,128]{2,1,0:T(8,128)S(1)} %multiply_add_fusion.5), channel_id=1, source_target_pairs={{0,24},{4,28},{1,25},{5,29},{2,26},{6,30},{3,27},{7,31}} | collective-permute-start | bytes 196616 | tf_op jit(solution)/shard_map/ppermute | solution.py:368
  23.5 1.4 %copy-start.14 = (bf16[3072,2,128]{2,1,0:T(2,128)(2,1)S(1)}, bf16[3072,2,128]{2,1,0:T(2,128)(2,1)}, u32[]{:S(2)}) copy-start(bf16[3072,2,128]{2,1,0:T(2,128)(2,1)} %param.5) | copy-start | bytes 4718596
  25.0 1.4 %copy-start.15 = (bf16[3072,2,128]{2,1,0:T(2,128)(2,1)S(1)}, bf16[3072,2,128]{2,1,0:T(2,128)(2,1)}, u32[]{:S(2)}) copy-start(bf16[3072,2,128]{2,1,0:T(2,128)(2,1)} %param.8) | copy-start | bytes 4718596
  34.0 1.7 %copy-start.6 = (bf16[2,3072,256]{2,1,0:T(8,128)(2,1)}, bf16[2,3072,256]{2,1,0:T(8,128)(2,1)S(1)}, u32[]{:S(2)}) copy-start(bf16[2,3072,256]{2,1,0:T(8,128)(2,1)S(1)} %get-tuple-element.52.p_ref) | copy-start | bytes 9437188
  35.6 3.2 %copy-start.2 = (bf16[3072,256]{1,0:T(8,128)(2,1)}, bf16[3072,256]{1,0:T(8,128)(2,1)S(1)}, u32[]{:S(2)}) copy-start(bf16[3072,256]{1,0:T(8,128)(2,1)S(1)} %get-tuple-element.39.qd_ref) | copy-start | bytes 4718596
  35.6 3.2 %copy-start.16 = (bf16[12,2,128,128]{3,2,1,0:T(8,128)(2,1)}, bf16[12,2,128,128]{3,2,1,0:T(8,128)(2,1)S(1)}, u32[]{:S(2)}) copy-start(bf16[12,2,128,128]{3,2,1,0:T(8,128)(2,1)S(1)} %get-tuple-element.53.sb_ref) | copy-start | bytes 2359300
  35.6 11.7 %copy-start.4 = (bf16[256,3072]{1,0:T(8,128)(2,1)}, bf16[256,3072]{1,0:T(8,128)(2,1)S(1)}, u32[]{:S(2)}) copy-start(bf16[256,3072]{1,0:T(8,128)(2,1)S(1)} %get-tuple-element.45.qt_ref) | copy-start | bytes 4718596
  35.7 1.3 %collective-permute-start.4 = (f32[1,128,128]{2,1,0:T(8,128)S(1)}, f32[1,128,128]{2,1,0:T(8,128)S(1)}, u32[]{:S(2)}, u32[]{:S(2)}) collective-permute-start(f32[1,128,128]{2,1,0:T(8,128)S(1)} %get-tuple-element.74), channel_id=1, source_target_pairs={{0,4},{4,0},{8,12},{12,8},{16,20},{20,16},{24,28},{28,24},{1,5},{5... | collective-permute-start | bytes 196616 | tf_op jit(solution)/shard_map/ppermute | solution.py:352
  38.9 11.2 %copy-start = (f32[3072,256]{1,0:T(8,128)}, f32[3072,256]{1,0:T(8,128)S(1)}, u32[]{:S(2)}) copy-start(f32[3072,256]{1,0:T(8,128)S(1)} %get-tuple-element.43.o_ref) | copy-start | bytes 9437188
  52.4 5.1 %collective-permute-start.5 = (f32[1,128,128]{2,1,0:T(8,128)S(1)}, f32[1,128,128]{2,1,0:T(8,128)S(1)}, u32[]{:S(2)}, u32[]{:S(2)}) collective-permute-start(f32[1,128,128]{2,1,0:T(8,128)S(1)} %get-tuple-element.46), channel_id=1, source_target_pairs={{0,4},{4,0},{8,12},{12,8},{16,20},{20,16},{24,28},{28,24},{1,5},{5... | collective-permute-start | bytes 196616 | tf_op jit(solution)/shard_map/ppermute | solution.py:352
  57.5 26.4 %collective-permute-start.6 = (f32[1,128,128]{2,1,0:T(8,128)S(1)}, f32[1,128,128]{2,1,0:T(8,128)S(1)}, u32[]{:S(2)}, u32[]{:S(2)}) collective-permute-start(f32[1,128,128]{2,1,0:T(8,128)S(1)} %multiply_add_fusion.2), channel_id=1, source_target_pairs={{8,0},{12,4},{16,8},{20,12},{24,16},{28,20},{9,1},{13,5},{17,9},{2... | collective-permute-start | bytes 196616 | tf_op jit(solution)/shard_map/ppermute | solution.py:368
  58.8 25.1 %collective-permute-start.7 = (f32[1,128,128]{2,1,0:T(8,128)S(1)}, f32[1,128,128]{2,1,0:T(8,128)S(1)}, u32[]{:S(2)}, u32[]{:S(2)}) collective-permute-start(f32[1,128,128]{2,1,0:T(8,128)S(1)} %multiply_add_fusion.2), channel_id=1, source_target_pairs={{16,0},{20,4},{24,8},{28,12},{17,1},{21,5},{25,9},{29,13},{18,2},{... | collective-permute-start | bytes 196616 | tf_op jit(solution)/shard_map/ppermute | solution.py:368
  60.1 23.8 %collective-permute-start.8 = (f32[1,128,128]{2,1,0:T(8,128)S(1)}, f32[1,128,128]{2,1,0:T(8,128)S(1)}, u32[]{:S(2)}, u32[]{:S(2)}) collective-permute-start(f32[1,128,128]{2,1,0:T(8,128)S(1)} %multiply_add_fusion.2), channel_id=1, source_target_pairs={{24,0},{28,4},{25,1},{29,5},{26,2},{30,6},{27,3},{31,7}} | collective-permute-start | bytes 196616 | tf_op jit(solution)/shard_map/ppermute | solution.py:368
  61.4 1.9 %copy-start.1 = (f32[3072,256]{1,0:T(8,128)S(1)}, f32[3072,256]{1,0:T(8,128)}, u32[]{:S(2)}) copy-start(f32[3072,256]{1,0:T(8,128)} %copy-done) | copy-start | bytes 9437188
  66.1 1.9 %copy-start.7 = (bf16[2,3072,256]{2,1,0:T(8,128)(2,1)S(1)}, bf16[2,3072,256]{2,1,0:T(8,128)(2,1)}, u32[]{:S(2)}) copy-start(bf16[2,3072,256]{2,1,0:T(8,128)(2,1)} %copy-done.6) | copy-start | bytes 9437188
  68.0 1.4 %copy-start.9 = (bf16[3072,256]{1,0:T(8,128)(2,1)S(1)}, bf16[3072,256]{1,0:T(8,128)(2,1)}, u32[]{:S(2)}) copy-start(bf16[3072,256]{1,0:T(8,128)(2,1)} %copy-done.8) | copy-start | bytes 4718596
  69.4 1.4 %copy-start.11 = (f32[3072,128]{1,0:T(8,128)S(1)}, f32[3072,128]{1,0:T(8,128)}, u32[]{:S(2)}) copy-start(f32[3072,128]{1,0:T(8,128)} %copy-done.10) | copy-start | bytes 4718596
  84.0 1.5 %collective-permute-start.9 = (f32[1,128,128]{2,1,0:T(8,128)S(1)}, f32[1,128,128]{2,1,0:T(8,128)S(1)}, u32[]{:S(2)}, u32[]{:S(2)}) collective-permute-start(f32[1,128,128]{2,1,0:T(8,128)S(1)} %get-tuple-element.72), channel_id=1, source_target_pairs={{0,4},{4,0},{8,12},{12,8},{16,20},{20,16},{24,28},{28,24},{1,5},{5... | collective-permute-start | bytes 196616 | tf_op jit(solution)/shard_map/ppermute | solution.py:352
  (6 other events, 6.9 us)

commit v2 on v1

--- a/solution.py
+++ b/solution.py
@@ -9,6 +9,8 @@
 
 GROUP = 256
 EPSILON = 1e-06
+UNROLL_MIX = 3
+UNROLL_GRAD = 3
 F32 = jnp.float32
 BF16 = jnp.bfloat16
 
@@ -62,19 +64,73 @@
     return jnp.where(keep, x.astype(F32), 0.0).astype(BF16)
 
 
-def split_heads(src_ref, tmp_ref, g, heads):
-    rows = pl.ds(pl.multiple_of(g * (GROUP * heads), GROUP * heads), GROUP * heads)
-    tmp_ref[rows, :] = src_ref[rows, :].astype(F32)
-    return [
-        tmp_ref[pl.ds(g * (GROUP * heads) + h, GROUP, stride=heads), :] for h in range(heads)
-    ]
+def pair_rows(g, heads):
+    return pl.ds(pl.multiple_of(g * (GROUP * heads), GROUP * heads), GROUP * heads)
+
+
+def fetch(src_ref, buf_ref, sem_ref, g, heads):
+    rows = pair_rows(g, heads)
+    return pltpu.make_async_copy(src_ref.at[rows], buf_ref.at[rows], sem_ref.at[g])
+
+
+def split_heads(buf_ref, tmp_ref, g, heads):
+    slot = g % tmp_ref.shape[0]
+    tmp_ref[slot] = buf_ref[pair_rows(g, heads), :].astype(F32)
+    return [tmp_ref[slot, pl.ds(h, GROUP, stride=heads), :] for h in range(heads)]
+
+
+def for_groups(n_groups, body, unroll):
+    if unroll >= n_groups:
+        for g in range(n_groups):
+            body(g)
+    else:
+
+        def step(i, carry):
+            for j in range(unroll):
+                body(i * unroll + j)
+            return carry
+
+        lax.fori_loop(0, n_groups // unroll, step, 0)
 
 
 def group_rows(g):
     return pl.ds(pl.multiple_of(g * GROUP, GROUP), GROUP)
 
 
-def state_kernel(doc_ref, k2_ref, v2_ref, kd_ref, vd_ref, mine_ref, send_ref, tmpk, tmpv, acc):
+def weights_of(out_ref, ends, shard, tokens, n_seq, sign):
+    core = shard % 2
+    chip_first = (shard - core) * tokens
+    middle = chip_first + tokens
+    chip_end = middle + tokens
+    if sign > 0:
+        join = start_of(ends, chip_end - 1) < middle
+        onward = start_of(ends, middle - 1) < chip_first
+        same = [
+            start_of(ends, chip_first - 1) < chip_first - 2 * tokens * k for k in range(n_seq // 2 - 1)
+        ]
+        is_near = core == 0
+    else:
+        join = end_of(ends, chip_first) > middle
+        onward = end_of(ends, middle) > chip_end
+        same = [end_of(ends, chip_end) > chip_end + 2 * tokens * k for k in range(n_seq // 2 - 1)]
+        is_near = core == 1
+    join, onward, is_near = (x.astype(F32) for x in (join, onward, is_near))
+    far = 1.0 - is_near
+    table = [
+        is_near * join + far,
+        is_near + far * join,
+        is_near + far * onward,
+        far,
+        is_near * onward + far,
+        is_near,
+    ] + [x.astype(F32) for x in same]
+    for i, x in enumerate(table):
+        out_ref[pl.ds(i, 1), :] = jnp.full((1, 128), x, F32)
+
+
+def state_kernel(
+    n_seq, doc_ref, k2_ref, v2_ref, kd_ref, vd_ref, mine_ref, send_ref, fore_ref, back_ref, tmpk, tmpv, acc
+):
     tokens, width = kd_ref.shape
     heads = width // 128
     half = heads // 2
@@ -96,10 +152,13 @@
             acc[h] += dot(jnp.where(keep, ks[h], 0.0).astype(BF16), v, TN)
     mine_ref[...] = acc[pl.ds(core * half, half)]
     send_ref[...] = acc[pl.ds((1 - core) * half, half)]
+    weights_of(fore_ref, ends, shard, tokens, n_seq, 1)
+    weights_of(back_ref, ends, shard, tokens, n_seq, -1)
 
 
 def local_kernel(
-    doc_ref, kd_ref, vd_ref, q2_ref, c2_ref, qd_ref, qt_ref, cd_ref, p_ref, o_ref, sb_ref, tmpq, tmpc, state
+    doc_ref, kd_ref, vd_ref, q2_ref, c2_ref, qd_ref, qt_ref, cd_ref, p_ref, o_ref, sb_ref,
+    tmpq, tmpc, state,
 ):
     tokens, width = kd_ref.shape
     heads = width // 128
@@ -107,7 +166,7 @@
     ends = doc_ends_of(doc_ref)
     state[...] = jnp.zeros_like(state)
 
-    def body(g, carry):
+    def body(g):
         first = anchor + g * GROUP
         rows = group_rows(g)
         mask = group_mask(ends, first)
@@ -132,9 +191,8 @@
             sb_ref[g, h] = sb
             o_ref[rows, lanes] = dot(p, v) + dot(jnp.where(opened, qs[h], 0.0).astype(BF16), sb)
             state[h] = state[h] * kept + dot(keep_rows(tail, k), v, TN)
-        return carry
-
-    lax.fori_loop(0, tokens // GROUP, body, 0)
+
+    for_groups(tokens // GROUP, body, UNROLL_MIX)
 
 
 def place_halves(core, out_ref, own_ref, other_ref):
@@ -223,8 +281,9 @@
             pltpu.make_async_copy(bufq.at[pairs], gq_ref.at[pairs], sems.at[1, g]),
         )
 
-    def body(i, carry):
+    def body(i):
         g = n_groups - 1 - i
+        slot = g % tmpq.shape[0]
         first = anchor + g * GROUP
         rows = group_rows(g)
         pairs = pl.ds(pl.multiple_of(g * GROUP * heads, GROUP * heads), GROUP * heads)
@@ -248,20 +307,19 @@
                 + dot(keep_rows(opened, dob), sb_ref[g, h], NT)
                 + dot(keep_rows(opened_far, dob), sin_ref[h], NT)
             )
-            mine = pl.ds(g * (GROUP * heads) + h, GROUP, stride=heads)
-            tmpq[mine, :] = gq
-            tmpo[mine, :] = o_ref[rows, lanes] * inv_ref[rows, :]
+            mine = pl.ds(h, GROUP, stride=heads)
+            tmpq[slot, mine, :] = gq
+            tmpo[slot, mine, :] = o_ref[rows, lanes] * inv_ref[rows, :]
             rb = state[h].astype(BF16)
             dk_ref[rows, lanes] = dot(dp, q, TN) + dot(keep_rows(closing, v), rb, NT)
             dv_ref[rows, lanes] = dot(p_ref[h, rows, :], dob, TN) + dot(keep_rows(closing, k), rb)
             state[h] = state[h] * kept + dot(qt_ref[lanes, rows], keep_rows(head_part, dob))
-        bufq[pairs, :] = tmpq[pairs, :].astype(BF16)
-        bufo[pairs, :] = tmpo[pairs, :].astype(BF16)
+        bufq[pairs, :] = tmpq[slot].astype(BF16)
+        bufo[pairs, :] = tmpo[slot].astype(BF16)
         for copy in copies(g):
             copy.start()
-        return carry
-
-    lax.fori_loop(0, n_groups, body, 0)
+
+    for_groups(n_groups, body, UNROLL_GRAD)
 
     def drain(g, carry):
         for copy in copies(g):
@@ -289,11 +347,12 @@
         closing = rows_iota(128) + g * GROUP >= begin
         for h in range(heads):
             lanes = slice(h * 128, (h + 1) * 128)
-            mine = pl.ds(g * (GROUP * heads) + h, GROUP, stride=heads)
-            tmpk[mine, :] = dk_ref[rows, lanes] + dot(keep_rows(closing, vd_ref[rows, lanes]), rin[h], NT)
-            tmpv[mine, :] = dv_ref[rows, lanes] + dot(keep_rows(closing, kd_ref[rows, lanes]), rin[h])
-        bufk[pairs, :] = tmpk[pairs, :].astype(BF16)
-        bufv[pairs, :] = tmpv[pairs, :].astype(BF16)
+            slot = g % tmpk.shape[0]
+            mine = pl.ds(h, GROUP, stride=heads)
+            tmpk[slot, mine, :] = dk_ref[rows, lanes] + dot(keep_rows(closing, vd_ref[rows, lanes]), rin[h], NT)
+            tmpv[slot, mine, :] = dv_ref[rows, lanes] + dot(keep_rows(closing, kd_ref[rows, lanes]), rin[h])
+        bufk[pairs, :] = tmpk[slot].astype(BF16)
+        bufv[pairs, :] = tmpv[slot].astype(BF16)
         for n, (buf, out) in enumerate(((bufk, gk_ref), (bufv, gv_ref))):
             copy = pltpu.make_async_copy(buf.at[pairs], out.at[pairs], sems.at[n, g])
             copy.start()
@@ -302,23 +361,20 @@
         copy.wait()
 
 
-def call(kernel, name, outs, scratch, out_any=(), flops=0, n_in=0):
+def call(kernel, name, outs, scratch, in_hbm=(), out_hbm=(), flops=0, n_in=0, limit=16):
     vmem = pl.BlockSpec(memory_space=pltpu.VMEM)
-    specs = [pl.BlockSpec(memory_space=pl.ANY) if i in out_any else vmem for i in range(len(outs))]
+    hbm = pl.BlockSpec(memory_space=pltpu.HBM)
     return pl.pallas_call(
         kernel,
         name=name,
         out_shape=[jax.ShapeDtypeStruct(s, d) for s, d in outs],
-        in_specs=[pl.BlockSpec(memory_space=pltpu.SMEM)] + [vmem] * n_in,
-        out_specs=specs,
+        in_specs=[pl.BlockSpec(memory_space=pltpu.SMEM)]
+        + [hbm if i in in_hbm else vmem for i in range(n_in)],
+        out_specs=[hbm if i in out_hbm else vmem for i in range(len(outs))],
         scratch_shapes=scratch,
         cost_estimate=pl.CostEstimate(flops=flops, bytes_accessed=8 << 20, transcendentals=0),
-        compiler_params=pltpu.CompilerParams(vmem_limit_bytes=30 << 20),
+        compiler_params=pltpu.CompilerParams(vmem_limit_bytes=limit << 20),
     )
-
-
-def segment(ends, place):
-    return jnp.sum((ends <= place).astype(jnp.int32))
 
 
 def per_device(queries, keys, values, cotangent, doc_lengths):
@@ -328,15 +384,7 @@
     n_groups = tokens // GROUP
     n_seq = lax.axis_size("seq")
     n_head = lax.axis_size("head")
-    shard = lax.axis_index("seq")
-    core = shard % 2
-    chip = shard // 2
     n_chips = n_seq // 2
-    ends = jnp.cumsum(doc_lengths)
-    seg = functools.partial(segment, ends)
-    chip_first = chip * (2 * tokens)
-    middle = chip_first + tokens
-    chip_end = middle + tokens
 
     def pairs(x):
         return x.reshape(tokens * heads, head_width)
@@ -346,50 +394,37 @@
     piece = (half, head_width, head_width)
     state_shape = (heads, head_width, head_width)
     flat = (tokens * heads, head_width)
+    buf = pltpu.VMEM(flat, BF16)
+    tmp = pltpu.VMEM((2, GROUP * heads, head_width), F32)
+    sems = pltpu.SemaphoreType.DMA((2, n_groups))
     swap_pairs = [(i, i ^ 1) for i in range(n_seq)]
 
     def swap(x):
         return lax.ppermute(x, "seq", swap_pairs)
 
-    def exchange(mine, got, sign, after):
-        near = jnp.where(core == (0 if sign > 0 else 1), mine, got)
-        far = jnp.where(core == (0 if sign > 0 else 1), got, mine)
-        if sign > 0:
-            joined = seg(middle - 1) == seg(chip_end - 1)
-            onward = seg(chip_first - 1) == seg(middle - 1)
-        else:
-            joined = seg(middle) == seg(chip_first)
-            onward = seg(chip_end) == seg(middle)
-        chip_state = far + joined.astype(F32) * near
-        chip_state, after = lax.optimization_barrier((chip_state, after))
+    def exchange(mine, send, weights, sign, after):
+        got = swap(send)
+        chip_state, after = lax.optimization_barrier((weights[0] * mine + weights[1] * got, after))
         total = jnp.zeros(piece, F32)
         for k in range(1, n_chips):
             links = [(i, i + 2 * k * sign) for i in range(n_seq) if 0 <= i + 2 * k * sign < n_seq]
-            arrived = lax.ppermute(chip_state, "seq", links)
-            if sign > 0:
-                same = seg(chip_first - 2 * tokens * (k - 1) - 1) == seg(chip_first - 1)
-            else:
-                same = seg(chip_end + 2 * tokens * (k - 1)) == seg(chip_end)
-            total = total + same.astype(F32) * arrived
-        return near, onward.astype(F32), total, after
-
-    def finish(near, onward, total, sign):
-        farther = near + onward * total
-        is_near = core == (0 if sign > 0 else 1)
-        own = jnp.where(is_near, total, farther)
-        send = jnp.where(is_near, farther, total)
-        return own, swap(send)
+            total = total + weights[5 + k] * lax.ppermute(chip_state, "seq", links)
+        return got, total, after
+
+    def finish(mine, got, total, weights):
+        return weights[2] * total + weights[3] * got, swap(weights[4] * total + weights[5] * mine)
 
     mm = 2 * tokens * heads * head_width * head_width
-    kd, vd, mine, send = call(
-        state_kernel,
+    table = ((5 + n_chips, 128), F32)
+    kd, vd, mine, send, fore, back = call(
+        functools.partial(state_kernel, n_seq),
         "shard_state",
-        [(full, BF16), (full, BF16), (piece, F32), (piece, F32)],
-        [pltpu.VMEM(flat, F32), pltpu.VMEM(flat, F32), pltpu.VMEM(state_shape, F32)],
+        [(full, BF16), (full, BF16), (piece, F32), (piece, F32), table, table],
+        [tmp, tmp, pltpu.VMEM(state_shape, F32)],
         n_in=2,
         flops=mm,
     )(doc_lengths, k2, v2)
-    near, onward, total, (kd_b, vd_b) = exchange(mine, swap(send), 1, (kd, vd))
+    got, total, (kd_b, vd_b) = exchange(mine, send, fore, 1, (kd, vd))
     qd, qt, cd, probs, o_local, sb = call(
         local_kernel,
         "local_mix",
@@ -401,11 +436,11 @@
             (full, F32),
             ((n_groups, heads, head_width, head_width), BF16),
         ],
-        [pltpu.VMEM(flat, F32), pltpu.VMEM(flat, F32), pltpu.VMEM(state_shape, F32)],
+        [tmp, tmp, pltpu.VMEM(state_shape, F32)],
         n_in=4,
         flops=6 * mm,
     )(doc_lengths, kd_b, vd_b, q2, c2)
-    own, other = finish(near, onward, total, 1)
+    own, other = finish(mine, got, total, fore)
     o, sin, stats = call(
         stats_kernel,
         "mix_and_stats",
@@ -423,38 +458,24 @@
         n_in=4,
         flops=mm,
     )(doc_lengths, stats, o, cd, qt)
-    near, onward, total, (dob_b, inv_b) = exchange(mine, swap(send), -1, (dob, inv))
+    got, total, (dob_b, inv_b) = exchange(mine, send, back, -1, (dob, inv))
     dk, dv, output, grad_q = call(
         grad_kernel,
         "local_grads",
         [(full, F32), (full, F32), (flat, BF16), (flat, BF16)],
-        [
-            pltpu.VMEM(flat, F32),
-            pltpu.VMEM(flat, F32),
-            pltpu.VMEM(flat, BF16),
-            pltpu.VMEM(flat, BF16),
-            pltpu.VMEM(state_shape, F32),
-            pltpu.SemaphoreType.DMA((2, n_groups)),
-        ],
+        [tmp, tmp, buf, buf, pltpu.VMEM(state_shape, F32), sems],
         n_in=10,
-        out_any=(2, 3),
+        out_hbm=(2, 3),
         flops=12 * mm,
     )(doc_lengths, o, inv_b, dob_b, probs, qd, qt, kd, vd, sb, sin)
-    own, other = finish(near, onward, total, -1)
+    own, other = finish(mine, got, total, back)
     grad_k, grad_v = call(
         final_kernel,
         "final_grads",
         [(flat, BF16), (flat, BF16)],
-        [
-            pltpu.VMEM(state_shape, BF16),
-            pltpu.VMEM(flat, F32),
-            pltpu.VMEM(flat, F32),
-            pltpu.VMEM(flat, BF16),
-            pltpu.VMEM(flat, BF16),
-            pltpu.SemaphoreType.DMA((2, n_groups)),
-        ],
+        [pltpu.VMEM(state_shape, BF16), tmp, tmp, buf, buf, sems],
         n_in=6,
-        out_any=(0, 1),
+        out_hbm=(0, 1),
         flops=2 * mm,
     )(doc_lengths, dk, dv, kd, vd, own, other)
     return tuple(x.reshape(queries.shape) for x in (output, grad_q, grad_k, grad_v))

time: 90 us -> 59.9 us (0.67)
  the two profiles are of different devices: /device:TPU:0 before, /device:TPU:25 now
where the time goes in v2:
time: 59.9 us; the launch traced here: 59.5 us
  Pallas kernels  25.9 us (43%)
  starting transfers between devices  17.3 us (29%)
  blocking collectives  7.02 us (12%)
  waiting for transfers between devices  4.93 us (8%)
  local copies, waits for them, and re-layouts  3.48 us (6%)
  between operations  0.79 us (1%)
    ppermute x6, starting transfers between devices, exchange(): total = total + weights[5 + k] * lax.ppermute(chip_state, 'seq', links)  12.6 us
    pallas_call x1, Pallas kernels, per_device(): call(grad_kernel, 'local_grads', [(full, F32), (full, F32), (flat, BF16),...  10.3 us
    all_to_all x1, blocking collectives, per_device(): stats = lax.all_to_all(stats, 'head', 0, 0)  7.02 us
    pallas_call x1, Pallas kernels, per_device(): call(local_kernel, 'local_mix', [(full, BF16), ((width, tokens), BF16), (...  5.89 us
    ppermute x4, starting transfers between devices, swap(): return lax.ppermute(x, 'seq', swap_pairs)  4.64 us
    ppermute x4, waiting for transfers between devices, swap(): return lax.ppermute(x, 'seq', swap_pairs)  3.57 us
    unnamed x10, local copies, waits for them, and re-layouts  3.47 us
    pallas_call x1, Pallas kernels, per_device(): call(final_kernel, 'final_grads', [(flat, BF16), (flat, BF16)], [pltpu.VM...  3.07 us
  transfers between devices with their start and end apart: 10, of which 5 were waited for; matrix products, arithmetic and copies ran while one was open for 0% of the time, Pallas kernels for 27%

profile of v2, /device:TPU:25, one launch (start us, length us, event | category | flops | bytes accessed | tf_op | source)
XLA Modules:
  0.0 59.5 jit_solution(18406496507424107388)
XLA Ops:
  0.6 1.4 %copy-done = bf16[3072,2,128]{2,1,0:T(2,128)(2,1)S(1)} copy-done((bf16[3072,2,128]{2,1,0:T(2,128)(2,1)S(1)}, bf16[3072,2,128]{2,1,0:T(2,128)(2,1)}, u32[]{:S(2)}) %copy-start) | copy-done | bytes 1572888
  2.0 1.4 %copy-done.1 = bf16[3072,2,128]{2,1,0:T(2,128)(2,1)S(1)} copy-done((bf16[3072,2,128]{2,1,0:T(2,128)(2,1)S(1)}, bf16[3072,2,128]{2,1,0:T(2,128)(2,1)}, u32[]{:S(2)}) %copy-start.1) | copy-done | bytes 1572888
  4.1 2.2 %shard_state.1 = (bf16[3072,256]{1,0:T(8,128)(2,1)S(1)}, bf16[3072,256]{1,0:T(8,128)(2,1)S(1)}, f32[1,128,128]{2,1,0:T(8,128)S(1)}, f32[1,128,128]{2,1,0:T(8,128...) custom-call(s32[6]{0:T(128)S(1)} %copy-done.4, bf16[6144,128]{1,0:T(8,128)(2,1)S(1)} %bitcast.44, ...), custom_call_target="tpu_custom_call" | custom-call | flops 201326592 | bytes 8388608 | tf_op jit(solution)/shard_map/shard_state/pallas_call | solution.py:419
  6.3 0.7 %collective-permute-start = (f32[1,128,128]{2,1,0:T(8,128)S(1)}, f32[1,128,128]{2,1,0:T(8,128)S(1)}, u32[]{:S(2)}, u32[]{:S(2)}) collective-permute-start(f32[1,128,128]{2,1,0:T(8,128)S(1)} %get-tuple-element.37), channel_id=1, source_target_pairs={{0,4},{4,0},{8,12},{12,8},{16,20},{20,16},{24,28},{28,24},{1,5},{5... | collective-permute-start | bytes 196616 | tf_op jit(solution)/shard_map/ppermute | solution.py:403
  7.0 0.9 %collective-permute-done = f32[1,128,128]{2,1,0:T(8,128)S(1)} collective-permute-done((f32[1,128,128]{2,1,0:T(8,128)S(1)}, f32[1,128,128]{2,1,0:T(8,128)S(1)}, u32[]{:S(2)}, u32[]{:S(2)}) %collective-permute-start) | collective-permute-done | bytes 65568 | tf_op jit(solution)/shard_map/ppermute | solution.py:403
  7.9 1.3 %collective-permute-start.1 = (f32[1,128,128]{2,1,0:T(8,128)S(1)}, f32[1,128,128]{2,1,0:T(8,128)S(1)}, u32[]{:S(2)}, u32[]{:S(2)}) collective-permute-start(f32[1,128,128]{2,1,0:T(8,128)S(1)} %multiply_add_fusion.7), channel_id=1, source_target_pairs={{0,8},{4,12},{8,16},{12,20},{16,24},{20,28},{1,9},{5,13},{9,17},{1... | collective-permute-start | bytes 196616 | tf_op jit(solution)/shard_map/ppermute | solution.py:411
  9.2 1.3 %collective-permute-start.2 = (f32[1,128,128]{2,1,0:T(8,128)S(1)}, f32[1,128,128]{2,1,0:T(8,128)S(1)}, u32[]{:S(2)}, u32[]{:S(2)}) collective-permute-start(f32[1,128,128]{2,1,0:T(8,128)S(1)} %multiply_add_fusion.7), channel_id=1, source_target_pairs={{0,16},{4,20},{8,24},{12,28},{1,17},{5,21},{9,25},{13,29},{2,18},{... | collective-permute-start | bytes 196616 | tf_op jit(solution)/shard_map/ppermute | solution.py:411
  10.5 1.3 %collective-permute-start.3 = (f32[1,128,128]{2,1,0:T(8,128)S(1)}, f32[1,128,128]{2,1,0:T(8,128)S(1)}, u32[]{:S(2)}, u32[]{:S(2)}) collective-permute-start(f32[1,128,128]{2,1,0:T(8,128)S(1)} %multiply_add_fusion.7), channel_id=1, source_target_pairs={{0,24},{4,28},{1,25},{5,29},{2,26},{6,30},{3,27},{7,31}} | collective-permute-start | bytes 196616 | tf_op jit(solution)/shard_map/ppermute | solution.py:411
  11.9 5.9 %local_mix.1 = (bf16[3072,256]{1,0:T(8,128)(2,1)S(1)}, bf16[256,3072]{1,0:T(8,128)(2,1)S(1)}, bf16[3072,256]{1,0:T(8,128)(2,1)S(1)}, bf16[2,3072,256]{2,1,0:T(8,...) custom-call(s32[6]{0:T(128)S(1)} %copy-done.4, ...), custom_call_target="tpu_custom_call" | custom-call | flops 1207959552 | bytes 8388608 | tf_op jit(solution)/shard_map/local_mix/pallas_call | solution.py:428
  17.8 1.3 %collective-permute-done.3 = f32[1,128,128]{2,1,0:T(8,128)S(1)} collective-permute-done((f32[1,128,128]{2,1,0:T(8,128)S(1)}, f32[1,128,128]{2,1,0:T(8,128)S(1)}, u32[]{:S(2)}, u32[]{:S(2)}) %collective-permute-start.3) | collective-permute-done | bytes 65568 | tf_op jit(solution)/shard_map/ppermute | solution.py:411
  19.1 1.1 %collective-permute-start.4 = (f32[1,128,128]{2,1,0:T(8,128)S(1)}, f32[1,128,128]{2,1,0:T(8,128)S(1)}, u32[]{:S(2)}, u32[]{:S(2)}) collective-permute-start(f32[1,128,128]{2,1,0:T(8,128)S(1)} %get-tuple-element.68), channel_id=1, source_target_pairs={{0,4},{4,0},{8,12},{12,8},{16,20},{20,16},{24,28},{28,24},{1,5},{5... | collective-permute-start | bytes 196616 | tf_op jit(solution)/shard_map/ppermute | solution.py:403
  20.2 0.9 %collective-permute-done.4.other_ref = f32[1,128,128]{2,1,0:T(8,128)S(1)} collective-permute-done((f32[1,128,128]{2,1,0:T(8,128)S(1)}, f32[1,128,128]{2,1,0:T(8,128)S(1)}, u32[]{:S(2)}, u32[]{:S(2)}) %collective-permute-start.4) | collective-permute-done | bytes 65568 | tf_op jit(solution)/shard_map/ppermute | solution.py:403
  21.1 1.8 %mix_and_stats.1 = (f32[3072,256]{1,0:T(8,128)S(1)}, bf16[2,128,128]{2,1,0:T(8,128)(2,1)S(1)}, f32[4,2,3072]{2,1,0:T(2,128)S(1)}) custom-call(s32[6]{0:T(128)S(1)} %copy-done.4, bf16[3072,256]{1,0:T(8,128)(2,1)S(1)} %get-tuple-element.42.qd_ref, f32[3072,256]{1,0:T(8,128)S(1)} %get-tuple-element.43.ol_ref, bf16[3072,256]{1,0:T(8,128)(2,1)S(1)} %get-tuple-element.44.cd_ref, ...), custom_call_target="tpu_custom_call" | custom-call | flops 201326592 | bytes 8388608 | tf_op jit(solution)/shard_map/mix_and_stats/pallas_call | solution.py:444
  23.0 7.0 %all_to_all.5.st_ref = f32[4,2,3072]{2,1,0:T(2,128)S(1)} all-to-all(f32[4,2,3072]{2,1,0:T(2,128)S(1)} %get-tuple-element.48), channel_id=1, replica_groups=mesh['seq'=8,'head'=4] {'head'}, dimensions={0} | all-to-all | bytes 196608 | tf_op jit(solution)/shard_map/all_to_all | solution.py:452
  30.0 2.7 %norm_back.1 = (bf16[3072,256]{1,0:T(8,128)(2,1)S(1)}, f32[3072,128]{1,0:T(8,128)S(1)}, f32[1,128,128]{2,1,0:T(8,128)S(1)}, f32[1,128,128]{2,1,0:T(8,128)S(1)}) custom-call(s32[6]{0:T(128)S(1)} %copy-done.4, f32[4,2,3072]{2,1,0:T(2,128)S(1)} %all_to_all.5.st_ref, f32[3072,256]{1,0:T(8,128)S(1)} %get-tuple-element.46.o_ref, ...), custom_call_target="tpu_custom_call" | custom-call | flops 201326592 | bytes 8388608 | tf_op jit(solution)/shard_map/norm_back/pallas_call | solution.py:453
  32.7 1.8 %collective-permute-start.5 = (f32[1,128,128]{2,1,0:T(8,128)S(1)}, f32[1,128,128]{2,1,0:T(8,128)S(1)}, u32[]{:S(2)}, u32[]{:S(2)}) collective-permute-start(f32[1,128,128]{2,1,0:T(8,128)S(1)} %get-tuple-element.51), channel_id=1, source_target_pairs={{0,4},{4,0},{8,12},{12,8},{16,20},{20,16},{24,28},{28,24},{1,5},{5... | collective-permute-start | bytes 196616 | tf_op jit(solution)/shard_map/ppermute | solution.py:403
  34.6 0.9 %collective-permute-done.5 = f32[1,128,128]{2,1,0:T(8,128)S(1)} collective-permute-done((f32[1,128,128]{2,1,0:T(8,128)S(1)}, f32[1,128,128]{2,1,0:T(8,128)S(1)}, u32[]{:S(2)}, u32[]{:S(2)}) %collective-permute-start.5) | collective-permute-done | bytes 65568 | tf_op jit(solution)/shard_map/ppermute | solution.py:403
  35.5 1.7 %collective-permute-start.6 = (f32[1,128,128]{2,1,0:T(8,128)S(1)}, f32[1,128,128]{2,1,0:T(8,128)S(1)}, u32[]{:S(2)}, u32[]{:S(2)}) collective-permute-start(f32[1,128,128]{2,1,0:T(8,128)S(1)} %multiply_add_fusion.3), channel_id=1, source_target_pairs={{8,0},{12,4},{16,8},{20,12},{24,16},{28,20},{9,1},{13,5},{17,9},{2... | collective-permute-start | bytes 196616 | tf_op jit(solution)/shard_map/ppermute | solution.py:411
  37.1 5.8 %collective-permute-start.7 = (f32[1,128,128]{2,1,0:T(8,128)S(1)}, f32[1,128,128]{2,1,0:T(8,128)S(1)}, u32[]{:S(2)}, u32[]{:S(2)}) collective-permute-start(f32[1,128,128]{2,1,0:T(8,128)S(1)} %multiply_add_fusion.3), channel_id=1, source_target_pairs={{16,0},{20,4},{24,8},{28,12},{17,1},{21,5},{25,9},{29,13},{18,2},{... | collective-permute-start | bytes 196616 | tf_op jit(solution)/shard_map/ppermute | solution.py:411
  42.9 1.3 %collective-permute-start.8 = (f32[1,128,128]{2,1,0:T(8,128)S(1)}, f32[1,128,128]{2,1,0:T(8,128)S(1)}, u32[]{:S(2)}, u32[]{:S(2)}) collective-permute-start(f32[1,128,128]{2,1,0:T(8,128)S(1)} %multiply_add_fusion.3), channel_id=1, source_target_pairs={{24,0},{28,4},{25,1},{29,5},{26,2},{30,6},{27,3},{31,7}} | collective-permute-start | bytes 196616 | tf_op jit(solution)/shard_map/ppermute | solution.py:411
  44.2 10.3 %local_grads.1 = (f32[3072,256]{1,0:T(8,128)S(1)}, f32[3072,256]{1,0:T(8,128)S(1)}, bf16[6144,128]{1,0:T(8,128)(2,1)}, bf16[6144,128]{1,0:T(8,128)(2,1)}) custom-call(s32[6]{0:T(128)S(1)} %copy-done.4, f32[3072,256]{1,0:T(8,128)S(1)} %get-tuple-element.46.o_ref, f32[3072,128]{1,0:T(8,128)S(1)} %get-tuple-element.54.inv_ref, ...), custom_call_target="tpu_custom_call" | custom-call | flops 2415919104 | bytes 8388608 | tf_op jit(solution)/shard_map/local_grads/pallas_call | solution.py:462
  54.6 1.0 %collective-permute-start.9 = (f32[1,128,128]{2,1,0:T(8,128)S(1)}, f32[1,128,128]{2,1,0:T(8,128)S(1)}, u32[]{:S(2)}, u32[]{:S(2)}) collective-permute-start(f32[1,128,128]{2,1,0:T(8,128)S(1)} %get-tuple-element.66), channel_id=1, source_target_pairs={{0,4},{4,0},{8,12},{12,8},{16,20},{20,16},{24,28},{28,24},{1,5},{5... | collective-permute-start | bytes 196616 | tf_op jit(solution)/shard_map/ppermute | solution.py:403
  55.6 0.9 %collective-permute-done.9.other_ref = f32[1,128,128]{2,1,0:T(8,128)S(1)} collective-permute-done((f32[1,128,128]{2,1,0:T(8,128)S(1)}, f32[1,128,128]{2,1,0:T(8,128)S(1)}, u32[]{:S(2)}, u32[]{:S(2)}) %collective-permute-start.9) | collective-permute-done | bytes 65568 | tf_op jit(solution)/shard_map/ppermute | solution.py:403
  56.5 3.1 %final_grads.1 = (bf16[6144,128]{1,0:T(8,128)(2,1)}, bf16[6144,128]{1,0:T(8,128)(2,1)}) custom-call(s32[6]{0:T(128)S(1)} %copy-done.4, f32[3072,256]{1,0:T(8,128)S(1)} %get-tuple-element.61.dk_ref, f32[3072,256]{1,0:T(8,128)S(1)} %get-tuple-element.62.dv_ref, bf16[3072,256]{1,0:T(8,128)(2,1)S(1)} %get-tuple-element.40.kd_ref, ...), custom_call_target="tpu_custom_call" | custom-call | flops 402653184 | bytes 8388608 | tf_op jit(solution)/shard_map/final_grads/pallas_call | solution.py:472
  (21 shorter events, 0.8 us)
Async XLA Ops:
  0.6 1.4 %copy-start = (bf16[3072,2,128]{2,1,0:T(2,128)(2,1)S(1)}, bf16[3072,2,128]{2,1,0:T(2,128)(2,1)}, u32[]{:S(2)}) copy-start(bf16[3072,2,128]{2,1,0:T(2,128)(2,1)} %param.6) | copy-start | bytes 4718596
  2.0 1.4 %copy-start.1 = (bf16[3072,2,128]{2,1,0:T(2,128)(2,1)S(1)}, bf16[3072,2,128]{2,1,0:T(2,128)(2,1)}, u32[]{:S(2)}) copy-start(bf16[3072,2,128]{2,1,0:T(2,128)(2,1)} %param.7) | copy-start | bytes 4718596
  3.4 0.7 %copy-start.4 = (s32[6]{0:T(128)S(1)}, s32[6]{0:T(128)}, u32[]{:S(2)}) copy-start(s32[6]{0:T(128)} %doc_ref.11) | copy-start | bytes 76
  4.1 7.7 %copy-start.2 = (bf16[3072,2,128]{2,1,0:T(2,128)(2,1)S(1)}, bf16[3072,2,128]{2,1,0:T(2,128)(2,1)}, u32[]{:S(2)}) copy-start(bf16[3072,2,128]{2,1,0:T(2,128)(2,1)} %param.5) | copy-start | bytes 4718596
  4.1 7.7 %copy-start.3 = (bf16[3072,2,128]{2,1,0:T(2,128)(2,1)S(1)}, bf16[3072,2,128]{2,1,0:T(2,128)(2,1)}, u32[]{:S(2)}) copy-start(bf16[3072,2,128]{2,1,0:T(2,128)(2,1)} %param.8) | copy-start | bytes 4718596
  6.3 1.7 %collective-permute-start = (f32[1,128,128]{2,1,0:T(8,128)S(1)}, f32[1,128,128]{2,1,0:T(8,128)S(1)}, u32[]{:S(2)}, u32[]{:S(2)}) collective-permute-start(f32[1,128,128]{2,1,0:T(8,128)S(1)} %get-tuple-element.37), channel_id=1, source_target_pairs={{0,4},{4,0},{8,12},{12,8},{16,20},{20,16},{24,28},{28,24},{1,5},{5... | collective-permute-start | bytes 196616 | tf_op jit(solution)/shard_map/ppermute | solution.py:403
  7.9 9.8 %collective-permute-start.1 = (f32[1,128,128]{2,1,0:T(8,128)S(1)}, f32[1,128,128]{2,1,0:T(8,128)S(1)}, u32[]{:S(2)}, u32[]{:S(2)}) collective-permute-start(f32[1,128,128]{2,1,0:T(8,128)S(1)} %multiply_add_fusion.7), channel_id=1, source_target_pairs={{0,8},{4,12},{8,16},{12,20},{16,24},{20,28},{1,9},{5,13},{9,17},{1... | collective-permute-start | bytes 196616 | tf_op jit(solution)/shard_map/ppermute | solution.py:411
  9.2 8.5 %collective-permute-start.2 = (f32[1,128,128]{2,1,0:T(8,128)S(1)}, f32[1,128,128]{2,1,0:T(8,128)S(1)}, u32[]{:S(2)}, u32[]{:S(2)}) collective-permute-start(f32[1,128,128]{2,1,0:T(8,128)S(1)} %multiply_add_fusion.7), channel_id=1, source_target_pairs={{0,16},{4,20},{8,24},{12,28},{1,17},{5,21},{9,25},{13,29},{2,18},{... | collective-permute-start | bytes 196616 | tf_op jit(solution)/shard_map/ppermute | solution.py:411
  10.5 8.6 %collective-permute-start.3 = (f32[1,128,128]{2,1,0:T(8,128)S(1)}, f32[1,128,128]{2,1,0:T(8,128)S(1)}, u32[]{:S(2)}, u32[]{:S(2)}) collective-permute-start(f32[1,128,128]{2,1,0:T(8,128)S(1)} %multiply_add_fusion.7), channel_id=1, source_target_pairs={{0,24},{4,28},{1,25},{5,29},{2,26},{6,30},{3,27},{7,31}} | collective-permute-start | bytes 196616 | tf_op jit(solution)/shard_map/ppermute | solution.py:411
  19.1 2.0 %collective-permute-start.4 = (f32[1,128,128]{2,1,0:T(8,128)S(1)}, f32[1,128,128]{2,1,0:T(8,128)S(1)}, u32[]{:S(2)}, u32[]{:S(2)}) collective-permute-start(f32[1,128,128]{2,1,0:T(8,128)S(1)} %get-tuple-element.68), channel_id=1, source_target_pairs={{0,4},{4,0},{8,12},{12,8},{16,20},{20,16},{24,28},{28,24},{1,5},{5... | collective-permute-start | bytes 196616 | tf_op jit(solution)/shard_map/ppermute | solution.py:403
  32.7 2.7 %collective-permute-start.5 = (f32[1,128,128]{2,1,0:T(8,128)S(1)}, f32[1,128,128]{2,1,0:T(8,128)S(1)}, u32[]{:S(2)}, u32[]{:S(2)}) collective-permute-start(f32[1,128,128]{2,1,0:T(8,128)S(1)} %get-tuple-element.51), channel_id=1, source_target_pairs={{0,4},{4,0},{8,12},{12,8},{16,20},{20,16},{24,28},{28,24},{1,5},{5... | collective-permute-start | bytes 196616 | tf_op jit(solution)/shard_map/ppermute | solution.py:403
  35.5 19.0 %collective-permute-start.6 = (f32[1,128,128]{2,1,0:T(8,128)S(1)}, f32[1,128,128]{2,1,0:T(8,128)S(1)}, u32[]{:S(2)}, u32[]{:S(2)}) collective-permute-start(f32[1,128,128]{2,1,0:T(8,128)S(1)} %multiply_add_fusion.3), channel_id=1, source_target_pairs={{8,0},{12,4},{16,8},{20,12},{24,16},{28,20},{9,1},{13,5},{17,9},{2... | collective-permute-start | bytes 196616 | tf_op jit(solution)/shard_map/ppermute | solution.py:411
  37.1 17.4 %collective-permute-start.7 = (f32[1,128,128]{2,1,0:T(8,128)S(1)}, f32[1,128,128]{2,1,0:T(8,128)S(1)}, u32[]{:S(2)}, u32[]{:S(2)}) collective-permute-start(f32[1,128,128]{2,1,0:T(8,128)S(1)} %multiply_add_fusion.3), channel_id=1, source_target_pairs={{16,0},{20,4},{24,8},{28,12},{17,1},{21,5},{25,9},{29,13},{18,2},{... | collective-permute-start | bytes 196616 | tf_op jit(solution)/shard_map/ppermute | solution.py:411
  42.9 11.6 %collective-permute-start.8 = (f32[1,128,128]{2,1,0:T(8,128)S(1)}, f32[1,128,128]{2,1,0:T(8,128)S(1)}, u32[]{:S(2)}, u32[]{:S(2)}) collective-permute-start(f32[1,128,128]{2,1,0:T(8,128)S(1)} %multiply_add_fusion.3), channel_id=1, source_target_pairs={{24,0},{28,4},{25,1},{29,5},{26,2},{30,6},{27,3},{31,7}} | collective-permute-start | bytes 196616 | tf_op jit(solution)/shard_map/ppermute | solution.py:411
  54.6 1.9 %collective-permute-start.9 = (f32[1,128,128]{2,1,0:T(8,128)S(1)}, f32[1,128,128]{2,1,0:T(8,128)S(1)}, u32[]{:S(2)}, u32[]{:S(2)}) collective-permute-start(f32[1,128,128]{2,1,0:T(8,128)S(1)} %get-tuple-element.66), channel_id=1, source_target_pairs={{0,4},{4,0},{8,12},{12,8},{16,20},{20,16},{24,28},{28,24},{1,5},{5... | collective-permute-start | bytes 196616 | tf_op jit(solution)/shard_map/ppermute | solution.py:403

commit v3 on v2

v3 whole, which is shorter than its diff:
```python
import functools

import jax
import jax.numpy as jnp
from jax import lax
from jax.experimental import pallas as pl
from jax.experimental.pallas import tpu as pltpu
from jax.sharding import PartitionSpec as P

GROUP = 256
EPSILON = 1e-06
F32 = jnp.float32
BF16 = jnp.bfloat16

NN = (((1,), (0,)), ((), ()))
NT = (((1,), (1,)), ((), ()))
TN = (((0,), (0,)), ((), ()))


def dot(a, b, dims=NN):
    return lax.dot_general(a, b, dims, preferred_element_type=F32)


def doc_ends_of(doc_ref):
    ends, total = [], jnp.int32(0)
    for j in range(doc_ref.shape[0]):
        total = total + doc_ref[j]
        ends.append(total)
    return ends


def start_of(ends, place):
    found = jnp.int32(0)
    for end in ends:
        found = jnp.where(end <= place, end, found)
    return found


def end_of(ends, place):
    found = jnp.int32(2**30)
    for end in reversed(ends):
        found = jnp.where(end > place, end, found)
    return found


def rows_iota(width):
    return lax.broadcasted_iota(jnp.int32, (GROUP, width), 0)


def lanes_iota(rows):
    return lax.broadcasted_iota(jnp.int32, (rows, GROUP), 1)


def group_mask(ends, first):
    place = lanes_iota(8) + first
    begin = jnp.zeros((8, GROUP), jnp.int32)
    for end in ends:
        begin = jnp.where(place >= end, end, begin)
    begin = begin - first
    begin = jnp.concatenate([begin] * (GROUP // 8), axis=0)
    row = rows_iota(GROUP)
    return (row >= begin) & (row <= lanes_iota(GROUP))


def keep_where(keep, x):
    return jnp.where(keep, x.astype(F32), 0.0).astype(BF16)


def at(h):
    return slice(h * 128, (h + 1) * 128)


def turn(x):
    return x.astype(BF16).T


def pair_rows(g, heads):
    return pl.ds(pl.multiple_of(g * (GROUP * heads), GROUP * heads), GROUP * heads)


def split_heads(buf_ref, tmp_ref, g, heads):
    slot = g % tmp_ref.shape[0]
    tmp_ref[slot] = buf_ref[pair_rows(g, heads), :].astype(F32)
    return [tmp_ref[slot, pl.ds(h, GROUP, stride=heads), :] for h in range(heads)]


def group_rows(g):
    return pl.ds(pl.multiple_of(g * GROUP, GROUP), GROUP)


def weights_of(out_ref, ends, shard, tokens, n_seq, sign):
    core = shard % 2
    chip_first = (shard - core) * tokens
    middle = chip_first + tokens
    chip_end = middle + tokens
    if sign > 0:
        join = start_of(ends, chip_end - 1) < middle
        onward = start_of(ends, middle - 1) < chip_first
        same = [
            start_of(ends, chip_first - 1) < chip_first - 2 * tokens * k for k in range(n_seq // 2 - 1)
        ]
        is_near = core == 0
    else:
        join = end_of(ends, chip_first) > middle
        onward = end_of(ends, middle) > chip_end
        same = [end_of(ends, chip_end) > chip_end + 2 * tokens * k for k in range(n_seq // 2 - 1)]
        is_near = core == 1
    join, onward, is_near = (x.astype(F32) for x in (join, onward, is_near))
    far = 1.0 - is_near
    table = [
        is_near * join + far,
        is_near + far * join,
        is_near + far * onward,
        far,
        is_near * onward + far,
        is_near,
    ] + [x.astype(F32) for x in same]
    for i, x in enumerate(table):
        out_ref[pl.ds(i, 1), :] = jnp.full((1, 128), x, F32)


def state_kernel(
    n_seq, doc_hbm, k2_ref, v2_ref, kd_ref, vd_ref, vt_ref, mine_ref, send_ref, fore_ref, back_ref,
    doc_ref, bufk, bufv, tmpk, tmpv, acc, sems, doc_sem,
):
    tokens, width = kd_ref.shape
    heads = width // 128
    half = heads // 2
    n_groups = tokens // GROUP

    def fetches(g):
        rows = pair_rows(g, heads)
        return (
            pltpu.make_async_copy(k2_ref.at[rows], bufk.at[rows], sems.at[0, g]),
            pltpu.make_async_copy(v2_ref.at[rows], bufv.at[rows], sems.at[1, g]),
        )

    doc_copy = pltpu.make_async_copy(doc_hbm, doc_ref, doc_sem)
    doc_copy.start()
    for g in range(n_groups):
        for copy in fetches(g):
            copy.start()
    doc_copy.wait()
    shard = lax.axis_index("seq")
    core = shard % 2
    anchor = shard * tokens
    ends = doc_ends_of(doc_ref)
    weights_of(fore_ref, ends, shard, tokens, n_seq, 1)
    weights_of(back_ref, ends, shard, tokens, n_seq, -1)
    tail = start_of(ends, anchor + tokens - 1) - anchor

    def prepare(g):
        for copy in fetches(g):
            copy.wait()
        rows = group_rows(g)
        keep = rows_iota(128) + g * GROUP >= tail
        ks = split_heads(bufk, tmpk, g, heads)
        vs = split_heads(bufv, tmpv, g, heads)
        ready = []
        for h in range(heads):
            vt = turn(vs[h])
            kd_ref[rows, at(h)] = ks[h].astype(BF16)
            vd_ref[rows, at(h)] = vs[h].astype(BF16)
            vt_ref[at(h), rows] = vt
            ready.append((vt, jnp.where(keep, ks[h], 0.0).astype(BF16)))
        return ready

    total = [jnp.zeros((128, 128), F32) for _ in range(heads)]
    ahead = prepare(0)
    for g in range(n_groups):
        ready = ahead
        if g + 1 < n_groups:
            ahead = prepare(g + 1)
        total = [t + dot(vt, k) for t, (vt, k) in zip(total, ready)]
    for h in range(heads):
        acc[h] = total[h]
    mine_ref[...] = acc[pl.ds(core * half, half)]
    send_ref[...] = acc[pl.ds((1 - core) * half, half)]


def local_kernel(
    doc_ref, kd_ref, vt_ref, q2_ref, c2_ref, qd_ref, qt_ref, kt_ref, ct_ref, pt_ref, ol_ref, sl_ref,
    tmpq, tmpc,
):
    tokens, width = kd_ref.shape
    heads = width // 128
    n_groups = tokens // GROUP
    anchor = lax.axis_index("seq") * tokens
    ends = doc_ends_of(doc_ref)

    def prepare(g):
        rows = group_rows(g)
        qs = split_heads(q2_ref, tmpq, g, heads)
        cs = split_heads(c2_ref, tmpc, g, heads)
        qts = []
        for h in range(heads):
            qt = turn(qs[h])
            qd_ref[rows, at(h)] = qs[h].astype(BF16)
            qt_ref[at(h), rows] = qt
            kt_ref[at(h), rows] = turn(kd_ref[rows, at(h)])
            ct_ref[at(h), rows] = turn(cs[h])
            qts.append(qt)
        return qts

    def scores(g, qts):
        rows = group_rows(g)
        mask = group_mask(ends, anchor + g * GROUP)
        pts = []
        for h in range(heads):
            pt = jnp.where(mask, dot(kd_ref[rows, at(h)], qts[h]), 0.0).astype(BF16)
            pt_ref[h, rows, :] = pt
            pts.append(pt)
        return pts

    state = [jnp.zeros((128, 128), F32) for _ in range(heads)]
    next_pts = scores(0, prepare(0))
    next_qts = prepare(1) if n_groups > 1 else None
    for g in range(n_groups):
        pts = next_pts
        if g + 1 < n_groups:
            next_pts = scores(g + 1, next_qts)
        if g + 2 < n_groups:
            next_qts = prepare(g + 2)
        first = anchor + g * GROUP
        rows = group_rows(g)
        begin = start_of(ends, first + GROUP - 1)
        tail = rows_iota(128) >= begin - first
        kept = (begin < first).astype(F32)
        for h in range(heads):
            vt = vt_ref[at(h), rows]
            sl_ref[g, h] = state[h]
            state[h] = state[h] * kept + dot(vt, keep_where(tail, kd_ref[rows, at(h)]))
            ol_ref[at(h), rows] = dot(vt, pts[h])


def place_halves(core, out_ref, own_ref, other_ref):
    half = own_ref.shape[0]
    out_ref[pl.ds(core * half, half)] = own_ref[...]
    out_ref[pl.ds((1 - core) * half, half)] = other_ref[...]


def stats_kernel(doc_ref, qt_ref, ol_ref, ct_ref, sl_ref, own_ref, other_ref, o_ref, sb_ref, st_ref, sin):
    width, tokens = qt_ref.shape
    heads = width // 128
    n_groups = tokens // GROUP
    shard = lax.axis_index("seq")
    anchor = shard * tokens
    ends = doc_ends_of(doc_ref)
    place_halves(shard % 2, sin, own_ref, other_ref)

    def opened_terms(g):
        rows = group_rows(g)
        first = anchor + g * GROUP
        opened = lanes_iota(128) < end_of(ends, first - 1) - first
        same = (start_of(ends, first - 1) < anchor).astype(F32)
        terms = []
        for h in range(heads):
            sb = (sl_ref[g, h] + same * sin[h]).astype(BF16)
            sb_ref[g, h] = sb
            terms.append(jnp.where(opened, dot(sb, qt_ref[at(h), rows]), 0.0))
        return terms

    ahead = opened_terms(0)
    for g in range(n_groups):
        terms = ahead
        if g + 1 < n_groups:
            ahead = opened_terms(g + 1)
        rows = group_rows(g)
        squares = jnp.zeros((1, GROUP), F32)
        inner = jnp.zeros((1, GROUP), F32)
        for h in range(heads):
            o = ol_ref[at(h), rows] + terms[h]
            o_ref[at(h), rows] = o
            squares += jnp.sum(o * o, axis=0, keepdims=True)
            inner += jnp.sum(o * ct_ref[at(h), rows].astype(F32), axis=0, keepdims=True)
        both = jnp.concatenate([squares, inner], axis=0)
        for r in range(st_ref.shape[0]):
            st_ref[r, :, rows] = both


def norm_kernel(
    width_all, doc_ref, st_ref, o_ref, ct_ref, qd_ref, dobt_ref, inv_ref, mine_ref, send_ref, acc
):
    tokens, width = qd_ref.shape
    heads = width // 128
    half = heads // 2
    n_groups = tokens // GROUP
    shard = lax.axis_index("seq")
    core = shard % 2
    anchor = shard * tokens
    ends = doc_ends_of(doc_ref)
    head_to = end_of(ends, anchor) - anchor

    def prepare(g):
        rows = group_rows(g)
        keep = lanes_iota(128) + g * GROUP < head_to
        total = st_ref[0, :, rows]
        for r in range(1, st_ref.shape[0]):
            total = total + st_ref[r, :, rows]
        total = total * (1.0 / width_all)
        inv = lax.rsqrt(total[0:1] + EPSILON)
        slope = total[1:2] * inv * inv * inv
        inv_ref[:, rows] = jnp.broadcast_to(inv, (8, GROUP))
        ready = []
        for h in range(heads):
            dob = inv * ct_ref[at(h), rows].astype(F32) - slope * o_ref[at(h), rows]
            dobt_ref[at(h), rows] = dob.astype(BF16)
            ready.append(jnp.where(keep, dob, 0.0).astype(BF16))
        return ready

    total = [jnp.zeros((128, 128), F32) for _ in range(heads)]
    ahead = prepare(0)
    for g in range(n_groups):
        ready = ahead
        if g + 1 < n_groups:
            ahead = prepare(g + 1)
        total = [total[h] + dot(ready[h], qd_ref[group_rows(g), at(h)]) for h in range(heads)]
    for h in range(heads):
        acc[h] = total[h]
    mine_ref[...] = acc[pl.ds(core * half, half)]
    send_ref[...] = acc[pl.ds((1 - core) * half, half)]


def grad_kernel(
    doc_ref, o_ref, inv_ref, dobt_ref, pt_ref, qd_ref, kt_ref, vd_ref, sb_ref,
    dk_ref, dv_ref, rl_ref, out_ref, gq_ref, tmpo, tmpq, bufo, bufq, sems,
):
    tokens, width = qd_ref.shape
    heads = width // 128
    n_groups = tokens // GROUP
    anchor = lax.axis_index("seq") * tokens
    ends = doc_ends_of(doc_ref)

    def scores(g):
        rows = group_rows(g)
        mask = group_mask(ends, anchor + g * GROUP)
        return [
            jnp.where(mask, dot(vd_ref[rows, at(h)], dobt_ref[at(h), rows]), 0.0).astype(BF16)
            for h in range(heads)
        ]

    state = [jnp.zeros((128, 128), F32) for _ in range(heads)]
    started = []
    ahead = scores(n_groups - 1)
    for g in reversed(range(n_groups)):
        dpts = ahead
        slot = g % tmpq.shape[0]
        first = anchor + g * GROUP
        rows = group_rows(g)
        pairs = pair_rows(g, heads)
        opened = lanes_iota(128) < end_of(ends, first - 1) - first
        end = end_of(ends, first)
        head_part = lanes_iota(128) < end - first
        kept = (end > first + GROUP).astype(F32)
        for h in range(heads):
            mine = pl.ds(h, GROUP, stride=heads)
            dv_ref[rows, at(h)] = dot(pt_ref[h, rows, :], turn(dobt_ref[at(h), rows]))
            tmpo[slot, mine, :] = turn(o_ref[at(h), rows] * inv_ref[0:1, rows]).astype(F32)
        bufo[pairs, :] = tmpo[slot].astype(BF16)
        if g > 0:
            ahead = scores(g - 1)
        near, grown = [], []
        for h in range(heads):
            dobt = dobt_ref[at(h), rows]
            near.append(jnp.where(opened, dot(turn(sb_ref[g, h]), dobt), 0.0))
            grown.append(dot(keep_where(head_part, dobt), qd_ref[rows, at(h)]))
        for h in range(heads):
            mine = pl.ds(h, GROUP, stride=heads)
            dk_ref[rows, at(h)] = dot(dpts[h], qd_ref[rows, at(h)])
            gq = dot(kt_ref[at(h), rows], dpts[h]) + near[h]
            tmpq[slot, mine, :] = turn(gq).astype(F32)
            rl_ref[g, h] = state[h]
            state[h] = state[h] * kept + grown[h]
        bufq[pairs, :] = tmpq[slot].astype(BF16)
        for n, (buf, out) in enumerate(((bufo, out_ref), (bufq, gq_ref))):
            copy = pltpu.make_async_copy(buf.at[pairs], out.at[pairs], sems.at[n, g])
            copy.start()
            started.append(copy)
    for copy in started:
        copy.wait()


def final_kernel(
    doc_ref, dk_ref, dv_ref, kd_ref, vd_ref, rl_ref, own_ref, other_ref, gk_ref, gv_ref,
    rin, tmpk, tmpv, bufk, bufv, sems,
):
    tokens, width = kd_ref.shape
    heads = width // 128
    n_groups = tokens // GROUP
    shard = lax.axis_index("seq")
    anchor = shard * tokens
    ends = doc_ends_of(doc_ref)
    place_halves(shard % 2, rin, own_ref, other_ref)

    def closing_terms(g):
        rows = group_rows(g)
        after = anchor + (g + 1) * GROUP
        closing = rows_iota(128) + (after - GROUP) >= start_of(ends, after)
        same = (end_of(ends, after) > anchor + tokens).astype(F32)
        terms = []
        for h in range(heads):
            rb = (rl_ref[g, h] + same * rin[h]).astype(BF16)
            terms.append(
                (
                    jnp.where(closing, dot(vd_ref[rows, at(h)], rb), 0.0),
                    jnp.where(closing, dot(kd_ref[rows, at(h)], rb, NT), 0.0),
                )
            )
        return terms

    started = []
    ahead = closing_terms(0)
    for g in range(n_groups):
        terms = ahead
        if g + 1 < n_groups:
            ahead = closing_terms(g + 1)
        rows = group_rows(g)
        pairs = pair_rows(g, heads)
        slot = g % tmpk.shape[0]
        for h in range(heads):
            mine = pl.ds(h, GROUP, stride=heads)
            tmpk[slot, mine, :] = dk_ref[rows, at(h)] + terms[h][0]
            tmpv[slot, mine, :] = dv_ref[rows, at(h)] + terms[h][1]
        bufk[pairs, :] = tmpk[slot].astype(BF16)
        bufv[pairs, :] = tmpv[slot].astype(BF16)
        for n, (buf, out) in enumerate(((bufk, gk_ref), (bufv, gv_ref))):
            copy = pltpu.make_async_copy(buf.at[pairs], out.at[pairs], sems.at[n, g])
            copy.start()
            started.append(copy)
    for copy in started:
        copy.wait()


def call(kernel, name, outs, scratch, in_hbm=(), out_hbm=(), flops=0, n_in=0, doc_hbm=False):
    vmem = pl.BlockSpec(memory_space=pltpu.VMEM)
    hbm = pl.BlockSpec(memory_space=pltpu.HBM)
    return pl.pallas_call(
        kernel,
        name=name,
        out_shape=[jax.ShapeDtypeStruct(s, d) for s, d in outs],
        in_specs=[hbm if doc_hbm else pl.BlockSpec(memory_space=pltpu.SMEM)]
        + [hbm if i in in_hbm else vmem for i in range(n_in)],
        out_specs=[hbm if i in out_hbm else vmem for i in range(len(outs))],
        scratch_shapes=scratch,
        cost_estimate=pl.CostEstimate(flops=flops, bytes_accessed=8 << 20, transcendentals=0),
        compiler_params=pltpu.CompilerParams(vmem_limit_bytes=16 << 20),
    )


def per_device(queries, keys, values, cotangent, doc_lengths):
    tokens, heads, head_width = queries.shape
    width = heads * head_width
    half = heads // 2
    n_groups = tokens // GROUP
    n_seq = lax.axis_size("seq")
    n_head = lax.axis_size("head")
    n_chips = n_seq // 2

    def pairs(x):
        return x.reshape(tokens * heads, head_width)

    q2, k2, v2, c2 = pairs(queries), pairs(keys), pairs(values), pairs(cotangent)
    full = (tokens, width)
    piece = (half, head_width, head_width)
    state_shape = (heads, head_width, head_width)
    flat = (tokens * heads, head_width)
    buf = pltpu.VMEM(flat, BF16)
    tmp = pltpu.VMEM((2, GROUP * heads, head_width), F32)
    sems = pltpu.SemaphoreType.DMA((2, n_groups))
    swap_pairs = [(i, i ^ 1) for i in range(n_seq)]

    def swap(x):
        return lax.ppermute(x, "seq", swap_pairs)

    def exchange(mine, send, weights, sign, after):
        got = swap(send)
        chip_state, after = lax.optimization_barrier((weights[0] * mine + weights[1] * got, after))
        total = jnp.zeros(piece, F32)
        for k in range(1, n_chips):
            links = [(i, i + 2 * k * sign) for i in range(n_seq) if 0 <= i + 2 * k * sign < n_seq]
            total = total + weights[5 + k] * lax.ppermute(chip_state, "seq", links)
        return got, total, after

    def finish(mine, got, total, weights):
        return weights[2] * total + weights[3] * got, swap(weights[4] * total + weights[5] * mine)

    mm = 2 * tokens * heads * head_width * head_width
    table = ((5 + n_chips, 128), F32)
    state = pltpu.VMEM(state_shape, F32)
    table = ((5 + n_chips, 128), F32)
    turned = (width, tokens)
    group_states = (n_groups, heads, head_width, head_width)
    kd, vd, vt, mine, send, fore, back = call(
        functools.partial(state_kernel, n_seq),
        "shard_state",
        [(full, BF16), (full, BF16), (turned, BF16), (piece, F32), (piece, F32), table, table],
        [
            pltpu.SMEM(doc_lengths.shape, jnp.int32),
            buf,
            buf,
            tmp,
            tmp,
            state,
            sems,
            pltpu.SemaphoreType.DMA,
        ],
        n_in=2,
        in_hbm=(0, 1),
        doc_hbm=True,
        flops=mm,
    )(*(pltpu.with_memory_space_constraint(x, pltpu.HBM) for x in (doc_lengths, k2, v2)))
    got, total, (kd_b, vt_b) = exchange(mine, send, fore, 1, (kd, vt))
    qd, qt, kt, ct, pt, o_local, sl = call(
        local_kernel,
        "local_mix",
        [
            (full, BF16),
            (turned, BF16),
            (turned, BF16),
            (turned, BF16),
            ((heads, tokens, GROUP), BF16),
            (turned, F32),
            (group_states, F32),
        ],
        [tmp, tmp],
        n_in=4,
        flops=6 * mm,
    )(doc_lengths, kd_b, vt_b, q2, c2)
    own, other = finish(mine, got, total, fore)
    o, sb, stats = call(
        stats_kernel,
        "mix_and_stats",
        [(turned, F32), (group_states, BF16), ((n_head, 2, tokens), F32)],
        [state],
        n_in=6,
        flops=mm,
    )(doc_lengths, qt, o_local, ct, sl, own, other)
    stats = lax.all_to_all(stats, "head", 0, 0)
    dobt, inv, mine, send = call(
        functools.partial(norm_kernel, float(width * n_head)),
        "norm_back",
        [(turned, BF16), ((8, tokens), F32), (piece, F32), (piece, F32)],
        [state],
        n_in=4,
        flops=mm,
    )(doc_lengths, stats, o, ct, qd)
    got, total, (dobt_b, inv_b) = exchange(mine, send, back, -1, (dobt, inv))
    dk, dv, rl, output, grad_q = call(
        grad_kernel,
        "local_grads",
        [(full, F32), (full, F32), (group_states, F32), (flat, BF16), (flat, BF16)],
        [tmp, tmp, buf, buf, sems],
        n_in=8,
        out_hbm=(3, 4),
        flops=12 * mm,
    )(doc_lengths, o, inv_b, dobt_b, pt, qd, kt, vd, sb)
    own, other = finish(mine, got, total, back)
    grad_k, grad_v = call(
        final_kernel,
        "final_grads",
        [(flat, BF16), (flat, BF16)],
        [state, tmp, tmp, buf, buf, sems],
        n_in=7,
        out_hbm=(0, 1),
        flops=2 * mm,
    )(doc_lengths, dk, dv, kd, vd, rl, own, other)
    return tuple(x.reshape(queries.shape) for x in (output, grad_q, grad_k, grad_v))


def solution(mesh):
    spec = P("seq", "head", None)
    return jax.shard_map(
        per_device,
        mesh=mesh,
        in_specs=(spec, spec, spec, spec, P()),
        out_specs=(spec, spec, spec, spec),
        check_vma=False,
    )
```

time: 59.9 us -> 52.1 us (0.87)
  the two profiles are of different devices: /device:TPU:25 before, /device:TPU:0 now
where the time goes in v3:
time: 52.1 us; the launch traced here: 51.9 us
  Pallas kernels  20.5 us (39%)
  starting transfers between devices  15.4 us (30%)
  blocking collectives  8.45 us (16%)
  waiting for transfers between devices  6.4 us (12%)
  between operations  1.02 us (2%)
    ppermute x6, starting transfers between devices, exchange(): total = total + weights[5 + k] * lax.ppermute(chip_state, 'seq', links)  14.7 us
    all_to_all x1, blocking collectives, per_device(): stats = lax.all_to_all(stats, 'head', 0, 0)  8.45 us
    pallas_call x1, Pallas kernels, per_device(): call(grad_kernel, 'local_grads', [(full, F32), (full, F32), (group_states...  5.91 us
    ppermute x4, waiting for transfers between devices, swap(): return lax.ppermute(x, 'seq', swap_pairs)  4.56 us
    pallas_call x1, Pallas kernels, per_device(): call(functools.partial(state_kernel, n_seq), 'shard_state', [(full, BF16)...  4.18 us
    pallas_call x1, Pallas kernels, per_device(): call(local_kernel, 'local_mix', [(full, BF16), (turned, BF16), (turned, B...  3.72 us
    pallas_call x1, Pallas kernels, per_device(): call(final_kernel, 'final_grads', [(flat, BF16), (flat, BF16)], [state, t...  3.3 us
    ppermute x6, waiting for transfers between devices, exchange(): total = total + weights[5 + k] * lax.ppermute(chip_state, 'seq', links)  1.84 us
  transfers between devices with their start and end apart: 10, of which 5 were waited for; matrix products, arithmetic and copies ran while one was open for 0% of the time, Pallas kernels for 19%

profile of v3, /device:TPU:0, one launch (start us, length us, event | category | flops | bytes accessed | tf_op | source)
XLA Modules:
  0.0 51.9 jit_solution(7559834759734133456)
XLA Ops:
  0.7 4.2 %shard_state.1 = (bf16[3072,256]{1,0:T(8,128)(2,1)S(1)}, bf16[3072,256]{1,0:T(8,128)(2,1)S(1)}, bf16[256,3072]{1,0:T(8,128)(2,1)S(1)}, f32[1,128,128]{2,1,0:T(8,...) custom-call(s32[6]{0:T(128)} %doc_ref.9, bf16[6144,128]{1,0:T(8,128)(2,1)} %bitcast.46, ...), custom_call_target="tpu_custom_call" | custom-call | flops 201326592 | bytes 8388608 | tf_op jit(solution)/shard_map/shard_state/pallas_call | solution.py:493
  4.8 0.5 collective-permute-start
  5.4 0.9 %collective-permute-done = f32[1,128,128]{2,1,0:T(8,128)S(1)} collective-permute-done((f32[1,128,128]{2,1,0:T(8,128)S(1)}, f32[1,128,128]{2,1,0:T(8,128)S(1)}, u32[]{:S(2)}, u32[]{:S(2)}) %collective-permute-start) | collective-permute-done | bytes 65568 | tf_op jit(solution)/shard_map/ppermute | solution.py:473
  6.3 4.8 %collective-permute-start.1 = (f32[1,128,128]{2,1,0:T(8,128)S(1)}, f32[1,128,128]{2,1,0:T(8,128)S(1)}, u32[]{:S(2)}, u32[]{:S(2)}) collective-permute-start(f32[1,128,128]{2,1,0:T(8,128)S(1)} %multiply_add_fusion.7), channel_id=1, source_target_pairs={{0,8},{4,12},{8,16},{12,20},{16,24},{20,28},{1,9},{5,13},{9,17},{1... | collective-permute-start | bytes 196616 | tf_op jit(solution)/shard_map/ppermute | solution.py:481
  11.1 4.5 %collective-permute-start.2 = (f32[1,128,128]{2,1,0:T(8,128)S(1)}, f32[1,128,128]{2,1,0:T(8,128)S(1)}, u32[]{:S(2)}, u32[]{:S(2)}) collective-permute-start(f32[1,128,128]{2,1,0:T(8,128)S(1)} %multiply_add_fusion.7), channel_id=1, source_target_pairs={{0,16},{4,20},{8,24},{12,28},{1,17},{5,21},{9,25},{13,29},{2,18},{... | collective-permute-start | bytes 196616 | tf_op jit(solution)/shard_map/ppermute | solution.py:481
  15.6 1.3 %collective-permute-start.3 = (f32[1,128,128]{2,1,0:T(8,128)S(1)}, f32[1,128,128]{2,1,0:T(8,128)S(1)}, u32[]{:S(2)}, u32[]{:S(2)}) collective-permute-start(f32[1,128,128]{2,1,0:T(8,128)S(1)} %multiply_add_fusion.7), channel_id=1, source_target_pairs={{0,24},{4,28},{1,25},{5,29},{2,26},{6,30},{3,27},{7,31}} | collective-permute-start | bytes 196616 | tf_op jit(solution)/shard_map/ppermute | solution.py:481
  17.0 3.7 %local_mix.1 = (bf16[3072,256]{1,0:T(8,128)(2,1)S(1)}, bf16[256,3072]{1,0:T(8,128)(2,1)S(1)}, bf16[256,3072]{1,0:T(8,128)(2,1)S(1)}, bf16[256,3072]{1,0:T(8,128)...) custom-call(s32[6]{0:T(128)S(1)} %copy-done.2, ...), custom_call_target="tpu_custom_call" | custom-call | flops 1207959552 | bytes 8388608 | tf_op jit(solution)/shard_map/local_mix/pallas_call | solution.py:513
  20.7 0.0 collective-permute-done.2
  20.7 0.0 collective-permute-done.3
  20.7 0.1 collective-permute-start.4
  20.8 1.2 %collective-permute-done.4.other_ref = f32[1,128,128]{2,1,0:T(8,128)S(1)} collective-permute-done((f32[1,128,128]{2,1,0:T(8,128)S(1)}, f32[1,128,128]{2,1,0:T(8,128)S(1)}, u32[]{:S(2)}, u32[]{:S(2)}) %collective-permute-start.4) | collective-permute-done | bytes 65568 | tf_op jit(solution)/shard_map/ppermute | solution.py:473
  22.1 1.7 %mix_and_stats.1 = (f32[256,3072]{1,0:T(8,128)S(1)}, bf16[12,2,128,128]{3,2,1,0:T(8,128)(2,1)S(1)}, f32[4,2,3072]{2,1,0:T(2,128)S(1)}) custom-call(s32[6]{0:T(128)S(1)} %copy-done.2, bf16[256,3072]{1,0:T(8,128)(2,1)S(1)} %get-tuple-element.45.qt_ref, f32[256,3072]{1,0:T(8,128)S(1)} %get-tuple-element.46.ol_ref, ...), custom_call_target="tpu_custom_call" | custom-call | flops 201326592 | bytes 8388608 | tf_op jit(solution)/shard_map/mix_and_stats/pallas_call | solution.py:530
  23.8 8.4 %all_to_all.5.st_ref = f32[4,2,3072]{2,1,0:T(2,128)S(1)} all-to-all(f32[4,2,3072]{2,1,0:T(2,128)S(1)} %get-tuple-element.52), channel_id=1, replica_groups=mesh['seq'=8,'head'=4] {'head'}, dimensions={0} | all-to-all | bytes 196608 | tf_op jit(solution)/shard_map/all_to_all | solution.py:538
  32.2 1.6 %norm_back.1 = (bf16[256,3072]{1,0:T(8,128)(2,1)S(1)}, f32[8,3072]{1,0:T(8,128)S(1)}, f32[1,128,128]{2,1,0:T(8,128)S(1)}, f32[1,128,128]{2,1,0:T(8,128)S(1)}) custom-call(s32[6]{0:T(128)S(1)} %copy-done.2, f32[4,2,3072]{2,1,0:T(2,128)S(1)} %all_to_all.5.st_ref, f32[256,3072]{1,0:T(8,128)S(1)} %get-tuple-element.50.o_ref, ...), custom_call_target="tpu_custom_call" | custom-call | flops 201326592 | bytes 8388608 | tf_op jit(solution)/shard_map/norm_back/pallas_call | solution.py:539
  33.9 0.1 collective-permute-start.5
  34.0 1.2 %collective-permute-done.5 = f32[1,128,128]{2,1,0:T(8,128)S(1)} collective-permute-done((f32[1,128,128]{2,1,0:T(8,128)S(1)}, f32[1,128,128]{2,1,0:T(8,128)S(1)}, u32[]{:S(2)}, u32[]{:S(2)}) %collective-permute-start.5) | collective-permute-done | bytes 65568 | tf_op jit(solution)/shard_map/ppermute | solution.py:473
  35.2 1.3 %collective-permute-start.6 = (f32[1,128,128]{2,1,0:T(8,128)S(1)}, f32[1,128,128]{2,1,0:T(8,128)S(1)}, u32[]{:S(2)}, u32[]{:S(2)}) collective-permute-start(f32[1,128,128]{2,1,0:T(8,128)S(1)} %multiply_add_fusion.3), channel_id=1, source_target_pairs={{8,0},{12,4},{16,8},{20,12},{24,16},{28,20},{9,1},{13,5},{17,9},{2... | collective-permute-start | bytes 196616 | tf_op jit(solution)/shard_map/ppermute | solution.py:481
  36.5 1.3 %collective-permute-start.7 = (f32[1,128,128]{2,1,0:T(8,128)S(1)}, f32[1,128,128]{2,1,0:T(8,128)S(1)}, u32[]{:S(2)}, u32[]{:S(2)}) collective-permute-start(f32[1,128,128]{2,1,0:T(8,128)S(1)} %multiply_add_fusion.3), channel_id=1, source_target_pairs={{16,0},{20,4},{24,8},{28,12},{17,1},{21,5},{25,9},{29,13},{18,2},{... | collective-permute-start | bytes 196616 | tf_op jit(solution)/shard_map/ppermute | solution.py:481
  37.8 1.5 %collective-permute-start.8 = (f32[1,128,128]{2,1,0:T(8,128)S(1)}, f32[1,128,128]{2,1,0:T(8,128)S(1)}, u32[]{:S(2)}, u32[]{:S(2)}) collective-permute-start(f32[1,128,128]{2,1,0:T(8,128)S(1)} %multiply_add_fusion.3), channel_id=1, source_target_pairs={{24,0},{28,4},{25,1},{29,5},{26,2},{30,6},{27,3},{31,7}} | collective-permute-start | bytes 196616 | tf_op jit(solution)/shard_map/ppermute | solution.py:481
  39.3 5.9 %local_grads.1 = (f32[3072,256]{1,0:T(8,128)S(1)}, f32[3072,256]{1,0:T(8,128)S(1)}, f32[12,2,128,128]{3,2,1,0:T(8,128)S(1)}, bf16[6144,128]{1,0:T(8,128)(2,1)}, bf16[6144,128]{1,0:T(8,128)(2,1)}) custom-call(s32[6]{0:T(128)S(1)} %copy-done.2, f32[256,3072]{1,0:T(8,128)S(1)} %get-tuple-element.50.o_ref, f32[8,3072]{1,0:T(8,128)S(1)} %get-tuple-element.58.inv_ref, ...), custom_call_target="tpu_custom_call" | custom-call | flops 2415919104 | bytes 8388608 | tf_op jit(solution)/shard_map/local_grads/pallas_call | solution.py:548
  45.2 1.8 %collective-permute-done.8 = f32[1,128,128]{2,1,0:T(8,128)S(1)} collective-permute-done((f32[1,128,128]{2,1,0:T(8,128)S(1)}, f32[1,128,128]{2,1,0:T(8,128)S(1)}, u32[]{:S(2)}, u32[]{:S(2)}) %collective-permute-start.8) | collective-permute-done | bytes 65568 | tf_op jit(solution)/shard_map/ppermute | solution.py:481
  47.1 0.1 collective-permute-start.9
  47.2 1.2 %collective-permute-done.9.other_ref = f32[1,128,128]{2,1,0:T(8,128)S(1)} collective-permute-done((f32[1,128,128]{2,1,0:T(8,128)S(1)}, f32[1,128,128]{2,1,0:T(8,128)S(1)}, u32[]{:S(2)}, u32[]{:S(2)}) %collective-permute-start.9) | collective-permute-done | bytes 65568 | tf_op jit(solution)/shard_map/ppermute | solution.py:473
  48.4 3.3 %final_grads.1 = (bf16[6144,128]{1,0:T(8,128)(2,1)}, bf16[6144,128]{1,0:T(8,128)(2,1)}) custom-call(s32[6]{0:T(128)S(1)} %copy-done.2, f32[3072,256]{1,0:T(8,128)S(1)} %get-tuple-element.66.dk_ref, f32[3072,256]{1,0:T(8,128)S(1)} %get-tuple-element.67.dv_ref, bf16[3072,256]{1,0:T(8,128)(2,1)S(1)} %get-tuple-element.43.kd_ref, ...), custom_call_target="tpu_custom_call" | custom-call | flops 402653184 | bytes 8388608 | tf_op jit(solution)/shard_map/final_grads/pallas_call | solution.py:558
  (17 shorter events, 0.1 us)
Async XLA Ops:
  0.6 16.3 %copy-start = (bf16[3072,2,128]{2,1,0:T(2,128)(2,1)S(1)}, bf16[3072,2,128]{2,1,0:T(2,128)(2,1)}, u32[]{:S(2)}) copy-start(bf16[3072,2,128]{2,1,0:T(2,128)(2,1)} %param.5) | copy-start | bytes 4718596
  0.6 16.3 %copy-start.1 = (bf16[3072,2,128]{2,1,0:T(2,128)(2,1)S(1)}, bf16[3072,2,128]{2,1,0:T(2,128)(2,1)}, u32[]{:S(2)}) copy-start(bf16[3072,2,128]{2,1,0:T(2,128)(2,1)} %param.8) | copy-start | bytes 4718596
  0.7 16.3 %copy-start.2 = (s32[6]{0:T(128)S(1)}, s32[6]{0:T(128)}, u32[]{:S(2)}) copy-start(s32[6]{0:T(128)} %doc_ref.9) | copy-start | bytes 76
  4.8 1.4 %collective-permute-start = (f32[1,128,128]{2,1,0:T(8,128)S(1)}, f32[1,128,128]{2,1,0:T(8,128)S(1)}, u32[]{:S(2)}, u32[]{:S(2)}) collective-permute-start(f32[1,128,128]{2,1,0:T(8,128)S(1)} %get-tuple-element.40), channel_id=1, source_target_pairs={{0,4},{4,0},{8,12},{12,8},{16,20},{20,16},{24,28},{28,24},{1,5},{5... | collective-permute-start | bytes 196616 | tf_op jit(solution)/shard_map/ppermute | solution.py:473
  6.3 14.4 %collective-permute-start.1 = (f32[1,128,128]{2,1,0:T(8,128)S(1)}, f32[1,128,128]{2,1,0:T(8,128)S(1)}, u32[]{:S(2)}, u32[]{:S(2)}) collective-permute-start(f32[1,128,128]{2,1,0:T(8,128)S(1)} %multiply_add_fusion.7), channel_id=1, source_target_pairs={{0,8},{4,12},{8,16},{12,20},{16,24},{20,28},{1,9},{5,13},{9,17},{1... | collective-permute-start | bytes 196616 | tf_op jit(solution)/shard_map/ppermute | solution.py:481
  11.1 9.6 %collective-permute-start.2 = (f32[1,128,128]{2,1,0:T(8,128)S(1)}, f32[1,128,128]{2,1,0:T(8,128)S(1)}, u32[]{:S(2)}, u32[]{:S(2)}) collective-permute-start(f32[1,128,128]{2,1,0:T(8,128)S(1)} %multiply_add_fusion.7), channel_id=1, source_target_pairs={{0,16},{4,20},{8,24},{12,28},{1,17},{5,21},{9,25},{13,29},{2,18},{... | collective-permute-start | bytes 196616 | tf_op jit(solution)/shard_map/ppermute | solution.py:481
  15.6 5.1 %collective-permute-start.3 = (f32[1,128,128]{2,1,0:T(8,128)S(1)}, f32[1,128,128]{2,1,0:T(8,128)S(1)}, u32[]{:S(2)}, u32[]{:S(2)}) collective-permute-start(f32[1,128,128]{2,1,0:T(8,128)S(1)} %multiply_add_fusion.7), channel_id=1, source_target_pairs={{0,24},{4,28},{1,25},{5,29},{2,26},{6,30},{3,27},{7,31}} | collective-permute-start | bytes 196616 | tf_op jit(solution)/shard_map/ppermute | solution.py:481
  20.7 1.3 %collective-permute-start.4 = (f32[1,128,128]{2,1,0:T(8,128)S(1)}, f32[1,128,128]{2,1,0:T(8,128)S(1)}, u32[]{:S(2)}, u32[]{:S(2)}) collective-permute-start(f32[1,128,128]{2,1,0:T(8,128)S(1)} %get-tuple-element.74), channel_id=1, source_target_pairs={{0,4},{4,0},{8,12},{12,8},{16,20},{20,16},{24,28},{28,24},{1,5},{5... | collective-permute-start | bytes 196616 | tf_op jit(solution)/shard_map/ppermute | solution.py:473
  33.9 1.3 %collective-permute-start.5 = (f32[1,128,128]{2,1,0:T(8,128)S(1)}, f32[1,128,128]{2,1,0:T(8,128)S(1)}, u32[]{:S(2)}, u32[]{:S(2)}) collective-permute-start(f32[1,128,128]{2,1,0:T(8,128)S(1)} %get-tuple-element.55), channel_id=1, source_target_pairs={{0,4},{4,0},{8,12},{12,8},{16,20},{20,16},{24,28},{28,24},{1,5},{5... | collective-permute-start | bytes 196616 | tf_op jit(solution)/shard_map/ppermute | solution.py:473
  35.2 10.0 %collective-permute-start.6 = (f32[1,128,128]{2,1,0:T(8,128)S(1)}, f32[1,128,128]{2,1,0:T(8,128)S(1)}, u32[]{:S(2)}, u32[]{:S(2)}) collective-permute-start(f32[1,128,128]{2,1,0:T(8,128)S(1)} %multiply_add_fusion.3), channel_id=1, source_target_pairs={{8,0},{12,4},{16,8},{20,12},{24,16},{28,20},{9,1},{13,5},{17,9},{2... | collective-permute-start | bytes 196616 | tf_op jit(solution)/shard_map/ppermute | solution.py:481
  36.5 8.7 %collective-permute-start.7 = (f32[1,128,128]{2,1,0:T(8,128)S(1)}, f32[1,128,128]{2,1,0:T(8,128)S(1)}, u32[]{:S(2)}, u32[]{:S(2)}) collective-permute-start(f32[1,128,128]{2,1,0:T(8,128)S(1)} %multiply_add_fusion.3), channel_id=1, source_target_pairs={{16,0},{20,4},{24,8},{28,12},{17,1},{21,5},{25,9},{29,13},{18,2},{... | collective-permute-start | bytes 196616 | tf_op jit(solution)/shard_map/ppermute | solution.py:481
  37.8 9.2 %collective-permute-start.8 = (f32[1,128,128]{2,1,0:T(8,128)S(1)}, f32[1,128,128]{2,1,0:T(8,128)S(1)}, u32[]{:S(2)}, u32[]{:S(2)}) collective-permute-start(f32[1,128,128]{2,1,0:T(8,128)S(1)} %multiply_add_fusion.3), channel_id=1, source_target_pairs={{24,0},{28,4},{25,1},{29,5},{26,2},{30,6},{27,3},{31,7}} | collective-permute-start | bytes 196616 | tf_op jit(solution)/shard_map/ppermute | solution.py:481
  47.1 1.3 %collective-permute-start.9 = (f32[1,128,128]{2,1,0:T(8,128)S(1)}, f32[1,128,128]{2,1,0:T(8,128)S(1)}, u32[]{:S(2)}, u32[]{:S(2)}) collective-permute-start(f32[1,128,128]{2,1,0:T(8,128)S(1)} %get-tuple-element.72), channel_id=1, source_target_pairs={{0,4},{4,0},{8,12},{12,8},{16,20},{20,16},{24,28},{28,24},{1,5},{5... | collective-permute-start | bytes 196616 | tf_op jit(solution)/shard_map/ppermute | solution.py:473

commit v4 on v3

--- a/solution.py
+++ b/solution.py
@@ -88,22 +88,35 @@
     return pl.ds(pl.multiple_of(g * GROUP, GROUP), GROUP)
 
 
+def source_of(index, step, size):
+    if size & (size - 1):
+        return (index + size - step) % size
+    return index ^ step
+
+
+def links_of(step, size):
+    return [(source_of(i, step, size), i) for i in range(size)]
+
+
 def weights_of(out_ref, ends, shard, tokens, n_seq, sign):
     core = shard % 2
+    chip = shard // 2
+    n_chips = n_seq // 2
+    others = [source_of(chip, k, n_chips) for k in range(1, n_chips)]
     chip_first = (shard - core) * tokens
     middle = chip_first + tokens
     chip_end = middle + tokens
     if sign > 0:
         join = start_of(ends, chip_end - 1) < middle
         onward = start_of(ends, middle - 1) < chip_first
-        same = [
-            start_of(ends, chip_first - 1) < chip_first - 2 * tokens * k for k in range(n_seq // 2 - 1)
-        ]
+        begin = start_of(ends, chip_first - 1)
+        same = [(other < chip) & (begin < (other + 1) * (2 * tokens)) for other in others]
         is_near = core == 0
     else:
         join = end_of(ends, chip_first) > middle
         onward = end_of(ends, middle) > chip_end
-        same = [end_of(ends, chip_end) > chip_end + 2 * tokens * k for k in range(n_seq // 2 - 1)]
+        end = end_of(ends, chip_end)
+        same = [(other > chip) & (end > other * (2 * tokens)) for other in others]
         is_near = core == 1
     join, onward, is_near = (x.astype(F32) for x in (join, onward, is_near))
     far = 1.0 - is_near
@@ -274,8 +287,7 @@
             squares += jnp.sum(o * o, axis=0, keepdims=True)
             inner += jnp.sum(o * ct_ref[at(h), rows].astype(F32), axis=0, keepdims=True)
         both = jnp.concatenate([squares, inner], axis=0)
-        for r in range(st_ref.shape[0]):
-            st_ref[r, :, rows] = both
+        st_ref[:, rows] = both
 
 
 def norm_kernel(
@@ -294,10 +306,7 @@
     def prepare(g):
         rows = group_rows(g)
         keep = lanes_iota(128) + g * GROUP < head_to
-        total = st_ref[0, :, rows]
-        for r in range(1, st_ref.shape[0]):
-            total = total + st_ref[r, :, rows]
-        total = total * (1.0 / width_all)
+        total = st_ref[:, rows] * (1.0 / width_all)
         inv = lax.rsqrt(total[0:1] + EPSILON)
         slope = total[1:2] * inv * inv * inv
         inv_ref[:, rows] = jnp.broadcast_to(inv, (8, GROUP))
@@ -472,12 +481,12 @@
     def swap(x):
         return lax.ppermute(x, "seq", swap_pairs)
 
-    def exchange(mine, send, weights, sign, after):
+    def exchange(mine, send, weights, after):
         got = swap(send)
         chip_state, after = lax.optimization_barrier((weights[0] * mine + weights[1] * got, after))
         total = jnp.zeros(piece, F32)
         for k in range(1, n_chips):
-            links = [(i, i + 2 * k * sign) for i in range(n_seq) if 0 <= i + 2 * k * sign < n_seq]
+            links = [(2 * i + c, 2 * j + c) for i, j in links_of(k, n_chips) for c in (0, 1)]
             total = total + weights[5 + k] * lax.ppermute(chip_state, "seq", links)
         return got, total, after
 
@@ -509,7 +518,7 @@
         doc_hbm=True,
         flops=mm,
     )(*(pltpu.with_memory_space_constraint(x, pltpu.HBM) for x in (doc_lengths, k2, v2)))
-    got, total, (kd_b, vt_b) = exchange(mine, send, fore, 1, (kd, vt))
+    got, total, (kd_b, vt_b) = exchange(mine, send, fore, (kd, vt))
     qd, qt, kt, ct, pt, o_local, sl = call(
         local_kernel,
         "local_mix",
@@ -530,12 +539,14 @@
     o, sb, stats = call(
         stats_kernel,
         "mix_and_stats",
-        [(turned, F32), (group_states, BF16), ((n_head, 2, tokens), F32)],
+        [(turned, F32), (group_states, BF16), ((2, tokens), F32)],
         [state],
         n_in=6,
         flops=mm,
     )(doc_lengths, qt, o_local, ct, sl, own, other)
-    stats = lax.all_to_all(stats, "head", 0, 0)
+    stats = stats + sum(
+        lax.ppermute(stats, "head", links_of(k, n_head)) for k in range(1, n_head)
+    )
     dobt, inv, mine, send = call(
         functools.partial(norm_kernel, float(width * n_head)),
         "norm_back",
@@ -544,7 +555,7 @@
         n_in=4,
         flops=mm,
     )(doc_lengths, stats, o, ct, qd)
-    got, total, (dobt_b, inv_b) = exchange(mine, send, back, -1, (dobt, inv))
+    got, total, (dobt_b, inv_b) = exchange(mine, send, back, (dobt, inv))
     dk, dv, rl, output, grad_q = call(
         grad_kernel,
         "local_grads",

time: 52.1 us -> 46.2 us (0.89)
  blocking collectives: 8.45 us -> 0 us
  waiting for transfers between devices: 6.4 us -> 11.2 us
  starting transfers between devices: 15.4 us -> 13.4 us
    all_to_all x1 -> x0, blocking collectives: 8.45 us -> none  [per_device(): stats = lax.all_to_all(stats, 'head', 0, 0)]
    ppermute x6, starting transfers between devices: 14.7 us -> 9.14 us  [exchange(): total = total + weights[5 + k] * lax.ppermute(chip_state, 'seq', links)]
    ppermute x0 -> x3, waiting for transfers between devices: none -> 4.24 us  [per_device(): lax.ppermute(stats, 'head', links_of(k, n_head))]
    ppermute x0 -> x3, starting transfers between devices: none -> 3.55 us  [per_device(): lax.ppermute(stats, 'head', links_of(k, n_head))]
    ppermute x6, waiting for transfers between devices: 1.84 us -> 2.41 us  [exchange(): total = total + weights[5 + k] * lax.ppermute(chip_state, 'seq', links)]
  transfers between devices with their start and end apart: 10 -> 13, of which waited for: 5 -> 9; matrix products, arithmetic and copies ran while one was open for 0% -> 0% of each run, Pallas kernels for 19% -> 21%
where the time goes in v4:
time: 46.2 us; the launch traced here: 46.1 us
  Pallas kernels  20.5 us (44%)
  starting transfers between devices  13.4 us (29%)
  waiting for transfers between devices  11.2 us (24%)
  between operations  0.8 us (2%)
    ppermute x6, starting transfers between devices, exchange(): total = total + weights[5 + k] * lax.ppermute(chip_state, 'seq', links)  9.14 us
    pallas_call x1, Pallas kernels, per_device(): call(grad_kernel, 'local_grads', [(full, F32), (full, F32), (group_states...  5.92 us
    ppermute x4, waiting for transfers between devices, swap(): return lax.ppermute(x, 'seq', swap_pairs)  4.56 us
    ppermute x3, waiting for transfers between devices, per_device(): lax.ppermute(stats, 'head', links_of(k, n_head))  4.24 us
    pallas_call x1, Pallas kernels, per_device(): call(functools.partial(state_kernel, n_seq), 'shard_state', [(full, BF16)...  4.18 us
    pallas_call x1, Pallas kernels, per_device(): call(local_kernel, 'local_mix', [(full, BF16), (turned, BF16), (turned, B...  3.73 us
    ppermute x3, starting transfers between devices, per_device(): lax.ppermute(stats, 'head', links_of(k, n_head))  3.55 us
    pallas_call x1, Pallas kernels, per_device(): call(final_kernel, 'final_grads', [(flat, BF16), (flat, BF16)], [state, t...  3.3 us
  transfers between devices with their start and end apart: 13, of which 9 were waited for; matrix products, arithmetic and copies ran while one was open for 0% of the time, Pallas kernels for 21%

profile of v4, /device:TPU:0, one launch (start us, length us, event | category | flops | bytes accessed | tf_op | source)
XLA Modules:
  0.0 46.1 jit_solution(15705474109604391989)
XLA Ops:
  0.7 4.2 %shard_state.1 = (bf16[3072,256]{1,0:T(8,128)(2,1)S(1)}, bf16[3072,256]{1,0:T(8,128)(2,1)S(1)}, bf16[256,3072]{1,0:T(8,128)(2,1)S(1)}, f32[1,128,128]{2,1,0:T(8,...) custom-call(s32[6]{0:T(128)} %doc_ref.9, bf16[6144,128]{1,0:T(8,128)(2,1)} %bitcast.46, ...), custom_call_target="tpu_custom_call" | custom-call | flops 201326592 | bytes 8388608 | tf_op jit(solution)/shard_map/shard_state/pallas_call | solution.py:502
  4.8 0.5 %collective-permute-start = (f32[1,128,128]{2,1,0:T(8,128)S(1)}, f32[1,128,128]{2,1,0:T(8,128)S(1)}, u32[]{:S(2)}, u32[]{:S(2)}) collective-permute-start(f32[1,128,128]{2,1,0:T(8,128)S(1)} %get-tuple-element.40), channel_id=1, source_target_pairs={{0,4},{4,0},{8,12},{12,8},{16,20},{20,16},{24,28},{28,24},{1,5},{5... | collective-permute-start | bytes 196616 | tf_op jit(solution)/shard_map/ppermute | solution.py:482
  5.4 0.9 %collective-permute-done = f32[1,128,128]{2,1,0:T(8,128)S(1)} collective-permute-done((f32[1,128,128]{2,1,0:T(8,128)S(1)}, f32[1,128,128]{2,1,0:T(8,128)S(1)}, u32[]{:S(2)}, u32[]{:S(2)}) %collective-permute-start) | collective-permute-done | bytes 65568 | tf_op jit(solution)/shard_map/ppermute | solution.py:482
  6.3 3.0 %collective-permute-start.1 = (f32[1,128,128]{2,1,0:T(8,128)S(1)}, f32[1,128,128]{2,1,0:T(8,128)S(1)}, u32[]{:S(2)}, u32[]{:S(2)}) collective-permute-start(f32[1,128,128]{2,1,0:T(8,128)S(1)} %multiply_add_fusion.7), channel_id=1, source_target_pairs={{8,0},{12,4},{0,8},{4,12},{24,16},{28,20},{16,24},{20,28},{9,1},{1... | collective-permute-start | bytes 196616 | tf_op jit(solution)/shard_map/ppermute | solution.py:490
  9.3 2.6 %collective-permute-start.2 = (f32[1,128,128]{2,1,0:T(8,128)S(1)}, f32[1,128,128]{2,1,0:T(8,128)S(1)}, u32[]{:S(2)}, u32[]{:S(2)}) collective-permute-start(f32[1,128,128]{2,1,0:T(8,128)S(1)} %multiply_add_fusion.7), channel_id=1, source_target_pairs={{16,0},{20,4},{24,8},{28,12},{0,16},{4,20},{8,24},{12,28},{17,1},{... | collective-permute-start | bytes 196616 | tf_op jit(solution)/shard_map/ppermute | solution.py:490
  11.9 3.7 %local_mix.1 = (bf16[3072,256]{1,0:T(8,128)(2,1)S(1)}, bf16[256,3072]{1,0:T(8,128)(2,1)S(1)}, bf16[256,3072]{1,0:T(8,128)(2,1)S(1)}, bf16[256,3072]{1,0:T(8,128)...) custom-call(s32[6]{0:T(128)S(1)} %copy-done.2, ...), custom_call_target="tpu_custom_call" | custom-call | flops 1207959552 | bytes 8388608 | tf_op jit(solution)/shard_map/local_mix/pallas_call | solution.py:522
  15.6 1.2 %collective-permute-done.2 = f32[1,128,128]{2,1,0:T(8,128)S(1)} collective-permute-done((f32[1,128,128]{2,1,0:T(8,128)S(1)}, f32[1,128,128]{2,1,0:T(8,128)S(1)}, u32[]{:S(2)}, u32[]{:S(2)}) %collective-permute-start.2) | collective-permute-done | bytes 65568 | tf_op jit(solution)/shard_map/ppermute | solution.py:490
  16.8 1.2 %collective-permute-done.3 = f32[1,128,128]{2,1,0:T(8,128)S(1)} collective-permute-done((f32[1,128,128]{2,1,0:T(8,128)S(1)}, f32[1,128,128]{2,1,0:T(8,128)S(1)}, u32[]{:S(2)}, u32[]{:S(2)}) %collective-permute-start.3) | collective-permute-done | bytes 65568 | tf_op jit(solution)/shard_map/ppermute | solution.py:490
  18.2 1.2 %collective-permute-done.4.other_ref = f32[1,128,128]{2,1,0:T(8,128)S(1)} collective-permute-done((f32[1,128,128]{2,1,0:T(8,128)S(1)}, f32[1,128,128]{2,1,0:T(8,128)S(1)}, u32[]{:S(2)}, u32[]{:S(2)}) %collective-permute-start.4) | collective-permute-done | bytes 65568 | tf_op jit(solution)/shard_map/ppermute | solution.py:482
  19.4 1.8 %mix_and_stats.1 = (f32[256,3072]{1,0:T(8,128)S(1)}, bf16[12,2,128,128]{3,2,1,0:T(8,128)(2,1)S(1)}, f32[2,3072]{1,0:T(2,128)S(1)}) custom-call(s32[6]{0:T(128)S(1)} %copy-done.2, bf16[256,3072]{1,0:T(8,128)(2,1)S(1)} %get-tuple-element.45.qt_ref, f32[256,3072]{1,0:T(8,128)S(1)} %get-tuple-element.46.ol_ref, bf16[256,3072]{1,0:T(8,128)(2,1)S(1)} %get-tuple-element.47.ct_ref, ...), custom_call_target="tpu_custom_call" | custom-call | flops 201326592 | bytes 8388608 | tf_op jit(solution)/shard_map/mix_and_stats/pallas_call | solution.py:539
  21.2 1.6 %collective-permute-start.5 = (f32[2,3072]{1,0:T(2,128)S(1)}, f32[2,3072]{1,0:T(2,128)S(1)}, u32[]{:S(2)}, u32[]{:S(2)}) collective-permute-start(f32[2,3072]{1,0:T(2,128)S(1)} %get-tuple-element.52), channel_id=1, source_target_pairs={{1,0},{0,1},{3,2},{2,3},{5,4},{4,5},{7,6},{6,7},{9,8},{8,9},{11,10... | collective-permute-start | bytes 73736 | tf_op jit(solution)/shard_map/ppermute | solution.py:548
  22.7 1.5 %collective-permute-start.6 = (f32[2,3072]{1,0:T(2,128)S(1)}, f32[2,3072]{1,0:T(2,128)S(1)}, u32[]{:S(2)}, u32[]{:S(2)}) collective-permute-start(f32[2,3072]{1,0:T(2,128)S(1)} %get-tuple-element.52), channel_id=1, source_target_pairs={{2,0},{3,1},{0,2},{1,3},{6,4},{7,5},{4,6},{5,7},{10,8},{11,9},{8,1... | collective-permute-start | bytes 73736 | tf_op jit(solution)/shard_map/ppermute | solution.py:548
  24.2 0.5 %collective-permute-start.7 = (f32[2,3072]{1,0:T(2,128)S(1)}, f32[2,3072]{1,0:T(2,128)S(1)}, u32[]{:S(2)}, u32[]{:S(2)}) collective-permute-start(f32[2,3072]{1,0:T(2,128)S(1)} %get-tuple-element.52), channel_id=1, source_target_pairs={{3,0},{2,1},{1,2},{0,3},{7,4},{6,5},{5,6},{4,7},{11,8},{10,9},{9,1... | collective-permute-start | bytes 73736 | tf_op jit(solution)/shard_map/ppermute | solution.py:548
  24.7 0.3 collective-permute-done.5
  25.0 1.5 %collective-permute-done.6 = f32[2,3072]{1,0:T(2,128)S(1)} collective-permute-done((f32[2,3072]{1,0:T(2,128)S(1)}, f32[2,3072]{1,0:T(2,128)S(1)}, u32[]{:S(2)}, u32[]{:S(2)}) %collective-permute-start.6) | collective-permute-done | bytes 24608 | tf_op jit(solution)/shard_map/ppermute | solution.py:548
  26.5 2.4 %collective-permute-done.7 = f32[2,3072]{1,0:T(2,128)S(1)} collective-permute-done((f32[2,3072]{1,0:T(2,128)S(1)}, f32[2,3072]{1,0:T(2,128)S(1)}, u32[]{:S(2)}, u32[]{:S(2)}) %collective-permute-start.7) | collective-permute-done | bytes 24608 | tf_op jit(solution)/shard_map/ppermute | solution.py:548
  29.0 1.6 %norm_back.1 = (bf16[256,3072]{1,0:T(8,128)(2,1)S(1)}, f32[8,3072]{1,0:T(8,128)S(1)}, f32[1,128,128]{2,1,0:T(8,128)S(1)}, f32[1,128,128]{2,1,0:T(8,128)S(1)}) custom-call(s32[6]{0:T(128)S(1)} %copy-done.2, f32[2,3072]{1,0:T(2,128)S(1)} %add_add_fusion.st_ref, f32[256,3072]{1,0:T(8,128)S(1)} %get-tuple-element.50.o_ref, ...), custom_call_target="tpu_custom_call" | custom-call | flops 201326592 | bytes 8388608 | tf_op jit(solution)/shard_map/norm_back/pallas_call | solution.py:550
  30.6 1.2 %collective-permute-done.8 = f32[1,128,128]{2,1,0:T(8,128)S(1)} collective-permute-done((f32[1,128,128]{2,1,0:T(8,128)S(1)}, f32[1,128,128]{2,1,0:T(8,128)S(1)}, u32[]{:S(2)}, u32[]{:S(2)}) %collective-permute-start.8) | collective-permute-done | bytes 65568 | tf_op jit(solution)/shard_map/ppermute | solution.py:482
  31.9 1.9 %collective-permute-start.10 = (f32[1,128,128]{2,1,0:T(8,128)S(1)}, f32[1,128,128]{2,1,0:T(8,128)S(1)}, u32[]{:S(2)}, u32[]{:S(2)}) collective-permute-start(f32[1,128,128]{2,1,0:T(8,128)S(1)} %multiply_add_fusion.3), channel_id=1, source_target_pairs={{16,0},{20,4},{24,8},{28,12},{0,16},{4,20},{8,24},{12,28},{17,1},{... | collective-permute-start | bytes 196616 | tf_op jit(solution)/shard_map/ppermute | solution.py:490
  33.8 1.4 %collective-permute-start.11 = (f32[1,128,128]{2,1,0:T(8,128)S(1)}, f32[1,128,128]{2,1,0:T(8,128)S(1)}, u32[]{:S(2)}, u32[]{:S(2)}) collective-permute-start(f32[1,128,128]{2,1,0:T(8,128)S(1)} %multiply_add_fusion.3), channel_id=1, source_target_pairs={{24,0},{28,4},{16,8},{20,12},{8,16},{12,20},{0,24},{4,28},{25,1},{... | collective-permute-start | bytes 196616 | tf_op jit(solution)/shard_map/ppermute | solution.py:490
  35.2 0.3 collective-permute-start.9
  35.4 5.9 %local_grads.1 = (f32[3072,256]{1,0:T(8,128)S(1)}, f32[3072,256]{1,0:T(8,128)S(1)}, f32[12,2,128,128]{3,2,1,0:T(8,128)S(1)}, bf16[6144,128]{1,0:T(8,128)(2,1)}, bf16[6144,128]{1,0:T(8,128)(2,1)}) custom-call(s32[6]{0:T(128)S(1)} %copy-done.2, f32[256,3072]{1,0:T(8,128)S(1)} %get-tuple-element.50.o_ref, f32[8,3072]{1,0:T(8,128)S(1)} %get-tuple-element.58.inv_ref, ...), custom_call_target="tpu_custom_call" | custom-call | flops 2415919104 | bytes 8388608 | tf_op jit(solution)/shard_map/local_grads/pallas_call | solution.py:559
  41.5 1.2 %collective-permute-done.12.other_ref = f32[1,128,128]{2,1,0:T(8,128)S(1)} collective-permute-done((f32[1,128,128]{2,1,0:T(8,128)S(1)}, f32[1,128,128]{2,1,0:T(8,128)S(1)}, u32[]{:S(2)}, u32[]{:S(2)}) %collective-permute-start.12) | collective-permute-done | bytes 65568 | tf_op jit(solution)/shard_map/ppermute | solution.py:482
  42.8 3.3 %final_grads.1 = (bf16[6144,128]{1,0:T(8,128)(2,1)}, bf16[6144,128]{1,0:T(8,128)(2,1)}) custom-call(s32[6]{0:T(128)S(1)} %copy-done.2, f32[3072,256]{1,0:T(8,128)S(1)} %get-tuple-element.66.dk_ref, f32[3072,256]{1,0:T(8,128)S(1)} %get-tuple-element.67.dv_ref, bf16[3072,256]{1,0:T(8,128)(2,1)S(1)} %get-tuple-element.43.kd_ref, ...), custom_call_target="tpu_custom_call" | custom-call | flops 402653184 | bytes 8388608 | tf_op jit(solution)/shard_map/final_grads/pallas_call | solution.py:569
  (23 shorter events, 0.4 us)
Async XLA Ops:
  0.6 11.2 %copy-start = (bf16[3072,2,128]{2,1,0:T(2,128)(2,1)S(1)}, bf16[3072,2,128]{2,1,0:T(2,128)(2,1)}, u32[]{:S(2)}) copy-start(bf16[3072,2,128]{2,1,0:T(2,128)(2,1)} %param.5) | copy-start | bytes 4718596
  0.6 11.2 %copy-start.1 = (bf16[3072,2,128]{2,1,0:T(2,128)(2,1)S(1)}, bf16[3072,2,128]{2,1,0:T(2,128)(2,1)}, u32[]{:S(2)}) copy-start(bf16[3072,2,128]{2,1,0:T(2,128)(2,1)} %param.8) | copy-start | bytes 4718596
  0.7 11.2 %copy-start.2 = (s32[6]{0:T(128)S(1)}, s32[6]{0:T(128)}, u32[]{:S(2)}) copy-start(s32[6]{0:T(128)} %doc_ref.9) | copy-start | bytes 76
  4.8 1.4 %collective-permute-start = (f32[1,128,128]{2,1,0:T(8,128)S(1)}, f32[1,128,128]{2,1,0:T(8,128)S(1)}, u32[]{:S(2)}, u32[]{:S(2)}) collective-permute-start(f32[1,128,128]{2,1,0:T(8,128)S(1)} %get-tuple-element.40), channel_id=1, source_target_pairs={{0,4},{4,0},{8,12},{12,8},{16,20},{20,16},{24,28},{28,24},{1,5},{5... | collective-permute-start | bytes 196616 | tf_op jit(solution)/shard_map/ppermute | solution.py:482
  6.3 9.3 %collective-permute-start.1 = (f32[1,128,128]{2,1,0:T(8,128)S(1)}, f32[1,128,128]{2,1,0:T(8,128)S(1)}, u32[]{:S(2)}, u32[]{:S(2)}) collective-permute-start(f32[1,128,128]{2,1,0:T(8,128)S(1)} %multiply_add_fusion.7), channel_id=1, source_target_pairs={{8,0},{12,4},{0,8},{4,12},{24,16},{28,20},{16,24},{20,28},{9,1},{1... | collective-permute-start | bytes 196616 | tf_op jit(solution)/shard_map/ppermute | solution.py:490
  9.3 7.5 %collective-permute-start.2 = (f32[1,128,128]{2,1,0:T(8,128)S(1)}, f32[1,128,128]{2,1,0:T(8,128)S(1)}, u32[]{:S(2)}, u32[]{:S(2)}) collective-permute-start(f32[1,128,128]{2,1,0:T(8,128)S(1)} %multiply_add_fusion.7), channel_id=1, source_target_pairs={{16,0},{20,4},{24,8},{28,12},{0,16},{4,20},{8,24},{12,28},{17,1},{... | collective-permute-start | bytes 196616 | tf_op jit(solution)/shard_map/ppermute | solution.py:490
  11.9 6.2 %collective-permute-start.3 = (f32[1,128,128]{2,1,0:T(8,128)S(1)}, f32[1,128,128]{2,1,0:T(8,128)S(1)}, u32[]{:S(2)}, u32[]{:S(2)}) collective-permute-start(f32[1,128,128]{2,1,0:T(8,128)S(1)} %multiply_add_fusion.7), channel_id=1, source_target_pairs={{24,0},{28,4},{16,8},{20,12},{8,16},{12,20},{0,24},{4,28},{25,1},{... | collective-permute-start | bytes 196616 | tf_op jit(solution)/shard_map/ppermute | solution.py:490
  18.1 1.3 %collective-permute-start.4 = (f32[1,128,128]{2,1,0:T(8,128)S(1)}, f32[1,128,128]{2,1,0:T(8,128)S(1)}, u32[]{:S(2)}, u32[]{:S(2)}) collective-permute-start(f32[1,128,128]{2,1,0:T(8,128)S(1)} %get-tuple-element.74), channel_id=1, source_target_pairs={{0,4},{4,0},{8,12},{12,8},{16,20},{20,16},{24,28},{28,24},{1,5},{5... | collective-permute-start | bytes 196616 | tf_op jit(solution)/shard_map/ppermute | solution.py:482
  21.2 3.9 %collective-permute-start.5 = (f32[2,3072]{1,0:T(2,128)S(1)}, f32[2,3072]{1,0:T(2,128)S(1)}, u32[]{:S(2)}, u32[]{:S(2)}) collective-permute-start(f32[2,3072]{1,0:T(2,128)S(1)} %get-tuple-element.52), channel_id=1, source_target_pairs={{1,0},{0,1},{3,2},{2,3},{5,4},{4,5},{7,6},{6,7},{9,8},{8,9},{11,10... | collective-permute-start | bytes 73736 | tf_op jit(solution)/shard_map/ppermute | solution.py:548
  22.7 3.8 %collective-permute-start.6 = (f32[2,3072]{1,0:T(2,128)S(1)}, f32[2,3072]{1,0:T(2,128)S(1)}, u32[]{:S(2)}, u32[]{:S(2)}) collective-permute-start(f32[2,3072]{1,0:T(2,128)S(1)} %get-tuple-element.52), channel_id=1, source_target_pairs={{2,0},{3,1},{0,2},{1,3},{6,4},{7,5},{4,6},{5,7},{10,8},{11,9},{8,1... | collective-permute-start | bytes 73736 | tf_op jit(solution)/shard_map/ppermute | solution.py:548
  24.2 4.7 %collective-permute-start.7 = (f32[2,3072]{1,0:T(2,128)S(1)}, f32[2,3072]{1,0:T(2,128)S(1)}, u32[]{:S(2)}, u32[]{:S(2)}) collective-permute-start(f32[2,3072]{1,0:T(2,128)S(1)} %get-tuple-element.52), channel_id=1, source_target_pairs={{3,0},{2,1},{1,2},{0,3},{7,4},{6,5},{5,6},{4,7},{11,8},{10,9},{9,1... | collective-permute-start | bytes 73736 | tf_op jit(solution)/shard_map/ppermute | solution.py:548
  30.6 1.3 %collective-permute-start.8 = (f32[1,128,128]{2,1,0:T(8,128)S(1)}, f32[1,128,128]{2,1,0:T(8,128)S(1)}, u32[]{:S(2)}, u32[]{:S(2)}) collective-permute-start(f32[1,128,128]{2,1,0:T(8,128)S(1)} %get-tuple-element.55), channel_id=1, source_target_pairs={{0,4},{4,0},{8,12},{12,8},{16,20},{20,16},{24,28},{28,24},{1,5},{5... | collective-permute-start | bytes 196616 | tf_op jit(solution)/shard_map/ppermute | solution.py:482
  31.9 9.5 %collective-permute-start.10 = (f32[1,128,128]{2,1,0:T(8,128)S(1)}, f32[1,128,128]{2,1,0:T(8,128)S(1)}, u32[]{:S(2)}, u32[]{:S(2)}) collective-permute-start(f32[1,128,128]{2,1,0:T(8,128)S(1)} %multiply_add_fusion.3), channel_id=1, source_target_pairs={{16,0},{20,4},{24,8},{28,12},{0,16},{4,20},{8,24},{12,28},{17,1},{... | collective-permute-start | bytes 196616 | tf_op jit(solution)/shard_map/ppermute | solution.py:490
  33.8 7.6 %collective-permute-start.11 = (f32[1,128,128]{2,1,0:T(8,128)S(1)}, f32[1,128,128]{2,1,0:T(8,128)S(1)}, u32[]{:S(2)}, u32[]{:S(2)}) collective-permute-start(f32[1,128,128]{2,1,0:T(8,128)S(1)} %multiply_add_fusion.3), channel_id=1, source_target_pairs={{24,0},{28,4},{16,8},{20,12},{8,16},{12,20},{0,24},{4,28},{25,1},{... | collective-permute-start | bytes 196616 | tf_op jit(solution)/shard_map/ppermute | solution.py:490
  35.2 6.2 %collective-permute-start.9 = (f32[1,128,128]{2,1,0:T(8,128)S(1)}, f32[1,128,128]{2,1,0:T(8,128)S(1)}, u32[]{:S(2)}, u32[]{:S(2)}) collective-permute-start(f32[1,128,128]{2,1,0:T(8,128)S(1)} %multiply_add_fusion.3), channel_id=1, source_target_pairs={{8,0},{12,4},{0,8},{4,12},{24,16},{28,20},{16,24},{20,28},{9,1},{1... | collective-permute-start | bytes 196616 | tf_op jit(solution)/shard_map/ppermute | solution.py:490
  41.4 1.3 %collective-permute-start.12 = (f32[1,128,128]{2,1,0:T(8,128)S(1)}, f32[1,128,128]{2,1,0:T(8,128)S(1)}, u32[]{:S(2)}, u32[]{:S(2)}) collective-permute-start(f32[1,128,128]{2,1,0:T(8,128)S(1)} %get-tuple-element.72), channel_id=1, source_target_pairs={{0,4},{4,0},{8,12},{12,8},{16,20},{20,16},{24,28},{28,24},{1,5},{5... | collective-permute-start | bytes 196616 | tf_op jit(solution)/shard_map/ppermute | solution.py:482

commit v5 on v4

--- a/solution.py
+++ b/solution.py
@@ -252,14 +252,23 @@
     out_ref[pl.ds((1 - core) * half, half)] = other_ref[...]
 
 
-def stats_kernel(doc_ref, qt_ref, ol_ref, ct_ref, sl_ref, own_ref, other_ref, o_ref, sb_ref, st_ref, sin):
+def part_of(core, own, half):
+    return (core if own else 1 - core) * half
+
+
+def head_rows(head):
+    return pl.ds(pl.multiple_of(head * 128, 128), 128)
+
+
+def stats_kernel(own, doc_ref, qt_ref, ol_ref, ct_ref, sl_ref, state_ref, *refs):
+    (before_ref, o_ref, sb_ref, st_ref) = refs if len(refs) == 4 else (None, *refs)
     width, tokens = qt_ref.shape
-    heads = width // 128
+    half = state_ref.shape[0]
     n_groups = tokens // GROUP
     shard = lax.axis_index("seq")
+    base = part_of(shard % 2, own, half)
     anchor = shard * tokens
     ends = doc_ends_of(doc_ref)
-    place_halves(shard % 2, sin, own_ref, other_ref)
 
     def opened_terms(g):
         rows = group_rows(g)
@@ -267,10 +276,10 @@
         opened = lanes_iota(128) < end_of(ends, first - 1) - first
         same = (start_of(ends, first - 1) < anchor).astype(F32)
         terms = []
-        for h in range(heads):
-            sb = (sl_ref[g, h] + same * sin[h]).astype(BF16)
+        for h in range(half):
+            sb = (sl_ref[g, base + h] + same * state_ref[h]).astype(BF16)
             sb_ref[g, h] = sb
-            terms.append(jnp.where(opened, dot(sb, qt_ref[at(h), rows]), 0.0))
+            terms.append(jnp.where(opened, dot(sb, qt_ref[head_rows(base + h), rows]), 0.0))
         return terms
 
     ahead = opened_terms(0)
@@ -281,57 +290,94 @@
         rows = group_rows(g)
         squares = jnp.zeros((1, GROUP), F32)
         inner = jnp.zeros((1, GROUP), F32)
-        for h in range(heads):
-            o = ol_ref[at(h), rows] + terms[h]
+        for h in range(half):
+            o = ol_ref[head_rows(base + h), rows] + terms[h]
             o_ref[at(h), rows] = o
             squares += jnp.sum(o * o, axis=0, keepdims=True)
-            inner += jnp.sum(o * ct_ref[at(h), rows].astype(F32), axis=0, keepdims=True)
+            inner += jnp.sum(o * ct_ref[head_rows(base + h), rows].astype(F32), axis=0, keepdims=True)
         both = jnp.concatenate([squares, inner], axis=0)
-        st_ref[:, rows] = both
-
-
-def norm_kernel(
-    width_all, doc_ref, st_ref, o_ref, ct_ref, qd_ref, dobt_ref, inv_ref, mine_ref, send_ref, acc
-):
-    tokens, width = qd_ref.shape
-    heads = width // 128
-    half = heads // 2
-    n_groups = tokens // GROUP
-    shard = lax.axis_index("seq")
-    core = shard % 2
-    anchor = shard * tokens
-    ends = doc_ends_of(doc_ref)
-    head_to = end_of(ends, anchor) - anchor
-
-    def prepare(g):
-        rows = group_rows(g)
-        keep = lanes_iota(128) + g * GROUP < head_to
-        total = st_ref[:, rows] * (1.0 / width_all)
-        inv = lax.rsqrt(total[0:1] + EPSILON)
-        slope = total[1:2] * inv * inv * inv
-        inv_ref[:, rows] = jnp.broadcast_to(inv, (8, GROUP))
-        ready = []
-        for h in range(heads):
-            dob = inv * ct_ref[at(h), rows].astype(F32) - slope * o_ref[at(h), rows]
-            dobt_ref[at(h), rows] = dob.astype(BF16)
-            ready.append(jnp.where(keep, dob, 0.0).astype(BF16))
-        return ready
-
-    total = [jnp.zeros((128, 128), F32) for _ in range(heads)]
+        st_ref[:, rows] = both if before_ref is None else both + before_ref[:, rows]
+
+
+def back_state(half, n_groups, prepare, qd_ref, base, out_ref):
+    total = [jnp.zeros((128, 128), F32) for _ in range(half)]
     ahead = prepare(0)
     for g in range(n_groups):
         ready = ahead
         if g + 1 < n_groups:
             ahead = prepare(g + 1)
-        total = [total[h] + dot(ready[h], qd_ref[group_rows(g), at(h)]) for h in range(heads)]
-    for h in range(heads):
-        acc[h] = total[h]
-    mine_ref[...] = acc[pl.ds(core * half, half)]
-    send_ref[...] = acc[pl.ds((1 - core) * half, half)]
+        total = [
+            total[h] + dot(ready[h], qd_ref[group_rows(g), head_rows(base + h)]) for h in range(half)
+        ]
+    for h in range(half):
+        out_ref[h] = total[h]
+
+
+def norm_kernel(
+    width_all, doc_ref, st_ref, o_ref, ct_ref, qd_ref, dobt_ref, rows_ref, send_ref
+):
+    tokens, width = qd_ref.shape
+    half = send_ref.shape[0]
+    shard = lax.axis_index("seq")
+    base = part_of(shard % 2, False, half)
+    anchor = shard * tokens
+    ends = doc_ends_of(doc_ref)
+    head_to = end_of(ends, anchor) - anchor
+
+    def prepare(g):
+        rows = group_rows(g)
+        keep = lanes_iota(128) + g * GROUP < head_to
+        total = st_ref[:, rows] * (1.0 / width_all)
+        inv = lax.rsqrt(total[0:1] + EPSILON)
+        slope = total[1:2] * inv * inv * inv
+        rows_ref[:, rows] = jnp.concatenate([inv, slope] * 4, axis=0)
+        ready = []
+        for h in range(half):
+            dob = inv * ct_ref[head_rows(base + h), rows].astype(F32) - slope * o_ref[at(h), rows]
+            dobt_ref[at(h), rows] = dob.astype(BF16)
+            ready.append(jnp.where(keep, dob, 0.0).astype(BF16))
+        return ready
+
+    back_state(half, tokens // GROUP, prepare, qd_ref, base, send_ref)
+
+
+def merge_kernel(
+    doc_ref, rows_ref, own_ref, other_ref, ct_ref, qd_ref, dob_other_ref, sb_own_ref, sb_other_ref,
+    dobt_ref, normed_ref, sb_ref, mine_ref,
+):
+    tokens, width = qd_ref.shape
+    half = mine_ref.shape[0]
+    shard = lax.axis_index("seq")
+    core = shard % 2
+    base, far = part_of(core, True, half), part_of(core, False, half)
+    anchor = shard * tokens
+    ends = doc_ends_of(doc_ref)
+    head_to = end_of(ends, anchor) - anchor
+
+    def prepare(g):
+        rows = group_rows(g)
+        keep = lanes_iota(128) + g * GROUP < head_to
+        inv = rows_ref[0:1, rows]
+        slope = rows_ref[1:2, rows]
+        ready = []
+        for h in range(half):
+            mine, others = head_rows(base + h), head_rows(far + h)
+            o = own_ref[at(h), rows]
+            dob = inv * ct_ref[mine, rows].astype(F32) - slope * o
+            dobt_ref[mine, rows] = dob.astype(BF16)
+            dobt_ref[others, rows] = dob_other_ref[at(h), rows]
+            normed_ref[mine, rows] = (o * inv).astype(BF16)
+            normed_ref[others, rows] = (other_ref[at(h), rows] * inv).astype(BF16)
+            sb_ref[g, base + h] = sb_own_ref[g, h]
+            sb_ref[g, far + h] = sb_other_ref[g, h]
+            ready.append(jnp.where(keep, dob, 0.0).astype(BF16))
+        return ready
+
+    back_state(half, tokens // GROUP, prepare, qd_ref, base, mine_ref)
 
 
 def grad_kernel(
-    doc_ref, o_ref, inv_ref, dobt_ref, pt_ref, qd_ref, kt_ref, vd_ref, sb_ref,
+    doc_ref, normed_ref, dobt_ref, pt_ref, qd_ref, kt_ref, vd_ref, sb_ref,
     dk_ref, dv_ref, rl_ref, out_ref, gq_ref, tmpo, tmpq, bufo, bufq, sems,
 ):
     tokens, width = qd_ref.shape
@@ -364,7 +410,7 @@
         for h in range(heads):
             mine = pl.ds(h, GROUP, stride=heads)
             dv_ref[rows, at(h)] = dot(pt_ref[h, rows, :], turn(dobt_ref[at(h), rows]))
-            tmpo[slot, mine, :] = turn(o_ref[at(h), rows] * inv_ref[0:1, rows]).astype(F32)
+            tmpo[slot, mine, :] = normed_ref[at(h), rows].T.astype(F32)
         bufo[pairs, :] = tmpo[slot].astype(BF16)
         if g > 0:
             ahead = scores(g - 1)
@@ -518,7 +564,7 @@
         doc_hbm=True,
         flops=mm,
     )(*(pltpu.with_memory_space_constraint(x, pltpu.HBM) for x in (doc_lengths, k2, v2)))
-    got, total, (kd_b, vt_b) = exchange(mine, send, fore, (kd, vt))
+    got, total, (kd_b, vt_b, q2_b, c2_b) = exchange(mine, send, fore, (kd, vt, q2, c2))
     qd, qt, kt, ct, pt, o_local, sl = call(
         local_kernel,
         "local_mix",
@@ -534,37 +580,54 @@
         [tmp, tmp],
         n_in=4,
         flops=6 * mm,
-    )(doc_lengths, kd_b, vt_b, q2, c2)
+    )(doc_lengths, kd_b, vt_b, q2_b, c2_b)
+    total, o_local = lax.optimization_barrier((total, o_local))
     own, other = finish(mine, got, total, fore)
-    o, sb, stats = call(
-        stats_kernel,
-        "mix_and_stats",
-        [(turned, F32), (group_states, BF16), ((2, tokens), F32)],
-        [state],
-        n_in=6,
-        flops=mm,
-    )(doc_lengths, qt, o_local, ct, sl, own, other)
+    half_turned = (half * head_width, tokens)
+    half_states = (n_groups, half, head_width, head_width)
+
+    def part(is_own, states, before, name):
+        return call(
+            functools.partial(stats_kernel, is_own),
+            name,
+            [(half_turned, F32), (half_states, BF16), ((2, tokens), F32)],
+            [],
+            n_in=5 + len(before),
+            flops=mm // 2,
+        )(doc_lengths, qt, o_local, ct, sl, states, *before)
+
+    o_own, sb_own, stats = part(True, own, (), "mix_own")
+    o_other, sb_other, stats = part(False, other, (stats,), "mix_other")
     stats = stats + sum(
         lax.ppermute(stats, "head", links_of(k, n_head)) for k in range(1, n_head)
     )
-    dobt, inv, mine, send = call(
+    dob_other, factors, send = call(
         functools.partial(norm_kernel, float(width * n_head)),
-        "norm_back",
-        [(turned, BF16), ((8, tokens), F32), (piece, F32), (piece, F32)],
-        [state],
+        "norm_other",
+        [(half_turned, BF16), ((8, tokens), F32), (piece, F32)],
+        [],
         n_in=4,
-        flops=mm,
-    )(doc_lengths, stats, o, ct, qd)
-    got, total, (dobt_b, inv_b) = exchange(mine, send, back, (dobt, inv))
+        flops=mm // 2,
+    )(doc_lengths, stats, o_other, ct, qd)
+    dobt, normed, sb, mine = call(
+        merge_kernel,
+        "norm_own",
+        [(turned, BF16), (turned, BF16), (group_states, BF16), (piece, F32)],
+        [],
+        n_in=8,
+        flops=mm // 2,
+    )(doc_lengths, factors, o_own, o_other, ct, qd, dob_other, sb_own, sb_other)
+    got, total, (dobt_b, normed_b) = exchange(mine, send, back, (dobt, normed))
     dk, dv, rl, output, grad_q = call(
         grad_kernel,
         "local_grads",
         [(full, F32), (full, F32), (group_states, F32), (flat, BF16), (flat, BF16)],
         [tmp, tmp, buf, buf, sems],
-        n_in=8,
+        n_in=7,
         out_hbm=(3, 4),
         flops=12 * mm,
-    )(doc_lengths, o, inv_b, dobt_b, pt, qd, kt, vd, sb)
+    )(doc_lengths, normed_b, dobt_b, pt, qd, kt, vd, sb)
+    total, dk = lax.optimization_barrier((total, dk))
     own, other = finish(mine, got, total, back)
     grad_k, grad_v = call(
         final_kernel,

time: 46.2 us -> 44.7 us (0.968)
  waiting for transfers between devices: 11.2 us -> 7 us
  Pallas kernels: 20.5 us -> 22 us
  starting transfers between devices: 13.4 us -> 14.4 us
    ppermute x4, waiting for transfers between devices: 4.56 us -> 2.21 us  [swap(): return lax.ppermute(x, 'seq', swap_pairs)]
    pallas_call x2 -> x4, Pallas kernels: 3.34 us -> 4.7 us  [the longest x2 2.33 us: part(): call(functools.partial(stats_kernel, is_own), name, [(half_turned, F32),...]
    ppermute x6, starting transfers between devices: 9.14 us -> 10.1 us  [exchange(): total = total + weights[5 + k] * lax.ppermute(chip_state, 'seq', links)]
    ppermute x3, waiting for transfers between devices: 4.24 us -> 3.29 us  [per_device(): lax.ppermute(stats, 'head', links_of(k, n_head))]
    ppermute x6, waiting for transfers between devices: 2.41 us -> 1.51 us  [exchange(): total = total + weights[5 + k] * lax.ppermute(chip_state, 'seq', links)]
  transfers between devices with their start and end apart: 13 -> 13, of which waited for: 9 -> 7; matrix products, arithmetic and copies ran while one was open for 0% -> 0% of each run, Pallas kernels for 21% -> 27%
where the time goes in v5:
time: 44.7 us; the launch traced here: 44.5 us
  Pallas kernels  22 us (49%)
  starting transfers between devices  14.4 us (32%)
  waiting for transfers between devices  7 us (16%)
  between operations  0.98 us (2%)
    ppermute x6, starting transfers between devices, exchange(): total = total + weights[5 + k] * lax.ppermute(chip_state, 'seq', links)  10.1 us
    pallas_call x1, Pallas kernels, per_device(): call(grad_kernel, 'local_grads', [(full, F32), (full, F32), (group_states...  6.04 us
    pallas_call x1, Pallas kernels, per_device(): call(functools.partial(state_kernel, n_seq), 'shard_state', [(full, BF16)...  4.18 us
    pallas_call x1, Pallas kernels, per_device(): call(local_kernel, 'local_mix', [(full, BF16), (turned, BF16), (turned, B...  3.74 us
    ppermute x3, starting transfers between devices, per_device(): lax.ppermute(stats, 'head', links_of(k, n_head))  3.55 us
    pallas_call x1, Pallas kernels, per_device(): call(final_kernel, 'final_grads', [(flat, BF16), (flat, BF16)], [state, t...  3.3 us
    ppermute x3, waiting for transfers between devices, per_device(): lax.ppermute(stats, 'head', links_of(k, n_head))  3.29 us
    pallas_call x2, Pallas kernels, part(): call(functools.partial(stats_kernel, is_own), name, [(half_turned, F32),...  2.33 us
  transfers between devices with their start and end apart: 13, of which 7 were waited for; matrix products, arithmetic and copies ran while one was open for 0% of the time, Pallas kernels for 27%

profile of v5, /device:TPU:0, one launch (start us, length us, event | category | flops | bytes accessed | tf_op | source)
XLA Modules:
  0.0 44.5 jit_solution(8539098352498477405)
XLA Ops:
  0.7 4.2 %shard_state.1 = (bf16[3072,256]{1,0:T(8,128)(2,1)S(1)}, bf16[3072,256]{1,0:T(8,128)(2,1)S(1)}, bf16[256,3072]{1,0:T(8,128)(2,1)S(1)}, f32[1,128,128]{2,1,0:T(8,...) custom-call(s32[6]{0:T(128)} %doc_ref.13, bf16[6144,128]{1,0:T(8,128)(2,1)} %bitcast.46, ...), custom_call_target="tpu_custom_call" | custom-call | flops 201326592 | bytes 8388608 | tf_op jit(solution)/shard_map/shard_state/pallas_call | solution.py:548
  4.8 0.5 %collective-permute-start = (f32[1,128,128]{2,1,0:T(8,128)S(1)}, f32[1,128,128]{2,1,0:T(8,128)S(1)}, u32[]{:S(2)}, u32[]{:S(2)}) collective-permute-start(f32[1,128,128]{2,1,0:T(8,128)S(1)} %get-tuple-element.53), channel_id=1, source_target_pairs={{0,4},{4,0},{8,12},{12,8},{16,20},{20,16},{24,28},{28,24},{1,5},{5... | collective-permute-start | bytes 196616 | tf_op jit(solution)/shard_map/ppermute | solution.py:528
  5.4 0.9 %collective-permute-done = f32[1,128,128]{2,1,0:T(8,128)S(1)} collective-permute-done((f32[1,128,128]{2,1,0:T(8,128)S(1)}, f32[1,128,128]{2,1,0:T(8,128)S(1)}, u32[]{:S(2)}, u32[]{:S(2)}) %collective-permute-start) | collective-permute-done | bytes 65568 | tf_op jit(solution)/shard_map/ppermute | solution.py:528
  6.3 5.0 %collective-permute-start.3 = (f32[1,128,128]{2,1,0:T(8,128)S(1)}, f32[1,128,128]{2,1,0:T(8,128)S(1)}, u32[]{:S(2)}, u32[]{:S(2)}) collective-permute-start(f32[1,128,128]{2,1,0:T(8,128)S(1)} %multiply_add_fusion.7), channel_id=1, source_target_pairs={{24,0},{28,4},{16,8},{20,12},{8,16},{12,20},{0,24},{4,28},{25,1},{... | collective-permute-start | bytes 196616 | tf_op jit(solution)/shard_map/ppermute | solution.py:536
  11.3 0.6 %collective-permute-start.1 = (f32[1,128,128]{2,1,0:T(8,128)S(1)}, f32[1,128,128]{2,1,0:T(8,128)S(1)}, u32[]{:S(2)}, u32[]{:S(2)}) collective-permute-start(f32[1,128,128]{2,1,0:T(8,128)S(1)} %multiply_add_fusion.7), channel_id=1, source_target_pairs={{8,0},{12,4},{0,8},{4,12},{24,16},{28,20},{16,24},{20,28},{9,1},{1... | collective-permute-start | bytes 196616 | tf_op jit(solution)/shard_map/ppermute | solution.py:536
  11.9 3.7 %local_mix.1 = (bf16[3072,256]{1,0:T(8,128)(2,1)S(1)}, bf16[256,3072]{1,0:T(8,128)(2,1)S(1)}, bf16[256,3072]{1,0:T(8,128)(2,1)S(1)}, bf16[256,3072]{1,0:T(8,128)...) custom-call(s32[6]{0:T(128)S(1)} %copy-done.2, ...), custom_call_target="tpu_custom_call" | custom-call | flops 1207959552 | bytes 8388608 | tf_op jit(solution)/shard_map/local_mix/pallas_call | solution.py:568
  15.7 1.5 %collective-permute-done.2 = f32[1,128,128]{2,1,0:T(8,128)S(1)} collective-permute-done((f32[1,128,128]{2,1,0:T(8,128)S(1)}, f32[1,128,128]{2,1,0:T(8,128)S(1)}, u32[]{:S(2)}, u32[]{:S(2)}) %collective-permute-start.2) | collective-permute-done | bytes 65568 | tf_op jit(solution)/shard_map/ppermute | solution.py:536
  17.2 0.1 collective-permute-start.4
  17.3 1.2 %mix_own.1 = (f32[128,3072]{1,0:T(8,128)S(1)}, bf16[12,1,128,128]{3,2,1,0:T(8,128)(2,1)S(1)}, f32[2,3072]{1,0:T(2,128)S(1)}) custom-call(s32[6]{0:T(128)S(1)} %copy-done.2, bf16[256,3072]{1,0:T(8,128)(2,1)S(1)} %get-tuple-element.60.qt_ref, f32[256,3072]{1,0:T(8,128)S(1)} %get-tuple-element.63.ol_ref, bf16[256,3072]{1,0:T(8,128)(2,1)S(1)} %get-tuple-element.64.ct_ref, ...), custom_call_target="tpu_custom_call" | custom-call | flops 100663296 | bytes 8388608 | tf_op jit(solution)/shard_map/mix_own/pallas_call | solution.py:590
  18.6 1.2 %mix_other.1 = (f32[128,3072]{1,0:T(8,128)S(1)}, bf16[12,1,128,128]{3,2,1,0:T(8,128)(2,1)S(1)}, f32[2,3072]{1,0:T(2,128)S(1)}) custom-call(s32[6]{0:T(128)S(1)} %copy-done.2, bf16[256,3072]{1,0:T(8,128)(2,1)S(1)} %get-tuple-element.60.qt_ref, f32[256,3072]{1,0:T(8,128)S(1)} %get-tuple-element.63.ol_ref, bf16[256,3072]{1,0:T(8,128)(2,1)S(1)} %get-tuple-element.64.ct_ref, ...), custom_call_target="tpu_custom_call" | custom-call | flops 100663296 | bytes 8388608 | tf_op jit(solution)/shard_map/mix_other/pallas_call | solution.py:590
  19.7 2.5 %collective-permute-start.7 = (f32[2,3072]{1,0:T(2,128)S(1)}, f32[2,3072]{1,0:T(2,128)S(1)}, u32[]{:S(2)}, u32[]{:S(2)}) collective-permute-start(f32[2,3072]{1,0:T(2,128)S(1)} %get-tuple-element.68), channel_id=1, source_target_pairs={{3,0},{2,1},{1,2},{0,3},{7,4},{6,5},{5,6},{4,7},{11,8},{10,9},{9,1... | collective-permute-start | bytes 73736 | tf_op jit(solution)/shard_map/ppermute | solution.py:602
  22.3 0.5 %collective-permute-start.6 = (f32[2,3072]{1,0:T(2,128)S(1)}, f32[2,3072]{1,0:T(2,128)S(1)}, u32[]{:S(2)}, u32[]{:S(2)}) collective-permute-start(f32[2,3072]{1,0:T(2,128)S(1)} %get-tuple-element.68), channel_id=1, source_target_pairs={{2,0},{3,1},{0,2},{1,3},{6,4},{7,5},{4,6},{5,7},{10,8},{11,9},{8,1... | collective-permute-start | bytes 73736 | tf_op jit(solution)/shard_map/ppermute | solution.py:602
  22.8 0.5 %collective-permute-start.5 = (f32[2,3072]{1,0:T(2,128)S(1)}, f32[2,3072]{1,0:T(2,128)S(1)}, u32[]{:S(2)}, u32[]{:S(2)}) collective-permute-start(f32[2,3072]{1,0:T(2,128)S(1)} %get-tuple-element.68), channel_id=1, source_target_pairs={{1,0},{0,1},{3,2},{2,3},{5,4},{4,5},{7,6},{6,7},{9,8},{8,9},{11,10... | collective-permute-start | bytes 73736 | tf_op jit(solution)/shard_map/ppermute | solution.py:602
  23.3 1.2 %collective-permute-done.7 = f32[2,3072]{1,0:T(2,128)S(1)} collective-permute-done((f32[2,3072]{1,0:T(2,128)S(1)}, f32[2,3072]{1,0:T(2,128)S(1)}, u32[]{:S(2)}, u32[]{:S(2)}) %collective-permute-start.7) | collective-permute-done | bytes 24608 | tf_op jit(solution)/shard_map/ppermute | solution.py:602
  24.5 1.5 %collective-permute-done.6 = f32[2,3072]{1,0:T(2,128)S(1)} collective-permute-done((f32[2,3072]{1,0:T(2,128)S(1)}, f32[2,3072]{1,0:T(2,128)S(1)}, u32[]{:S(2)}, u32[]{:S(2)}) %collective-permute-start.6) | collective-permute-done | bytes 24608 | tf_op jit(solution)/shard_map/ppermute | solution.py:602
  26.1 0.5 %collective-permute-done.5 = f32[2,3072]{1,0:T(2,128)S(1)} collective-permute-done((f32[2,3072]{1,0:T(2,128)S(1)}, f32[2,3072]{1,0:T(2,128)S(1)}, u32[]{:S(2)}, u32[]{:S(2)}) %collective-permute-start.5) | collective-permute-done | bytes 24608 | tf_op jit(solution)/shard_map/ppermute | solution.py:602
  26.6 1.1 %norm_other.1 = (bf16[128,3072]{1,0:T(8,128)(2,1)S(1)}, f32[8,3072]{1,0:T(8,128)S(1)}, f32[1,128,128]{2,1,0:T(8,128)S(1)}) custom-call(s32[6]{0:T(128)S(1)} %copy-done.2, f32[2,3072]{1,0:T(2,128)S(1)} %add_add_fusion.st_ref, f32[128,3072]{1,0:T(8,128)S(1)} %get-tuple-element.69.o_ref.other_ref, bf16[256,3072]{1,0:T(8,128)(2,1)S(1)} %get-tuple-element.64.ct_ref, ...), custom_call_target="tpu_custom_call" | custom-call | flops 100663296 | bytes 8388608 | tf_op jit(solution)/shard_map/norm_other/pallas_call | solution.py:604
  27.8 1.3 %norm_own.1 = (bf16[256,3072]{1,0:T(8,128)(2,1)S(1)}, bf16[256,3072]{1,0:T(8,128)(2,1)S(1)}, bf16[12,2,128,128]{3,2,1,0:T(8,128)(2,1)S(1)}, f32[1,128,128]{2,1,0:T(8,128)S(1)}) custom-call(s32[6]{0:T(128)S(1)} %copy-done.2, f32[8,3072]{1,0:T(8,128)S(1)} %get-tuple-element.71.rows_ref, f32[128,3072]{1,0:T(8,128)S(1)} %get-tuple-element.72.own_ref, ...), custom_call_target="tpu_custom_call" | custom-call | flops 100663296 | bytes 8388608 | tf_op jit(solution)/shard_map/norm_own/pallas_call | solution.py:612
  29.1 2.5 %collective-permute-start.11 = (f32[1,128,128]{2,1,0:T(8,128)S(1)}, f32[1,128,128]{2,1,0:T(8,128)S(1)}, u32[]{:S(2)}, u32[]{:S(2)}) collective-permute-start(f32[1,128,128]{2,1,0:T(8,128)S(1)} %multiply_add_fusion.3), channel_id=1, source_target_pairs={{24,0},{28,4},{16,8},{20,12},{8,16},{12,20},{0,24},{4,28},{25,1},{... | collective-permute-start | bytes 196616 | tf_op jit(solution)/shard_map/ppermute | solution.py:536
  31.7 0.1 collective-permute-start.10
  31.8 1.8 %collective-permute-start.9 = (f32[1,128,128]{2,1,0:T(8,128)S(1)}, f32[1,128,128]{2,1,0:T(8,128)S(1)}, u32[]{:S(2)}, u32[]{:S(2)}) collective-permute-start(f32[1,128,128]{2,1,0:T(8,128)S(1)} %multiply_add_fusion.3), channel_id=1, source_target_pairs={{8,0},{12,4},{0,8},{4,12},{24,16},{28,20},{16,24},{20,28},{9,1},{1... | collective-permute-start | bytes 196616 | tf_op jit(solution)/shard_map/ppermute | solution.py:536
  33.6 6.0 %local_grads.1 = (f32[3072,256]{1,0:T(8,128)S(1)}, f32[3072,256]{1,0:T(8,128)S(1)}, f32[12,2,128,128]{3,2,1,0:T(8,128)S(1)}, bf16[6144,128]{1,0:T(8,128)(2,1)}, bf16[6144,128]{1,0:T(8,128)(2,1)}) custom-call(s32[6]{0:T(128)S(1)} %copy-done.2, bf16[256,3072]{1,0:T(8,128)(2,1)S(1)} %get-tuple-element.80.normed_ref, ...), custom_call_target="tpu_custom_call" | custom-call | flops 2415919104 | bytes 8388608 | tf_op jit(solution)/shard_map/local_grads/pallas_call | solution.py:621
  39.8 1.2 %collective-permute-done.12.other_ref = f32[1,128,128]{2,1,0:T(8,128)S(1)} collective-permute-done((f32[1,128,128]{2,1,0:T(8,128)S(1)}, f32[1,128,128]{2,1,0:T(8,128)S(1)}, u32[]{:S(2)}, u32[]{:S(2)}) %collective-permute-start.12) | collective-permute-done | bytes 65568 | tf_op jit(solution)/shard_map/ppermute | solution.py:528
  41.0 3.3 %final_grads.1 = (bf16[6144,128]{1,0:T(8,128)(2,1)}, bf16[6144,128]{1,0:T(8,128)(2,1)}) custom-call(s32[6]{0:T(128)S(1)} %copy-done.2, f32[3072,256]{1,0:T(8,128)S(1)} %get-tuple-element.90.dk_ref, f32[3072,256]{1,0:T(8,128)S(1)} %get-tuple-element.91.dv_ref, bf16[3072,256]{1,0:T(8,128)(2,1)S(1)} %get-tuple-element.56.kd_ref, ...), custom_call_target="tpu_custom_call" | custom-call | flops 402653184 | bytes 8388608 | tf_op jit(solution)/shard_map/final_grads/pallas_call | solution.py:632
  (25 shorter events, 0.4 us)
Async XLA Ops:
  0.6 11.3 %copy-start = (bf16[3072,2,128]{2,1,0:T(2,128)(2,1)S(1)}, bf16[3072,2,128]{2,1,0:T(2,128)(2,1)}, u32[]{:S(2)}) copy-start(bf16[3072,2,128]{2,1,0:T(2,128)(2,1)} %param.5) | copy-start | bytes 4718596
  0.6 11.3 %copy-start.1 = (bf16[3072,2,128]{2,1,0:T(2,128)(2,1)S(1)}, bf16[3072,2,128]{2,1,0:T(2,128)(2,1)}, u32[]{:S(2)}) copy-start(bf16[3072,2,128]{2,1,0:T(2,128)(2,1)} %param.8) | copy-start | bytes 4718596
  0.7 11.3 %copy-start.2 = (s32[6]{0:T(128)S(1)}, s32[6]{0:T(128)}, u32[]{:S(2)}) copy-start(s32[6]{0:T(128)} %doc_ref.13) | copy-start | bytes 76
  4.8 1.4 %collective-permute-start = (f32[1,128,128]{2,1,0:T(8,128)S(1)}, f32[1,128,128]{2,1,0:T(8,128)S(1)}, u32[]{:S(2)}, u32[]{:S(2)}) collective-permute-start(f32[1,128,128]{2,1,0:T(8,128)S(1)} %get-tuple-element.53), channel_id=1, source_target_pairs={{0,4},{4,0},{8,12},{12,8},{16,20},{20,16},{24,28},{28,24},{1,5},{5... | collective-permute-start | bytes 196616 | tf_op jit(solution)/shard_map/ppermute | solution.py:528
  6.3 9.4 %collective-permute-start.3 = (f32[1,128,128]{2,1,0:T(8,128)S(1)}, f32[1,128,128]{2,1,0:T(8,128)S(1)}, u32[]{:S(2)}, u32[]{:S(2)}) collective-permute-start(f32[1,128,128]{2,1,0:T(8,128)S(1)} %multiply_add_fusion.7), channel_id=1, source_target_pairs={{24,0},{28,4},{16,8},{20,12},{8,16},{12,20},{0,24},{4,28},{25,1},{... | collective-permute-start | bytes 196616 | tf_op jit(solution)/shard_map/ppermute | solution.py:536
  11.3 5.9 %collective-permute-start.2 = (f32[1,128,128]{2,1,0:T(8,128)S(1)}, f32[1,128,128]{2,1,0:T(8,128)S(1)}, u32[]{:S(2)}, u32[]{:S(2)}) collective-permute-start(f32[1,128,128]{2,1,0:T(8,128)S(1)} %multiply_add_fusion.7), channel_id=1, source_target_pairs={{16,0},{20,4},{24,8},{28,12},{0,16},{4,20},{8,24},{12,28},{17,1},{... | collective-permute-start | bytes 196616 | tf_op jit(solution)/shard_map/ppermute | solution.py:536
  11.3 5.9 %collective-permute-start.1 = (f32[1,128,128]{2,1,0:T(8,128)S(1)}, f32[1,128,128]{2,1,0:T(8,128)S(1)}, u32[]{:S(2)}, u32[]{:S(2)}) collective-permute-start(f32[1,128,128]{2,1,0:T(8,128)S(1)} %multiply_add_fusion.7), channel_id=1, source_target_pairs={{8,0},{12,4},{0,8},{4,12},{24,16},{28,20},{16,24},{20,28},{9,1},{1... | collective-permute-start | bytes 196616 | tf_op jit(solution)/shard_map/ppermute | solution.py:536
  17.2 1.3 %collective-permute-start.4 = (f32[1,128,128]{2,1,0:T(8,128)S(1)}, f32[1,128,128]{2,1,0:T(8,128)S(1)}, u32[]{:S(2)}, u32[]{:S(2)}) collective-permute-start(f32[1,128,128]{2,1,0:T(8,128)S(1)} %get-tuple-element.99), channel_id=1, source_target_pairs={{0,4},{4,0},{8,12},{12,8},{16,20},{20,16},{24,28},{28,24},{1,5},{5... | collective-permute-start | bytes 196616 | tf_op jit(solution)/shard_map/ppermute | solution.py:528
  19.7 4.8 %collective-permute-start.7 = (f32[2,3072]{1,0:T(2,128)S(1)}, f32[2,3072]{1,0:T(2,128)S(1)}, u32[]{:S(2)}, u32[]{:S(2)}) collective-permute-start(f32[2,3072]{1,0:T(2,128)S(1)} %get-tuple-element.68), channel_id=1, source_target_pairs={{3,0},{2,1},{1,2},{0,3},{7,4},{6,5},{5,6},{4,7},{11,8},{10,9},{9,1... | collective-permute-start | bytes 73736 | tf_op jit(solution)/shard_map/ppermute | solution.py:602
  22.3 3.8 %collective-permute-start.6 = (f32[2,3072]{1,0:T(2,128)S(1)}, f32[2,3072]{1,0:T(2,128)S(1)}, u32[]{:S(2)}, u32[]{:S(2)}) collective-permute-start(f32[2,3072]{1,0:T(2,128)S(1)} %get-tuple-element.68), channel_id=1, source_target_pairs={{2,0},{3,1},{0,2},{1,3},{6,4},{7,5},{4,6},{5,7},{10,8},{11,9},{8,1... | collective-permute-start | bytes 73736 | tf_op jit(solution)/shard_map/ppermute | solution.py:602
  22.8 3.8 %collective-permute-start.5 = (f32[2,3072]{1,0:T(2,128)S(1)}, f32[2,3072]{1,0:T(2,128)S(1)}, u32[]{:S(2)}, u32[]{:S(2)}) collective-permute-start(f32[2,3072]{1,0:T(2,128)S(1)} %get-tuple-element.68), channel_id=1, source_target_pairs={{1,0},{0,1},{3,2},{2,3},{5,4},{4,5},{7,6},{6,7},{9,8},{8,9},{11,10... | collective-permute-start | bytes 73736 | tf_op jit(solution)/shard_map/ppermute | solution.py:602
  27.7 1.4 %collective-permute-start.8 = (f32[1,128,128]{2,1,0:T(8,128)S(1)}, f32[1,128,128]{2,1,0:T(8,128)S(1)}, u32[]{:S(2)}, u32[]{:S(2)}) collective-permute-start(f32[1,128,128]{2,1,0:T(8,128)S(1)} %get-tuple-element.77), channel_id=1, source_target_pairs={{0,4},{4,0},{8,12},{12,8},{16,20},{20,16},{24,28},{28,24},{1,5},{5... | collective-permute-start | bytes 196616 | tf_op jit(solution)/shard_map/ppermute | solution.py:528
  29.1 10.5 %collective-permute-start.11 = (f32[1,128,128]{2,1,0:T(8,128)S(1)}, f32[1,128,128]{2,1,0:T(8,128)S(1)}, u32[]{:S(2)}, u32[]{:S(2)}) collective-permute-start(f32[1,128,128]{2,1,0:T(8,128)S(1)} %multiply_add_fusion.3), channel_id=1, source_target_pairs={{24,0},{28,4},{16,8},{20,12},{8,16},{12,20},{0,24},{4,28},{25,1},{... | collective-permute-start | bytes 196616 | tf_op jit(solution)/shard_map/ppermute | solution.py:536
  31.7 8.0 %collective-permute-start.10 = (f32[1,128,128]{2,1,0:T(8,128)S(1)}, f32[1,128,128]{2,1,0:T(8,128)S(1)}, u32[]{:S(2)}, u32[]{:S(2)}) collective-permute-start(f32[1,128,128]{2,1,0:T(8,128)S(1)} %multiply_add_fusion.3), channel_id=1, source_target_pairs={{16,0},{20,4},{24,8},{28,12},{0,16},{4,20},{8,24},{12,28},{17,1},{... | collective-permute-start | bytes 196616 | tf_op jit(solution)/shard_map/ppermute | solution.py:536
  31.8 7.9 %collective-permute-start.9 = (f32[1,128,128]{2,1,0:T(8,128)S(1)}, f32[1,128,128]{2,1,0:T(8,128)S(1)}, u32[]{:S(2)}, u32[]{:S(2)}) collective-permute-start(f32[1,128,128]{2,1,0:T(8,128)S(1)} %multiply_add_fusion.3), channel_id=1, source_target_pairs={{8,0},{12,4},{0,8},{4,12},{24,16},{28,20},{16,24},{20,28},{9,1},{1... | collective-permute-start | bytes 196616 | tf_op jit(solution)/shard_map/ppermute | solution.py:536
  39.7 1.3 %collective-permute-start.12 = (f32[1,128,128]{2,1,0:T(8,128)S(1)}, f32[1,128,128]{2,1,0:T(8,128)S(1)}, u32[]{:S(2)}, u32[]{:S(2)}) collective-permute-start(f32[1,128,128]{2,1,0:T(8,128)S(1)} %get-tuple-element.96), channel_id=1, source_target_pairs={{0,4},{4,0},{8,12},{12,8},{16,20},{20,16},{24,28},{28,24},{1,5},{5... | collective-permute-start | bytes 196616 | tf_op jit(solution)/shard_map/ppermute | solution.py:528

commit v6 on v5

--- a/solution.py
+++ b/solution.py
@@ -9,6 +9,7 @@
 
 GROUP = 256
 EPSILON = 1e-06
+OPENED, SAME_OPENED, HEAD, KEPT, SHARD_HEAD, CLOSING, SAME_CLOSING, BEGIN = range(8)
 F32 = jnp.float32
 BF16 = jnp.bfloat16
 
@@ -51,15 +52,43 @@
     return lax.broadcasted_iota(jnp.int32, (rows, GROUP), 1)
 
 
-def group_mask(ends, first):
+def begin_row(ends, first):
     place = lanes_iota(8) + first
     begin = jnp.zeros((8, GROUP), jnp.int32)
     for end in ends:
         begin = jnp.where(place >= end, end, begin)
-    begin = begin - first
-    begin = jnp.concatenate([begin] * (GROUP // 8), axis=0)
+    return begin - first
+
+
+def group_mask(begin):
     row = rows_iota(GROUP)
     return (row >= begin) & (row <= lanes_iota(GROUP))
+
+
+def write_table(table_ref, ends, anchor, tokens):
+    for g in range(tokens // GROUP):
+        first = anchor + g * GROUP
+        after = first + GROUP
+        numbers = {
+            OPENED: end_of(ends, first - 1) - first,
+            SAME_OPENED: (start_of(ends, first - 1) < anchor).astype(jnp.int32),
+            HEAD: end_of(ends, first) - first,
+            KEPT: (end_of(ends, first) > after).astype(jnp.int32),
+            SHARD_HEAD: end_of(ends, anchor) - first,
+            CLOSING: start_of(ends, after) - first,
+            SAME_CLOSING: (end_of(ends, after) > anchor + tokens).astype(jnp.int32),
+        }
+        for kind, number in numbers.items():
+            table_ref[kind, pl.ds(g, 1), :] = jnp.full((1, GROUP), number, jnp.int32)
+        table_ref[BEGIN, pl.ds(g, 1), :] = begin_row(ends, first)[:1]
+
+
+def known(table_ref, kind, g, width=GROUP):
+    return table_ref[kind, pl.ds(g, 1), :width]
+
+
+def factor(table_ref, kind, g):
+    return known(table_ref, kind, g, 128).astype(F32)
 
 
 def keep_where(keep, x):
@@ -192,7 +221,7 @@
 
 
 def local_kernel(
-    doc_ref, kd_ref, vt_ref, q2_ref, c2_ref, qd_ref, qt_ref, kt_ref, ct_ref, pt_ref, ol_ref, sl_ref,
+    doc_ref, kd_ref, vt_ref, q2_ref, c2_ref, qd_ref, qt_ref, kt_ref, ct_ref, pt_ref, ol_ref, sl_ref, table_ref,
     tmpq, tmpc,
 ):
     tokens, width = kd_ref.shape
@@ -217,7 +246,7 @@
 
     def scores(g, qts):
         rows = group_rows(g)
-        mask = group_mask(ends, anchor + g * GROUP)
+        mask = group_mask(known(table_ref, BEGIN, g))
         pts = []
         for h in range(heads):
             pt = jnp.where(mask, dot(kd_ref[rows, at(h)], qts[h]), 0.0).astype(BF16)
@@ -225,6 +254,7 @@
             pts.append(pt)
         return pts
 
+    write_table(table_ref, ends, anchor, tokens)
     state = [jnp.zeros((128, 128), F32) for _ in range(heads)]
     next_pts = scores(0, prepare(0))
     next_qts = prepare(1) if n_groups > 1 else None
@@ -260,21 +290,17 @@
     return pl.ds(pl.multiple_of(head * 128, 128), 128)
 
 
-def stats_kernel(own, doc_ref, qt_ref, ol_ref, ct_ref, sl_ref, state_ref, *refs):
+def stats_kernel(own, table_ref, qt_ref, ol_ref, ct_ref, sl_ref, state_ref, *refs):
     (before_ref, o_ref, sb_ref, st_ref) = refs if len(refs) == 4 else (None, *refs)
     width, tokens = qt_ref.shape
     half = state_ref.shape[0]
     n_groups = tokens // GROUP
-    shard = lax.axis_index("seq")
-    base = part_of(shard % 2, own, half)
-    anchor = shard * tokens
-    ends = doc_ends_of(doc_ref)
+    base = part_of(lax.axis_index("seq") % 2, own, half)
 
     def opened_terms(g):
         rows = group_rows(g)
-        first = anchor + g * GROUP
-        opened = lanes_iota(128) < end_of(ends, first - 1) - first
-        same = (start_of(ends, first - 1) < anchor).astype(F32)
+        opened = lanes_iota(128) < known(table_ref, OPENED, g)
+        same = factor(table_ref, SAME_OPENED, g)
         terms = []
         for h in range(half):
             sb = (sl_ref[g, base + h] + same * state_ref[h]).astype(BF16)
@@ -314,19 +340,15 @@
 
 
 def norm_kernel(
-    width_all, doc_ref, st_ref, o_ref, ct_ref, qd_ref, dobt_ref, rows_ref, send_ref
+    width_all, table_ref, st_ref, o_ref, ct_ref, qd_ref, dobt_ref, rows_ref, send_ref
 ):
     tokens, width = qd_ref.shape
     half = send_ref.shape[0]
-    shard = lax.axis_index("seq")
-    base = part_of(shard % 2, False, half)
-    anchor = shard * tokens
-    ends = doc_ends_of(doc_ref)
-    head_to = end_of(ends, anchor) - anchor
+    base = part_of(lax.axis_index("seq") % 2, False, half)
 
     def prepare(g):
         rows = group_rows(g)
-        keep = lanes_iota(128) + g * GROUP < head_to
+        keep = lanes_iota(128) < known(table_ref, SHARD_HEAD, g)
         total = st_ref[:, rows] * (1.0 / width_all)
         inv = lax.rsqrt(total[0:1] + EPSILON)
         slope = total[1:2] * inv * inv * inv
@@ -342,21 +364,17 @@
 
 
 def merge_kernel(
-    doc_ref, rows_ref, own_ref, other_ref, ct_ref, qd_ref, dob_other_ref, sb_own_ref, sb_other_ref,
+    table_ref, rows_ref, own_ref, other_ref, ct_ref, qd_ref, dob_other_ref, sb_own_ref, sb_other_ref,
     dobt_ref, normed_ref, sb_ref, mine_ref,
 ):
     tokens, width = qd_ref.shape
     half = mine_ref.shape[0]
-    shard = lax.axis_index("seq")
-    core = shard % 2
+    core = lax.axis_index("seq") % 2
     base, far = part_of(core, True, half), part_of(core, False, half)
-    anchor = shard * tokens
-    ends = doc_ends_of(doc_ref)
-    head_to = end_of(ends, anchor) - anchor
 
     def prepare(g):
         rows = group_rows(g)
-        keep = lanes_iota(128) + g * GROUP < head_to
+        keep = lanes_iota(128) < known(table_ref, SHARD_HEAD, g)
         inv = rows_ref[0:1, rows]
         slope = rows_ref[1:2, rows]
         ready = []
@@ -376,43 +394,45 @@
     back_state(half, tokens // GROUP, prepare, qd_ref, base, mine_ref)
 
 
-def grad_kernel(
-    doc_ref, normed_ref, dobt_ref, pt_ref, qd_ref, kt_ref, vd_ref, sb_ref,
-    dk_ref, dv_ref, rl_ref, out_ref, gq_ref, tmpo, tmpq, bufo, bufq, sems,
-):
-    tokens, width = qd_ref.shape
+def grad_kernel(groups, *refs):
+    table_ref, normed_ref, dobt_ref, pt_ref, qd_ref, kt_ref, vd_ref, sb_ref, *refs = refs
+    width = dobt_ref.shape[0]
     heads = width // 128
-    n_groups = tokens // GROUP
-    anchor = lax.axis_index("seq") * tokens
-    ends = doc_ends_of(doc_ref)
+    n_groups = dobt_ref.shape[1] // GROUP
+    state = [jnp.zeros((128, 128), F32) for _ in range(heads)]
+    if groups.stop < n_groups:
+        state_ref, _, _, *refs = refs
+        state = [state_ref[h] for h in range(heads)]
+    left_ref = None
+    if groups.start > 0:
+        left_ref, *refs = refs
+    dk_ref, dv_ref, rl_ref, out_ref, gq_ref, tmpo, tmpq, bufo, bufq, sems = refs
 
     def scores(g):
         rows = group_rows(g)
-        mask = group_mask(ends, anchor + g * GROUP)
+        mask = group_mask(known(table_ref, BEGIN, g))
         return [
             jnp.where(mask, dot(vd_ref[rows, at(h)], dobt_ref[at(h), rows]), 0.0).astype(BF16)
             for h in range(heads)
         ]
 
-    state = [jnp.zeros((128, 128), F32) for _ in range(heads)]
     started = []
-    ahead = scores(n_groups - 1)
-    for g in reversed(range(n_groups)):
+    ahead = scores(groups[-1])
+    for g in reversed(groups):
         dpts = ahead
         slot = g % tmpq.shape[0]
-        first = anchor + g * GROUP
-        rows = group_rows(g)
-        pairs = pair_rows(g, heads)
-        opened = lanes_iota(128) < end_of(ends, first - 1) - first
-        end = end_of(ends, first)
-        head_part = lanes_iota(128) < end - first
-        kept = (end > first + GROUP).astype(F32)
+        rows = group_rows(g)
+        here = group_rows(g - groups.start)
+        buffered = pair_rows(g - groups.start, heads)
+        opened = lanes_iota(128) < known(table_ref, OPENED, g)
+        head_part = lanes_iota(128) < known(table_ref, HEAD, g)
+        kept = factor(table_ref, KEPT, g)
         for h in range(heads):
             mine = pl.ds(h, GROUP, stride=heads)
-            dv_ref[rows, at(h)] = dot(pt_ref[h, rows, :], turn(dobt_ref[at(h), rows]))
+            dv_ref[here, at(h)] = dot(pt_ref[h, rows, :], turn(dobt_ref[at(h), rows]))
             tmpo[slot, mine, :] = normed_ref[at(h), rows].T.astype(F32)
-        bufo[pairs, :] = tmpo[slot].astype(BF16)
-        if g > 0:
+        bufo[buffered, :] = tmpo[slot].astype(BF16)
+        if g > groups.start:
             ahead = scores(g - 1)
         near, grown = [], []
         for h in range(heads):
@@ -421,40 +441,43 @@
             grown.append(dot(keep_where(head_part, dobt), qd_ref[rows, at(h)]))
         for h in range(heads):
             mine = pl.ds(h, GROUP, stride=heads)
-            dk_ref[rows, at(h)] = dot(dpts[h], qd_ref[rows, at(h)])
+            dk_ref[here, at(h)] = dot(dpts[h], qd_ref[rows, at(h)])
             gq = dot(kt_ref[at(h), rows], dpts[h]) + near[h]
             tmpq[slot, mine, :] = turn(gq).astype(F32)
-            rl_ref[g, h] = state[h]
+            rl_ref[g - groups.start, h] = state[h]
             state[h] = state[h] * kept + grown[h]
-        bufq[pairs, :] = tmpq[slot].astype(BF16)
+        bufq[buffered, :] = tmpq[slot].astype(BF16)
         for n, (buf, out) in enumerate(((bufo, out_ref), (bufq, gq_ref))):
-            copy = pltpu.make_async_copy(buf.at[pairs], out.at[pairs], sems.at[n, g])
+            copy = pltpu.make_async_copy(
+                buf.at[buffered], out.at[pair_rows(g, heads)], sems.at[n, g]
+            )
             copy.start()
             started.append(copy)
+    if left_ref is not None:
+        for h in range(heads):
+            left_ref[h] = state[h]
     for copy in started:
         copy.wait()
 
 
-def final_kernel(
-    doc_ref, dk_ref, dv_ref, kd_ref, vd_ref, rl_ref, own_ref, other_ref, gk_ref, gv_ref,
-    rin, tmpk, tmpv, bufk, bufv, sems,
-):
+def final_kernel(table_ref, kd_ref, vd_ref, own_ref, other_ref, *refs):
+    *parts, gk_ref, gv_ref, rin, tmpk, tmpv, bufk, bufv, sems = refs
     tokens, width = kd_ref.shape
     heads = width // 128
     n_groups = tokens // GROUP
-    shard = lax.axis_index("seq")
-    anchor = shard * tokens
-    ends = doc_ends_of(doc_ref)
-    place_halves(shard % 2, rin, own_ref, other_ref)
+    place_halves(lax.axis_index("seq") % 2, rin, own_ref, other_ref)
+    held = []
+    for dk_ref, dv_ref, rl_ref in zip(parts[0::3], parts[1::3], parts[2::3]):
+        held += [(dk_ref, dv_ref, rl_ref, i) for i in range(rl_ref.shape[0])]
 
     def closing_terms(g):
         rows = group_rows(g)
-        after = anchor + (g + 1) * GROUP
-        closing = rows_iota(128) + (after - GROUP) >= start_of(ends, after)
-        same = (end_of(ends, after) > anchor + tokens).astype(F32)
+        rl_ref, i = held[g][2:]
+        closing = rows_iota(128) >= known(table_ref, CLOSING, g, 128)
+        same = factor(table_ref, SAME_CLOSING, g)
         terms = []
         for h in range(heads):
-            rb = (rl_ref[g, h] + same * rin[h]).astype(BF16)
+            rb = (rl_ref[i, h] + same * rin[h]).astype(BF16)
             terms.append(
                 (
                     jnp.where(closing, dot(vd_ref[rows, at(h)], rb), 0.0),
@@ -469,13 +492,13 @@
         terms = ahead
         if g + 1 < n_groups:
             ahead = closing_terms(g + 1)
-        rows = group_rows(g)
+        dk_ref, dv_ref, _, i = held[g]
         pairs = pair_rows(g, heads)
         slot = g % tmpk.shape[0]
         for h in range(heads):
             mine = pl.ds(h, GROUP, stride=heads)
-            tmpk[slot, mine, :] = dk_ref[rows, at(h)] + terms[h][0]
-            tmpv[slot, mine, :] = dv_ref[rows, at(h)] + terms[h][1]
+            tmpk[slot, mine, :] = dk_ref[group_rows(i), at(h)] + terms[h][0]
+            tmpv[slot, mine, :] = dv_ref[group_rows(i), at(h)] + terms[h][1]
         bufk[pairs, :] = tmpk[slot].astype(BF16)
         bufv[pairs, :] = tmpv[slot].astype(BF16)
         for n, (buf, out) in enumerate(((bufk, gk_ref), (bufv, gv_ref))):
@@ -486,17 +509,18 @@
         copy.wait()
 
 
-def call(kernel, name, outs, scratch, in_hbm=(), out_hbm=(), flops=0, n_in=0, doc_hbm=False):
+def call(kernel, name, outs, scratch, n_in, in_hbm=(), out_hbm=(), in_smem=(), alias=None, flops=0):
     vmem = pl.BlockSpec(memory_space=pltpu.VMEM)
     hbm = pl.BlockSpec(memory_space=pltpu.HBM)
+    smem = pl.BlockSpec(memory_space=pltpu.SMEM)
     return pl.pallas_call(
         kernel,
         name=name,
         out_shape=[jax.ShapeDtypeStruct(s, d) for s, d in outs],
-        in_specs=[hbm if doc_hbm else pl.BlockSpec(memory_space=pltpu.SMEM)]
-        + [hbm if i in in_hbm else vmem for i in range(n_in)],
+        in_specs=[hbm if i in in_hbm else smem if i in in_smem else vmem for i in range(n_in)],
         out_specs=[hbm if i in out_hbm else vmem for i in range(len(outs))],
         scratch_shapes=scratch,
+        input_output_aliases=alias or {},
         cost_estimate=pl.CostEstimate(flops=flops, bytes_accessed=8 << 20, transcendentals=0),
         compiler_params=pltpu.CompilerParams(vmem_limit_bytes=16 << 20),
     )
@@ -559,13 +583,13 @@
             sems,
             pltpu.SemaphoreType.DMA,
         ],
-        n_in=2,
-        in_hbm=(0, 1),
-        doc_hbm=True,
+        n_in=3,
+        in_hbm=(0, 1, 2),
         flops=mm,
     )(*(pltpu.with_memory_space_constraint(x, pltpu.HBM) for x in (doc_lengths, k2, v2)))
     got, total, (kd_b, vt_b, q2_b, c2_b) = exchange(mine, send, fore, (kd, vt, q2, c2))
-    qd, qt, kt, ct, pt, o_local, sl = call(
+    facts = (8, n_groups, GROUP)
+    qd, qt, kt, ct, pt, o_local, sl, known_of = call(
         local_kernel,
         "local_mix",
         [
@@ -576,9 +600,11 @@
             ((heads, tokens, GROUP), BF16),
             (turned, F32),
             (group_states, F32),
+            (facts, jnp.int32),
         ],
         [tmp, tmp],
-        n_in=4,
+        n_in=5,
+        in_smem=(0,),
         flops=6 * mm,
     )(doc_lengths, kd_b, vt_b, q2_b, c2_b)
     total, o_local = lax.optimization_barrier((total, o_local))
@@ -592,9 +618,9 @@
             name,
             [(half_turned, F32), (half_states, BF16), ((2, tokens), F32)],
             [],
-            n_in=5 + len(before),
+            n_in=6 + len(before),
             flops=mm // 2,
-        )(doc_lengths, qt, o_local, ct, sl, states, *before)
+        )(known_of, qt, o_local, ct, sl, states, *before)
 
     o_own, sb_own, stats = part(True, own, (), "mix_own")
     o_other, sb_other, stats = part(False, other, (stats,), "mix_other")
@@ -606,38 +632,53 @@
         "norm_other",
         [(half_turned, BF16), ((8, tokens), F32), (piece, F32)],
         [],
-        n_in=4,
+        n_in=5,
         flops=mm // 2,
-    )(doc_lengths, stats, o_other, ct, qd)
+    )(known_of, stats, o_other, ct, qd)
     dobt, normed, sb, mine = call(
         merge_kernel,
         "norm_own",
         [(turned, BF16), (turned, BF16), (group_states, BF16), (piece, F32)],
         [],
-        n_in=8,
+        n_in=9,
         flops=mm // 2,
-    )(doc_lengths, factors, o_own, o_other, ct, qd, dob_other, sb_own, sb_other)
+    )(known_of, factors, o_own, o_other, ct, qd, dob_other, sb_own, sb_other)
     got, total, (dobt_b, normed_b) = exchange(mine, send, back, (dobt, normed))
-    dk, dv, rl, output, grad_q = call(
-        grad_kernel,
-        "local_grads",
-        [(full, F32), (full, F32), (group_states, F32), (flat, BF16), (flat, BF16)],
-        [tmp, tmp, buf, buf, sems],
-        n_in=7,
-        out_hbm=(3, 4),
-        flops=12 * mm,
-    )(doc_lengths, normed_b, dobt_b, pt, qd, kt, vd, sb)
-    total, dk = lax.optimization_barrier((total, dk))
+    cut = max(1, n_groups // 4)
+    earlier, later = range(0, cut), range(cut, n_groups)
+
+    def grads(groups, name, before):
+        count = len(groups)
+        held = (count * GROUP, width)
+        left = [(state_shape, F32)] if groups.start else []
+        kept = [(held, F32), (held, F32), ((count, *state_shape), F32)]
+        whole = len(left) + len(kept)
+        return call(
+            functools.partial(grad_kernel, groups),
+            name,
+            [*left, *kept, (flat, BF16), (flat, BF16)],
+            [tmp, tmp, pltpu.VMEM((count * GROUP * heads, head_width), BF16)]
+            + [pltpu.VMEM((count * GROUP * heads, head_width), BF16), sems],
+            n_in=8 + len(before),
+            in_hbm=(9, 10),
+            out_hbm=(whole, whole + 1),
+            alias={9: whole, 10: whole + 1} if before else None,
+            flops=count * mm,
+        )(known_of, normed_b, dobt_b, pt, qd, kt, vd, sb, *before)
+
+    left, dk1, dv1, rl1, output, grad_q = grads(later, "grads_later", ())
+    total, left = lax.optimization_barrier((total, left))
     own, other = finish(mine, got, total, back)
+    dk0, dv0, rl0, output, grad_q = grads(earlier, "grads_earlier", (left, output, grad_q))
     grad_k, grad_v = call(
         final_kernel,
         "final_grads",
         [(flat, BF16), (flat, BF16)],
         [state, tmp, tmp, buf, buf, sems],
-        n_in=7,
+        n_in=11,
         out_hbm=(0, 1),
         flops=2 * mm,
-    )(doc_lengths, dk, dv, kd, vd, rl, own, other)
+    )(known_of, kd, vd, own, other, dk0, dv0, rl0, dk1, dv1, rl1)
     return tuple(x.reshape(queries.shape) for x in (output, grad_q, grad_k, grad_v))
 
 

time: 44.7 us -> 42.4 us (0.949)
  Pallas kernels: 22 us -> 19.6 us
    pallas_call x2, Pallas kernels: 2.33 us -> 1.27 us  [part(): call(functools.partial(stats_kernel, is_own), name, [(half_turned, F32),...]
    pallas_call x1, Pallas kernels: 3.3 us -> 2.68 us  [per_device(): call(final_kernel, 'final_grads', [(flat, BF16), (flat, BF16)], [state, t...]
    pallas_call x1, Pallas kernels: 1.26 us -> 0.74 us  [per_device(): call(merge_kernel, 'norm_own', [(turned, BF16), (turned, BF16), (group_st...]
    pallas_call x1, Pallas kernels: 1.12 us -> 0.6 us  [per_device(): call(functools.partial(norm_kernel, float(width * n_head)), 'norm_other',...]
    pallas_call x1 -> x2, Pallas kernels: 6.04 us -> 6.44 us  [grads(): call(functools.partial(grad_kernel, groups), name, [*left, *kept, (flat,...]
  transfers between devices with their start and end apart: 13 -> 13, of which waited for: 7 -> 8; matrix products, arithmetic and copies ran while one was open for 0% -> 0% of each run, Pallas kernels for 27% -> 27%
where the time goes in v6:
time: 42.4 us; the launch traced here: 42.2 us
  Pallas kernels  19.6 us (46%)
  starting transfers between devices  14.4 us (34%)
  waiting for transfers between devices  7 us (17%)
  between operations  0.96 us (2%)
    ppermute x6, starting transfers between devices, exchange(): total = total + weights[5 + k] * lax.ppermute(chip_state, 'seq', links)  10.1 us
    pallas_call x2, Pallas kernels, grads(): call(functools.partial(grad_kernel, groups), name, [*left, *kept, (flat,...  6.44 us
    pallas_call x1, Pallas kernels, per_device(): call(functools.partial(state_kernel, n_seq), 'shard_state', [(full, BF16)...  4.18 us
    pallas_call x1, Pallas kernels, per_device(): call(local_kernel, 'local_mix', [(full, BF16), (turned, BF16), (turned, B...  3.74 us
    ppermute x3, starting transfers between devices, per_device(): lax.ppermute(stats, 'head', links_of(k, n_head))  3.55 us
    ppermute x3, waiting for transfers between devices, per_device(): lax.ppermute(stats, 'head', links_of(k, n_head))  3.29 us
    pallas_call x1, Pallas kernels, per_device(): call(final_kernel, 'final_grads', [(flat, BF16), (flat, BF16)], [state, t...  2.68 us
    ppermute x4, waiting for transfers between devices, swap(): return lax.ppermute(x, 'seq', swap_pairs)  1.97 us
  transfers between devices with their start and end apart: 13, of which 8 were waited for; matrix products, arithmetic and copies ran while one was open for 0% of the time, Pallas kernels for 27%

profile of v6, /device:TPU:0, one launch (start us, length us, event | category | flops | bytes accessed | tf_op | source)
XLA Modules:
  0.0 42.2 jit_solution(17085297835738591088)
XLA Ops:
  0.7 4.2 %shard_state.1 = (bf16[3072,256]{1,0:T(8,128)(2,1)S(1)}, bf16[3072,256]{1,0:T(8,128)(2,1)S(1)}, bf16[256,3072]{1,0:T(8,128)(2,1)S(1)}, f32[1,128,128]{2,1,0:T(8,...) custom-call(s32[6]{0:T(128)} %doc_ref.1, bf16[6144,128]{1,0:T(8,128)(2,1)} %bitcast.48, ...), custom_call_target="tpu_custom_call" | custom-call | flops 201326592 | bytes 8388608 | tf_op jit(solution)/shard_map/shard_state/pallas_call | solution.py:572
  4.8 0.5 %collective-permute-start = (f32[1,128,128]{2,1,0:T(8,128)S(1)}, f32[1,128,128]{2,1,0:T(8,128)S(1)}, u32[]{:S(2)}, u32[]{:S(2)}) collective-permute-start(f32[1,128,128]{2,1,0:T(8,128)S(1)} %get-tuple-element.59), channel_id=1, source_target_pairs={{0,4},{4,0},{8,12},{12,8},{16,20},{20,16},{24,28},{28,24},{1,5},{5... | collective-permute-start | bytes 196616 | tf_op jit(solution)/shard_map/ppermute | solution.py:552
  5.4 0.9 %collective-permute-done = f32[1,128,128]{2,1,0:T(8,128)S(1)} collective-permute-done((f32[1,128,128]{2,1,0:T(8,128)S(1)}, f32[1,128,128]{2,1,0:T(8,128)S(1)}, u32[]{:S(2)}, u32[]{:S(2)}) %collective-permute-start) | collective-permute-done | bytes 65568 | tf_op jit(solution)/shard_map/ppermute | solution.py:552
  6.3 5.0 %collective-permute-start.3 = (f32[1,128,128]{2,1,0:T(8,128)S(1)}, f32[1,128,128]{2,1,0:T(8,128)S(1)}, u32[]{:S(2)}, u32[]{:S(2)}) collective-permute-start(f32[1,128,128]{2,1,0:T(8,128)S(1)} %multiply_add_fusion.7), channel_id=1, source_target_pairs={{24,0},{28,4},{16,8},{20,12},{8,16},{12,20},{0,24},{4,28},{25,1},{... | collective-permute-start | bytes 196616 | tf_op jit(solution)/shard_map/ppermute | solution.py:560
  11.3 0.6 %collective-permute-start.1 = (f32[1,128,128]{2,1,0:T(8,128)S(1)}, f32[1,128,128]{2,1,0:T(8,128)S(1)}, u32[]{:S(2)}, u32[]{:S(2)}) collective-permute-start(f32[1,128,128]{2,1,0:T(8,128)S(1)} %multiply_add_fusion.7), channel_id=1, source_target_pairs={{8,0},{12,4},{0,8},{4,12},{24,16},{28,20},{16,24},{20,28},{9,1},{1... | collective-permute-start | bytes 196616 | tf_op jit(solution)/shard_map/ppermute | solution.py:560
  11.9 3.7 %local_mix.1 = (bf16[3072,256]{1,0:T(8,128)(2,1)S(1)}, bf16[256,3072]{1,0:T(8,128)(2,1)S(1)}, bf16[256,3072]{1,0:T(8,128)(2,1)S(1)}, bf16[256,3072]{1,0:T(8,128)...) custom-call(s32[6]{0:T(128)S(1)} %copy-done.2, ...), custom_call_target="tpu_custom_call" | custom-call | flops 1207959552 | bytes 8388608 | tf_op jit(solution)/shard_map/local_mix/pallas_call | solution.py:592
  15.7 1.5 %collective-permute-done.2 = f32[1,128,128]{2,1,0:T(8,128)S(1)} collective-permute-done((f32[1,128,128]{2,1,0:T(8,128)S(1)}, f32[1,128,128]{2,1,0:T(8,128)S(1)}, u32[]{:S(2)}, u32[]{:S(2)}) %collective-permute-start.2) | collective-permute-done | bytes 65568 | tf_op jit(solution)/shard_map/ppermute | solution.py:560
  17.3 0.6 %mix_own.1 = (f32[128,3072]{1,0:T(8,128)S(1)}, bf16[12,1,128,128]{3,2,1,0:T(8,128)(2,1)S(1)}, f32[2,3072]{1,0:T(2,128)S(1)}) custom-call(s32[8,12,256]{2,1,0:T(8,128)S(1)} %get-tuple-element.66.table_ref.refs_0_, bf16[256,3072]{1,0:T(8,128)(2,1)S(1)} %get-tuple-element.68.qt_ref, f32[256,3072]{1,0:T(8,128)S(1)} %get-tuple-element.71.ol_ref, ...), custom_call_target="tpu_custom_call" | custom-call | flops 100663296 | bytes 8388608 | tf_op jit(solution)/shard_map/mix_own/pallas_call | solution.py:616
  18.0 0.6 %collective-permute-done.4.state_ref = f32[1,128,128]{2,1,0:T(8,128)S(1)} collective-permute-done((f32[1,128,128]{2,1,0:T(8,128)S(1)}, f32[1,128,128]{2,1,0:T(8,128)S(1)}, u32[]{:S(2)}, u32[]{:S(2)}) %collective-permute-start.4) | collective-permute-done | bytes 65568 | tf_op jit(solution)/shard_map/ppermute | solution.py:552
  18.6 0.6 %mix_other.1 = (f32[128,3072]{1,0:T(8,128)S(1)}, bf16[12,1,128,128]{3,2,1,0:T(8,128)(2,1)S(1)}, f32[2,3072]{1,0:T(2,128)S(1)}) custom-call(s32[8,12,256]{2,1,0:T(8,128)S(1)} %get-tuple-element.66.table_ref.refs_0_, bf16[256,3072]{1,0:T(8,128)(2,1)S(1)} %get-tuple-element.68.qt_ref, f32[256,3072]{1,0:T(8,128)S(1)} %get-tuple-element.71.ol_ref, ...), custom_call_target="tpu_custom_call" | custom-call | flops 100663296 | bytes 8388608 | tf_op jit(solution)/shard_map/mix_other/pallas_call | solution.py:616
  19.2 2.5 %collective-permute-start.7 = (f32[2,3072]{1,0:T(2,128)S(1)}, f32[2,3072]{1,0:T(2,128)S(1)}, u32[]{:S(2)}, u32[]{:S(2)}) collective-permute-start(f32[2,3072]{1,0:T(2,128)S(1)} %get-tuple-element.76), channel_id=1, source_target_pairs={{3,0},{2,1},{1,2},{0,3},{7,4},{6,5},{5,6},{4,7},{11,8},{10,9},{9,1... | collective-permute-start | bytes 73736 | tf_op jit(solution)/shard_map/ppermute | solution.py:628
  21.7 0.5 %collective-permute-start.6 = (f32[2,3072]{1,0:T(2,128)S(1)}, f32[2,3072]{1,0:T(2,128)S(1)}, u32[]{:S(2)}, u32[]{:S(2)}) collective-permute-start(f32[2,3072]{1,0:T(2,128)S(1)} %get-tuple-element.76), channel_id=1, source_target_pairs={{2,0},{3,1},{0,2},{1,3},{6,4},{7,5},{4,6},{5,7},{10,8},{11,9},{8,1... | collective-permute-start | bytes 73736 | tf_op jit(solution)/shard_map/ppermute | solution.py:628
  22.2 0.5 %collective-permute-start.5 = (f32[2,3072]{1,0:T(2,128)S(1)}, f32[2,3072]{1,0:T(2,128)S(1)}, u32[]{:S(2)}, u32[]{:S(2)}) collective-permute-start(f32[2,3072]{1,0:T(2,128)S(1)} %get-tuple-element.76), channel_id=1, source_target_pairs={{1,0},{0,1},{3,2},{2,3},{5,4},{4,5},{7,6},{6,7},{9,8},{8,9},{11,10... | collective-permute-start | bytes 73736 | tf_op jit(solution)/shard_map/ppermute | solution.py:628
  22.8 1.2 %collective-permute-done.7 = f32[2,3072]{1,0:T(2,128)S(1)} collective-permute-done((f32[2,3072]{1,0:T(2,128)S(1)}, f32[2,3072]{1,0:T(2,128)S(1)}, u32[]{:S(2)}, u32[]{:S(2)}) %collective-permute-start.7) | collective-permute-done | bytes 24608 | tf_op jit(solution)/shard_map/ppermute | solution.py:628
  24.0 1.6 %collective-permute-done.6 = f32[2,3072]{1,0:T(2,128)S(1)} collective-permute-done((f32[2,3072]{1,0:T(2,128)S(1)}, f32[2,3072]{1,0:T(2,128)S(1)}, u32[]{:S(2)}, u32[]{:S(2)}) %collective-permute-start.6) | collective-permute-done | bytes 24608 | tf_op jit(solution)/shard_map/ppermute | solution.py:628
  25.5 0.5 %collective-permute-done.5 = f32[2,3072]{1,0:T(2,128)S(1)} collective-permute-done((f32[2,3072]{1,0:T(2,128)S(1)}, f32[2,3072]{1,0:T(2,128)S(1)}, u32[]{:S(2)}, u32[]{:S(2)}) %collective-permute-start.5) | collective-permute-done | bytes 24608 | tf_op jit(solution)/shard_map/ppermute | solution.py:628
  26.1 0.6 %norm_other.1 = (bf16[128,3072]{1,0:T(8,128)(2,1)S(1)}, f32[8,3072]{1,0:T(8,128)S(1)}, f32[1,128,128]{2,1,0:T(8,128)S(1)}) custom-call(s32[8,12,256]{2,1,0:T(8,128)S(1)} %get-tuple-element.66.table_ref.refs_0_, f32[2,3072]{1,0:T(2,128)S(1)} %add_add_fusion.st_ref, f32[128,3072]{1,0:T(8,128)S(1)} %get-tuple-element.77.o_ref.other_ref, ...), custom_call_target="tpu_custom_call" | custom-call | flops 100663296 | bytes 8388608 | tf_op jit(solution)/shard_map/norm_other/pallas_call | solution.py:630
  26.8 0.7 %norm_own.1 = (bf16[256,3072]{1,0:T(8,128)(2,1)S(1)}, bf16[256,3072]{1,0:T(8,128)(2,1)S(1)}, bf16[12,2,128,128]{3,2,1,0:T(8,128)(2,1)S(1)}, f32[1,128,128]{2,1,0:T(8,128)S(1)}) custom-call(s32[8,12,256]{2,1,0:T(8,128)S(1)} %get-tuple-element.66.table_ref.refs_0_, f32[8,3072]{1,0:T(8,128)S(1)} %get-tuple-element.79.rows_ref, ...), custom_call_target="tpu_custom_call" | custom-call | flops 100663296 | bytes 8388608 | tf_op jit(solution)/shard_map/norm_own/pallas_call | solution.py:638
  27.5 0.5 %collective-permute-done.8 = f32[1,128,128]{2,1,0:T(8,128)S(1)} collective-permute-done((f32[1,128,128]{2,1,0:T(8,128)S(1)}, f32[1,128,128]{2,1,0:T(8,128)S(1)}, u32[]{:S(2)}, u32[]{:S(2)}) %collective-permute-start.8) | collective-permute-done | bytes 65568 | tf_op jit(solution)/shard_map/ppermute | solution.py:552
  28.0 2.5 %collective-permute-start.11 = (f32[1,128,128]{2,1,0:T(8,128)S(1)}, f32[1,128,128]{2,1,0:T(8,128)S(1)}, u32[]{:S(2)}, u32[]{:S(2)}) collective-permute-start(f32[1,128,128]{2,1,0:T(8,128)S(1)} %multiply_add_fusion.3), channel_id=1, source_target_pairs={{24,0},{28,4},{16,8},{20,12},{8,16},{12,20},{0,24},{4,28},{25,1},{... | collective-permute-start | bytes 196616 | tf_op jit(solution)/shard_map/ppermute | solution.py:560
  30.7 1.8 %collective-permute-start.9 = (f32[1,128,128]{2,1,0:T(8,128)S(1)}, f32[1,128,128]{2,1,0:T(8,128)S(1)}, u32[]{:S(2)}, u32[]{:S(2)}) collective-permute-start(f32[1,128,128]{2,1,0:T(8,128)S(1)} %multiply_add_fusion.3), channel_id=1, source_target_pairs={{8,0},{12,4},{0,8},{4,12},{24,16},{28,20},{16,24},{20,28},{9,1},{1... | collective-permute-start | bytes 196616 | tf_op jit(solution)/shard_map/ppermute | solution.py:560
  32.5 4.4 %grads_later.1 = (f32[2,128,128]{2,1,0:T(8,128)S(1)}, f32[2304,256]{1,0:T(8,128)S(1)}, f32[2304,256]{1,0:T(8,128)S(1)}, f32[9,2,128,128]{3,2,1,0:T(8,128)S(1)}, ...) custom-call(s32[8,12,256]{2,1,0:T(8,128)S(1)} %get-tuple-element.66.table_ref.refs_0_, ...), custom_call_target="tpu_custom_call" | custom-call | flops 1811939328 | bytes 8388608 | tf_op jit(solution)/shard_map/grads_later/pallas_call | solution.py:656
  37.2 2.1 %grads_earlier.1 = (f32[768,256]{1,0:T(8,128)S(1)}, f32[768,256]{1,0:T(8,128)S(1)}, f32[3,2,128,128]{3,2,1,0:T(8,128)S(1)}, bf16[6144,128]{1,0:T(8,128)(2,1)}, bf16[6144,128]{1,0:T(8,128)(2,1)}) custom-call(s32[8,12,256]{2,1,0:T(8,128)S(1)} %get-tuple-element.66.table_ref.refs_0_, ...), custom_call_target="tpu_custom_call", output_to_operand_aliasing={{3}: (9, {}), {4}: (10, {})} | custom-call | flops 603979776 | bytes 8388608 | tf_op jit(solution)/shard_map/grads_earlier/pallas_call | solution.py:656
  39.3 2.7 %final_grads.1 = (bf16[6144,128]{1,0:T(8,128)(2,1)}, bf16[6144,128]{1,0:T(8,128)(2,1)}) custom-call(s32[8,12,256]{2,1,0:T(8,128)S(1)} %get-tuple-element.66.table_ref.refs_0_, bf16[3072,256]{1,0:T(8,128)(2,1)S(1)} %get-tuple-element.62.kd_ref, bf16[3072,256]{1,0:T(8,128)(2,1)S(1)} %get-tuple-element.92.refs_6_.vd_ref, ...), custom_call_target="tpu_custom_call" | custom-call | flops 402653184 | bytes 8388608 | tf_op jit(solution)/shard_map/final_grads/pallas_call | solution.py:673
  (26 shorter events, 0.7 us)
Async XLA Ops:
  0.6 11.3 %copy-start = (bf16[3072,2,128]{2,1,0:T(2,128)(2,1)S(1)}, bf16[3072,2,128]{2,1,0:T(2,128)(2,1)}, u32[]{:S(2)}) copy-start(bf16[3072,2,128]{2,1,0:T(2,128)(2,1)} %param.5) | copy-start | bytes 4718596
  0.6 11.3 %copy-start.1 = (bf16[3072,2,128]{2,1,0:T(2,128)(2,1)S(1)}, bf16[3072,2,128]{2,1,0:T(2,128)(2,1)}, u32[]{:S(2)}) copy-start(bf16[3072,2,128]{2,1,0:T(2,128)(2,1)} %param.8) | copy-start | bytes 4718596
  0.7 11.3 %copy-start.2 = (s32[6]{0:T(128)S(1)}, s32[6]{0:T(128)}, u32[]{:S(2)}) copy-start(s32[6]{0:T(128)} %doc_ref.1) | copy-start | bytes 76
  4.8 1.4 %collective-permute-start = (f32[1,128,128]{2,1,0:T(8,128)S(1)}, f32[1,128,128]{2,1,0:T(8,128)S(1)}, u32[]{:S(2)}, u32[]{:S(2)}) collective-permute-start(f32[1,128,128]{2,1,0:T(8,128)S(1)} %get-tuple-element.59), channel_id=1, source_target_pairs={{0,4},{4,0},{8,12},{12,8},{16,20},{20,16},{24,28},{28,24},{1,5},{5... | collective-permute-start | bytes 196616 | tf_op jit(solution)/shard_map/ppermute | solution.py:552
  6.3 9.4 %collective-permute-start.3 = (f32[1,128,128]{2,1,0:T(8,128)S(1)}, f32[1,128,128]{2,1,0:T(8,128)S(1)}, u32[]{:S(2)}, u32[]{:S(2)}) collective-permute-start(f32[1,128,128]{2,1,0:T(8,128)S(1)} %multiply_add_fusion.7), channel_id=1, source_target_pairs={{24,0},{28,4},{16,8},{20,12},{8,16},{12,20},{0,24},{4,28},{25,1},{... | collective-permute-start | bytes 196616 | tf_op jit(solution)/shard_map/ppermute | solution.py:560
  11.3 5.9 %collective-permute-start.2 = (f32[1,128,128]{2,1,0:T(8,128)S(1)}, f32[1,128,128]{2,1,0:T(8,128)S(1)}, u32[]{:S(2)}, u32[]{:S(2)}) collective-permute-start(f32[1,128,128]{2,1,0:T(8,128)S(1)} %multiply_add_fusion.7), channel_id=1, source_target_pairs={{16,0},{20,4},{24,8},{28,12},{0,16},{4,20},{8,24},{12,28},{17,1},{... | collective-permute-start | bytes 196616 | tf_op jit(solution)/shard_map/ppermute | solution.py:560
  11.3 5.9 %collective-permute-start.1 = (f32[1,128,128]{2,1,0:T(8,128)S(1)}, f32[1,128,128]{2,1,0:T(8,128)S(1)}, u32[]{:S(2)}, u32[]{:S(2)}) collective-permute-start(f32[1,128,128]{2,1,0:T(8,128)S(1)} %multiply_add_fusion.7), channel_id=1, source_target_pairs={{8,0},{12,4},{0,8},{4,12},{24,16},{28,20},{16,24},{20,28},{9,1},{1... | collective-permute-start | bytes 196616 | tf_op jit(solution)/shard_map/ppermute | solution.py:560
  17.2 1.3 %collective-permute-start.4 = (f32[1,128,128]{2,1,0:T(8,128)S(1)}, f32[1,128,128]{2,1,0:T(8,128)S(1)}, u32[]{:S(2)}, u32[]{:S(2)}) collective-permute-start(f32[1,128,128]{2,1,0:T(8,128)S(1)} %get-tuple-element.113), channel_id=1, source_target_pairs={{0,4},{4,0},{8,12},{12,8},{16,20},{20,16},{24,28},{28,24},{1,5},{5... | collective-permute-start | bytes 196616 | tf_op jit(solution)/shard_map/ppermute | solution.py:552
  19.2 4.8 %collective-permute-start.7 = (f32[2,3072]{1,0:T(2,128)S(1)}, f32[2,3072]{1,0:T(2,128)S(1)}, u32[]{:S(2)}, u32[]{:S(2)}) collective-permute-start(f32[2,3072]{1,0:T(2,128)S(1)} %get-tuple-element.76), channel_id=1, source_target_pairs={{3,0},{2,1},{1,2},{0,3},{7,4},{6,5},{5,6},{4,7},{11,8},{10,9},{9,1... | collective-permute-start | bytes 73736 | tf_op jit(solution)/shard_map/ppermute | solution.py:628
  21.7 3.8 %collective-permute-start.6 = (f32[2,3072]{1,0:T(2,128)S(1)}, f32[2,3072]{1,0:T(2,128)S(1)}, u32[]{:S(2)}, u32[]{:S(2)}) collective-permute-start(f32[2,3072]{1,0:T(2,128)S(1)} %get-tuple-element.76), channel_id=1, source_target_pairs={{2,0},{3,1},{0,2},{1,3},{6,4},{7,5},{4,6},{5,7},{10,8},{11,9},{8,1... | collective-permute-start | bytes 73736 | tf_op jit(solution)/shard_map/ppermute | solution.py:628
  22.2 3.8 %collective-permute-start.5 = (f32[2,3072]{1,0:T(2,128)S(1)}, f32[2,3072]{1,0:T(2,128)S(1)}, u32[]{:S(2)}, u32[]{:S(2)}) collective-permute-start(f32[2,3072]{1,0:T(2,128)S(1)} %get-tuple-element.76), channel_id=1, source_target_pairs={{1,0},{0,1},{3,2},{2,3},{5,4},{4,5},{7,6},{6,7},{9,8},{8,9},{11,10... | collective-permute-start | bytes 73736 | tf_op jit(solution)/shard_map/ppermute | solution.py:628
  26.7 1.3 %collective-permute-start.8 = (f32[1,128,128]{2,1,0:T(8,128)S(1)}, f32[1,128,128]{2,1,0:T(8,128)S(1)}, u32[]{:S(2)}, u32[]{:S(2)}) collective-permute-start(f32[1,128,128]{2,1,0:T(8,128)S(1)} %get-tuple-element.85), channel_id=1, source_target_pairs={{0,4},{4,0},{8,12},{12,8},{16,20},{20,16},{24,28},{28,24},{1,5},{5... | collective-permute-start | bytes 196616 | tf_op jit(solution)/shard_map/ppermute | solution.py:552
  28.0 8.8 %collective-permute-start.11 = (f32[1,128,128]{2,1,0:T(8,128)S(1)}, f32[1,128,128]{2,1,0:T(8,128)S(1)}, u32[]{:S(2)}, u32[]{:S(2)}) collective-permute-start(f32[1,128,128]{2,1,0:T(8,128)S(1)} %multiply_add_fusion.3), channel_id=1, source_target_pairs={{24,0},{28,4},{16,8},{20,12},{8,16},{12,20},{0,24},{4,28},{25,1},{... | collective-permute-start | bytes 196616 | tf_op jit(solution)/shard_map/ppermute | solution.py:560
  30.6 6.6 %collective-permute-start.10 = (f32[1,128,128]{2,1,0:T(8,128)S(1)}, f32[1,128,128]{2,1,0:T(8,128)S(1)}, u32[]{:S(2)}, u32[]{:S(2)}) collective-permute-start(f32[1,128,128]{2,1,0:T(8,128)S(1)} %multiply_add_fusion.3), channel_id=1, source_target_pairs={{16,0},{20,4},{24,8},{28,12},{0,16},{4,20},{8,24},{12,28},{17,1},{... | collective-permute-start | bytes 196616 | tf_op jit(solution)/shard_map/ppermute | solution.py:560
  30.7 6.5 %collective-permute-start.9 = (f32[1,128,128]{2,1,0:T(8,128)S(1)}, f32[1,128,128]{2,1,0:T(8,128)S(1)}, u32[]{:S(2)}, u32[]{:S(2)}) collective-permute-start(f32[1,128,128]{2,1,0:T(8,128)S(1)} %multiply_add_fusion.3), channel_id=1, source_target_pairs={{8,0},{12,4},{0,8},{4,12},{24,16},{28,20},{16,24},{20,28},{9,1},{1... | collective-permute-start | bytes 196616 | tf_op jit(solution)/shard_map/ppermute | solution.py:560
  37.2 2.1 %collective-permute-start.12 = (f32[1,128,128]{2,1,0:T(8,128)S(1)}, f32[1,128,128]{2,1,0:T(8,128)S(1)}, u32[]{:S(2)}, u32[]{:S(2)}) collective-permute-start(f32[1,128,128]{2,1,0:T(8,128)S(1)} %get-tuple-element.110), channel_id=1, source_target_pairs={{0,4},{4,0},{8,12},{12,8},{16,20},{20,16},{24,28},{28,24},{1,5},{5... | collective-permute-start | bytes 196616 | tf_op jit(solution)/shard_map/ppermute | solution.py:552

commit v7 on v6

--- a/solution.py
+++ b/solution.py
@@ -170,8 +170,14 @@
     half = heads // 2
     n_groups = tokens // GROUP
 
+    sizes = [max(1, n_groups // 6), max(1, n_groups // 3)]
+    sizes = [*sizes, n_groups - sum(sizes)] if n_groups > 2 else [1] * n_groups
+    chunks = {sum(sizes[:i]): size for i, size in enumerate(sizes)}
+
     def fetches(g):
-        rows = pair_rows(g, heads)
+        if g not in chunks:
+            return ()
+        rows = pl.ds(g * GROUP * heads, chunks[g] * GROUP * heads)
         return (
             pltpu.make_async_copy(k2_ref.at[rows], bufk.at[rows], sems.at[0, g]),
             pltpu.make_async_copy(v2_ref.at[rows], bufv.at[rows], sems.at[1, g]),

time: 42.4 us -> 41.4 us (0.976)
  Pallas kernels: 19.6 us -> 18.6 us
    pallas_call x1, Pallas kernels: 4.18 us -> 3.33 us  [per_device(): call(functools.partial(state_kernel, n_seq), 'shard_state', [(full, BF16)...]
  transfers between devices with their start and end apart: 13 -> 13, of which waited for: 8 -> 8; matrix products, arithmetic and copies ran while one was open for 0% -> 0% of each run, Pallas kernels for 27% -> 28%
where the time goes in v7:
time: 41.4 us; the launch traced here: 41.2 us
  Pallas kernels  18.6 us (45%)
  starting transfers between devices  14.4 us (35%)
  waiting for transfers between devices  7.18 us (17%)
  between operations  0.81 us (2%)
    ppermute x6, starting transfers between devices, exchange(): total = total + weights[5 + k] * lax.ppermute(chip_state, 'seq', links)  10.1 us
    pallas_call x2, Pallas kernels, grads(): call(functools.partial(grad_kernel, groups), name, [*left, *kept, (flat,...  6.26 us
    pallas_call x1, Pallas kernels, per_device(): call(local_kernel, 'local_mix', [(full, BF16), (turned, BF16), (turned, B...  3.74 us
    ppermute x3, starting transfers between devices, per_device(): lax.ppermute(stats, 'head', links_of(k, n_head))  3.55 us
    pallas_call x1, Pallas kernels, per_device(): call(functools.partial(state_kernel, n_seq), 'shard_state', [(full, BF16)...  3.33 us
    ppermute x3, waiting for transfers between devices, per_device(): lax.ppermute(stats, 'head', links_of(k, n_head))  3.29 us
    pallas_call x1, Pallas kernels, per_device(): call(final_kernel, 'final_grads', [(flat, BF16), (flat, BF16)], [state, t...  2.68 us
    ppermute x4, waiting for transfers between devices, swap(): return lax.ppermute(x, 'seq', swap_pairs)  1.97 us
  transfers between devices with their start and end apart: 13, of which 8 were waited for; matrix products, arithmetic and copies ran while one was open for 0% of the time, Pallas kernels for 28%

profile of v7, /device:TPU:0, one launch (start us, length us, event | category | flops | bytes accessed | tf_op | source)
XLA Modules:
  0.0 41.2 jit_solution(18217932109775064568)
XLA Ops:
  0.7 3.3 %shard_state.1 = (bf16[3072,256]{1,0:T(8,128)(2,1)S(1)}, bf16[3072,256]{1,0:T(8,128)(2,1)S(1)}, bf16[256,3072]{1,0:T(8,128)(2,1)S(1)}, f32[1,128,128]{2,1,0:T(8,...) custom-call(s32[6]{0:T(128)} %doc_ref.1, bf16[6144,128]{1,0:T(8,128)(2,1)} %bitcast.48, ...), custom_call_target="tpu_custom_call" | custom-call | flops 201326592 | bytes 8388608 | tf_op jit(solution)/shard_map/shard_state/pallas_call | solution.py:578
  4.0 0.5 %collective-permute-start = (f32[1,128,128]{2,1,0:T(8,128)S(1)}, f32[1,128,128]{2,1,0:T(8,128)S(1)}, u32[]{:S(2)}, u32[]{:S(2)}) collective-permute-start(f32[1,128,128]{2,1,0:T(8,128)S(1)} %get-tuple-element.59), channel_id=1, source_target_pairs={{0,4},{4,0},{8,12},{12,8},{16,20},{20,16},{24,28},{28,24},{1,5},{5... | collective-permute-start | bytes 196616 | tf_op jit(solution)/shard_map/ppermute | solution.py:558
  4.5 0.9 %collective-permute-done = f32[1,128,128]{2,1,0:T(8,128)S(1)} collective-permute-done((f32[1,128,128]{2,1,0:T(8,128)S(1)}, f32[1,128,128]{2,1,0:T(8,128)S(1)}, u32[]{:S(2)}, u32[]{:S(2)}) %collective-permute-start) | collective-permute-done | bytes 65568 | tf_op jit(solution)/shard_map/ppermute | solution.py:558
  5.4 5.0 %collective-permute-start.3 = (f32[1,128,128]{2,1,0:T(8,128)S(1)}, f32[1,128,128]{2,1,0:T(8,128)S(1)}, u32[]{:S(2)}, u32[]{:S(2)}) collective-permute-start(f32[1,128,128]{2,1,0:T(8,128)S(1)} %multiply_add_fusion.7), channel_id=1, source_target_pairs={{24,0},{28,4},{16,8},{20,12},{8,16},{12,20},{0,24},{4,28},{25,1},{... | collective-permute-start | bytes 196616 | tf_op jit(solution)/shard_map/ppermute | solution.py:566
  10.5 0.6 %collective-permute-start.1 = (f32[1,128,128]{2,1,0:T(8,128)S(1)}, f32[1,128,128]{2,1,0:T(8,128)S(1)}, u32[]{:S(2)}, u32[]{:S(2)}) collective-permute-start(f32[1,128,128]{2,1,0:T(8,128)S(1)} %multiply_add_fusion.7), channel_id=1, source_target_pairs={{8,0},{12,4},{0,8},{4,12},{24,16},{28,20},{16,24},{20,28},{9,1},{1... | collective-permute-start | bytes 196616 | tf_op jit(solution)/shard_map/ppermute | solution.py:566
  11.1 3.7 %local_mix.1 = (bf16[3072,256]{1,0:T(8,128)(2,1)S(1)}, bf16[256,3072]{1,0:T(8,128)(2,1)S(1)}, bf16[256,3072]{1,0:T(8,128)(2,1)S(1)}, bf16[256,3072]{1,0:T(8,128)...) custom-call(s32[6]{0:T(128)S(1)} %copy-done.2, ...), custom_call_target="tpu_custom_call" | custom-call | flops 1207959552 | bytes 8388608 | tf_op jit(solution)/shard_map/local_mix/pallas_call | solution.py:598
  14.8 1.5 %collective-permute-done.2 = f32[1,128,128]{2,1,0:T(8,128)S(1)} collective-permute-done((f32[1,128,128]{2,1,0:T(8,128)S(1)}, f32[1,128,128]{2,1,0:T(8,128)S(1)}, u32[]{:S(2)}, u32[]{:S(2)}) %collective-permute-start.2) | collective-permute-done | bytes 65568 | tf_op jit(solution)/shard_map/ppermute | solution.py:566
  16.5 0.6 %mix_own.1 = (f32[128,3072]{1,0:T(8,128)S(1)}, bf16[12,1,128,128]{3,2,1,0:T(8,128)(2,1)S(1)}, f32[2,3072]{1,0:T(2,128)S(1)}) custom-call(s32[8,12,256]{2,1,0:T(8,128)S(1)} %get-tuple-element.66.table_ref.refs_0_, bf16[256,3072]{1,0:T(8,128)(2,1)S(1)} %get-tuple-element.68.qt_ref, f32[256,3072]{1,0:T(8,128)S(1)} %get-tuple-element.71.ol_ref, ...), custom_call_target="tpu_custom_call" | custom-call | flops 100663296 | bytes 8388608 | tf_op jit(solution)/shard_map/mix_own/pallas_call | solution.py:622
  17.1 0.6 %collective-permute-done.4.state_ref = f32[1,128,128]{2,1,0:T(8,128)S(1)} collective-permute-done((f32[1,128,128]{2,1,0:T(8,128)S(1)}, f32[1,128,128]{2,1,0:T(8,128)S(1)}, u32[]{:S(2)}, u32[]{:S(2)}) %collective-permute-start.4) | collective-permute-done | bytes 65568 | tf_op jit(solution)/shard_map/ppermute | solution.py:558
  17.7 0.6 %mix_other.1 = (f32[128,3072]{1,0:T(8,128)S(1)}, bf16[12,1,128,128]{3,2,1,0:T(8,128)(2,1)S(1)}, f32[2,3072]{1,0:T(2,128)S(1)}) custom-call(s32[8,12,256]{2,1,0:T(8,128)S(1)} %get-tuple-element.66.table_ref.refs_0_, bf16[256,3072]{1,0:T(8,128)(2,1)S(1)} %get-tuple-element.68.qt_ref, f32[256,3072]{1,0:T(8,128)S(1)} %get-tuple-element.71.ol_ref, ...), custom_call_target="tpu_custom_call" | custom-call | flops 100663296 | bytes 8388608 | tf_op jit(solution)/shard_map/mix_other/pallas_call | solution.py:622
  18.3 2.5 %collective-permute-start.7 = (f32[2,3072]{1,0:T(2,128)S(1)}, f32[2,3072]{1,0:T(2,128)S(1)}, u32[]{:S(2)}, u32[]{:S(2)}) collective-permute-start(f32[2,3072]{1,0:T(2,128)S(1)} %get-tuple-element.76), channel_id=1, source_target_pairs={{3,0},{2,1},{1,2},{0,3},{7,4},{6,5},{5,6},{4,7},{11,8},{10,9},{9,1... | collective-permute-start | bytes 73736 | tf_op jit(solution)/shard_map/ppermute | solution.py:634
  20.9 0.5 %collective-permute-start.6 = (f32[2,3072]{1,0:T(2,128)S(1)}, f32[2,3072]{1,0:T(2,128)S(1)}, u32[]{:S(2)}, u32[]{:S(2)}) collective-permute-start(f32[2,3072]{1,0:T(2,128)S(1)} %get-tuple-element.76), channel_id=1, source_target_pairs={{2,0},{3,1},{0,2},{1,3},{6,4},{7,5},{4,6},{5,7},{10,8},{11,9},{8,1... | collective-permute-start | bytes 73736 | tf_op jit(solution)/shard_map/ppermute | solution.py:634
  21.4 0.5 %collective-permute-start.5 = (f32[2,3072]{1,0:T(2,128)S(1)}, f32[2,3072]{1,0:T(2,128)S(1)}, u32[]{:S(2)}, u32[]{:S(2)}) collective-permute-start(f32[2,3072]{1,0:T(2,128)S(1)} %get-tuple-element.76), channel_id=1, source_target_pairs={{1,0},{0,1},{3,2},{2,3},{5,4},{4,5},{7,6},{6,7},{9,8},{8,9},{11,10... | collective-permute-start | bytes 73736 | tf_op jit(solution)/shard_map/ppermute | solution.py:634
  21.9 1.2 %collective-permute-done.7 = f32[2,3072]{1,0:T(2,128)S(1)} collective-permute-done((f32[2,3072]{1,0:T(2,128)S(1)}, f32[2,3072]{1,0:T(2,128)S(1)}, u32[]{:S(2)}, u32[]{:S(2)}) %collective-permute-start.7) | collective-permute-done | bytes 24608 | tf_op jit(solution)/shard_map/ppermute | solution.py:634
  23.1 1.5 %collective-permute-done.6 = f32[2,3072]{1,0:T(2,128)S(1)} collective-permute-done((f32[2,3072]{1,0:T(2,128)S(1)}, f32[2,3072]{1,0:T(2,128)S(1)}, u32[]{:S(2)}, u32[]{:S(2)}) %collective-permute-start.6) | collective-permute-done | bytes 24608 | tf_op jit(solution)/shard_map/ppermute | solution.py:634
  24.7 0.5 %collective-permute-done.5 = f32[2,3072]{1,0:T(2,128)S(1)} collective-permute-done((f32[2,3072]{1,0:T(2,128)S(1)}, f32[2,3072]{1,0:T(2,128)S(1)}, u32[]{:S(2)}, u32[]{:S(2)}) %collective-permute-start.5) | collective-permute-done | bytes 24608 | tf_op jit(solution)/shard_map/ppermute | solution.py:634
  25.2 0.6 %norm_other.1 = (bf16[128,3072]{1,0:T(8,128)(2,1)S(1)}, f32[8,3072]{1,0:T(8,128)S(1)}, f32[1,128,128]{2,1,0:T(8,128)S(1)}) custom-call(s32[8,12,256]{2,1,0:T(8,128)S(1)} %get-tuple-element.66.table_ref.refs_0_, f32[2,3072]{1,0:T(2,128)S(1)} %add_add_fusion.st_ref, f32[128,3072]{1,0:T(8,128)S(1)} %get-tuple-element.77.o_ref.other_ref, ...), custom_call_target="tpu_custom_call" | custom-call | flops 100663296 | bytes 8388608 | tf_op jit(solution)/shard_map/norm_other/pallas_call | solution.py:636
  25.9 0.7 %norm_own.1 = (bf16[256,3072]{1,0:T(8,128)(2,1)S(1)}, bf16[256,3072]{1,0:T(8,128)(2,1)S(1)}, bf16[12,2,128,128]{3,2,1,0:T(8,128)(2,1)S(1)}, f32[1,128,128]{2,1,0:T(8,128)S(1)}) custom-call(s32[8,12,256]{2,1,0:T(8,128)S(1)} %get-tuple-element.66.table_ref.refs_0_, f32[8,3072]{1,0:T(8,128)S(1)} %get-tuple-element.79.rows_ref, ...), custom_call_target="tpu_custom_call" | custom-call | flops 100663296 | bytes 8388608 | tf_op jit(solution)/shard_map/norm_own/pallas_call | solution.py:644
  26.7 0.5 %collective-permute-done.8 = f32[1,128,128]{2,1,0:T(8,128)S(1)} collective-permute-done((f32[1,128,128]{2,1,0:T(8,128)S(1)}, f32[1,128,128]{2,1,0:T(8,128)S(1)}, u32[]{:S(2)}, u32[]{:S(2)}) %collective-permute-start.8) | collective-permute-done | bytes 65568 | tf_op jit(solution)/shard_map/ppermute | solution.py:558
  27.2 2.5 %collective-permute-start.11 = (f32[1,128,128]{2,1,0:T(8,128)S(1)}, f32[1,128,128]{2,1,0:T(8,128)S(1)}, u32[]{:S(2)}, u32[]{:S(2)}) collective-permute-start(f32[1,128,128]{2,1,0:T(8,128)S(1)} %multiply_add_fusion.3), channel_id=1, source_target_pairs={{24,0},{28,4},{16,8},{20,12},{8,16},{12,20},{0,24},{4,28},{25,1},{... | collective-permute-start | bytes 196616 | tf_op jit(solution)/shard_map/ppermute | solution.py:566
  29.8 1.8 %collective-permute-start.9 = (f32[1,128,128]{2,1,0:T(8,128)S(1)}, f32[1,128,128]{2,1,0:T(8,128)S(1)}, u32[]{:S(2)}, u32[]{:S(2)}) collective-permute-start(f32[1,128,128]{2,1,0:T(8,128)S(1)} %multiply_add_fusion.3), channel_id=1, source_target_pairs={{8,0},{12,4},{0,8},{4,12},{24,16},{28,20},{16,24},{20,28},{9,1},{1... | collective-permute-start | bytes 196616 | tf_op jit(solution)/shard_map/ppermute | solution.py:566
  31.6 4.2 %grads_later.1 = (f32[2,128,128]{2,1,0:T(8,128)S(1)}, f32[2304,256]{1,0:T(8,128)S(1)}, f32[2304,256]{1,0:T(8,128)S(1)}, f32[9,2,128,128]{3,2,1,0:T(8,128)S(1)}, ...) custom-call(s32[8,12,256]{2,1,0:T(8,128)S(1)} %get-tuple-element.66.table_ref.refs_0_, ...), custom_call_target="tpu_custom_call" | custom-call | flops 1811939328 | bytes 8388608 | tf_op jit(solution)/shard_map/grads_later/pallas_call | solution.py:662
  36.4 2.1 %grads_earlier.1 = (f32[768,256]{1,0:T(8,128)S(1)}, f32[768,256]{1,0:T(8,128)S(1)}, f32[3,2,128,128]{3,2,1,0:T(8,128)S(1)}, bf16[6144,128]{1,0:T(8,128)(2,1)}, bf16[6144,128]{1,0:T(8,128)(2,1)}) custom-call(s32[8,12,256]{2,1,0:T(8,128)S(1)} %get-tuple-element.66.table_ref.refs_0_, ...), custom_call_target="tpu_custom_call", output_to_operand_aliasing={{3}: (9, {}), {4}: (10, {})} | custom-call | flops 603979776 | bytes 8388608 | tf_op jit(solution)/shard_map/grads_earlier/pallas_call | solution.py:662
  38.5 2.7 %final_grads.1 = (bf16[6144,128]{1,0:T(8,128)(2,1)}, bf16[6144,128]{1,0:T(8,128)(2,1)}) custom-call(s32[8,12,256]{2,1,0:T(8,128)S(1)} %get-tuple-element.66.table_ref.refs_0_, bf16[3072,256]{1,0:T(8,128)(2,1)S(1)} %get-tuple-element.62.kd_ref, bf16[3072,256]{1,0:T(8,128)(2,1)S(1)} %get-tuple-element.92.refs_6_.vd_ref, ...), custom_call_target="tpu_custom_call" | custom-call | flops 402653184 | bytes 8388608 | tf_op jit(solution)/shard_map/final_grads/pallas_call | solution.py:679
  (26 shorter events, 0.9 us)
Async XLA Ops:
  0.6 10.5 %copy-start = (bf16[3072,2,128]{2,1,0:T(2,128)(2,1)S(1)}, bf16[3072,2,128]{2,1,0:T(2,128)(2,1)}, u32[]{:S(2)}) copy-start(bf16[3072,2,128]{2,1,0:T(2,128)(2,1)} %param.5) | copy-start | bytes 4718596
  0.6 10.5 %copy-start.1 = (bf16[3072,2,128]{2,1,0:T(2,128)(2,1)S(1)}, bf16[3072,2,128]{2,1,0:T(2,128)(2,1)}, u32[]{:S(2)}) copy-start(bf16[3072,2,128]{2,1,0:T(2,128)(2,1)} %param.8) | copy-start | bytes 4718596
  0.7 10.5 %copy-start.2 = (s32[6]{0:T(128)S(1)}, s32[6]{0:T(128)}, u32[]{:S(2)}) copy-start(s32[6]{0:T(128)} %doc_ref.1) | copy-start | bytes 76
  4.0 1.4 %collective-permute-start = (f32[1,128,128]{2,1,0:T(8,128)S(1)}, f32[1,128,128]{2,1,0:T(8,128)S(1)}, u32[]{:S(2)}, u32[]{:S(2)}) collective-permute-start(f32[1,128,128]{2,1,0:T(8,128)S(1)} %get-tuple-element.59), channel_id=1, source_target_pairs={{0,4},{4,0},{8,12},{12,8},{16,20},{20,16},{24,28},{28,24},{1,5},{5... | collective-permute-start | bytes 196616 | tf_op jit(solution)/shard_map/ppermute | solution.py:558
  5.4 9.4 %collective-permute-start.3 = (f32[1,128,128]{2,1,0:T(8,128)S(1)}, f32[1,128,128]{2,1,0:T(8,128)S(1)}, u32[]{:S(2)}, u32[]{:S(2)}) collective-permute-start(f32[1,128,128]{2,1,0:T(8,128)S(1)} %multiply_add_fusion.7), channel_id=1, source_target_pairs={{24,0},{28,4},{16,8},{20,12},{8,16},{12,20},{0,24},{4,28},{25,1},{... | collective-permute-start | bytes 196616 | tf_op jit(solution)/shard_map/ppermute | solution.py:566
  10.5 5.9 %collective-permute-start.2 = (f32[1,128,128]{2,1,0:T(8,128)S(1)}, f32[1,128,128]{2,1,0:T(8,128)S(1)}, u32[]{:S(2)}, u32[]{:S(2)}) collective-permute-start(f32[1,128,128]{2,1,0:T(8,128)S(1)} %multiply_add_fusion.7), channel_id=1, source_target_pairs={{16,0},{20,4},{24,8},{28,12},{0,16},{4,20},{8,24},{12,28},{17,1},{... | collective-permute-start | bytes 196616 | tf_op jit(solution)/shard_map/ppermute | solution.py:566
  10.5 5.9 %collective-permute-start.1 = (f32[1,128,128]{2,1,0:T(8,128)S(1)}, f32[1,128,128]{2,1,0:T(8,128)S(1)}, u32[]{:S(2)}, u32[]{:S(2)}) collective-permute-start(f32[1,128,128]{2,1,0:T(8,128)S(1)} %multiply_add_fusion.7), channel_id=1, source_target_pairs={{8,0},{12,4},{0,8},{4,12},{24,16},{28,20},{16,24},{20,28},{9,1},{1... | collective-permute-start | bytes 196616 | tf_op jit(solution)/shard_map/ppermute | solution.py:566
  16.4 1.3 %collective-permute-start.4 = (f32[1,128,128]{2,1,0:T(8,128)S(1)}, f32[1,128,128]{2,1,0:T(8,128)S(1)}, u32[]{:S(2)}, u32[]{:S(2)}) collective-permute-start(f32[1,128,128]{2,1,0:T(8,128)S(1)} %get-tuple-element.113), channel_id=1, source_target_pairs={{0,4},{4,0},{8,12},{12,8},{16,20},{20,16},{24,28},{28,24},{1,5},{5... | collective-permute-start | bytes 196616 | tf_op jit(solution)/shard_map/ppermute | solution.py:558
  18.3 4.8 %collective-permute-start.7 = (f32[2,3072]{1,0:T(2,128)S(1)}, f32[2,3072]{1,0:T(2,128)S(1)}, u32[]{:S(2)}, u32[]{:S(2)}) collective-permute-start(f32[2,3072]{1,0:T(2,128)S(1)} %get-tuple-element.76), channel_id=1, source_target_pairs={{3,0},{2,1},{1,2},{0,3},{7,4},{6,5},{5,6},{4,7},{11,8},{10,9},{9,1... | collective-permute-start | bytes 73736 | tf_op jit(solution)/shard_map/ppermute | solution.py:634
  20.9 3.8 %collective-permute-start.6 = (f32[2,3072]{1,0:T(2,128)S(1)}, f32[2,3072]{1,0:T(2,128)S(1)}, u32[]{:S(2)}, u32[]{:S(2)}) collective-permute-start(f32[2,3072]{1,0:T(2,128)S(1)} %get-tuple-element.76), channel_id=1, source_target_pairs={{2,0},{3,1},{0,2},{1,3},{6,4},{7,5},{4,6},{5,7},{10,8},{11,9},{8,1... | collective-permute-start | bytes 73736 | tf_op jit(solution)/shard_map/ppermute | solution.py:634
  21.4 3.8 %collective-permute-start.5 = (f32[2,3072]{1,0:T(2,128)S(1)}, f32[2,3072]{1,0:T(2,128)S(1)}, u32[]{:S(2)}, u32[]{:S(2)}) collective-permute-start(f32[2,3072]{1,0:T(2,128)S(1)} %get-tuple-element.76), channel_id=1, source_target_pairs={{1,0},{0,1},{3,2},{2,3},{5,4},{4,5},{7,6},{6,7},{9,8},{8,9},{11,10... | collective-permute-start | bytes 73736 | tf_op jit(solution)/shard_map/ppermute | solution.py:634
  25.8 1.3 %collective-permute-start.8 = (f32[1,128,128]{2,1,0:T(8,128)S(1)}, f32[1,128,128]{2,1,0:T(8,128)S(1)}, u32[]{:S(2)}, u32[]{:S(2)}) collective-permute-start(f32[1,128,128]{2,1,0:T(8,128)S(1)} %get-tuple-element.85), channel_id=1, source_target_pairs={{0,4},{4,0},{8,12},{12,8},{16,20},{20,16},{24,28},{28,24},{1,5},{5... | collective-permute-start | bytes 196616 | tf_op jit(solution)/shard_map/ppermute | solution.py:558
  27.2 8.7 %collective-permute-start.11 = (f32[1,128,128]{2,1,0:T(8,128)S(1)}, f32[1,128,128]{2,1,0:T(8,128)S(1)}, u32[]{:S(2)}, u32[]{:S(2)}) collective-permute-start(f32[1,128,128]{2,1,0:T(8,128)S(1)} %multiply_add_fusion.3), channel_id=1, source_target_pairs={{24,0},{28,4},{16,8},{20,12},{8,16},{12,20},{0,24},{4,28},{25,1},{... | collective-permute-start | bytes 196616 | tf_op jit(solution)/shard_map/ppermute | solution.py:566
  29.7 6.6 %collective-permute-start.10 = (f32[1,128,128]{2,1,0:T(8,128)S(1)}, f32[1,128,128]{2,1,0:T(8,128)S(1)}, u32[]{:S(2)}, u32[]{:S(2)}) collective-permute-start(f32[1,128,128]{2,1,0:T(8,128)S(1)} %multiply_add_fusion.3), channel_id=1, source_target_pairs={{16,0},{20,4},{24,8},{28,12},{0,16},{4,20},{8,24},{12,28},{17,1},{... | collective-permute-start | bytes 196616 | tf_op jit(solution)/shard_map/ppermute | solution.py:566
  29.8 6.5 %collective-permute-start.9 = (f32[1,128,128]{2,1,0:T(8,128)S(1)}, f32[1,128,128]{2,1,0:T(8,128)S(1)}, u32[]{:S(2)}, u32[]{:S(2)}) collective-permute-start(f32[1,128,128]{2,1,0:T(8,128)S(1)} %multiply_add_fusion.3), channel_id=1, source_target_pairs={{8,0},{12,4},{0,8},{4,12},{24,16},{28,20},{16,24},{20,28},{9,1},{1... | collective-permute-start | bytes 196616 | tf_op jit(solution)/shard_map/ppermute | solution.py:566
  36.3 2.1 %collective-permute-start.12 = (f32[1,128,128]{2,1,0:T(8,128)S(1)}, f32[1,128,128]{2,1,0:T(8,128)S(1)}, u32[]{:S(2)}, u32[]{:S(2)}) collective-permute-start(f32[1,128,128]{2,1,0:T(8,128)S(1)} %get-tuple-element.110), channel_id=1, source_target_pairs={{0,4},{4,0},{8,12},{12,8},{16,20},{20,16},{24,28},{28,24},{1,5},{5... | collective-permute-start | bytes 196616 | tf_op jit(solution)/shard_map/ppermute | solution.py:558

commit v8 on v7

--- a/solution.py
+++ b/solution.py
@@ -162,10 +162,10 @@
 
 
 def state_kernel(
-    n_seq, doc_hbm, k2_ref, v2_ref, kd_ref, vd_ref, vt_ref, mine_ref, send_ref, fore_ref, back_ref,
-    doc_ref, bufk, bufv, tmpk, tmpv, acc, sems, doc_sem,
+    n_seq, doc_hbm, k2_ref, v2_ref, bufk, bufv, vt_ref, mine_ref, send_ref, fore_ref, back_ref,
+    doc_ref, tmpk, tmpv, acc, sems, doc_sem,
 ):
-    tokens, width = kd_ref.shape
+    width, tokens = vt_ref.shape
     heads = width // 128
     half = heads // 2
     n_groups = tokens // GROUP
@@ -207,8 +207,6 @@
         ready = []
         for h in range(heads):
             vt = turn(vs[h])
-            kd_ref[rows, at(h)] = ks[h].astype(BF16)
-            vd_ref[rows, at(h)] = vs[h].astype(BF16)
             vt_ref[at(h), rows] = vt
             ready.append((vt, jnp.where(keep, ks[h], 0.0).astype(BF16)))
         return ready
@@ -226,8 +224,26 @@
     send_ref[...] = acc[pl.ds((1 - core) * half, half)]
 
 
+def split_kernel(pairs_ref, out_ref, tmp):
+    tokens, width = out_ref.shape
+    heads = width // 128
+    for g in range(tokens // GROUP):
+        parts = split_heads(pairs_ref, tmp, g, heads)
+        for h in range(heads):
+            out_ref[group_rows(g), at(h)] = parts[h].astype(BF16)
+
+
+def later_forms_kernel(k_ref, v2_ref, kt_ref, vd_ref, tmp):
+    split_kernel(v2_ref, vd_ref, tmp)
+    width, tokens = kt_ref.shape
+    for g in range(tokens // GROUP):
+        rows = group_rows(g)
+        for h in range(width // 128):
+            kt_ref[at(h), rows] = k_ref[rows, at(h)].T
+
+
 def local_kernel(
-    doc_ref, kd_ref, vt_ref, q2_ref, c2_ref, qd_ref, qt_ref, kt_ref, ct_ref, pt_ref, ol_ref, sl_ref, table_ref,
+    doc_ref, kd_ref, vt_ref, q2_ref, c2_ref, qd_ref, qt_ref, ct_ref, pt_ref, ol_ref, sl_ref, table_ref,
     tmpq, tmpc,
 ):
     tokens, width = kd_ref.shape
@@ -245,7 +261,6 @@
             qt = turn(qs[h])
             qd_ref[rows, at(h)] = qs[h].astype(BF16)
             qt_ref[at(h), rows] = qt
-            kt_ref[at(h), rows] = turn(kd_ref[rows, at(h)])
             ct_ref[at(h), rows] = turn(cs[h])
             qts.append(qt)
         return qts
@@ -575,14 +590,12 @@
     table = ((5 + n_chips, 128), F32)
     turned = (width, tokens)
     group_states = (n_groups, heads, head_width, head_width)
-    kd, vd, vt, mine, send, fore, back = call(
+    raw_k, raw_v, vt, mine, send, fore, back = call(
         functools.partial(state_kernel, n_seq),
         "shard_state",
-        [(full, BF16), (full, BF16), (turned, BF16), (piece, F32), (piece, F32), table, table],
+        [(flat, BF16), (flat, BF16), (turned, BF16), (piece, F32), (piece, F32), table, table],
         [
             pltpu.SMEM(doc_lengths.shape, jnp.int32),
-            buf,
-            buf,
             tmp,
             tmp,
             state,
@@ -593,14 +606,20 @@
         in_hbm=(0, 1, 2),
         flops=mm,
     )(*(pltpu.with_memory_space_constraint(x, pltpu.HBM) for x in (doc_lengths, k2, v2)))
-    got, total, (kd_b, vt_b, q2_b, c2_b) = exchange(mine, send, fore, (kd, vt, q2, c2))
+    (kd,) = call(
+        split_kernel,
+        "split_keys",
+        [(full, BF16)],
+        [tmp],
+        n_in=1,
+    )(raw_k)
+    got, total, (kd, vt) = exchange(mine, send, fore, (kd, vt))
     facts = (8, n_groups, GROUP)
-    qd, qt, kt, ct, pt, o_local, sl, known_of = call(
+    qd, qt, ct, pt, o_local, sl, known_of = call(
         local_kernel,
         "local_mix",
         [
             (full, BF16),
-            (turned, BF16),
             (turned, BF16),
             (turned, BF16),
             ((heads, tokens, GROUP), BF16),
@@ -612,7 +631,7 @@
         n_in=5,
         in_smem=(0,),
         flops=6 * mm,
-    )(doc_lengths, kd_b, vt_b, q2_b, c2_b)
+    )(doc_lengths, kd, vt, q2, c2)
     total, o_local = lax.optimization_barrier((total, o_local))
     own, other = finish(mine, got, total, fore)
     half_turned = (half * head_width, tokens)
@@ -630,9 +649,18 @@
 
     o_own, sb_own, stats = part(True, own, (), "mix_own")
     o_other, sb_other, stats = part(False, other, (stats,), "mix_other")
+    stats, kd_late, raw_v = lax.optimization_barrier((stats, kd, raw_v))
+    kt, vd = call(
+        later_forms_kernel,
+        "later_forms",
+        [(turned, BF16), (full, BF16)],
+        [tmp],
+        n_in=2,
+    )(kd_late, raw_v)
     stats = stats + sum(
         lax.ppermute(stats, "head", links_of(k, n_head)) for k in range(1, n_head)
     )
+    stats, kt, vd = lax.optimization_barrier((stats, kt, vd))
     dob_other, factors, send = call(
         functools.partial(norm_kernel, float(width * n_head)),
         "norm_other",

time: 41.4 us -> 41 us (level)
  waiting for transfers between devices: 7.18 us -> 5.9 us
  Pallas kernels: 18.6 us -> 19.3 us
    ppermute x3, waiting for transfers between devices: 3.29 us -> 2.41 us  [per_device(): lax.ppermute(stats, 'head', links_of(k, n_head))]
    pallas_call x1 -> x3, Pallas kernels: 3.33 us -> 4.13 us  [the longest x1 2.76 us: per_device(): call(functools.partial(state_kernel, n_seq), 'shard_state', [(flat, BF16)...]
    ppermute x4, waiting for transfers between devices: 1.97 us -> 1.46 us  [swap(): return lax.ppermute(x, 'seq', swap_pairs)]
  transfers between devices with their start and end apart: 13 -> 13, of which waited for: 8 -> 8; matrix products, arithmetic and copies ran while one was open for 0% -> 0% of each run, Pallas kernels for 28% -> 31%
where the time goes in v8:
time: 41 us; the launch traced here: 40.8 us
  Pallas kernels  19.3 us (47%)
  starting transfers between devices  14.4 us (35%)
  waiting for transfers between devices  5.9 us (14%)
  between operations  0.97 us (2%)
    ppermute x6, starting transfers between devices, exchange(): total = total + weights[5 + k] * lax.ppermute(chip_state, 'seq', links)  10.1 us
    pallas_call x2, Pallas kernels, grads(): call(functools.partial(grad_kernel, groups), name, [*left, *kept, (flat,...  6.26 us
    pallas_call x1, Pallas kernels, per_device(): call(local_kernel, 'local_mix', [(full, BF16), (turned, BF16), (turned, B...  3.63 us
    ppermute x3, starting transfers between devices, per_device(): lax.ppermute(stats, 'head', links_of(k, n_head))  3.55 us
    pallas_call x1, Pallas kernels, per_device(): call(final_kernel, 'final_grads', [(flat, BF16), (flat, BF16)], [state, t...  2.76 us
    pallas_call x1, Pallas kernels, per_device(): call(functools.partial(state_kernel, n_seq), 'shard_state', [(flat, BF16)...  2.76 us
    ppermute x3, waiting for transfers between devices, per_device(): lax.ppermute(stats, 'head', links_of(k, n_head))  2.41 us
    ppermute x6, waiting for transfers between devices, exchange(): total = total + weights[5 + k] * lax.ppermute(chip_state, 'seq', links)  2.03 us
  transfers between devices with their start and end apart: 13, of which 8 were waited for; matrix products, arithmetic and copies ran while one was open for 0% of the time, Pallas kernels for 31%

profile of v8, /device:TPU:0, one launch (start us, length us, event | category | flops | bytes accessed | tf_op | source)
XLA Modules:
  0.0 40.8 jit_solution(15266466665533576164)
XLA Ops:
  0.6 2.8 %shard_state.1 = (bf16[6144,128]{1,0:T(8,128)(2,1)S(1)}, bf16[6144,128]{1,0:T(8,128)(2,1)S(1)}, bf16[256,3072]{1,0:T(8,128)(2,1)S(1)}, f32[1,128,128]{2,1,0:T(8,...) custom-call(s32[6]{0:T(128)} %doc_ref.1, bf16[6144,128]{1,0:T(8,128)(2,1)} %bitcast.48, ...), custom_call_target="tpu_custom_call" | custom-call | flops 201326592 | bytes 8388608 | tf_op jit(solution)/shard_map/shard_state/pallas_call | solution.py:593
  3.4 0.5 %collective-permute-start = (f32[1,128,128]{2,1,0:T(8,128)S(1)}, f32[1,128,128]{2,1,0:T(8,128)S(1)}, u32[]{:S(2)}, u32[]{:S(2)}) collective-permute-start(f32[1,128,128]{2,1,0:T(8,128)S(1)} %get-tuple-element.64), channel_id=1, source_target_pairs={{0,4},{4,0},{8,12},{12,8},{16,20},{20,16},{24,28},{28,24},{1,5},{5... | collective-permute-start | bytes 196616 | tf_op jit(solution)/shard_map/ppermute | solution.py:573
  3.9 0.5 %split_keys.1.kd_ref.k_ref = bf16[3072,256]{1,0:T(8,128)(2,1)S(1)} custom-call(bf16[6144,128]{1,0:T(8,128)(2,1)S(1)} %get-tuple-element.65.pairs_ref), custom_call_target="tpu_custom_call" | custom-call | bytes 8388608 | tf_op jit(solution)/shard_map/split_keys/pallas_call | solution.py:609
  4.8 5.0 %collective-permute-start.3 = (f32[1,128,128]{2,1,0:T(8,128)S(1)}, f32[1,128,128]{2,1,0:T(8,128)S(1)}, u32[]{:S(2)}, u32[]{:S(2)}) collective-permute-start(f32[1,128,128]{2,1,0:T(8,128)S(1)} %multiply_add_fusion.7), channel_id=1, source_target_pairs={{24,0},{28,4},{16,8},{20,12},{8,16},{12,20},{0,24},{4,28},{25,1},{... | collective-permute-start | bytes 196616 | tf_op jit(solution)/shard_map/ppermute | solution.py:581
  9.9 0.6 %collective-permute-start.1 = (f32[1,128,128]{2,1,0:T(8,128)S(1)}, f32[1,128,128]{2,1,0:T(8,128)S(1)}, u32[]{:S(2)}, u32[]{:S(2)}) collective-permute-start(f32[1,128,128]{2,1,0:T(8,128)S(1)} %multiply_add_fusion.7), channel_id=1, source_target_pairs={{8,0},{12,4},{0,8},{4,12},{24,16},{28,20},{16,24},{20,28},{9,1},{1... | collective-permute-start | bytes 196616 | tf_op jit(solution)/shard_map/ppermute | solution.py:581
  10.5 3.6 %local_mix.1 = (bf16[3072,256]{1,0:T(8,128)(2,1)S(1)}, bf16[256,3072]{1,0:T(8,128)(2,1)S(1)}, bf16[256,3072]{1,0:T(8,128)(2,1)S(1)}, bf16[2,3072,256]{2,1,0:T(8,...) custom-call(s32[6]{0:T(128)S(1)} %copy-done.2, ...), custom_call_target="tpu_custom_call" | custom-call | flops 1207959552 | bytes 8388608 | tf_op jit(solution)/shard_map/local_mix/pallas_call | solution.py:618
  14.1 1.6 %collective-permute-done.2 = f32[1,128,128]{2,1,0:T(8,128)S(1)} collective-permute-done((f32[1,128,128]{2,1,0:T(8,128)S(1)}, f32[1,128,128]{2,1,0:T(8,128)S(1)}, u32[]{:S(2)}, u32[]{:S(2)}) %collective-permute-start.2) | collective-permute-done | bytes 65568 | tf_op jit(solution)/shard_map/ppermute | solution.py:581
  15.9 0.6 %mix_own.1 = (f32[128,3072]{1,0:T(8,128)S(1)}, bf16[12,1,128,128]{3,2,1,0:T(8,128)(2,1)S(1)}, f32[2,3072]{1,0:T(2,128)S(1)}) custom-call(s32[8,12,256]{2,1,0:T(8,128)S(1)} %get-tuple-element.69.table_ref.refs_0_, bf16[256,3072]{1,0:T(8,128)(2,1)S(1)} %get-tuple-element.71.qt_ref, f32[256,3072]{1,0:T(8,128)S(1)} %get-tuple-element.74.ol_ref, ...), custom_call_target="tpu_custom_call" | custom-call | flops 100663296 | bytes 8388608 | tf_op jit(solution)/shard_map/mix_own/pallas_call | solution.py:641
  16.5 0.6 %collective-permute-done.4.state_ref = f32[1,128,128]{2,1,0:T(8,128)S(1)} collective-permute-done((f32[1,128,128]{2,1,0:T(8,128)S(1)}, f32[1,128,128]{2,1,0:T(8,128)S(1)}, u32[]{:S(2)}, u32[]{:S(2)}) %collective-permute-start.4) | collective-permute-done | bytes 65568 | tf_op jit(solution)/shard_map/ppermute | solution.py:573
  17.1 0.6 %mix_other.1 = (f32[128,3072]{1,0:T(8,128)S(1)}, bf16[12,1,128,128]{3,2,1,0:T(8,128)(2,1)S(1)}, f32[2,3072]{1,0:T(2,128)S(1)}) custom-call(s32[8,12,256]{2,1,0:T(8,128)S(1)} %get-tuple-element.69.table_ref.refs_0_, bf16[256,3072]{1,0:T(8,128)(2,1)S(1)} %get-tuple-element.71.qt_ref, f32[256,3072]{1,0:T(8,128)S(1)} %get-tuple-element.74.ol_ref, ...), custom_call_target="tpu_custom_call" | custom-call | flops 100663296 | bytes 8388608 | tf_op jit(solution)/shard_map/mix_other/pallas_call | solution.py:641
  17.7 2.5 %collective-permute-start.7 = (f32[2,3072]{1,0:T(2,128)S(1)}, f32[2,3072]{1,0:T(2,128)S(1)}, u32[]{:S(2)}, u32[]{:S(2)}) collective-permute-start(f32[2,3072]{1,0:T(2,128)S(1)} %get-tuple-element.81), channel_id=1, source_target_pairs={{3,0},{2,1},{1,2},{0,3},{7,4},{6,5},{5,6},{4,7},{11,8},{10,9},{9,1... | collective-permute-start | bytes 73736 | tf_op jit(solution)/shard_map/ppermute | solution.py:661
  20.2 0.5 %collective-permute-start.6 = (f32[2,3072]{1,0:T(2,128)S(1)}, f32[2,3072]{1,0:T(2,128)S(1)}, u32[]{:S(2)}, u32[]{:S(2)}) collective-permute-start(f32[2,3072]{1,0:T(2,128)S(1)} %get-tuple-element.81), channel_id=1, source_target_pairs={{2,0},{3,1},{0,2},{1,3},{6,4},{7,5},{4,6},{5,7},{10,8},{11,9},{8,1... | collective-permute-start | bytes 73736 | tf_op jit(solution)/shard_map/ppermute | solution.py:661
  20.8 0.5 %collective-permute-start.5 = (f32[2,3072]{1,0:T(2,128)S(1)}, f32[2,3072]{1,0:T(2,128)S(1)}, u32[]{:S(2)}, u32[]{:S(2)}) collective-permute-start(f32[2,3072]{1,0:T(2,128)S(1)} %get-tuple-element.81), channel_id=1, source_target_pairs={{1,0},{0,1},{3,2},{2,3},{5,4},{4,5},{7,6},{6,7},{9,8},{8,9},{11,10... | collective-permute-start | bytes 73736 | tf_op jit(solution)/shard_map/ppermute | solution.py:661
  21.3 0.9 %later_forms.1 = (bf16[256,3072]{1,0:T(8,128)(2,1)S(1)}, bf16[3072,256]{1,0:T(8,128)(2,1)S(1)}) custom-call(bf16[3072,256]{1,0:T(8,128)(2,1)S(1)} %split_keys.1.kd_ref.k_ref, bf16[6144,128]{1,0:T(8,128)(2,1)S(1)} %get-tuple-element.83.v2_ref), custom_call_target="tpu_custom_call" | custom-call | bytes 8388608 | tf_op jit(solution)/shard_map/later_forms/pallas_call | solution.py:653
  22.5 1.5 %collective-permute-done.6 = f32[2,3072]{1,0:T(2,128)S(1)} collective-permute-done((f32[2,3072]{1,0:T(2,128)S(1)}, f32[2,3072]{1,0:T(2,128)S(1)}, u32[]{:S(2)}, u32[]{:S(2)}) %collective-permute-start.6) | collective-permute-done | bytes 24608 | tf_op jit(solution)/shard_map/ppermute | solution.py:661
  24.1 0.5 %collective-permute-done.5 = f32[2,3072]{1,0:T(2,128)S(1)} collective-permute-done((f32[2,3072]{1,0:T(2,128)S(1)}, f32[2,3072]{1,0:T(2,128)S(1)}, u32[]{:S(2)}, u32[]{:S(2)}) %collective-permute-start.5) | collective-permute-done | bytes 24608 | tf_op jit(solution)/shard_map/ppermute | solution.py:661
  24.6 0.6 %norm_other.1 = (bf16[128,3072]{1,0:T(8,128)(2,1)S(1)}, f32[8,3072]{1,0:T(8,128)S(1)}, f32[1,128,128]{2,1,0:T(8,128)S(1)}) custom-call(s32[8,12,256]{2,1,0:T(8,128)S(1)} %get-tuple-element.69.table_ref.refs_0_, f32[2,3072]{1,0:T(2,128)S(1)} %add_add_fusion.st_ref, f32[128,3072]{1,0:T(8,128)S(1)} %get-tuple-element.87.o_ref.other_ref, ...), custom_call_target="tpu_custom_call" | custom-call | flops 100663296 | bytes 8388608 | tf_op jit(solution)/shard_map/norm_other/pallas_call | solution.py:664
  25.3 0.7 %norm_own.1 = (bf16[256,3072]{1,0:T(8,128)(2,1)S(1)}, bf16[256,3072]{1,0:T(8,128)(2,1)S(1)}, bf16[12,2,128,128]{3,2,1,0:T(8,128)(2,1)S(1)}, f32[1,128,128]{2,1,0:T(8,128)S(1)}) custom-call(s32[8,12,256]{2,1,0:T(8,128)S(1)} %get-tuple-element.69.table_ref.refs_0_, f32[8,3072]{1,0:T(8,128)S(1)} %get-tuple-element.89.rows_ref, ...), custom_call_target="tpu_custom_call" | custom-call | flops 100663296 | bytes 8388608 | tf_op jit(solution)/shard_map/norm_own/pallas_call | solution.py:672
  26.0 0.5 %collective-permute-done.8 = f32[1,128,128]{2,1,0:T(8,128)S(1)} collective-permute-done((f32[1,128,128]{2,1,0:T(8,128)S(1)}, f32[1,128,128]{2,1,0:T(8,128)S(1)}, u32[]{:S(2)}, u32[]{:S(2)}) %collective-permute-start.8) | collective-permute-done | bytes 65568 | tf_op jit(solution)/shard_map/ppermute | solution.py:573
  26.5 2.5 %collective-permute-start.11 = (f32[1,128,128]{2,1,0:T(8,128)S(1)}, f32[1,128,128]{2,1,0:T(8,128)S(1)}, u32[]{:S(2)}, u32[]{:S(2)}) collective-permute-start(f32[1,128,128]{2,1,0:T(8,128)S(1)} %multiply_add_fusion.3), channel_id=1, source_target_pairs={{24,0},{28,4},{16,8},{20,12},{8,16},{12,20},{0,24},{4,28},{25,1},{... | collective-permute-start | bytes 196616 | tf_op jit(solution)/shard_map/ppermute | solution.py:581
  29.2 1.8 %collective-permute-start.9 = (f32[1,128,128]{2,1,0:T(8,128)S(1)}, f32[1,128,128]{2,1,0:T(8,128)S(1)}, u32[]{:S(2)}, u32[]{:S(2)}) collective-permute-start(f32[1,128,128]{2,1,0:T(8,128)S(1)} %multiply_add_fusion.3), channel_id=1, source_target_pairs={{8,0},{12,4},{0,8},{4,12},{24,16},{28,20},{16,24},{20,28},{9,1},{1... | collective-permute-start | bytes 196616 | tf_op jit(solution)/shard_map/ppermute | solution.py:581
  31.0 4.2 %grads_later.1 = (f32[2,128,128]{2,1,0:T(8,128)S(1)}, f32[2304,256]{1,0:T(8,128)S(1)}, f32[2304,256]{1,0:T(8,128)S(1)}, f32[9,2,128,128]{3,2,1,0:T(8,128)S(1)}, ...) custom-call(s32[8,12,256]{2,1,0:T(8,128)S(1)} %get-tuple-element.69.table_ref.refs_0_, ...), custom_call_target="tpu_custom_call" | custom-call | flops 1811939328 | bytes 8388608 | tf_op jit(solution)/shard_map/grads_later/pallas_call | solution.py:690
  35.8 2.1 %grads_earlier.1 = (f32[768,256]{1,0:T(8,128)S(1)}, f32[768,256]{1,0:T(8,128)S(1)}, f32[3,2,128,128]{3,2,1,0:T(8,128)S(1)}, bf16[6144,128]{1,0:T(8,128)(2,1)}, bf16[6144,128]{1,0:T(8,128)(2,1)}) custom-call(s32[8,12,256]{2,1,0:T(8,128)S(1)} %get-tuple-element.69.table_ref.refs_0_, ...), custom_call_target="tpu_custom_call", output_to_operand_aliasing={{3}: (9, {}), {4}: (10, {})} | custom-call | flops 603979776 | bytes 8388608 | tf_op jit(solution)/shard_map/grads_earlier/pallas_call | solution.py:690
  37.8 2.8 %final_grads.1 = (bf16[6144,128]{1,0:T(8,128)(2,1)}, bf16[6144,128]{1,0:T(8,128)(2,1)}) custom-call(s32[8,12,256]{2,1,0:T(8,128)S(1)} %get-tuple-element.69.table_ref.refs_0_, bf16[3072,256]{1,0:T(8,128)(2,1)S(1)} %split_keys.1.kd_ref.k_ref, bf16[3072,256]{1,0:T(8,128)(2,1)S(1)} %get-tuple-element.102.refs_6_.vd_ref, ...), custom_call_target="tpu_custom_call" | custom-call | flops 402653184 | bytes 8388608 | tf_op jit(solution)/shard_map/final_grads/pallas_call | solution.py:707
  (28 shorter events, 1.6 us)
Async XLA Ops:
  3.4 1.4 %collective-permute-start = (f32[1,128,128]{2,1,0:T(8,128)S(1)}, f32[1,128,128]{2,1,0:T(8,128)S(1)}, u32[]{:S(2)}, u32[]{:S(2)}) collective-permute-start(f32[1,128,128]{2,1,0:T(8,128)S(1)} %get-tuple-element.64), channel_id=1, source_target_pairs={{0,4},{4,0},{8,12},{12,8},{16,20},{20,16},{24,28},{28,24},{1,5},{5... | collective-permute-start | bytes 196616 | tf_op jit(solution)/shard_map/ppermute | solution.py:573
  3.9 6.6 %copy-start = (bf16[3072,2,128]{2,1,0:T(2,128)(2,1)S(1)}, bf16[3072,2,128]{2,1,0:T(2,128)(2,1)}, u32[]{:S(2)}) copy-start(bf16[3072,2,128]{2,1,0:T(2,128)(2,1)} %param.5) | copy-start | bytes 4718596
  3.9 6.6 %copy-start.1 = (bf16[3072,2,128]{2,1,0:T(2,128)(2,1)S(1)}, bf16[3072,2,128]{2,1,0:T(2,128)(2,1)}, u32[]{:S(2)}) copy-start(bf16[3072,2,128]{2,1,0:T(2,128)(2,1)} %param.8) | copy-start | bytes 4718596
  3.9 6.6 %copy-start.2 = (s32[6]{0:T(128)S(1)}, s32[6]{0:T(128)}, u32[]{:S(2)}) copy-start(s32[6]{0:T(128)} %doc_ref.1) | copy-start | bytes 76
  4.8 9.3 %collective-permute-start.3 = (f32[1,128,128]{2,1,0:T(8,128)S(1)}, f32[1,128,128]{2,1,0:T(8,128)S(1)}, u32[]{:S(2)}, u32[]{:S(2)}) collective-permute-start(f32[1,128,128]{2,1,0:T(8,128)S(1)} %multiply_add_fusion.7), channel_id=1, source_target_pairs={{24,0},{28,4},{16,8},{20,12},{8,16},{12,20},{0,24},{4,28},{25,1},{... | collective-permute-start | bytes 196616 | tf_op jit(solution)/shard_map/ppermute | solution.py:581
  9.8 5.9 %collective-permute-start.2 = (f32[1,128,128]{2,1,0:T(8,128)S(1)}, f32[1,128,128]{2,1,0:T(8,128)S(1)}, u32[]{:S(2)}, u32[]{:S(2)}) collective-permute-start(f32[1,128,128]{2,1,0:T(8,128)S(1)} %multiply_add_fusion.7), channel_id=1, source_target_pairs={{16,0},{20,4},{24,8},{28,12},{0,16},{4,20},{8,24},{12,28},{17,1},{... | collective-permute-start | bytes 196616 | tf_op jit(solution)/shard_map/ppermute | solution.py:581
  9.9 5.9 %collective-permute-start.1 = (f32[1,128,128]{2,1,0:T(8,128)S(1)}, f32[1,128,128]{2,1,0:T(8,128)S(1)}, u32[]{:S(2)}, u32[]{:S(2)}) collective-permute-start(f32[1,128,128]{2,1,0:T(8,128)S(1)} %multiply_add_fusion.7), channel_id=1, source_target_pairs={{8,0},{12,4},{0,8},{4,12},{24,16},{28,20},{16,24},{20,28},{9,1},{1... | collective-permute-start | bytes 196616 | tf_op jit(solution)/shard_map/ppermute | solution.py:581
  15.8 1.3 %collective-permute-start.4 = (f32[1,128,128]{2,1,0:T(8,128)S(1)}, f32[1,128,128]{2,1,0:T(8,128)S(1)}, u32[]{:S(2)}, u32[]{:S(2)}) collective-permute-start(f32[1,128,128]{2,1,0:T(8,128)S(1)} %get-tuple-element.123), channel_id=1, source_target_pairs={{0,4},{4,0},{8,12},{12,8},{16,20},{20,16},{24,28},{28,24},{1,5},{5... | collective-permute-start | bytes 196616 | tf_op jit(solution)/shard_map/ppermute | solution.py:573
  17.7 4.8 %collective-permute-start.7 = (f32[2,3072]{1,0:T(2,128)S(1)}, f32[2,3072]{1,0:T(2,128)S(1)}, u32[]{:S(2)}, u32[]{:S(2)}) collective-permute-start(f32[2,3072]{1,0:T(2,128)S(1)} %get-tuple-element.81), channel_id=1, source_target_pairs={{3,0},{2,1},{1,2},{0,3},{7,4},{6,5},{5,6},{4,7},{11,8},{10,9},{9,1... | collective-permute-start | bytes 73736 | tf_op jit(solution)/shard_map/ppermute | solution.py:661
  20.2 3.8 %collective-permute-start.6 = (f32[2,3072]{1,0:T(2,128)S(1)}, f32[2,3072]{1,0:T(2,128)S(1)}, u32[]{:S(2)}, u32[]{:S(2)}) collective-permute-start(f32[2,3072]{1,0:T(2,128)S(1)} %get-tuple-element.81), channel_id=1, source_target_pairs={{2,0},{3,1},{0,2},{1,3},{6,4},{7,5},{4,6},{5,7},{10,8},{11,9},{8,1... | collective-permute-start | bytes 73736 | tf_op jit(solution)/shard_map/ppermute | solution.py:661
  20.8 3.8 %collective-permute-start.5 = (f32[2,3072]{1,0:T(2,128)S(1)}, f32[2,3072]{1,0:T(2,128)S(1)}, u32[]{:S(2)}, u32[]{:S(2)}) collective-permute-start(f32[2,3072]{1,0:T(2,128)S(1)} %get-tuple-element.81), channel_id=1, source_target_pairs={{1,0},{0,1},{3,2},{2,3},{5,4},{4,5},{7,6},{6,7},{9,8},{8,9},{11,10... | collective-permute-start | bytes 73736 | tf_op jit(solution)/shard_map/ppermute | solution.py:661
  25.2 1.3 %collective-permute-start.8 = (f32[1,128,128]{2,1,0:T(8,128)S(1)}, f32[1,128,128]{2,1,0:T(8,128)S(1)}, u32[]{:S(2)}, u32[]{:S(2)}) collective-permute-start(f32[1,128,128]{2,1,0:T(8,128)S(1)} %get-tuple-element.95), channel_id=1, source_target_pairs={{0,4},{4,0},{8,12},{12,8},{16,20},{20,16},{24,28},{28,24},{1,5},{5... | collective-permute-start | bytes 196616 | tf_op jit(solution)/shard_map/ppermute | solution.py:573
  26.5 8.7 %collective-permute-start.11 = (f32[1,128,128]{2,1,0:T(8,128)S(1)}, f32[1,128,128]{2,1,0:T(8,128)S(1)}, u32[]{:S(2)}, u32[]{:S(2)}) collective-permute-start(f32[1,128,128]{2,1,0:T(8,128)S(1)} %multiply_add_fusion.3), channel_id=1, source_target_pairs={{24,0},{28,4},{16,8},{20,12},{8,16},{12,20},{0,24},{4,28},{25,1},{... | collective-permute-start | bytes 196616 | tf_op jit(solution)/shard_map/ppermute | solution.py:581
  29.1 6.6 %collective-permute-start.10 = (f32[1,128,128]{2,1,0:T(8,128)S(1)}, f32[1,128,128]{2,1,0:T(8,128)S(1)}, u32[]{:S(2)}, u32[]{:S(2)}) collective-permute-start(f32[1,128,128]{2,1,0:T(8,128)S(1)} %multiply_add_fusion.3), channel_id=1, source_target_pairs={{16,0},{20,4},{24,8},{28,12},{0,16},{4,20},{8,24},{12,28},{17,1},{... | collective-permute-start | bytes 196616 | tf_op jit(solution)/shard_map/ppermute | solution.py:581
  29.2 6.5 %collective-permute-start.9 = (f32[1,128,128]{2,1,0:T(8,128)S(1)}, f32[1,128,128]{2,1,0:T(8,128)S(1)}, u32[]{:S(2)}, u32[]{:S(2)}) collective-permute-start(f32[1,128,128]{2,1,0:T(8,128)S(1)} %multiply_add_fusion.3), channel_id=1, source_target_pairs={{8,0},{12,4},{0,8},{4,12},{24,16},{28,20},{16,24},{20,28},{9,1},{1... | collective-permute-start | bytes 196616 | tf_op jit(solution)/shard_map/ppermute | solution.py:581
  35.7 2.1 %collective-permute-start.12 = (f32[1,128,128]{2,1,0:T(8,128)S(1)}, f32[1,128,128]{2,1,0:T(8,128)S(1)}, u32[]{:S(2)}, u32[]{:S(2)}) collective-permute-start(f32[1,128,128]{2,1,0:T(8,128)S(1)} %get-tuple-element.120), channel_id=1, source_target_pairs={{0,4},{4,0},{8,12},{12,8},{16,20},{20,16},{24,28},{28,24},{1,5},{5... | collective-permute-start | bytes 196616 | tf_op jit(solution)/shard_map/ppermute | solution.py:573

commit v9 on v8

--- a/solution.py
+++ b/solution.py
@@ -233,10 +233,15 @@
             out_ref[group_rows(g), at(h)] = parts[h].astype(BF16)
 
 
-def later_forms_kernel(k_ref, v2_ref, kt_ref, vd_ref, tmp):
+def later_forms_kernel(k_ref, v2_ref, own_ref, other_ref, kt_ref, vd_ref, st_ref, tmp):
     split_kernel(v2_ref, vd_ref, tmp)
     width, tokens = kt_ref.shape
+    half = own_ref.shape[1]
+    core = lax.axis_index("seq") % 2
     for g in range(tokens // GROUP):
+        for h in range(half):
+            st_ref[g, part_of(core, True, half) + h] = own_ref[g, h].T
+            st_ref[g, part_of(core, False, half) + h] = other_ref[g, h].T
         rows = group_rows(g)
         for h in range(width // 128):
             kt_ref[at(h), rows] = k_ref[rows, at(h)].T
@@ -385,8 +390,8 @@
 
 
 def merge_kernel(
-    table_ref, rows_ref, own_ref, other_ref, ct_ref, qd_ref, dob_other_ref, sb_own_ref, sb_other_ref,
-    dobt_ref, normed_ref, sb_ref, mine_ref,
+    table_ref, rows_ref, own_ref, other_ref, ct_ref, qd_ref, dob_other_ref,
+    dobt_ref, normed_ref, mine_ref,
 ):
     tokens, width = qd_ref.shape
     half = mine_ref.shape[0]
@@ -407,8 +412,6 @@
             dobt_ref[others, rows] = dob_other_ref[at(h), rows]
             normed_ref[mine, rows] = (o * inv).astype(BF16)
             normed_ref[others, rows] = (other_ref[at(h), rows] * inv).astype(BF16)
-            sb_ref[g, base + h] = sb_own_ref[g, h]
-            sb_ref[g, far + h] = sb_other_ref[g, h]
             ready.append(jnp.where(keep, dob, 0.0).astype(BF16))
         return ready
 
@@ -458,7 +461,7 @@
         near, grown = [], []
         for h in range(heads):
             dobt = dobt_ref[at(h), rows]
-            near.append(jnp.where(opened, dot(turn(sb_ref[g, h]), dobt), 0.0))
+            near.append(jnp.where(opened, dot(sb_ref[g, h], dobt), 0.0))
             grown.append(dot(keep_where(head_part, dobt), qd_ref[rows, at(h)]))
         for h in range(heads):
             mine = pl.ds(h, GROUP, stride=heads)
@@ -650,17 +653,17 @@
     o_own, sb_own, stats = part(True, own, (), "mix_own")
     o_other, sb_other, stats = part(False, other, (stats,), "mix_other")
     stats, kd_late, raw_v = lax.optimization_barrier((stats, kd, raw_v))
-    kt, vd = call(
+    kt, vd, sb = call(
         later_forms_kernel,
         "later_forms",
-        [(turned, BF16), (full, BF16)],
+        [(turned, BF16), (full, BF16), (group_states, BF16)],
         [tmp],
-        n_in=2,
-    )(kd_late, raw_v)
+        n_in=4,
+    )(kd_late, raw_v, sb_own, sb_other)
     stats = stats + sum(
         lax.ppermute(stats, "head", links_of(k, n_head)) for k in range(1, n_head)
     )
-    stats, kt, vd = lax.optimization_barrier((stats, kt, vd))
+    stats, kt, vd, sb = lax.optimization_barrier((stats, kt, vd, sb))
     dob_other, factors, send = call(
         functools.partial(norm_kernel, float(width * n_head)),
         "norm_other",
@@ -669,16 +672,16 @@
         n_in=5,
         flops=mm // 2,
     )(known_of, stats, o_other, ct, qd)
-    dobt, normed, sb, mine = call(
+    dobt, normed, mine = call(
         merge_kernel,
         "norm_own",
-        [(turned, BF16), (turned, BF16), (group_states, BF16), (piece, F32)],
+        [(turned, BF16), (turned, BF16), (piece, F32)],
         [],
-        n_in=9,
+        n_in=7,
         flops=mm // 2,
-    )(known_of, factors, o_own, o_other, ct, qd, dob_other, sb_own, sb_other)
+    )(known_of, factors, o_own, o_other, ct, qd, dob_other)
     got, total, (dobt_b, normed_b) = exchange(mine, send, back, (dobt, normed))
-    cut = max(1, n_groups // 4)
+    cut = max(1, n_groups // 12)
     earlier, later = range(0, cut), range(cut, n_groups)
 
     def grads(groups, name, before):

time: 41 us -> 40.6 us (level)
  transfers between devices with their start and end apart: 13 -> 13, of which waited for: 8 -> 7; matrix products, arithmetic and copies ran while one was open for 0% -> 0% of each run, Pallas kernels for 31% -> 32%
where the time goes in v9:
time: 40.6 us; the launch traced here: 40.4 us
  Pallas kernels  19.3 us (48%)
  starting transfers between devices  14.4 us (35%)
  waiting for transfers between devices  5.52 us (14%)
  between operations  0.98 us (2%)
    ppermute x6, starting transfers between devices, exchange(): total = total + weights[5 + k] * lax.ppermute(chip_state, 'seq', links)  10.1 us
    pallas_call x2, Pallas kernels, grads(): call(functools.partial(grad_kernel, groups), name, [*left, *kept, (flat,...  6.4 us
    ppermute x3, starting transfers between devices, per_device(): lax.ppermute(stats, 'head', links_of(k, n_head))  3.55 us
    pallas_call x1, Pallas kernels, per_device(): call(local_kernel, 'local_mix', [(full, BF16), (turned, BF16), (turned, B...  3.47 us
    pallas_call x1, Pallas kernels, per_device(): call(functools.partial(state_kernel, n_seq), 'shard_state', [(flat, BF16)...  2.76 us
    pallas_call x1, Pallas kernels, per_device(): call(final_kernel, 'final_grads', [(flat, BF16), (flat, BF16)], [state, t...  2.62 us
    ppermute x3, waiting for transfers between devices, per_device(): lax.ppermute(stats, 'head', links_of(k, n_head))  2.22 us
    ppermute x6, waiting for transfers between devices, exchange(): total = total + weights[5 + k] * lax.ppermute(chip_state, 'seq', links)  1.78 us
  transfers between devices with their start and end apart: 13, of which 7 were waited for; matrix products, arithmetic and copies ran while one was open for 0% of the time, Pallas kernels for 32%

profile of v9, /device:TPU:0, one launch (start us, length us, event | category | flops | bytes accessed | tf_op | source)
XLA Modules:
  0.0 40.4 jit_solution(12064609838625681427)
XLA Ops:
  0.6 2.8 %shard_state.1 = (bf16[6144,128]{1,0:T(8,128)(2,1)S(1)}, bf16[6144,128]{1,0:T(8,128)(2,1)S(1)}, bf16[256,3072]{1,0:T(8,128)(2,1)S(1)}, f32[1,128,128]{2,1,0:T(8,...) custom-call(s32[6]{0:T(128)} %doc_ref.1, bf16[6144,128]{1,0:T(8,128)(2,1)} %bitcast.48, ...), custom_call_target="tpu_custom_call" | custom-call | flops 201326592 | bytes 8388608 | tf_op jit(solution)/shard_map/shard_state/pallas_call | solution.py:596
  3.4 0.5 %collective-permute-start = (f32[1,128,128]{2,1,0:T(8,128)S(1)}, f32[1,128,128]{2,1,0:T(8,128)S(1)}, u32[]{:S(2)}, u32[]{:S(2)}) collective-permute-start(f32[1,128,128]{2,1,0:T(8,128)S(1)} %get-tuple-element.65), channel_id=1, source_target_pairs={{0,4},{4,0},{8,12},{12,8},{16,20},{20,16},{24,28},{28,24},{1,5},{5... | collective-permute-start | bytes 196616 | tf_op jit(solution)/shard_map/ppermute | solution.py:576
  3.9 0.5 %split_keys.1.kd_ref.k_ref = bf16[3072,256]{1,0:T(8,128)(2,1)S(1)} custom-call(bf16[6144,128]{1,0:T(8,128)(2,1)S(1)} %get-tuple-element.66.pairs_ref), custom_call_target="tpu_custom_call" | custom-call | bytes 8388608 | tf_op jit(solution)/shard_map/split_keys/pallas_call | solution.py:612
  4.8 5.0 %collective-permute-start.3 = (f32[1,128,128]{2,1,0:T(8,128)S(1)}, f32[1,128,128]{2,1,0:T(8,128)S(1)}, u32[]{:S(2)}, u32[]{:S(2)}) collective-permute-start(f32[1,128,128]{2,1,0:T(8,128)S(1)} %multiply_add_fusion.7), channel_id=1, source_target_pairs={{24,0},{28,4},{16,8},{20,12},{8,16},{12,20},{0,24},{4,28},{25,1},{... | collective-permute-start | bytes 196616 | tf_op jit(solution)/shard_map/ppermute | solution.py:584
  9.8 0.6 %collective-permute-start.1 = (f32[1,128,128]{2,1,0:T(8,128)S(1)}, f32[1,128,128]{2,1,0:T(8,128)S(1)}, u32[]{:S(2)}, u32[]{:S(2)}) collective-permute-start(f32[1,128,128]{2,1,0:T(8,128)S(1)} %multiply_add_fusion.7), channel_id=1, source_target_pairs={{8,0},{12,4},{0,8},{4,12},{24,16},{28,20},{16,24},{20,28},{9,1},{1... | collective-permute-start | bytes 196616 | tf_op jit(solution)/shard_map/ppermute | solution.py:584
  10.5 3.5 %local_mix.1 = (bf16[3072,256]{1,0:T(8,128)(2,1)S(1)}, bf16[256,3072]{1,0:T(8,128)(2,1)S(1)}, bf16[256,3072]{1,0:T(8,128)(2,1)S(1)}, bf16[2,3072,256]{2,1,0:T(8,...) custom-call(s32[6]{0:T(128)S(1)} %copy-done.2, ...), custom_call_target="tpu_custom_call" | custom-call | flops 1207959552 | bytes 8388608 | tf_op jit(solution)/shard_map/local_mix/pallas_call | solution.py:621
  14.0 1.8 %collective-permute-done.2 = f32[1,128,128]{2,1,0:T(8,128)S(1)} collective-permute-done((f32[1,128,128]{2,1,0:T(8,128)S(1)}, f32[1,128,128]{2,1,0:T(8,128)S(1)}, u32[]{:S(2)}, u32[]{:S(2)}) %collective-permute-start.2) | collective-permute-done | bytes 65568 | tf_op jit(solution)/shard_map/ppermute | solution.py:584
  15.9 0.6 %mix_own.1 = (f32[128,3072]{1,0:T(8,128)S(1)}, bf16[12,1,128,128]{3,2,1,0:T(8,128)(2,1)S(1)}, f32[2,3072]{1,0:T(2,128)S(1)}) custom-call(s32[8,12,256]{2,1,0:T(8,128)S(1)} %get-tuple-element.70.table_ref.refs_0_, bf16[256,3072]{1,0:T(8,128)(2,1)S(1)} %get-tuple-element.72.qt_ref, f32[256,3072]{1,0:T(8,128)S(1)} %get-tuple-element.75.ol_ref, ...), custom_call_target="tpu_custom_call" | custom-call | flops 100663296 | bytes 8388608 | tf_op jit(solution)/shard_map/mix_own/pallas_call | solution.py:644
  16.5 0.6 %collective-permute-done.4.state_ref = f32[1,128,128]{2,1,0:T(8,128)S(1)} collective-permute-done((f32[1,128,128]{2,1,0:T(8,128)S(1)}, f32[1,128,128]{2,1,0:T(8,128)S(1)}, u32[]{:S(2)}, u32[]{:S(2)}) %collective-permute-start.4) | collective-permute-done | bytes 65568 | tf_op jit(solution)/shard_map/ppermute | solution.py:576
  17.1 0.6 %mix_other.1 = (f32[128,3072]{1,0:T(8,128)S(1)}, bf16[12,1,128,128]{3,2,1,0:T(8,128)(2,1)S(1)}, f32[2,3072]{1,0:T(2,128)S(1)}) custom-call(s32[8,12,256]{2,1,0:T(8,128)S(1)} %get-tuple-element.70.table_ref.refs_0_, bf16[256,3072]{1,0:T(8,128)(2,1)S(1)} %get-tuple-element.72.qt_ref, f32[256,3072]{1,0:T(8,128)S(1)} %get-tuple-element.75.ol_ref, ...), custom_call_target="tpu_custom_call" | custom-call | flops 100663296 | bytes 8388608 | tf_op jit(solution)/shard_map/mix_other/pallas_call | solution.py:644
  17.7 2.5 %collective-permute-start.7 = (f32[2,3072]{1,0:T(2,128)S(1)}, f32[2,3072]{1,0:T(2,128)S(1)}, u32[]{:S(2)}, u32[]{:S(2)}) collective-permute-start(f32[2,3072]{1,0:T(2,128)S(1)} %get-tuple-element.82), channel_id=1, source_target_pairs={{3,0},{2,1},{1,2},{0,3},{7,4},{6,5},{5,6},{4,7},{11,8},{10,9},{9,1... | collective-permute-start | bytes 73736 | tf_op jit(solution)/shard_map/ppermute | solution.py:664
  20.3 0.5 %collective-permute-start.6 = (f32[2,3072]{1,0:T(2,128)S(1)}, f32[2,3072]{1,0:T(2,128)S(1)}, u32[]{:S(2)}, u32[]{:S(2)}) collective-permute-start(f32[2,3072]{1,0:T(2,128)S(1)} %get-tuple-element.82), channel_id=1, source_target_pairs={{2,0},{3,1},{0,2},{1,3},{6,4},{7,5},{4,6},{5,7},{10,8},{11,9},{8,1... | collective-permute-start | bytes 73736 | tf_op jit(solution)/shard_map/ppermute | solution.py:664
  20.8 0.5 %collective-permute-start.5 = (f32[2,3072]{1,0:T(2,128)S(1)}, f32[2,3072]{1,0:T(2,128)S(1)}, u32[]{:S(2)}, u32[]{:S(2)}) collective-permute-start(f32[2,3072]{1,0:T(2,128)S(1)} %get-tuple-element.82), channel_id=1, source_target_pairs={{1,0},{0,1},{3,2},{2,3},{5,4},{4,5},{7,6},{6,7},{9,8},{8,9},{11,10... | collective-permute-start | bytes 73736 | tf_op jit(solution)/shard_map/ppermute | solution.py:664
  21.3 1.1 %later_forms.1 = (bf16[256,3072]{1,0:T(8,128)(2,1)S(1)}, bf16[3072,256]{1,0:T(8,128)(2,1)S(1)}, bf16[12,2,128,128]{3,2,1,0:T(8,128)(2,1)S(1)}) custom-call(bf16[3072,256]{1,0:T(8,128)(2,1)S(1)} %split_keys.1.kd_ref.k_ref, bf16[6144,128]{1,0:T(8,128)(2,1)S(1)} %get-tuple-element.84.v2_ref, bf16[12,1,128,128]{3,2,1,0:T(8,128)(2,1)S(1)} %get-tuple-element.85.own_ref, ...), custom_call_target="tpu_custom_call" | custom-call | bytes 8388608 | tf_op jit(solution)/shard_map/later_forms/pallas_call | solution.py:656
  22.5 1.5 %collective-permute-done.6 = f32[2,3072]{1,0:T(2,128)S(1)} collective-permute-done((f32[2,3072]{1,0:T(2,128)S(1)}, f32[2,3072]{1,0:T(2,128)S(1)}, u32[]{:S(2)}, u32[]{:S(2)}) %collective-permute-start.6) | collective-permute-done | bytes 24608 | tf_op jit(solution)/shard_map/ppermute | solution.py:664
  24.1 0.5 %collective-permute-done.5 = f32[2,3072]{1,0:T(2,128)S(1)} collective-permute-done((f32[2,3072]{1,0:T(2,128)S(1)}, f32[2,3072]{1,0:T(2,128)S(1)}, u32[]{:S(2)}, u32[]{:S(2)}) %collective-permute-start.5) | collective-permute-done | bytes 24608 | tf_op jit(solution)/shard_map/ppermute | solution.py:664
  24.6 0.6 %norm_other.1 = (bf16[128,3072]{1,0:T(8,128)(2,1)S(1)}, f32[8,3072]{1,0:T(8,128)S(1)}, f32[1,128,128]{2,1,0:T(8,128)S(1)}) custom-call(s32[8,12,256]{2,1,0:T(8,128)S(1)} %get-tuple-element.70.table_ref.refs_0_, f32[2,3072]{1,0:T(2,128)S(1)} %add_add_fusion.st_ref, f32[128,3072]{1,0:T(8,128)S(1)} %get-tuple-element.91.o_ref.other_ref, ...), custom_call_target="tpu_custom_call" | custom-call | flops 100663296 | bytes 8388608 | tf_op jit(solution)/shard_map/norm_other/pallas_call | solution.py:667
  25.3 0.7 %norm_own.1 = (bf16[256,3072]{1,0:T(8,128)(2,1)S(1)}, bf16[256,3072]{1,0:T(8,128)(2,1)S(1)}, f32[1,128,128]{2,1,0:T(8,128)S(1)}) custom-call(s32[8,12,256]{2,1,0:T(8,128)S(1)} %get-tuple-element.70.table_ref.refs_0_, f32[8,3072]{1,0:T(8,128)S(1)} %get-tuple-element.93.rows_ref, f32[128,3072]{1,0:T(8,128)S(1)} %get-tuple-element.94.own_ref, ...), custom_call_target="tpu_custom_call" | custom-call | flops 100663296 | bytes 8388608 | tf_op jit(solution)/shard_map/norm_own/pallas_call | solution.py:675
  26.0 0.5 %collective-permute-done.8 = f32[1,128,128]{2,1,0:T(8,128)S(1)} collective-permute-done((f32[1,128,128]{2,1,0:T(8,128)S(1)}, f32[1,128,128]{2,1,0:T(8,128)S(1)}, u32[]{:S(2)}, u32[]{:S(2)}) %collective-permute-start.8) | collective-permute-done | bytes 65568 | tf_op jit(solution)/shard_map/ppermute | solution.py:576
  26.6 2.5 %collective-permute-start.11 = (f32[1,128,128]{2,1,0:T(8,128)S(1)}, f32[1,128,128]{2,1,0:T(8,128)S(1)}, u32[]{:S(2)}, u32[]{:S(2)}) collective-permute-start(f32[1,128,128]{2,1,0:T(8,128)S(1)} %multiply_add_fusion.3), channel_id=1, source_target_pairs={{24,0},{28,4},{16,8},{20,12},{8,16},{12,20},{0,24},{4,28},{25,1},{... | collective-permute-start | bytes 196616 | tf_op jit(solution)/shard_map/ppermute | solution.py:584
  29.2 1.8 %collective-permute-start.9 = (f32[1,128,128]{2,1,0:T(8,128)S(1)}, f32[1,128,128]{2,1,0:T(8,128)S(1)}, u32[]{:S(2)}, u32[]{:S(2)}) collective-permute-start(f32[1,128,128]{2,1,0:T(8,128)S(1)} %multiply_add_fusion.3), channel_id=1, source_target_pairs={{8,0},{12,4},{0,8},{4,12},{24,16},{28,20},{16,24},{20,28},{9,1},{1... | collective-permute-start | bytes 196616 | tf_op jit(solution)/shard_map/ppermute | solution.py:584
  31.0 5.0 %grads_later.1 = (f32[2,128,128]{2,1,0:T(8,128)S(1)}, f32[2816,256]{1,0:T(8,128)S(1)}, f32[2816,256]{1,0:T(8,128)S(1)}, f32[11,2,128,128]{3,2,1,0:T(8,128)S(1)},...) custom-call(s32[8,12,256]{2,1,0:T(8,128)S(1)} %get-tuple-element.70.table_ref.refs_0_, ...), custom_call_target="tpu_custom_call" | custom-call | flops 2214592512 | bytes 8388608 | tf_op jit(solution)/shard_map/grads_later/pallas_call | solution.py:693
  36.2 1.4 %grads_earlier.1 = (f32[256,256]{1,0:T(8,128)S(1)}, f32[256,256]{1,0:T(8,128)S(1)}, f32[1,2,128,128]{3,2,1,0:T(8,128)S(1)}, bf16[6144,128]{1,0:T(8,128)(2,1)}, bf16[6144,128]{1,0:T(8,128)(2,1)}) custom-call(s32[8,12,256]{2,1,0:T(8,128)S(1)} %get-tuple-element.70.table_ref.refs_0_, ...), custom_call_target="tpu_custom_call", output_to_operand_aliasing={{3}: (9, {}), {4}: (10, {})} | custom-call | flops 201326592 | bytes 8388608 | tf_op jit(solution)/shard_map/grads_earlier/pallas_call | solution.py:693
  37.6 2.6 %final_grads.1 = (bf16[6144,128]{1,0:T(8,128)(2,1)}, bf16[6144,128]{1,0:T(8,128)(2,1)}) custom-call(s32[8,12,256]{2,1,0:T(8,128)S(1)} %get-tuple-element.70.table_ref.refs_0_, bf16[3072,256]{1,0:T(8,128)(2,1)S(1)} %split_keys.1.kd_ref.k_ref, bf16[3072,256]{1,0:T(8,128)(2,1)S(1)} %get-tuple-element.104.refs_6_.vd_ref, ...), custom_call_target="tpu_custom_call" | custom-call | flops 402653184 | bytes 8388608 | tf_op jit(solution)/shard_map/final_grads/pallas_call | solution.py:710
  (28 shorter events, 1.0 us)
Async XLA Ops:
  3.4 1.4 %collective-permute-start = (f32[1,128,128]{2,1,0:T(8,128)S(1)}, f32[1,128,128]{2,1,0:T(8,128)S(1)}, u32[]{:S(2)}, u32[]{:S(2)}) collective-permute-start(f32[1,128,128]{2,1,0:T(8,128)S(1)} %get-tuple-element.65), channel_id=1, source_target_pairs={{0,4},{4,0},{8,12},{12,8},{16,20},{20,16},{24,28},{28,24},{1,5},{5... | collective-permute-start | bytes 196616 | tf_op jit(solution)/shard_map/ppermute | solution.py:576
  3.9 6.6 %copy-start = (bf16[3072,2,128]{2,1,0:T(2,128)(2,1)S(1)}, bf16[3072,2,128]{2,1,0:T(2,128)(2,1)}, u32[]{:S(2)}) copy-start(bf16[3072,2,128]{2,1,0:T(2,128)(2,1)} %param.5) | copy-start | bytes 4718596
  3.9 6.6 %copy-start.1 = (bf16[3072,2,128]{2,1,0:T(2,128)(2,1)S(1)}, bf16[3072,2,128]{2,1,0:T(2,128)(2,1)}, u32[]{:S(2)}) copy-start(bf16[3072,2,128]{2,1,0:T(2,128)(2,1)} %param.8) | copy-start | bytes 4718596
  3.9 6.6 %copy-start.2 = (s32[6]{0:T(128)S(1)}, s32[6]{0:T(128)}, u32[]{:S(2)}) copy-start(s32[6]{0:T(128)} %doc_ref.1) | copy-start | bytes 76
  4.8 9.1 %collective-permute-start.3 = (f32[1,128,128]{2,1,0:T(8,128)S(1)}, f32[1,128,128]{2,1,0:T(8,128)S(1)}, u32[]{:S(2)}, u32[]{:S(2)}) collective-permute-start(f32[1,128,128]{2,1,0:T(8,128)S(1)} %multiply_add_fusion.7), channel_id=1, source_target_pairs={{24,0},{28,4},{16,8},{20,12},{8,16},{12,20},{0,24},{4,28},{25,1},{... | collective-permute-start | bytes 196616 | tf_op jit(solution)/shard_map/ppermute | solution.py:584
  9.8 5.9 %collective-permute-start.2 = (f32[1,128,128]{2,1,0:T(8,128)S(1)}, f32[1,128,128]{2,1,0:T(8,128)S(1)}, u32[]{:S(2)}, u32[]{:S(2)}) collective-permute-start(f32[1,128,128]{2,1,0:T(8,128)S(1)} %multiply_add_fusion.7), channel_id=1, source_target_pairs={{16,0},{20,4},{24,8},{28,12},{0,16},{4,20},{8,24},{12,28},{17,1},{... | collective-permute-start | bytes 196616 | tf_op jit(solution)/shard_map/ppermute | solution.py:584
  9.8 5.9 %collective-permute-start.1 = (f32[1,128,128]{2,1,0:T(8,128)S(1)}, f32[1,128,128]{2,1,0:T(8,128)S(1)}, u32[]{:S(2)}, u32[]{:S(2)}) collective-permute-start(f32[1,128,128]{2,1,0:T(8,128)S(1)} %multiply_add_fusion.7), channel_id=1, source_target_pairs={{8,0},{12,4},{0,8},{4,12},{24,16},{28,20},{16,24},{20,28},{9,1},{1... | collective-permute-start | bytes 196616 | tf_op jit(solution)/shard_map/ppermute | solution.py:584
  15.8 1.3 %collective-permute-start.4 = (f32[1,128,128]{2,1,0:T(8,128)S(1)}, f32[1,128,128]{2,1,0:T(8,128)S(1)}, u32[]{:S(2)}, u32[]{:S(2)}) collective-permute-start(f32[1,128,128]{2,1,0:T(8,128)S(1)} %get-tuple-element.125), channel_id=1, source_target_pairs={{0,4},{4,0},{8,12},{12,8},{16,20},{20,16},{24,28},{28,24},{1,5},{5... | collective-permute-start | bytes 196616 | tf_op jit(solution)/shard_map/ppermute | solution.py:576
  17.7 4.8 %collective-permute-start.7 = (f32[2,3072]{1,0:T(2,128)S(1)}, f32[2,3072]{1,0:T(2,128)S(1)}, u32[]{:S(2)}, u32[]{:S(2)}) collective-permute-start(f32[2,3072]{1,0:T(2,128)S(1)} %get-tuple-element.82), channel_id=1, source_target_pairs={{3,0},{2,1},{1,2},{0,3},{7,4},{6,5},{5,6},{4,7},{11,8},{10,9},{9,1... | collective-permute-start | bytes 73736 | tf_op jit(solution)/shard_map/ppermute | solution.py:664
  20.3 3.8 %collective-permute-start.6 = (f32[2,3072]{1,0:T(2,128)S(1)}, f32[2,3072]{1,0:T(2,128)S(1)}, u32[]{:S(2)}, u32[]{:S(2)}) collective-permute-start(f32[2,3072]{1,0:T(2,128)S(1)} %get-tuple-element.82), channel_id=1, source_target_pairs={{2,0},{3,1},{0,2},{1,3},{6,4},{7,5},{4,6},{5,7},{10,8},{11,9},{8,1... | collective-permute-start | bytes 73736 | tf_op jit(solution)/shard_map/ppermute | solution.py:664
  20.8 3.8 %collective-permute-start.5 = (f32[2,3072]{1,0:T(2,128)S(1)}, f32[2,3072]{1,0:T(2,128)S(1)}, u32[]{:S(2)}, u32[]{:S(2)}) collective-permute-start(f32[2,3072]{1,0:T(2,128)S(1)} %get-tuple-element.82), channel_id=1, source_target_pairs={{1,0},{0,1},{3,2},{2,3},{5,4},{4,5},{7,6},{6,7},{9,8},{8,9},{11,10... | collective-permute-start | bytes 73736 | tf_op jit(solution)/shard_map/ppermute | solution.py:664
  25.2 1.3 %collective-permute-start.8 = (f32[1,128,128]{2,1,0:T(8,128)S(1)}, f32[1,128,128]{2,1,0:T(8,128)S(1)}, u32[]{:S(2)}, u32[]{:S(2)}) collective-permute-start(f32[1,128,128]{2,1,0:T(8,128)S(1)} %get-tuple-element.97), channel_id=1, source_target_pairs={{0,4},{4,0},{8,12},{12,8},{16,20},{20,16},{24,28},{28,24},{1,5},{5... | collective-permute-start | bytes 196616 | tf_op jit(solution)/shard_map/ppermute | solution.py:576
  26.6 9.5 %collective-permute-start.11 = (f32[1,128,128]{2,1,0:T(8,128)S(1)}, f32[1,128,128]{2,1,0:T(8,128)S(1)}, u32[]{:S(2)}, u32[]{:S(2)}) collective-permute-start(f32[1,128,128]{2,1,0:T(8,128)S(1)} %multiply_add_fusion.3), channel_id=1, source_target_pairs={{24,0},{28,4},{16,8},{20,12},{8,16},{12,20},{0,24},{4,28},{25,1},{... | collective-permute-start | bytes 196616 | tf_op jit(solution)/shard_map/ppermute | solution.py:584
  29.1 7.0 %collective-permute-start.10 = (f32[1,128,128]{2,1,0:T(8,128)S(1)}, f32[1,128,128]{2,1,0:T(8,128)S(1)}, u32[]{:S(2)}, u32[]{:S(2)}) collective-permute-start(f32[1,128,128]{2,1,0:T(8,128)S(1)} %multiply_add_fusion.3), channel_id=1, source_target_pairs={{16,0},{20,4},{24,8},{28,12},{0,16},{4,20},{8,24},{12,28},{17,1},{... | collective-permute-start | bytes 196616 | tf_op jit(solution)/shard_map/ppermute | solution.py:584
  29.2 6.9 %collective-permute-start.9 = (f32[1,128,128]{2,1,0:T(8,128)S(1)}, f32[1,128,128]{2,1,0:T(8,128)S(1)}, u32[]{:S(2)}, u32[]{:S(2)}) collective-permute-start(f32[1,128,128]{2,1,0:T(8,128)S(1)} %multiply_add_fusion.3), channel_id=1, source_target_pairs={{8,0},{12,4},{0,8},{4,12},{24,16},{28,20},{16,24},{20,28},{9,1},{1... | collective-permute-start | bytes 196616 | tf_op jit(solution)/shard_map/ppermute | solution.py:584
  36.1 1.5 %collective-permute-start.12 = (f32[1,128,128]{2,1,0:T(8,128)S(1)}, f32[1,128,128]{2,1,0:T(8,128)S(1)}, u32[]{:S(2)}, u32[]{:S(2)}) collective-permute-start(f32[1,128,128]{2,1,0:T(8,128)S(1)} %get-tuple-element.122), channel_id=1, source_target_pairs={{0,4},{4,0},{8,12},{12,8},{16,20},{20,16},{24,28},{28,24},{1,5},{5... | collective-permute-start | bytes 196616 | tf_op jit(solution)/shard_map/ppermute | solution.py:576

commit v10 on v9

--- a/solution.py
+++ b/solution.py
@@ -233,7 +233,9 @@
             out_ref[group_rows(g), at(h)] = parts[h].astype(BF16)
 
 
-def later_forms_kernel(k_ref, v2_ref, own_ref, other_ref, kt_ref, vd_ref, st_ref, tmp):
+def later_forms_kernel(
+    table_ref, k_ref, v2_ref, own_ref, other_ref, q_ref, kt_ref, vd_ref, st_ref, q_back_ref, tmp
+):
     split_kernel(v2_ref, vd_ref, tmp)
     width, tokens = kt_ref.shape
     half = own_ref.shape[1]
@@ -245,6 +247,8 @@
         rows = group_rows(g)
         for h in range(width // 128):
             kt_ref[at(h), rows] = k_ref[rows, at(h)].T
+            keep = rows_iota(128) < known(table_ref, SHARD_HEAD, g, 128)
+            q_back_ref[rows, at(h)] = keep_where(keep, q_ref[rows, at(h)])
 
 
 def local_kernel(
@@ -261,11 +265,12 @@
         rows = group_rows(g)
         qs = split_heads(q2_ref, tmpq, g, heads)
         cs = split_heads(c2_ref, tmpc, g, heads)
+        opened = lanes_iota(128) < known(table_ref, OPENED, g)
         qts = []
         for h in range(heads):
             qt = turn(qs[h])
             qd_ref[rows, at(h)] = qs[h].astype(BF16)
-            qt_ref[at(h), rows] = qt
+            qt_ref[at(h), rows] = keep_where(opened, qt)
             ct_ref[at(h), rows] = turn(cs[h])
             qts.append(qt)
         return qts
@@ -325,13 +330,12 @@
 
     def opened_terms(g):
         rows = group_rows(g)
-        opened = lanes_iota(128) < known(table_ref, OPENED, g)
         same = factor(table_ref, SAME_OPENED, g)
         terms = []
         for h in range(half):
             sb = (sl_ref[g, base + h] + same * state_ref[h]).astype(BF16)
             sb_ref[g, h] = sb
-            terms.append(jnp.where(opened, dot(sb, qt_ref[head_rows(base + h), rows]), 0.0))
+            terms.append(dot(sb, qt_ref[head_rows(base + h), rows]))
         return terms
 
     ahead = opened_terms(0)
@@ -366,7 +370,7 @@
 
 
 def norm_kernel(
-    width_all, table_ref, st_ref, o_ref, ct_ref, qd_ref, dobt_ref, rows_ref, send_ref
+    width_all, st_ref, o_ref, ct_ref, qd_ref, dobt_ref, rows_ref, send_ref
 ):
     tokens, width = qd_ref.shape
     half = send_ref.shape[0]
@@ -374,7 +378,6 @@
 
     def prepare(g):
         rows = group_rows(g)
-        keep = lanes_iota(128) < known(table_ref, SHARD_HEAD, g)
         total = st_ref[:, rows] * (1.0 / width_all)
         inv = lax.rsqrt(total[0:1] + EPSILON)
         slope = total[1:2] * inv * inv * inv
@@ -382,15 +385,16 @@
         ready = []
         for h in range(half):
             dob = inv * ct_ref[head_rows(base + h), rows].astype(F32) - slope * o_ref[at(h), rows]
-            dobt_ref[at(h), rows] = dob.astype(BF16)
-            ready.append(jnp.where(keep, dob, 0.0).astype(BF16))
+            dob = dob.astype(BF16)
+            dobt_ref[at(h), rows] = dob
+            ready.append(dob)
         return ready
 
     back_state(half, tokens // GROUP, prepare, qd_ref, base, send_ref)
 
 
 def merge_kernel(
-    table_ref, rows_ref, own_ref, other_ref, ct_ref, qd_ref, dob_other_ref,
+    rows_ref, own_ref, other_ref, ct_ref, qd_ref, dob_other_ref,
     dobt_ref, normed_ref, mine_ref,
 ):
     tokens, width = qd_ref.shape
@@ -400,7 +404,6 @@
 
     def prepare(g):
         rows = group_rows(g)
-        keep = lanes_iota(128) < known(table_ref, SHARD_HEAD, g)
         inv = rows_ref[0:1, rows]
         slope = rows_ref[1:2, rows]
         ready = []
@@ -408,11 +411,12 @@
             mine, others = head_rows(base + h), head_rows(far + h)
             o = own_ref[at(h), rows]
             dob = inv * ct_ref[mine, rows].astype(F32) - slope * o
-            dobt_ref[mine, rows] = dob.astype(BF16)
+            dob = dob.astype(BF16)
+            dobt_ref[mine, rows] = dob
             dobt_ref[others, rows] = dob_other_ref[at(h), rows]
             normed_ref[mine, rows] = (o * inv).astype(BF16)
             normed_ref[others, rows] = (other_ref[at(h), rows] * inv).astype(BF16)
-            ready.append(jnp.where(keep, dob, 0.0).astype(BF16))
+            ready.append(dob)
         return ready
 
     back_state(half, tokens // GROUP, prepare, qd_ref, base, mine_ref)
@@ -653,33 +657,33 @@
     o_own, sb_own, stats = part(True, own, (), "mix_own")
     o_other, sb_other, stats = part(False, other, (stats,), "mix_other")
     stats, kd_late, raw_v = lax.optimization_barrier((stats, kd, raw_v))
-    kt, vd, sb = call(
+    kt, vd, sb, q_back = call(
         later_forms_kernel,
         "later_forms",
-        [(turned, BF16), (full, BF16), (group_states, BF16)],
+        [(turned, BF16), (full, BF16), (group_states, BF16), (full, BF16)],
         [tmp],
-        n_in=4,
-    )(kd_late, raw_v, sb_own, sb_other)
+        n_in=6,
+    )(known_of, kd_late, raw_v, sb_own, sb_other, qd)
     stats = stats + sum(
         lax.ppermute(stats, "head", links_of(k, n_head)) for k in range(1, n_head)
     )
-    stats, kt, vd, sb = lax.optimization_barrier((stats, kt, vd, sb))
+    stats, kt, vd, sb, q_back = lax.optimization_barrier((stats, kt, vd, sb, q_back))
     dob_other, factors, send = call(
         functools.partial(norm_kernel, float(width * n_head)),
         "norm_other",
         [(half_turned, BF16), ((8, tokens), F32), (piece, F32)],
         [],
-        n_in=5,
+        n_in=4,
         flops=mm // 2,
-    )(known_of, stats, o_other, ct, qd)
+    )(stats, o_other, ct, q_back)
     dobt, normed, mine = call(
         merge_kernel,
         "norm_own",
         [(turned, BF16), (turned, BF16), (piece, F32)],
         [],
-        n_in=7,
+        n_in=6,
         flops=mm // 2,
-    )(known_of, factors, o_own, o_other, ct, qd, dob_other)
+    )(factors, o_own, o_other, ct, q_back, dob_other)
     got, total, (dobt_b, normed_b) = exchange(mine, send, back, (dobt, normed))
     cut = max(1, n_groups // 12)
     earlier, later = range(0, cut), range(cut, n_groups)

time: 40.6 us -> 40.5 us (level)
  waiting for transfers between devices: 5.52 us -> 4.81 us
  Pallas kernels: 19.3 us -> 20 us
    ppermute x3, waiting for transfers between devices: 2.22 us -> 1.63 us  [per_device(): lax.ppermute(stats, 'head', links_of(k, n_head))]
    pallas_call x1, Pallas kernels: 1.07 us -> 1.64 us  [per_device(): call(later_forms_kernel, 'later_forms', [(turned, BF16), (full, BF16), (g...]
  transfers between devices with their start and end apart: 13 -> 13, of which waited for: 7 -> 6; matrix products, arithmetic and copies ran while one was open for 0% -> 0% of each run, Pallas kernels for 32% -> 33%
where the time goes in v10:
time: 40.5 us; the launch traced here: 40.3 us
  Pallas kernels  20 us (49%)
  starting transfers between devices  14.4 us (36%)
  waiting for transfers between devices  4.81 us (12%)
  between operations  0.99 us (2%)
    ppermute x6, starting transfers between devices, exchange(): total = total + weights[5 + k] * lax.ppermute(chip_state, 'seq', links)  10.1 us
    pallas_call x2, Pallas kernels, grads(): call(functools.partial(grad_kernel, groups), name, [*left, *kept, (flat,...  6.42 us
    pallas_call x1, Pallas kernels, per_device(): call(local_kernel, 'local_mix', [(full, BF16), (turned, BF16), (turned, B...  3.59 us
    ppermute x3, starting transfers between devices, per_device(): lax.ppermute(stats, 'head', links_of(k, n_head))  3.55 us
    pallas_call x1, Pallas kernels, per_device(): call(functools.partial(state_kernel, n_seq), 'shard_state', [(flat, BF16)...  2.75 us
    pallas_call x1, Pallas kernels, per_device(): call(final_kernel, 'final_grads', [(flat, BF16), (flat, BF16)], [state, t...  2.62 us
    ppermute x6, waiting for transfers between devices, exchange(): total = total + weights[5 + k] * lax.ppermute(chip_state, 'seq', links)  1.65 us
    pallas_call x1, Pallas kernels, per_device(): call(later_forms_kernel, 'later_forms', [(turned, BF16), (full, BF16), (g...  1.64 us
  transfers between devices with their start and end apart: 13, of which 6 were waited for; matrix products, arithmetic and copies ran while one was open for 0% of the time, Pallas kernels for 33%

profile of v10, /device:TPU:0, one launch (start us, length us, event | category | flops | bytes accessed | tf_op | source)
XLA Modules:
  0.0 40.3 jit_solution(9920586123094637774)
XLA Ops:
  0.6 2.8 %shard_state.1 = (bf16[6144,128]{1,0:T(8,128)(2,1)S(1)}, bf16[6144,128]{1,0:T(8,128)(2,1)S(1)}, bf16[256,3072]{1,0:T(8,128)(2,1)S(1)}, f32[1,128,128]{2,1,0:T(8,...) custom-call(s32[6]{0:T(128)} %doc_ref.1, bf16[6144,128]{1,0:T(8,128)(2,1)} %bitcast.48, ...), custom_call_target="tpu_custom_call" | custom-call | flops 201326592 | bytes 8388608 | tf_op jit(solution)/shard_map/shard_state/pallas_call | solution.py:600
  3.4 0.5 %collective-permute-start = (f32[1,128,128]{2,1,0:T(8,128)S(1)}, f32[1,128,128]{2,1,0:T(8,128)S(1)}, u32[]{:S(2)}, u32[]{:S(2)}) collective-permute-start(f32[1,128,128]{2,1,0:T(8,128)S(1)} %get-tuple-element.67), channel_id=1, source_target_pairs={{0,4},{4,0},{8,12},{12,8},{16,20},{20,16},{24,28},{28,24},{1,5},{5... | collective-permute-start | bytes 196616 | tf_op jit(solution)/shard_map/ppermute | solution.py:580
  3.9 0.5 %split_keys.1.kd_ref.k_ref = bf16[3072,256]{1,0:T(8,128)(2,1)S(1)} custom-call(bf16[6144,128]{1,0:T(8,128)(2,1)S(1)} %get-tuple-element.68.pairs_ref), custom_call_target="tpu_custom_call" | custom-call | bytes 8388608 | tf_op jit(solution)/shard_map/split_keys/pallas_call | solution.py:616
  4.8 5.0 %collective-permute-start.3 = (f32[1,128,128]{2,1,0:T(8,128)S(1)}, f32[1,128,128]{2,1,0:T(8,128)S(1)}, u32[]{:S(2)}, u32[]{:S(2)}) collective-permute-start(f32[1,128,128]{2,1,0:T(8,128)S(1)} %multiply_add_fusion.7), channel_id=1, source_target_pairs={{24,0},{28,4},{16,8},{20,12},{8,16},{12,20},{0,24},{4,28},{25,1},{... | collective-permute-start | bytes 196616 | tf_op jit(solution)/shard_map/ppermute | solution.py:588
  9.8 0.6 %collective-permute-start.1 = (f32[1,128,128]{2,1,0:T(8,128)S(1)}, f32[1,128,128]{2,1,0:T(8,128)S(1)}, u32[]{:S(2)}, u32[]{:S(2)}) collective-permute-start(f32[1,128,128]{2,1,0:T(8,128)S(1)} %multiply_add_fusion.7), channel_id=1, source_target_pairs={{8,0},{12,4},{0,8},{4,12},{24,16},{28,20},{16,24},{20,28},{9,1},{1... | collective-permute-start | bytes 196616 | tf_op jit(solution)/shard_map/ppermute | solution.py:588
  10.5 3.6 %local_mix.1 = (bf16[3072,256]{1,0:T(8,128)(2,1)S(1)}, bf16[256,3072]{1,0:T(8,128)(2,1)S(1)}, bf16[256,3072]{1,0:T(8,128)(2,1)S(1)}, bf16[2,3072,256]{2,1,0:T(8,...) custom-call(s32[6]{0:T(128)S(1)} %copy-done.2, ...), custom_call_target="tpu_custom_call" | custom-call | flops 1207959552 | bytes 8388608 | tf_op jit(solution)/shard_map/local_mix/pallas_call | solution.py:625
  14.1 1.6 %collective-permute-done.2 = f32[1,128,128]{2,1,0:T(8,128)S(1)} collective-permute-done((f32[1,128,128]{2,1,0:T(8,128)S(1)}, f32[1,128,128]{2,1,0:T(8,128)S(1)}, u32[]{:S(2)}, u32[]{:S(2)}) %collective-permute-start.2) | collective-permute-done | bytes 65568 | tf_op jit(solution)/shard_map/ppermute | solution.py:588
  15.9 0.6 %mix_own.1 = (f32[128,3072]{1,0:T(8,128)S(1)}, bf16[12,1,128,128]{3,2,1,0:T(8,128)(2,1)S(1)}, f32[2,3072]{1,0:T(2,128)S(1)}) custom-call(s32[8,12,256]{2,1,0:T(8,128)S(1)} %get-tuple-element.72.table_ref.refs_0_, bf16[256,3072]{1,0:T(8,128)(2,1)S(1)} %get-tuple-element.74.qt_ref, f32[256,3072]{1,0:T(8,128)S(1)} %get-tuple-element.77.ol_ref, ...), custom_call_target="tpu_custom_call" | custom-call | flops 100663296 | bytes 8388608 | tf_op jit(solution)/shard_map/mix_own/pallas_call | solution.py:648
  16.5 0.6 %collective-permute-done.4.state_ref = f32[1,128,128]{2,1,0:T(8,128)S(1)} collective-permute-done((f32[1,128,128]{2,1,0:T(8,128)S(1)}, f32[1,128,128]{2,1,0:T(8,128)S(1)}, u32[]{:S(2)}, u32[]{:S(2)}) %collective-permute-start.4) | collective-permute-done | bytes 65568 | tf_op jit(solution)/shard_map/ppermute | solution.py:580
  17.1 0.6 %mix_other.1 = (f32[128,3072]{1,0:T(8,128)S(1)}, bf16[12,1,128,128]{3,2,1,0:T(8,128)(2,1)S(1)}, f32[2,3072]{1,0:T(2,128)S(1)}) custom-call(s32[8,12,256]{2,1,0:T(8,128)S(1)} %get-tuple-element.72.table_ref.refs_0_, bf16[256,3072]{1,0:T(8,128)(2,1)S(1)} %get-tuple-element.74.qt_ref, f32[256,3072]{1,0:T(8,128)S(1)} %get-tuple-element.77.ol_ref, ...), custom_call_target="tpu_custom_call" | custom-call | flops 100663296 | bytes 8388608 | tf_op jit(solution)/shard_map/mix_other/pallas_call | solution.py:648
  17.7 2.5 %collective-permute-start.7 = (f32[2,3072]{1,0:T(2,128)S(1)}, f32[2,3072]{1,0:T(2,128)S(1)}, u32[]{:S(2)}, u32[]{:S(2)}) collective-permute-start(f32[2,3072]{1,0:T(2,128)S(1)} %get-tuple-element.84), channel_id=1, source_target_pairs={{3,0},{2,1},{1,2},{0,3},{7,4},{6,5},{5,6},{4,7},{11,8},{10,9},{9,1... | collective-permute-start | bytes 73736 | tf_op jit(solution)/shard_map/ppermute | solution.py:668
  20.2 0.5 %collective-permute-start.6 = (f32[2,3072]{1,0:T(2,128)S(1)}, f32[2,3072]{1,0:T(2,128)S(1)}, u32[]{:S(2)}, u32[]{:S(2)}) collective-permute-start(f32[2,3072]{1,0:T(2,128)S(1)} %get-tuple-element.84), channel_id=1, source_target_pairs={{2,0},{3,1},{0,2},{1,3},{6,4},{7,5},{4,6},{5,7},{10,8},{11,9},{8,1... | collective-permute-start | bytes 73736 | tf_op jit(solution)/shard_map/ppermute | solution.py:668
  20.7 0.5 %collective-permute-start.5 = (f32[2,3072]{1,0:T(2,128)S(1)}, f32[2,3072]{1,0:T(2,128)S(1)}, u32[]{:S(2)}, u32[]{:S(2)}) collective-permute-start(f32[2,3072]{1,0:T(2,128)S(1)} %get-tuple-element.84), channel_id=1, source_target_pairs={{1,0},{0,1},{3,2},{2,3},{5,4},{4,5},{7,6},{6,7},{9,8},{8,9},{11,10... | collective-permute-start | bytes 73736 | tf_op jit(solution)/shard_map/ppermute | solution.py:668
  21.3 1.6 %later_forms.1 = (bf16[256,3072]{1,0:T(8,128)(2,1)S(1)}, bf16[3072,256]{1,0:T(8,128)(2,1)S(1)}, bf16[12,2,128,128]{3,2,1,0:T(8,128)(2,1)S(1)}, bf16[3072,256]{1,0:T(8,128)(2,1)S(1)}) custom-call(s32[8,12,256]{2,1,0:T(8,128)S(1)} %get-tuple-element.72.table_ref.refs_0_, bf16[3072,256]{1,0:T(8,128)(2,1)S(1)} %split_keys.1.kd_ref.k_ref, ...), custom_call_target="tpu_custom_call" | custom-call | bytes 8388608 | tf_op jit(solution)/shard_map/later_forms/pallas_call | solution.py:660
  22.9 1.1 %collective-permute-done.6 = f32[2,3072]{1,0:T(2,128)S(1)} collective-permute-done((f32[2,3072]{1,0:T(2,128)S(1)}, f32[2,3072]{1,0:T(2,128)S(1)}, u32[]{:S(2)}, u32[]{:S(2)}) %collective-permute-start.6) | collective-permute-done | bytes 24608 | tf_op jit(solution)/shard_map/ppermute | solution.py:668
  24.0 0.5 %collective-permute-done.5 = f32[2,3072]{1,0:T(2,128)S(1)} collective-permute-done((f32[2,3072]{1,0:T(2,128)S(1)}, f32[2,3072]{1,0:T(2,128)S(1)}, u32[]{:S(2)}, u32[]{:S(2)}) %collective-permute-start.5) | collective-permute-done | bytes 24608 | tf_op jit(solution)/shard_map/ppermute | solution.py:668
  24.6 0.6 %norm_other.1 = (bf16[128,3072]{1,0:T(8,128)(2,1)S(1)}, f32[8,3072]{1,0:T(8,128)S(1)}, f32[1,128,128]{2,1,0:T(8,128)S(1)}) custom-call(f32[2,3072]{1,0:T(2,128)S(1)} %add_add_fusion.st_ref, f32[128,3072]{1,0:T(8,128)S(1)} %get-tuple-element.95.o_ref.other_ref, bf16[256,3072]{1,0:T(8,128)(2,1)S(1)} %get-tuple-element.78.ct_ref, ...), custom_call_target="tpu_custom_call" | custom-call | flops 100663296 | bytes 8388608 | tf_op jit(solution)/shard_map/norm_other/pallas_call | solution.py:671
  25.2 0.7 %norm_own.1 = (bf16[256,3072]{1,0:T(8,128)(2,1)S(1)}, bf16[256,3072]{1,0:T(8,128)(2,1)S(1)}, f32[1,128,128]{2,1,0:T(8,128)S(1)}) custom-call(f32[8,3072]{1,0:T(8,128)S(1)} %get-tuple-element.97.rows_ref, f32[128,3072]{1,0:T(8,128)S(1)} %get-tuple-element.98.own_ref, f32[128,3072]{1,0:T(8,128)S(1)} %get-tuple-element.95.o_ref.other_ref, ...), custom_call_target="tpu_custom_call" | custom-call | flops 100663296 | bytes 8388608 | tf_op jit(solution)/shard_map/norm_own/pallas_call | solution.py:679
  26.0 0.5 %collective-permute-done.8 = f32[1,128,128]{2,1,0:T(8,128)S(1)} collective-permute-done((f32[1,128,128]{2,1,0:T(8,128)S(1)}, f32[1,128,128]{2,1,0:T(8,128)S(1)}, u32[]{:S(2)}, u32[]{:S(2)}) %collective-permute-start.8) | collective-permute-done | bytes 65568 | tf_op jit(solution)/shard_map/ppermute | solution.py:580
  26.5 2.5 %collective-permute-start.11 = (f32[1,128,128]{2,1,0:T(8,128)S(1)}, f32[1,128,128]{2,1,0:T(8,128)S(1)}, u32[]{:S(2)}, u32[]{:S(2)}) collective-permute-start(f32[1,128,128]{2,1,0:T(8,128)S(1)} %multiply_add_fusion.3), channel_id=1, source_target_pairs={{24,0},{28,4},{16,8},{20,12},{8,16},{12,20},{0,24},{4,28},{25,1},{... | collective-permute-start | bytes 196616 | tf_op jit(solution)/shard_map/ppermute | solution.py:588
  29.1 1.8 %collective-permute-start.9 = (f32[1,128,128]{2,1,0:T(8,128)S(1)}, f32[1,128,128]{2,1,0:T(8,128)S(1)}, u32[]{:S(2)}, u32[]{:S(2)}) collective-permute-start(f32[1,128,128]{2,1,0:T(8,128)S(1)} %multiply_add_fusion.3), channel_id=1, source_target_pairs={{8,0},{12,4},{0,8},{4,12},{24,16},{28,20},{16,24},{20,28},{9,1},{1... | collective-permute-start | bytes 196616 | tf_op jit(solution)/shard_map/ppermute | solution.py:588
  30.9 5.0 %grads_later.1 = (f32[2,128,128]{2,1,0:T(8,128)S(1)}, f32[2816,256]{1,0:T(8,128)S(1)}, f32[2816,256]{1,0:T(8,128)S(1)}, f32[11,2,128,128]{3,2,1,0:T(8,128)S(1)},...) custom-call(s32[8,12,256]{2,1,0:T(8,128)S(1)} %get-tuple-element.72.table_ref.refs_0_, ...), custom_call_target="tpu_custom_call" | custom-call | flops 2214592512 | bytes 8388608 | tf_op jit(solution)/shard_map/grads_later/pallas_call | solution.py:697
  36.1 1.4 %grads_earlier.1 = (f32[256,256]{1,0:T(8,128)S(1)}, f32[256,256]{1,0:T(8,128)S(1)}, f32[1,2,128,128]{3,2,1,0:T(8,128)S(1)}, bf16[6144,128]{1,0:T(8,128)(2,1)}, bf16[6144,128]{1,0:T(8,128)(2,1)}) custom-call(s32[8,12,256]{2,1,0:T(8,128)S(1)} %get-tuple-element.72.table_ref.refs_0_, ...), custom_call_target="tpu_custom_call", output_to_operand_aliasing={{3}: (9, {}), {4}: (10, {})} | custom-call | flops 201326592 | bytes 8388608 | tf_op jit(solution)/shard_map/grads_earlier/pallas_call | solution.py:697
  37.6 2.6 %final_grads.1 = (bf16[6144,128]{1,0:T(8,128)(2,1)}, bf16[6144,128]{1,0:T(8,128)(2,1)}) custom-call(s32[8,12,256]{2,1,0:T(8,128)S(1)} %get-tuple-element.72.table_ref.refs_0_, bf16[3072,256]{1,0:T(8,128)(2,1)S(1)} %split_keys.1.kd_ref.k_ref, bf16[3072,256]{1,0:T(8,128)(2,1)S(1)} %get-tuple-element.108.refs_6_.vd_ref, ...), custom_call_target="tpu_custom_call" | custom-call | flops 402653184 | bytes 8388608 | tf_op jit(solution)/shard_map/final_grads/pallas_call | solution.py:714
  (28 shorter events, 0.9 us)
Async XLA Ops:
  3.4 1.4 %collective-permute-start = (f32[1,128,128]{2,1,0:T(8,128)S(1)}, f32[1,128,128]{2,1,0:T(8,128)S(1)}, u32[]{:S(2)}, u32[]{:S(2)}) collective-permute-start(f32[1,128,128]{2,1,0:T(8,128)S(1)} %get-tuple-element.67), channel_id=1, source_target_pairs={{0,4},{4,0},{8,12},{12,8},{16,20},{20,16},{24,28},{28,24},{1,5},{5... | collective-permute-start | bytes 196616 | tf_op jit(solution)/shard_map/ppermute | solution.py:580
  3.9 6.6 %copy-start = (bf16[3072,2,128]{2,1,0:T(2,128)(2,1)S(1)}, bf16[3072,2,128]{2,1,0:T(2,128)(2,1)}, u32[]{:S(2)}) copy-start(bf16[3072,2,128]{2,1,0:T(2,128)(2,1)} %param.5) | copy-start | bytes 4718596
  3.9 6.6 %copy-start.1 = (bf16[3072,2,128]{2,1,0:T(2,128)(2,1)S(1)}, bf16[3072,2,128]{2,1,0:T(2,128)(2,1)}, u32[]{:S(2)}) copy-start(bf16[3072,2,128]{2,1,0:T(2,128)(2,1)} %param.8) | copy-start | bytes 4718596
  3.9 6.6 %copy-start.2 = (s32[6]{0:T(128)S(1)}, s32[6]{0:T(128)}, u32[]{:S(2)}) copy-start(s32[6]{0:T(128)} %doc_ref.1) | copy-start | bytes 76
  4.8 9.3 %collective-permute-start.3 = (f32[1,128,128]{2,1,0:T(8,128)S(1)}, f32[1,128,128]{2,1,0:T(8,128)S(1)}, u32[]{:S(2)}, u32[]{:S(2)}) collective-permute-start(f32[1,128,128]{2,1,0:T(8,128)S(1)} %multiply_add_fusion.7), channel_id=1, source_target_pairs={{24,0},{28,4},{16,8},{20,12},{8,16},{12,20},{0,24},{4,28},{25,1},{... | collective-permute-start | bytes 196616 | tf_op jit(solution)/shard_map/ppermute | solution.py:588
  9.8 5.9 %collective-permute-start.2 = (f32[1,128,128]{2,1,0:T(8,128)S(1)}, f32[1,128,128]{2,1,0:T(8,128)S(1)}, u32[]{:S(2)}, u32[]{:S(2)}) collective-permute-start(f32[1,128,128]{2,1,0:T(8,128)S(1)} %multiply_add_fusion.7), channel_id=1, source_target_pairs={{16,0},{20,4},{24,8},{28,12},{0,16},{4,20},{8,24},{12,28},{17,1},{... | collective-permute-start | bytes 196616 | tf_op jit(solution)/shard_map/ppermute | solution.py:588
  9.8 5.9 %collective-permute-start.1 = (f32[1,128,128]{2,1,0:T(8,128)S(1)}, f32[1,128,128]{2,1,0:T(8,128)S(1)}, u32[]{:S(2)}, u32[]{:S(2)}) collective-permute-start(f32[1,128,128]{2,1,0:T(8,128)S(1)} %multiply_add_fusion.7), channel_id=1, source_target_pairs={{8,0},{12,4},{0,8},{4,12},{24,16},{28,20},{16,24},{20,28},{9,1},{1... | collective-permute-start | bytes 196616 | tf_op jit(solution)/shard_map/ppermute | solution.py:588
  15.8 1.3 %collective-permute-start.4 = (f32[1,128,128]{2,1,0:T(8,128)S(1)}, f32[1,128,128]{2,1,0:T(8,128)S(1)}, u32[]{:S(2)}, u32[]{:S(2)}) collective-permute-start(f32[1,128,128]{2,1,0:T(8,128)S(1)} %get-tuple-element.129), channel_id=1, source_target_pairs={{0,4},{4,0},{8,12},{12,8},{16,20},{20,16},{24,28},{28,24},{1,5},{5... | collective-permute-start | bytes 196616 | tf_op jit(solution)/shard_map/ppermute | solution.py:580
  17.7 5.2 %collective-permute-start.7 = (f32[2,3072]{1,0:T(2,128)S(1)}, f32[2,3072]{1,0:T(2,128)S(1)}, u32[]{:S(2)}, u32[]{:S(2)}) collective-permute-start(f32[2,3072]{1,0:T(2,128)S(1)} %get-tuple-element.84), channel_id=1, source_target_pairs={{3,0},{2,1},{1,2},{0,3},{7,4},{6,5},{5,6},{4,7},{11,8},{10,9},{9,1... | collective-permute-start | bytes 73736 | tf_op jit(solution)/shard_map/ppermute | solution.py:668
  20.2 3.8 %collective-permute-start.6 = (f32[2,3072]{1,0:T(2,128)S(1)}, f32[2,3072]{1,0:T(2,128)S(1)}, u32[]{:S(2)}, u32[]{:S(2)}) collective-permute-start(f32[2,3072]{1,0:T(2,128)S(1)} %get-tuple-element.84), channel_id=1, source_target_pairs={{2,0},{3,1},{0,2},{1,3},{6,4},{7,5},{4,6},{5,7},{10,8},{11,9},{8,1... | collective-permute-start | bytes 73736 | tf_op jit(solution)/shard_map/ppermute | solution.py:668
  20.7 3.8 %collective-permute-start.5 = (f32[2,3072]{1,0:T(2,128)S(1)}, f32[2,3072]{1,0:T(2,128)S(1)}, u32[]{:S(2)}, u32[]{:S(2)}) collective-permute-start(f32[2,3072]{1,0:T(2,128)S(1)} %get-tuple-element.84), channel_id=1, source_target_pairs={{1,0},{0,1},{3,2},{2,3},{5,4},{4,5},{7,6},{6,7},{9,8},{8,9},{11,10... | collective-permute-start | bytes 73736 | tf_op jit(solution)/shard_map/ppermute | solution.py:668
  25.2 1.3 %collective-permute-start.8 = (f32[1,128,128]{2,1,0:T(8,128)S(1)}, f32[1,128,128]{2,1,0:T(8,128)S(1)}, u32[]{:S(2)}, u32[]{:S(2)}) collective-permute-start(f32[1,128,128]{2,1,0:T(8,128)S(1)} %get-tuple-element.101), channel_id=1, source_target_pairs={{0,4},{4,0},{8,12},{12,8},{16,20},{20,16},{24,28},{28,24},{1,5},{5... | collective-permute-start | bytes 196616 | tf_op jit(solution)/shard_map/ppermute | solution.py:580
  26.5 9.5 %collective-permute-start.11 = (f32[1,128,128]{2,1,0:T(8,128)S(1)}, f32[1,128,128]{2,1,0:T(8,128)S(1)}, u32[]{:S(2)}, u32[]{:S(2)}) collective-permute-start(f32[1,128,128]{2,1,0:T(8,128)S(1)} %multiply_add_fusion.3), channel_id=1, source_target_pairs={{24,0},{28,4},{16,8},{20,12},{8,16},{12,20},{0,24},{4,28},{25,1},{... | collective-permute-start | bytes 196616 | tf_op jit(solution)/shard_map/ppermute | solution.py:588
  29.0 7.0 %collective-permute-start.10 = (f32[1,128,128]{2,1,0:T(8,128)S(1)}, f32[1,128,128]{2,1,0:T(8,128)S(1)}, u32[]{:S(2)}, u32[]{:S(2)}) collective-permute-start(f32[1,128,128]{2,1,0:T(8,128)S(1)} %multiply_add_fusion.3), channel_id=1, source_target_pairs={{16,0},{20,4},{24,8},{28,12},{0,16},{4,20},{8,24},{12,28},{17,1},{... | collective-permute-start | bytes 196616 | tf_op jit(solution)/shard_map/ppermute | solution.py:588
  29.1 6.9 %collective-permute-start.9 = (f32[1,128,128]{2,1,0:T(8,128)S(1)}, f32[1,128,128]{2,1,0:T(8,128)S(1)}, u32[]{:S(2)}, u32[]{:S(2)}) collective-permute-start(f32[1,128,128]{2,1,0:T(8,128)S(1)} %multiply_add_fusion.3), channel_id=1, source_target_pairs={{8,0},{12,4},{0,8},{4,12},{24,16},{28,20},{16,24},{20,28},{9,1},{1... | collective-permute-start | bytes 196616 | tf_op jit(solution)/shard_map/ppermute | solution.py:588
  36.1 1.5 %collective-permute-start.12 = (f32[1,128,128]{2,1,0:T(8,128)S(1)}, f32[1,128,128]{2,1,0:T(8,128)S(1)}, u32[]{:S(2)}, u32[]{:S(2)}) collective-permute-start(f32[1,128,128]{2,1,0:T(8,128)S(1)} %get-tuple-element.126), channel_id=1, source_target_pairs={{0,4},{4,0},{8,12},{12,8},{16,20},{20,16},{24,28},{28,24},{1,5},{5... | collective-permute-start | bytes 196616 | tf_op jit(solution)/shard_map/ppermute | solution.py:580

commit v11 on v10

--- a/solution.py
+++ b/solution.py
@@ -201,14 +201,14 @@
         for copy in fetches(g):
             copy.wait()
         rows = group_rows(g)
-        keep = rows_iota(128) + g * GROUP >= tail
+        keep = jnp.where(lanes_iota(1) + g * GROUP >= tail, 1.0, 0.0).astype(BF16)
         ks = split_heads(bufk, tmpk, g, heads)
         vs = split_heads(bufv, tmpv, g, heads)
         ready = []
         for h in range(heads):
             vt = turn(vs[h])
             vt_ref[at(h), rows] = vt
-            ready.append((vt, jnp.where(keep, ks[h], 0.0).astype(BF16)))
+            ready.append((vt * keep, ks[h].astype(BF16)))
         return ready
 
     total = [jnp.zeros((128, 128), F32) for _ in range(heads)]

time: 40.5 us -> 40.5 us (level)
  no operation moved by 1% of the time
where the time goes in v11:
time: 40.5 us; the launch traced here: 40.3 us
  Pallas kernels  19.9 us (49%)
  starting transfers between devices  14.4 us (36%)
  waiting for transfers between devices  4.82 us (12%)
  between operations  0.99 us (2%)
    ppermute x6, starting transfers between devices, exchange(): total = total + weights[5 + k] * lax.ppermute(chip_state, 'seq', links)  10.1 us
    pallas_call x2, Pallas kernels, grads(): call(functools.partial(grad_kernel, groups), name, [*left, *kept, (flat,...  6.42 us
    pallas_call x1, Pallas kernels, per_device(): call(local_kernel, 'local_mix', [(full, BF16), (turned, BF16), (turned, B...  3.58 us
    ppermute x3, starting transfers between devices, per_device(): lax.ppermute(stats, 'head', links_of(k, n_head))  3.55 us
    pallas_call x1, Pallas kernels, per_device(): call(functools.partial(state_kernel, n_seq), 'shard_state', [(flat, BF16)...  2.69 us
    pallas_call x1, Pallas kernels, per_device(): call(final_kernel, 'final_grads', [(flat, BF16), (flat, BF16)], [state, t...  2.62 us
    ppermute x6, waiting for transfers between devices, exchange(): total = total + weights[5 + k] * lax.ppermute(chip_state, 'seq', links)  1.65 us
    pallas_call x1, Pallas kernels, per_device(): call(later_forms_kernel, 'later_forms', [(turned, BF16), (full, BF16), (g...  1.64 us
  transfers between devices with their start and end apart: 13, of which 6 were waited for; matrix products, arithmetic and copies ran while one was open for 0% of the time, Pallas kernels for 33%

profile of v11, /device:TPU:0, one launch (start us, length us, event | category | flops | bytes accessed | tf_op | source)
XLA Modules:
  0.0 40.3 jit_solution(939781554567707111)
XLA Ops:
  0.6 2.7 %shard_state.1 = (bf16[6144,128]{1,0:T(8,128)(2,1)S(1)}, bf16[6144,128]{1,0:T(8,128)(2,1)S(1)}, bf16[256,3072]{1,0:T(8,128)(2,1)S(1)}, f32[1,128,128]{2,1,0:T(8,...) custom-call(s32[6]{0:T(128)} %doc_ref.1, bf16[6144,128]{1,0:T(8,128)(2,1)} %bitcast.48, ...), custom_call_target="tpu_custom_call" | custom-call | flops 201326592 | bytes 8388608 | tf_op jit(solution)/shard_map/shard_state/pallas_call | solution.py:600
  3.3 0.5 %collective-permute-start = (f32[1,128,128]{2,1,0:T(8,128)S(1)}, f32[1,128,128]{2,1,0:T(8,128)S(1)}, u32[]{:S(2)}, u32[]{:S(2)}) collective-permute-start(f32[1,128,128]{2,1,0:T(8,128)S(1)} %get-tuple-element.67), channel_id=1, source_target_pairs={{0,4},{4,0},{8,12},{12,8},{16,20},{20,16},{24,28},{28,24},{1,5},{5... | collective-permute-start | bytes 196616 | tf_op jit(solution)/shard_map/ppermute | solution.py:580
  3.9 0.5 %split_keys.1.kd_ref.k_ref = bf16[3072,256]{1,0:T(8,128)(2,1)S(1)} custom-call(bf16[6144,128]{1,0:T(8,128)(2,1)S(1)} %get-tuple-element.68.pairs_ref), custom_call_target="tpu_custom_call" | custom-call | bytes 8388608 | tf_op jit(solution)/shard_map/split_keys/pallas_call | solution.py:616
  4.8 5.0 %collective-permute-start.3 = (f32[1,128,128]{2,1,0:T(8,128)S(1)}, f32[1,128,128]{2,1,0:T(8,128)S(1)}, u32[]{:S(2)}, u32[]{:S(2)}) collective-permute-start(f32[1,128,128]{2,1,0:T(8,128)S(1)} %multiply_add_fusion.7), channel_id=1, source_target_pairs={{24,0},{28,4},{16,8},{20,12},{8,16},{12,20},{0,24},{4,28},{25,1},{... | collective-permute-start | bytes 196616 | tf_op jit(solution)/shard_map/ppermute | solution.py:588
  9.8 0.6 %collective-permute-start.1 = (f32[1,128,128]{2,1,0:T(8,128)S(1)}, f32[1,128,128]{2,1,0:T(8,128)S(1)}, u32[]{:S(2)}, u32[]{:S(2)}) collective-permute-start(f32[1,128,128]{2,1,0:T(8,128)S(1)} %multiply_add_fusion.7), channel_id=1, source_target_pairs={{8,0},{12,4},{0,8},{4,12},{24,16},{28,20},{16,24},{20,28},{9,1},{1... | collective-permute-start | bytes 196616 | tf_op jit(solution)/shard_map/ppermute | solution.py:588
  10.4 3.6 %local_mix.1 = (bf16[3072,256]{1,0:T(8,128)(2,1)S(1)}, bf16[256,3072]{1,0:T(8,128)(2,1)S(1)}, bf16[256,3072]{1,0:T(8,128)(2,1)S(1)}, bf16[2,3072,256]{2,1,0:T(8,...) custom-call(s32[6]{0:T(128)S(1)} %copy-done.2, ...), custom_call_target="tpu_custom_call" | custom-call | flops 1207959552 | bytes 8388608 | tf_op jit(solution)/shard_map/local_mix/pallas_call | solution.py:625
  14.0 1.6 %collective-permute-done.2 = f32[1,128,128]{2,1,0:T(8,128)S(1)} collective-permute-done((f32[1,128,128]{2,1,0:T(8,128)S(1)}, f32[1,128,128]{2,1,0:T(8,128)S(1)}, u32[]{:S(2)}, u32[]{:S(2)}) %collective-permute-start.2) | collective-permute-done | bytes 65568 | tf_op jit(solution)/shard_map/ppermute | solution.py:588
  15.8 0.6 %mix_own.1 = (f32[128,3072]{1,0:T(8,128)S(1)}, bf16[12,1,128,128]{3,2,1,0:T(8,128)(2,1)S(1)}, f32[2,3072]{1,0:T(2,128)S(1)}) custom-call(s32[8,12,256]{2,1,0:T(8,128)S(1)} %get-tuple-element.72.table_ref.refs_0_, bf16[256,3072]{1,0:T(8,128)(2,1)S(1)} %get-tuple-element.74.qt_ref, f32[256,3072]{1,0:T(8,128)S(1)} %get-tuple-element.77.ol_ref, ...), custom_call_target="tpu_custom_call" | custom-call | flops 100663296 | bytes 8388608 | tf_op jit(solution)/shard_map/mix_own/pallas_call | solution.py:648
  16.4 0.6 %collective-permute-done.4.state_ref = f32[1,128,128]{2,1,0:T(8,128)S(1)} collective-permute-done((f32[1,128,128]{2,1,0:T(8,128)S(1)}, f32[1,128,128]{2,1,0:T(8,128)S(1)}, u32[]{:S(2)}, u32[]{:S(2)}) %collective-permute-start.4) | collective-permute-done | bytes 65568 | tf_op jit(solution)/shard_map/ppermute | solution.py:580
  17.0 0.6 %mix_other.1 = (f32[128,3072]{1,0:T(8,128)S(1)}, bf16[12,1,128,128]{3,2,1,0:T(8,128)(2,1)S(1)}, f32[2,3072]{1,0:T(2,128)S(1)}) custom-call(s32[8,12,256]{2,1,0:T(8,128)S(1)} %get-tuple-element.72.table_ref.refs_0_, bf16[256,3072]{1,0:T(8,128)(2,1)S(1)} %get-tuple-element.74.qt_ref, f32[256,3072]{1,0:T(8,128)S(1)} %get-tuple-element.77.ol_ref, ...), custom_call_target="tpu_custom_call" | custom-call | flops 100663296 | bytes 8388608 | tf_op jit(solution)/shard_map/mix_other/pallas_call | solution.py:648
  17.6 2.5 %collective-permute-start.7 = (f32[2,3072]{1,0:T(2,128)S(1)}, f32[2,3072]{1,0:T(2,128)S(1)}, u32[]{:S(2)}, u32[]{:S(2)}) collective-permute-start(f32[2,3072]{1,0:T(2,128)S(1)} %get-tuple-element.84), channel_id=1, source_target_pairs={{3,0},{2,1},{1,2},{0,3},{7,4},{6,5},{5,6},{4,7},{11,8},{10,9},{9,1... | collective-permute-start | bytes 73736 | tf_op jit(solution)/shard_map/ppermute | solution.py:668
  20.1 0.5 %collective-permute-start.6 = (f32[2,3072]{1,0:T(2,128)S(1)}, f32[2,3072]{1,0:T(2,128)S(1)}, u32[]{:S(2)}, u32[]{:S(2)}) collective-permute-start(f32[2,3072]{1,0:T(2,128)S(1)} %get-tuple-element.84), channel_id=1, source_target_pairs={{2,0},{3,1},{0,2},{1,3},{6,4},{7,5},{4,6},{5,7},{10,8},{11,9},{8,1... | collective-permute-start | bytes 73736 | tf_op jit(solution)/shard_map/ppermute | solution.py:668
  20.6 0.5 %collective-permute-start.5 = (f32[2,3072]{1,0:T(2,128)S(1)}, f32[2,3072]{1,0:T(2,128)S(1)}, u32[]{:S(2)}, u32[]{:S(2)}) collective-permute-start(f32[2,3072]{1,0:T(2,128)S(1)} %get-tuple-element.84), channel_id=1, source_target_pairs={{1,0},{0,1},{3,2},{2,3},{5,4},{4,5},{7,6},{6,7},{9,8},{8,9},{11,10... | collective-permute-start | bytes 73736 | tf_op jit(solution)/shard_map/ppermute | solution.py:668
  21.2 1.6 %later_forms.1 = (bf16[256,3072]{1,0:T(8,128)(2,1)S(1)}, bf16[3072,256]{1,0:T(8,128)(2,1)S(1)}, bf16[12,2,128,128]{3,2,1,0:T(8,128)(2,1)S(1)}, bf16[3072,256]{1,0:T(8,128)(2,1)S(1)}) custom-call(s32[8,12,256]{2,1,0:T(8,128)S(1)} %get-tuple-element.72.table_ref.refs_0_, bf16[3072,256]{1,0:T(8,128)(2,1)S(1)} %split_keys.1.kd_ref.k_ref, ...), custom_call_target="tpu_custom_call" | custom-call | bytes 8388608 | tf_op jit(solution)/shard_map/later_forms/pallas_call | solution.py:660
  22.8 1.1 %collective-permute-done.6 = f32[2,3072]{1,0:T(2,128)S(1)} collective-permute-done((f32[2,3072]{1,0:T(2,128)S(1)}, f32[2,3072]{1,0:T(2,128)S(1)}, u32[]{:S(2)}, u32[]{:S(2)}) %collective-permute-start.6) | collective-permute-done | bytes 24608 | tf_op jit(solution)/shard_map/ppermute | solution.py:668
  24.0 0.5 %collective-permute-done.5 = f32[2,3072]{1,0:T(2,128)S(1)} collective-permute-done((f32[2,3072]{1,0:T(2,128)S(1)}, f32[2,3072]{1,0:T(2,128)S(1)}, u32[]{:S(2)}, u32[]{:S(2)}) %collective-permute-start.5) | collective-permute-done | bytes 24608 | tf_op jit(solution)/shard_map/ppermute | solution.py:668
  24.5 0.6 %norm_other.1 = (bf16[128,3072]{1,0:T(8,128)(2,1)S(1)}, f32[8,3072]{1,0:T(8,128)S(1)}, f32[1,128,128]{2,1,0:T(8,128)S(1)}) custom-call(f32[2,3072]{1,0:T(2,128)S(1)} %add_add_fusion.st_ref, f32[128,3072]{1,0:T(8,128)S(1)} %get-tuple-element.95.o_ref.other_ref, bf16[256,3072]{1,0:T(8,128)(2,1)S(1)} %get-tuple-element.78.ct_ref, ...), custom_call_target="tpu_custom_call" | custom-call | flops 100663296 | bytes 8388608 | tf_op jit(solution)/shard_map/norm_other/pallas_call | solution.py:671
  25.2 0.7 %norm_own.1 = (bf16[256,3072]{1,0:T(8,128)(2,1)S(1)}, bf16[256,3072]{1,0:T(8,128)(2,1)S(1)}, f32[1,128,128]{2,1,0:T(8,128)S(1)}) custom-call(f32[8,3072]{1,0:T(8,128)S(1)} %get-tuple-element.97.rows_ref, f32[128,3072]{1,0:T(8,128)S(1)} %get-tuple-element.98.own_ref, f32[128,3072]{1,0:T(8,128)S(1)} %get-tuple-element.95.o_ref.other_ref, ...), custom_call_target="tpu_custom_call" | custom-call | flops 100663296 | bytes 8388608 | tf_op jit(solution)/shard_map/norm_own/pallas_call | solution.py:679
  25.9 0.5 %collective-permute-done.8 = f32[1,128,128]{2,1,0:T(8,128)S(1)} collective-permute-done((f32[1,128,128]{2,1,0:T(8,128)S(1)}, f32[1,128,128]{2,1,0:T(8,128)S(1)}, u32[]{:S(2)}, u32[]{:S(2)}) %collective-permute-start.8) | collective-permute-done | bytes 65568 | tf_op jit(solution)/shard_map/ppermute | solution.py:580
  26.4 2.5 %collective-permute-start.11 = (f32[1,128,128]{2,1,0:T(8,128)S(1)}, f32[1,128,128]{2,1,0:T(8,128)S(1)}, u32[]{:S(2)}, u32[]{:S(2)}) collective-permute-start(f32[1,128,128]{2,1,0:T(8,128)S(1)} %multiply_add_fusion.3), channel_id=1, source_target_pairs={{24,0},{28,4},{16,8},{20,12},{8,16},{12,20},{0,24},{4,28},{25,1},{... | collective-permute-start | bytes 196616 | tf_op jit(solution)/shard_map/ppermute | solution.py:588
  29.1 1.8 %collective-permute-start.9 = (f32[1,128,128]{2,1,0:T(8,128)S(1)}, f32[1,128,128]{2,1,0:T(8,128)S(1)}, u32[]{:S(2)}, u32[]{:S(2)}) collective-permute-start(f32[1,128,128]{2,1,0:T(8,128)S(1)} %multiply_add_fusion.3), channel_id=1, source_target_pairs={{8,0},{12,4},{0,8},{4,12},{24,16},{28,20},{16,24},{20,28},{9,1},{1... | collective-permute-start | bytes 196616 | tf_op jit(solution)/shard_map/ppermute | solution.py:588
  30.9 5.0 %grads_later.1 = (f32[2,128,128]{2,1,0:T(8,128)S(1)}, f32[2816,256]{1,0:T(8,128)S(1)}, f32[2816,256]{1,0:T(8,128)S(1)}, f32[11,2,128,128]{3,2,1,0:T(8,128)S(1)},...) custom-call(s32[8,12,256]{2,1,0:T(8,128)S(1)} %get-tuple-element.72.table_ref.refs_0_, ...), custom_call_target="tpu_custom_call" | custom-call | flops 2214592512 | bytes 8388608 | tf_op jit(solution)/shard_map/grads_later/pallas_call | solution.py:697
  36.1 1.4 %grads_earlier.1 = (f32[256,256]{1,0:T(8,128)S(1)}, f32[256,256]{1,0:T(8,128)S(1)}, f32[1,2,128,128]{3,2,1,0:T(8,128)S(1)}, bf16[6144,128]{1,0:T(8,128)(2,1)}, bf16[6144,128]{1,0:T(8,128)(2,1)}) custom-call(s32[8,12,256]{2,1,0:T(8,128)S(1)} %get-tuple-element.72.table_ref.refs_0_, ...), custom_call_target="tpu_custom_call", output_to_operand_aliasing={{3}: (9, {}), {4}: (10, {})} | custom-call | flops 201326592 | bytes 8388608 | tf_op jit(solution)/shard_map/grads_earlier/pallas_call | solution.py:697
  37.5 2.6 %final_grads.1 = (bf16[6144,128]{1,0:T(8,128)(2,1)}, bf16[6144,128]{1,0:T(8,128)(2,1)}) custom-call(s32[8,12,256]{2,1,0:T(8,128)S(1)} %get-tuple-element.72.table_ref.refs_0_, bf16[3072,256]{1,0:T(8,128)(2,1)S(1)} %split_keys.1.kd_ref.k_ref, bf16[3072,256]{1,0:T(8,128)(2,1)S(1)} %get-tuple-element.108.refs_6_.vd_ref, ...), custom_call_target="tpu_custom_call" | custom-call | flops 402653184 | bytes 8388608 | tf_op jit(solution)/shard_map/final_grads/pallas_call | solution.py:714
  (28 shorter events, 0.9 us)
Async XLA Ops:
  3.3 1.4 %collective-permute-start = (f32[1,128,128]{2,1,0:T(8,128)S(1)}, f32[1,128,128]{2,1,0:T(8,128)S(1)}, u32[]{:S(2)}, u32[]{:S(2)}) collective-permute-start(f32[1,128,128]{2,1,0:T(8,128)S(1)} %get-tuple-element.67), channel_id=1, source_target_pairs={{0,4},{4,0},{8,12},{12,8},{16,20},{20,16},{24,28},{28,24},{1,5},{5... | collective-permute-start | bytes 196616 | tf_op jit(solution)/shard_map/ppermute | solution.py:580
  3.8 6.6 %copy-start = (bf16[3072,2,128]{2,1,0:T(2,128)(2,1)S(1)}, bf16[3072,2,128]{2,1,0:T(2,128)(2,1)}, u32[]{:S(2)}) copy-start(bf16[3072,2,128]{2,1,0:T(2,128)(2,1)} %param.5) | copy-start | bytes 4718596
  3.8 6.6 %copy-start.1 = (bf16[3072,2,128]{2,1,0:T(2,128)(2,1)S(1)}, bf16[3072,2,128]{2,1,0:T(2,128)(2,1)}, u32[]{:S(2)}) copy-start(bf16[3072,2,128]{2,1,0:T(2,128)(2,1)} %param.8) | copy-start | bytes 4718596
  3.9 6.6 %copy-start.2 = (s32[6]{0:T(128)S(1)}, s32[6]{0:T(128)}, u32[]{:S(2)}) copy-start(s32[6]{0:T(128)} %doc_ref.1) | copy-start | bytes 76
  4.8 9.3 %collective-permute-start.3 = (f32[1,128,128]{2,1,0:T(8,128)S(1)}, f32[1,128,128]{2,1,0:T(8,128)S(1)}, u32[]{:S(2)}, u32[]{:S(2)}) collective-permute-start(f32[1,128,128]{2,1,0:T(8,128)S(1)} %multiply_add_fusion.7), channel_id=1, source_target_pairs={{24,0},{28,4},{16,8},{20,12},{8,16},{12,20},{0,24},{4,28},{25,1},{... | collective-permute-start | bytes 196616 | tf_op jit(solution)/shard_map/ppermute | solution.py:588
  9.8 5.9 %collective-permute-start.2 = (f32[1,128,128]{2,1,0:T(8,128)S(1)}, f32[1,128,128]{2,1,0:T(8,128)S(1)}, u32[]{:S(2)}, u32[]{:S(2)}) collective-permute-start(f32[1,128,128]{2,1,0:T(8,128)S(1)} %multiply_add_fusion.7), channel_id=1, source_target_pairs={{16,0},{20,4},{24,8},{28,12},{0,16},{4,20},{8,24},{12,28},{17,1},{... | collective-permute-start | bytes 196616 | tf_op jit(solution)/shard_map/ppermute | solution.py:588
  9.8 5.9 %collective-permute-start.1 = (f32[1,128,128]{2,1,0:T(8,128)S(1)}, f32[1,128,128]{2,1,0:T(8,128)S(1)}, u32[]{:S(2)}, u32[]{:S(2)}) collective-permute-start(f32[1,128,128]{2,1,0:T(8,128)S(1)} %multiply_add_fusion.7), channel_id=1, source_target_pairs={{8,0},{12,4},{0,8},{4,12},{24,16},{28,20},{16,24},{20,28},{9,1},{1... | collective-permute-start | bytes 196616 | tf_op jit(solution)/shard_map/ppermute | solution.py:588
  15.7 1.3 %collective-permute-start.4 = (f32[1,128,128]{2,1,0:T(8,128)S(1)}, f32[1,128,128]{2,1,0:T(8,128)S(1)}, u32[]{:S(2)}, u32[]{:S(2)}) collective-permute-start(f32[1,128,128]{2,1,0:T(8,128)S(1)} %get-tuple-element.129), channel_id=1, source_target_pairs={{0,4},{4,0},{8,12},{12,8},{16,20},{20,16},{24,28},{28,24},{1,5},{5... | collective-permute-start | bytes 196616 | tf_op jit(solution)/shard_map/ppermute | solution.py:580
  17.6 5.2 %collective-permute-start.7 = (f32[2,3072]{1,0:T(2,128)S(1)}, f32[2,3072]{1,0:T(2,128)S(1)}, u32[]{:S(2)}, u32[]{:S(2)}) collective-permute-start(f32[2,3072]{1,0:T(2,128)S(1)} %get-tuple-element.84), channel_id=1, source_target_pairs={{3,0},{2,1},{1,2},{0,3},{7,4},{6,5},{5,6},{4,7},{11,8},{10,9},{9,1... | collective-permute-start | bytes 73736 | tf_op jit(solution)/shard_map/ppermute | solution.py:668
  20.1 3.8 %collective-permute-start.6 = (f32[2,3072]{1,0:T(2,128)S(1)}, f32[2,3072]{1,0:T(2,128)S(1)}, u32[]{:S(2)}, u32[]{:S(2)}) collective-permute-start(f32[2,3072]{1,0:T(2,128)S(1)} %get-tuple-element.84), channel_id=1, source_target_pairs={{2,0},{3,1},{0,2},{1,3},{6,4},{7,5},{4,6},{5,7},{10,8},{11,9},{8,1... | collective-permute-start | bytes 73736 | tf_op jit(solution)/shard_map/ppermute | solution.py:668
  20.6 3.8 %collective-permute-start.5 = (f32[2,3072]{1,0:T(2,128)S(1)}, f32[2,3072]{1,0:T(2,128)S(1)}, u32[]{:S(2)}, u32[]{:S(2)}) collective-permute-start(f32[2,3072]{1,0:T(2,128)S(1)} %get-tuple-element.84), channel_id=1, source_target_pairs={{1,0},{0,1},{3,2},{2,3},{5,4},{4,5},{7,6},{6,7},{9,8},{8,9},{11,10... | collective-permute-start | bytes 73736 | tf_op jit(solution)/shard_map/ppermute | solution.py:668
  25.1 1.3 %collective-permute-start.8 = (f32[1,128,128]{2,1,0:T(8,128)S(1)}, f32[1,128,128]{2,1,0:T(8,128)S(1)}, u32[]{:S(2)}, u32[]{:S(2)}) collective-permute-start(f32[1,128,128]{2,1,0:T(8,128)S(1)} %get-tuple-element.101), channel_id=1, source_target_pairs={{0,4},{4,0},{8,12},{12,8},{16,20},{20,16},{24,28},{28,24},{1,5},{5... | collective-permute-start | bytes 196616 | tf_op jit(solution)/shard_map/ppermute | solution.py:580
  26.4 9.5 %collective-permute-start.11 = (f32[1,128,128]{2,1,0:T(8,128)S(1)}, f32[1,128,128]{2,1,0:T(8,128)S(1)}, u32[]{:S(2)}, u32[]{:S(2)}) collective-permute-start(f32[1,128,128]{2,1,0:T(8,128)S(1)} %multiply_add_fusion.3), channel_id=1, source_target_pairs={{24,0},{28,4},{16,8},{20,12},{8,16},{12,20},{0,24},{4,28},{25,1},{... | collective-permute-start | bytes 196616 | tf_op jit(solution)/shard_map/ppermute | solution.py:588
  29.0 7.0 %collective-permute-start.10 = (f32[1,128,128]{2,1,0:T(8,128)S(1)}, f32[1,128,128]{2,1,0:T(8,128)S(1)}, u32[]{:S(2)}, u32[]{:S(2)}) collective-permute-start(f32[1,128,128]{2,1,0:T(8,128)S(1)} %multiply_add_fusion.3), channel_id=1, source_target_pairs={{16,0},{20,4},{24,8},{28,12},{0,16},{4,20},{8,24},{12,28},{17,1},{... | collective-permute-start | bytes 196616 | tf_op jit(solution)/shard_map/ppermute | solution.py:588
  29.1 6.9 %collective-permute-start.9 = (f32[1,128,128]{2,1,0:T(8,128)S(1)}, f32[1,128,128]{2,1,0:T(8,128)S(1)}, u32[]{:S(2)}, u32[]{:S(2)}) collective-permute-start(f32[1,128,128]{2,1,0:T(8,128)S(1)} %multiply_add_fusion.3), channel_id=1, source_target_pairs={{8,0},{12,4},{0,8},{4,12},{24,16},{28,20},{16,24},{20,28},{9,1},{1... | collective-permute-start | bytes 196616 | tf_op jit(solution)/shard_map/ppermute | solution.py:588
  36.0 1.5 %collective-permute-start.12 = (f32[1,128,128]{2,1,0:T(8,128)S(1)}, f32[1,128,128]{2,1,0:T(8,128)S(1)}, u32[]{:S(2)}, u32[]{:S(2)}) collective-permute-start(f32[1,128,128]{2,1,0:T(8,128)S(1)} %get-tuple-element.126), channel_id=1, source_target_pairs={{0,4},{4,0},{8,12},{12,8},{16,20},{20,16},{24,28},{28,24},{1,5},{5... | collective-permute-start | bytes 196616 | tf_op jit(solution)/shard_map/ppermute | solution.py:580
